TPU v7x, 256 devices: a whole 4x4x8 slice. The times are simulated.
256 devices in a mesh: blk: 8 (over y, x_lo), fsdp: 32 (over x_hi, z, core).
Axes of the slice: x: 4 (x_hi: 2, x_lo: 2; x = x_hi * 2 + x_lo), y: 4, z: 8, core: 2. Of those that a mesh axis runs over, the one named last changes fastest.
Arguments:
- hidden: bfloat16 [131072, 8192], P(('blk', 'fsdp')), may hold values from -24 to 24
- gain: bfloat16 [8, 8192], P('blk', 'fsdp'), may hold values from 0.099609375 to 1.8984375
- value_weight: bfloat16 [8, 8192, 512], P('blk', 'fsdp'), may hold values from -0.0625 to 0.0625
- cotangent: bfloat16 [131072, 512], P(('blk', 'fsdp')), may hold values from -0.059814453 to 0.059814453
- grad_weight_in: float32 [8, 8192, 512], P('blk', 'fsdp'), may hold values from -6 to 6
- grad_gain_in: float32 [8, 8192], P('blk', 'fsdp'), may hold values from -1.8 to 1.8
Outputs:
- values: bfloat16 [131072, 512], P(('blk', 'fsdp'))
- grad_weight: float32 [8, 8192, 512], P('blk', 'fsdp')
- grad_gain: float32 [8, 8192], P('blk', 'fsdp')
All inputs are finite; a program needn't handle non-finite values.
Results may differ from a plain program's by a relative error of at most 0.018.
Values may be sent and summed in bfloat16 or wider, within the bound.
No kernel may reach another device: no remote copies, remote signals or barrier semaphores. Data moves between devices by JAX's collectives and lax.ppermute only.
A program may use at most 128 MiB of HBM per device.

v0:
```python
import jax
import jax.numpy as jnp
from jax import lax
from jax.sharding import PartitionSpec as P


def from_behind(value, axis, steps):
    count = lax.axis_size(axis)
    pairs = [(source, (source + steps) % count) for source in range(count)]
    return lax.ppermute(value, axis, pairs)


def per_device(hidden, gain, value_weight, cotangent, grad_weight_in, grad_gain_in):
    local_w, local_g = (
        lax.all_gather(value_weight, "fsdp", axis=1, tiled=True),
        lax.all_gather(gain, "fsdp", axis=1, tiled=True),
    )
    full_w, full_g = from_behind((local_w, local_g), "blk", 1)
    weight = full_w[0]
    rows = hidden.astype(jnp.float32)
    normed = rows * lax.rsqrt(jnp.mean(rows * rows, axis=-1, keepdims=True) + 1e-05)
    scaled = (normed * full_g[0].astype(jnp.float32)).astype(jnp.bfloat16)
    values = jnp.dot(scaled, weight, preferred_element_type=jnp.float32).astype(jnp.bfloat16)
    back = lax.dot_general(
        cotangent, weight, (((1,), (1,)), ((), ())), preferred_element_type=jnp.float32
    )
    gain_terms = jnp.sum(back * normed, axis=0)
    weight_share = lax.psum_scatter(
        lax.dot_general(
            scaled, cotangent, (((0,), (0,)), ((), ())), preferred_element_type=jnp.float32
        ).astype(jnp.bfloat16),
        "fsdp",
        scatter_dimension=0,
        tiled=True,
    ).astype(jnp.float32)
    gain_share = lax.psum_scatter(
        gain_terms[None, :].astype(jnp.bfloat16), "fsdp", scatter_dimension=1, tiled=True
    ).astype(jnp.float32)
    back_w, back_g = (
        from_behind(weight_share[None].astype(jnp.bfloat16), "blk", -1).astype(jnp.float32),
        from_behind(gain_share.astype(jnp.bfloat16), "blk", -1).astype(gain_share.dtype),
    )
    return (values, grad_weight_in + back_w, grad_gain_in + back_g)


def solution(mesh):
    return jax.shard_map(
        per_device,
        mesh=mesh,
        in_specs=(
            P(("blk", "fsdp"), None),
            P("blk", "fsdp"),
            P("blk", "fsdp", None),
            P(("blk", "fsdp"), None),
            P("blk", "fsdp", None),
            P("blk", "fsdp"),
        ),
        out_specs=(P(("blk", "fsdp"), None), P("blk", "fsdp", None), P("blk", "fsdp")),
        check_vma=False,
    )
```

profile of v0, /device:TPU:4, one launch (start us, length us, event | category | flops | bytes accessed | tf_op | source)
XLA Modules:
  0.0 473.5 jit_solution(12306534163197769348)
XLA Ops:
  7.2 0.0 copy-start
  7.2 0.0 all-gather.2.cloned.1.call-start
  7.2 0.7 all-gather.2.cloned.1.call-update
  7.9 0.0 reduce-scatter.5.cloned.1.call-start
  8.0 0.0 copy-start.1
  8.0 42.6 %all_gather.6 = bf16[1,8192]{1,0:T(2,128)(2,1)S(1)} all-gather(bf16[1,256]{1,0:T(2,128)(2,1)} %param.7), channel_id=1, replica_groups=mesh['blk'=8,'fsdp'=32] {'fsdp'}, dimensions={1}, use_global_device_ids=true | all-gather | bytes 16896 | tf_op jit(solution)/shard_map/all_gather | solution.py:16
  50.6 2.1 collective-permute-start
  52.7 5.1 %fusion.4 = f32[512]{0:T(512)S(1)} fusion(bf16[512,8192]{1,0:T(8,128)(2,1)} %param.6), kind=kLoop, calls=%fused_computation.6 | loop fusion | flops 12582400 | bytes 8390656 | tf_op jit(solution)/shard_map/reduce_sum | solution.py:21
  57.8 0.0 collective-permute-done
  57.8 0.0 copy-done
  57.8 0.0 copy-done.1
  57.8 7.3 %convolution_convert_fusion = bf16[8192,512]{1,0:T(8,128)(2,1)} fusion(bf16[512,512]{1,0:T(8,128)(2,1)S(1)} %copy-done, bf16[512,8192]{1,0:T(8,128)(2,1)S(1)} %copy-done.1, f32[8192]{0:T(1024)S(1)} %bitcast.15, f32[512]{0:T(512)S(1)} %add_rsqrt_fusion), kind=kOutput, calls=%fused_computation.7 | convolution fusion | flops 4315938816 | bytes 17336320 | tf_op jit(solution)/shard_map/dot_general | solution.py:29
  65.2 0.0 reduce-scatter.5.cloned.1.call-update
  65.2 0.0 reduce-scatter.7.cloned.1.call-start
  65.2 47.5 %all-gather.2.cloned.1.call-done = bf16[1,8192,512]{2,1,0:T(8,128)(2,1)} async-done(((bf16[1,256,512]{2,1,0:T(8,128)(2,1)}), bf16[1,8192,512]{2,1,0:T(8,128)(2,1)}) %all-gather.2.cloned.1.call-update) | async-done | bytes 8388624 | tf_op jit(solution)/shard_map/all_gather | solution.py:15
  112.7 2.1 collective-permute-start.1
  114.8 181.3 %reduce-scatter.5.cloned.1.call-done = bf16[256,512]{1,0:T(8,128)(2,1)} async-done(((bf16[8192,512]{1,0:T(8,128)(2,1)}), bf16[256,512]{1,0:T(8,128)(2,1)}) %reduce-scatter.5.cloned.1.call-update) | async-done | bytes 262160 | tf_op jit(solution)/shard_map/reduce_scatter | solution.py:28
  296.1 0.0 copy-start.2
  296.1 4.2 collective-permute-start.2
  300.3 23.5 %collective-permute-done.1 = bf16[1,8192,512]{2,1,0:T(8,128)(2,1)} collective-permute-done((bf16[1,8192,512]{2,1,0:T(8,128)(2,1)}, bf16[1,8192,512]{2,1,0:T(8,128)(2,1)}, u32[]{:S(2)}, u32[]{:S(2)}) %collective-permute-start.1) | collective-permute-done | bytes 8388640 | tf_op jit(solution)/shard_map/ppermute | solution.py:10
  323.8 9.5 %fusion.3 = bf16[8192]{0:T(1024)(128)(2,1)S(1)} fusion(bf16[512,8192]{1,0:T(8,128)(2,1)} %param.6, bf16[512,512]{1,0:T(8,128)(2,1)S(1)} %copy-done, bf16[1,8192,512]{2,1,0:T(8,128)(2,1)} %collective-permute-done.1, f32[512]{0:T(512)S(1)} %add_rsqrt_fusion), kind=kOutput, calls=%fused_computation.5 | convolution fusion | flops 4311736320 | bytes 17319936 | tf_op jit(solution)/shard_map/dot_general | solution.py:24
  333.3 2.2 reshape_bitcast_fusion
  335.5 0.0 reduce-scatter.7.cloned.1.call-update
  335.5 0.0 collective-permute-done.2
  335.5 0.0 copy-done.2
  335.5 0.9 convert_add_fusion
  336.4 114.4 %reduce-scatter.7.cloned.1.call-done = bf16[256,1]{1,0:T(8,128)(2,1)} async-done(((bf16[8192,1]{1,0:T(8,128)(2,1)}), bf16[256,1]{1,0:T(8,128)(2,1)}) %reduce-scatter.7.cloned.1.call-update) | async-done | bytes 528
  450.8 0.9 copy.10
  451.7 0.0 copy-start.3
  451.7 3.6 collective-permute-start.3
  455.3 11.1 %fusion.10 = bf16[512,512]{1,0:T(8,128)(2,1)} fusion(bf16[1,8192,512]{2,1,0:T(8,128)(2,1)} %collective-permute-done.1, bf16[512,8192]{1,0:T(8,128)(2,1)} %param.6, f32[8192]{0:T(1024)S(1)} %bitcast.16, f32[512]{0:T(512)S(1)} %add_rsqrt_fusion), kind=kOutput, calls=%fused_computation.12 | convolution fusion | flops 4312006656 | bytes 17336320 | tf_op jit(solution)/shard_map/dot_general | solution.py:23
  466.4 0.0 collective-permute-done.3
  466.4 0.0 copy-done.3
  466.4 0.6 convert_add_fusion.1
  (2 shorter events, 0.0 us)
Async XLA Ops:
  7.2 50.7 %copy-start = (bf16[512,512]{1,0:T(8,128)(2,1)S(1)}, bf16[512,512]{1,0:T(8,128)(2,1)}, u32[]{:S(2)}) copy-start(bf16[512,512]{1,0:T(8,128)(2,1)} %param.9) | copy-start | bytes 1572868
  7.2 105.6 %all-gather.2.cloned.1.call-start = ((), (), s32[]{:S(2)}) async-start(), calls=%async_computation.2 | async-start | bytes 8650752 | tf_op jit(solution)/shard_map/all_gather | solution.py:15
  7.9 288.2 %reduce-scatter.5.cloned.1.call-start = ((), (), s32[]{:S(2)}) async-start(), calls=%async_computation.3 | async-start | bytes 8650752 | tf_op jit(solution)/shard_map/reduce_scatter | solution.py:28
  8.0 49.9 %copy-start.1 = (bf16[512,8192]{1,0:T(8,128)(2,1)S(1)}, bf16[512,8192]{1,0:T(8,128)(2,1)}, u32[]{:S(2)}) copy-start(bf16[512,8192]{1,0:T(8,128)(2,1)} %param.6) | copy-start | bytes 25165828
  50.6 7.2 %collective-permute-start = (bf16[1,8192]{1,0:T(2,128)(2,1)S(1)}, bf16[1,8192]{1,0:T(2,128)(2,1)S(1)}, u32[]{:S(2)}, u32[]{:S(2)}) collective-permute-start(bf16[1,8192]{1,0:T(2,128)(2,1)S(1)} %all_gather.6), channel_id=1, source_target_pairs={{0,32},{32,64},{64,96},{96,128},{128,160},{160,192},{192,224},{224... | collective-permute-start | bytes 49160 | tf_op jit(solution)/shard_map/ppermute | solution.py:10
  65.2 385.6 %reduce-scatter.7.cloned.1.call-start = ((), (), s32[]{:S(2)}) async-start(), calls=%async_computation.4 | async-start | bytes 2162688
  112.7 211.1 %collective-permute-start.1 = (bf16[1,8192,512]{2,1,0:T(8,128)(2,1)}, bf16[1,8192,512]{2,1,0:T(8,128)(2,1)}, u32[]{:S(2)}, u32[]{:S(2)}) collective-permute-start(bf16[1,8192,512]{2,1,0:T(8,128)(2,1)} %all-gather.2.cloned.1.call-done), channel_id=1, source_target_pairs={{0,32},{32,64},{64,96},{96,128},{128,160},{160,192},{192,224},{224... | collective-permute-start | bytes 25165832 | tf_op jit(solution)/shard_map/ppermute | solution.py:10
  296.1 39.4 %copy-start.2 = (f32[1,256,512]{2,1,0:T(8,128)S(1)}, f32[1,256,512]{2,1,0:T(8,128)}, u32[]{:S(2)}) copy-start(f32[1,256,512]{2,1,0:T(8,128)} %param.10) | copy-start | bytes 1572868
  296.1 39.4 %collective-permute-start.2 = (bf16[1,256,512]{2,1,0:T(8,128)(2,1)}, bf16[1,256,512]{2,1,0:T(8,128)(2,1)S(1)}, u32[]{:S(2)}, u32[]{:S(2)}) collective-permute-start(bf16[1,256,512]{2,1,0:T(8,128)(2,1)} %bitcast.17), channel_id=1, source_target_pairs={{0,224},{32,0},{64,32},{96,64},{128,96},{160,128},{192,160},{224,1... | collective-permute-start | bytes 786440 | tf_op jit(solution)/shard_map/ppermute | solution.py:10
  451.7 14.7 %copy-start.3 = (f32[1,256]{1,0:T(1,128)S(1)}, f32[1,256]{1,0:T(1,128)}, u32[]{:S(2)}) copy-start(f32[1,256]{1,0:T(1,128)} %param.11) | copy-start | bytes 3076
  451.7 14.7 %collective-permute-start.3 = (bf16[1,256]{1,0:T(2,128)(2,1)S(1)}, bf16[1,256]{1,0:T(2,128)(2,1)S(1)}, u32[]{:S(2)}, u32[]{:S(2)}) collective-permute-start(bf16[1,256]{1,0:T(2,128)(2,1)S(1)} %copy.10), channel_id=1, source_target_pairs={{0,224},{32,0},{64,32},{96,64},{128,96},{160,128},{192,160},{224,1... | collective-permute-start | bytes 1544 | tf_op jit(solution)/shard_map/ppermute | solution.py:10
Sparse Core Ops, SparseCore 0:
  10.8 101.9 all-gather.1
  117.1 178.8 reduce-scatter.4
  335.6 115.0 reduce-scatter.6
where the time goes:
time: 474 us; the launch traced here: 473 us
  waiting for transfers between devices  367 us (77%)
  blocking collectives  42.6 us (9%)
  matrix products  27.9 us (6%)
  between operations  13.8 us (3%)
  starting transfers between devices  12.1 us (3%)
  other arithmetic  6.58 us (1%)
    reduce_scatter x1, waiting for transfers between devices, per_device(): lax.psum_scatter(lax.dot_general(scaled, cotangent, (((0,), (0,)), ((), (...  181 us
    unnamed x4, waiting for transfers between devices  115 us
    all_gather x1, waiting for transfers between devices, per_device(): lax.all_gather(value_weight, 'fsdp', axis=1, tiled=True)  47.5 us
    all_gather x1, blocking collectives, per_device(): lax.all_gather(gain, 'fsdp', axis=1, tiled=True)  42.6 us
    ppermute x4, waiting for transfers between devices, from_behind(): return lax.ppermute(value, axis, pairs)  23.5 us
    ppermute x4, starting transfers between devices, from_behind(): return lax.ppermute(value, axis, pairs)  12 us
    dot_general x1, matrix products, per_device(): jnp.dot(scaled, weight, preferred_element_type=jnp.float32)  11.1 us
  transfers between devices with their start and end apart: 7, of which 4 were waited for; matrix products, arithmetic and copies ran while one was open for 8% of the time, Pallas kernels for 0%

commit v1 on v0

v1 whole, which is shorter than its diff:
```python
import functools

import jax
import jax.numpy as jnp
from jax import lax
from jax.experimental import pallas as pl
from jax.experimental.pallas import tpu as pltpu
from jax.sharding import PartitionSpec as P

NX, NZ, NC = 2, 8, 2
NB = 8
EPS = 1e-05
BF16 = jnp.bfloat16
F32 = jnp.float32
OFFSETS = (4, 3, -3, 2, -2, 1, -1, 0)
FIRST = 2
VMEM_LIMIT = 56 * 1024 * 1024


def fsdp_index(x, z, core):
    return (x * NZ + z) * NC + core


def move(value, change):
    pairs = [
        (fsdp_index(x, z, c), fsdp_index(*change(x, z, c)))
        for x in range(NX)
        for z in range(NZ)
        for c in range(NC)
    ]
    return lax.ppermute(value, "fsdp", pairs)


def along_z(value, steps):
    return move(value, lambda x, z, c: (x, (z + steps) % NZ, c))


def swap_x(value):
    return move(value, lambda x, z, c: (1 - x, z, c))


def swap_core(value):
    return move(value, lambda x, z, c: (x, z, 1 - c))


def along_blk(value, steps, flip_x):
    size = NX * NZ * NC
    pairs = [
        (b * size + fsdp_index(x, z, c), ((b + steps) % NB) * size + fsdp_index(x ^ flip_x, z, c))
        for b in range(NB)
        for x in range(NX)
        for z in range(NZ)
        for c in range(NC)
    ]
    return lax.ppermute(value, ("blk", "fsdp"), pairs)


def params(**more):
    return pltpu.CompilerParams(vmem_limit_bytes=VMEM_LIMIT, **more)


def prepare_kernel(width, table, hidden, cot, scale, cot_t, send_a, send_b):
    rows = hidden.shape[0]
    total = jnp.zeros((rows, width), F32)
    for j in range(hidden.shape[1] // width):
        part = hidden[:, j * width:(j + 1) * width].astype(F32)
        total += part * part
    mean = jnp.sum(total, axis=1, keepdims=True) * (1.0 / hidden.shape[1])
    inverse = lax.rsqrt(mean + EPS)
    scale[...] = inverse
    cot_t[...] = (cot[...].astype(F32) * inverse).T.astype(BF16)
    for i in range(2 * len(OFFSETS)):
        start = pl.multiple_of((table[i] ^ 1) * width, width)
        part = hidden[:, pl.ds(start, width)]
        if i < 2 * FIRST:
            send_a[:, i * width:(i + 1) * width] = part
        else:
            j = i - 2 * FIRST
            send_b[:, j * width:(j + 1) * width] = part


def prepare(table, hidden, cot, width):
    tokens, features = hidden.shape
    values = cot.shape[1]
    step = 128
    first, rest = 2 * FIRST * width, 2 * (len(OFFSETS) - FIRST) * width
    row = lambda i, table: (i, 0)
    return pl.pallas_call(
        functools.partial(prepare_kernel, width),
        grid_spec=pltpu.PrefetchScalarGridSpec(
            num_scalar_prefetch=1,
            grid=(tokens // step,),
            in_specs=[pl.BlockSpec((step, features), row), pl.BlockSpec((step, values), row)],
            out_specs=[
                pl.BlockSpec((step, 1), row),
                pl.BlockSpec((values, step), lambda i, table: (0, i)),
                pl.BlockSpec((step, first), row),
                pl.BlockSpec((step, rest), row),
            ],
        ),
        out_shape=[
            jax.ShapeDtypeStruct((tokens, 1), F32),
            jax.ShapeDtypeStruct((values, tokens), BF16),
            jax.ShapeDtypeStruct((tokens, first), BF16),
            jax.ShapeDtypeStruct((tokens, rest), BF16),
        ],
        compiler_params=params(),
        cost_estimate=pl.CostEstimate(flops=3 * tokens * features, bytes_accessed=3 * tokens * features, transcendentals=0),
    )(table, hidden, cot)


def gradient_kernel(count, width, table, own_other, own_same, visiting, cot_t, cot_t_sibling, *outs):
    def part(own, at):
        total = jnp.dot(cot_t[...], own[...], preferred_element_type=F32)
        theirs = visiting[:, at * width:(at + 1) * width]
        return (total + jnp.dot(cot_t_sibling[...], theirs, preferred_element_type=F32)).astype(BF16)

    other, same = part(own_other, 0), part(own_same, 1)
    for i in range(count):
        @pl.when(pl.program_id(0) == i)
        def _():
            outs[2 * i][...] = other
            outs[2 * i + 1][...] = same


def gradient(table, hidden, visiting, cot_t, cot_t_sibling, base, count, width):
    tokens = hidden.shape[0]
    values = cot_t.shape[0]
    whole = pl.BlockSpec((values, tokens), lambda i, table: (0, 0))
    outs = pl.pallas_call(
        functools.partial(gradient_kernel, count, width),
        grid_spec=pltpu.PrefetchScalarGridSpec(
            num_scalar_prefetch=1,
            grid=(count,),
            in_specs=[
                pl.BlockSpec((tokens, width), lambda i, table: (0, table[2 * (base + i)])),
                pl.BlockSpec((tokens, width), lambda i, table: (0, table[2 * (base + i) + 1])),
                pl.BlockSpec((tokens, 2 * width), lambda i, table: (0, i)),
                whole,
                whole,
            ],
            out_specs=[pl.BlockSpec((values, width), lambda i, table: (0, 0))] * (2 * count),
        ),
        out_shape=[jax.ShapeDtypeStruct((values, width), BF16)] * (2 * count),
        compiler_params=params(),
        cost_estimate=pl.CostEstimate(
            flops=8 * count * tokens * values * width, bytes_accessed=8 * count * tokens * width + 4 * count * values * width, transcendentals=0
        ),
    )(table, hidden, hidden, visiting, cot_t, cot_t_sibling)
    return outs[0::2], outs[1::2]


def project_kernel(blocks, width, table, *refs):
    own = refs[:blocks]
    visit_a, visit_b = refs[blocks:blocks + 2]
    weights = refs[blocks + 2:-2]
    mine, theirs = refs[-2:]
    total = jnp.zeros(mine.shape, F32)
    total_theirs = jnp.zeros(theirs.shape, F32)
    at = 0
    for i in range(blocks):
        if i < 2 * FIRST:
            visitor = visit_a[:, i * width:(i + 1) * width]
        else:
            j = i - 2 * FIRST
            visitor = visit_b[:, j * width:(j + 1) * width]
        first = 0
        while first < width:
            weight = weights[at][...]
            last = first + weight.shape[0]
            total += jnp.dot(own[i][:, first:last], weight, preferred_element_type=F32)
            total_theirs += jnp.dot(visitor[:, first:last], weight, preferred_element_type=F32)
            first, at = last, at + 1
    mine[...] = total
    theirs[...] = total_theirs


def project(table, hidden, visit_a, visit_b, weights, width):
    tokens = hidden.shape[0]
    values = weights[0].shape[1]
    blocks = 2 * len(OFFSETS)
    step = 256 if tokens % 256 == 0 else tokens
    row = lambda t, table: (t, 0)
    specs = [pl.BlockSpec((step, width), lambda t, table, i=i: (t, table[i])) for i in range(blocks)]
    specs += [pl.BlockSpec((step, v.shape[1]), row) for v in (visit_a, visit_b)]
    specs += [pl.BlockSpec(w.shape, lambda t, table: (0, 0)) for w in weights]
    return pl.pallas_call(
        functools.partial(project_kernel, blocks, width),
        grid_spec=pltpu.PrefetchScalarGridSpec(
            num_scalar_prefetch=1,
            grid=(tokens // step,),
            in_specs=specs,
            out_specs=[pl.BlockSpec((step, values), row)] * 2,
        ),
        out_shape=[jax.ShapeDtypeStruct((tokens, values), F32)] * 2,
        compiler_params=params(),
        cost_estimate=pl.CostEstimate(
            flops=4 * tokens * blocks * width * values, bytes_accessed=4 * tokens * blocks * width + 2 * blocks * width * values, transcendentals=0
        ),
    )(table, *([hidden] * blocks), visit_a, visit_b, *weights)


def add(*terms):
    return sum(t.astype(F32) for t in terms).astype(BF16)


def per_device(hidden, gain, value_weight, cotangent, grad_weight_in, grad_gain_in):
    weight = value_weight[0].astype(F32)
    gains = gain[0].astype(F32)
    width = weight.shape[0]
    place = lax.axis_index("fsdp")
    core, z, x = place % NC, (place // NC) % NZ, place // (NC * NZ)
    table = jnp.stack(
        [fsdp_index(x ^ flip, (z + off + NZ) % NZ, core) for off in OFFSETS for flip in (1, 0)]
    ).astype(jnp.int32)

    scaled_weight = (weight * gains[:, None]).astype(BF16)
    layer = [along_blk(scaled_weight, 1, 0), along_blk(scaled_weight, 1, 1)]

    scale, cot_t, send_a, send_b = prepare(table, hidden, cotangent, width)
    visit_a = swap_core(send_a)
    cot_t_sibling = swap_core(cot_t)
    visit_b = swap_core(send_b)

    send_1, keep_1 = gradient(table, hidden, visit_a, cot_t, cot_t_sibling, 0, FIRST, width)
    send_2, keep_2 = gradient(table, hidden, visit_b, cot_t, cot_t_sibling, FIRST, len(OFFSETS) - FIRST, width)
    sends, keeps = [*send_1, *send_2], [*keep_1, *keep_2]
    arrived = [swap_x(s) for s in sends]
    mine = {off: (keeps[i], arrived[i]) for i, off in enumerate(OFFSETS)}

    half = sends[0].shape[0] // 2
    farthest = add(*mine[4])
    up = along_z(farthest[:half], 1)
    down = along_z(farthest[half:], -1)
    sum_up = jnp.concatenate([add(mine[3][0][:half], mine[3][1][:half], up), add(mine[3][0][half:], mine[3][1][half:])], axis=0)
    sum_down = jnp.concatenate([add(mine[-3][0][:half], mine[-3][1][:half]), add(mine[-3][0][half:], mine[-3][1][half:], down)], axis=0)
    for off in (2, 1, 0):
        up, down = along_z(sum_up, 1), along_z(sum_down, -1)
        if off:
            sum_up, sum_down = add(*mine[off], up), add(*mine[-off], down)
    total = along_blk(add(*mine[0], up, down), -1, 0)

    blocks = {(0, flip): [layer[flip]] for flip in (0, 1)}
    for flip in (0, 1):
        from_below, from_above = layer[flip], layer[flip]
        for step in (1, 2, 3):
            from_below, from_above = along_z(from_below, 1), along_z(from_above, -1)
            blocks[-step, flip], blocks[step, flip] = [from_below], [from_above]
        blocks[4, flip] = [along_z(from_below[:width // 2], 1), along_z(from_above[width // 2:], -1)]
    weights = [w for off in OFFSETS for flip in (1, 0) for w in blocks[off, flip]]
    product, product_sibling = project(table, hidden, visit_a, visit_b, weights, width)
    values = ((product + swap_core(product_sibling)) * scale).astype(BF16)

    summed = total.astype(F32).T
    grad_weight = grad_weight_in + (gains[:, None] * summed)[None]
    grad_gain = grad_gain_in + jnp.sum(weight * summed, axis=1)[None]
    return values, grad_weight, grad_gain


def solution(mesh):
    return jax.shard_map(
        per_device,
        mesh=mesh,
        in_specs=(
            P(("blk", "fsdp"), None),
            P("blk", "fsdp"),
            P("blk", "fsdp", None),
            P(("blk", "fsdp"), None),
            P("blk", "fsdp", None),
            P("blk", "fsdp"),
        ),
        out_specs=(P(("blk", "fsdp"), None), P("blk", "fsdp", None), P("blk", "fsdp")),
        check_vma=False,
    )
```

time: 474 us -> 189 us (0.40)
  waiting for transfers between devices: 367 us -> 61 us
  starting transfers between devices: 12.1 us -> 56.4 us
  blocking collectives: 42.6 us -> 0 us
  Pallas kernels: 0 us -> 33.1 us
  matrix products: 27.9 us -> 0 us
  local copies, waits for them, and re-layouts: 3.14 us -> 26.8 us
  between operations: 13.8 us -> 1.04 us
    reduce_scatter x1 -> x0, waiting for transfers between devices: 181 us -> none  [per_device(): lax.psum_scatter(lax.dot_general(scaled, cotangent, (((0,), (0,)), ((), (...]
    unnamed x4 -> x0, waiting for transfers between devices: 115 us -> none
    all_gather x1 -> x0, waiting for transfers between devices: 47.5 us -> none  [per_device(): lax.all_gather(value_weight, 'fsdp', axis=1, tiled=True)]
    ppermute x4 -> x39, starting transfers between devices: 12 us -> 56.4 us  [the longest x36 50.2 us: move(): return lax.ppermute(value, 'fsdp', pairs)]
    all_gather x1 -> x0, blocking collectives: 42.6 us -> none  [per_device(): lax.all_gather(gain, 'fsdp', axis=1, tiled=True)]
    ppermute x4 -> x39, waiting for transfers between devices: 23.5 us -> 61 us  [the longest x36 48.1 us: move(): return lax.ppermute(value, 'fsdp', pairs)]
    pallas_call x0 -> x4, Pallas kernels: none -> 33.1 us  [the longest x2 14.8 us: gradient(): pl.pallas_call(functools.partial(gradient_kernel, count, width), grid_spe...]
    dot_general x3 -> x0, matrix products: 27.9 us -> none  [the longest x1 11.1 us: per_device(): jnp.dot(scaled, weight, preferred_element_type=jnp.float32)]
  transfers between devices with their start and end apart: 7 -> 39, of which waited for: 4 -> 15; matrix products, arithmetic and copies ran while one was open for 8% -> 14% of each run, Pallas kernels for 0% -> 8%
where the time goes in v1:
time: 189 us; the launch traced here: 185 us
  waiting for transfers between devices  61 us (32%)
  starting transfers between devices  56.4 us (30%)
  Pallas kernels  33.1 us (18%)
  local copies, waits for them, and re-layouts  26.8 us (14%)
  other arithmetic  6.5 us (3%)
    ppermute x36, starting transfers between devices, move(): return lax.ppermute(value, 'fsdp', pairs)  50.2 us
    ppermute x36, waiting for transfers between devices, move(): return lax.ppermute(value, 'fsdp', pairs)  48.1 us
    ppermute x16, local copies, waits for them, and re-layouts, move(): return lax.ppermute(value, 'fsdp', pairs)  17 us
    pallas_call x2, Pallas kernels, gradient(): pl.pallas_call(functools.partial(gradient_kernel, count, width), grid_spe...  14.8 us
    ppermute x3, waiting for transfers between devices, along_blk(): return lax.ppermute(value, ('blk', 'fsdp'), pairs)  12.9 us
    pallas_call x1, Pallas kernels, project(): pl.pallas_call(functools.partial(project_kernel, blocks, width), grid_spe...  10.8 us
    pallas_call x1, Pallas kernels, prepare(): pl.pallas_call(functools.partial(prepare_kernel, width), grid_spec=pltpu....  7.58 us
    ppermute x3, starting transfers between devices, along_blk(): return lax.ppermute(value, ('blk', 'fsdp'), pairs)  6.19 us
  transfers between devices with their start and end apart: 39, of which 15 were waited for; matrix products, arithmetic and copies ran while one was open for 14% of the time, Pallas kernels for 8%

profile of v1, /device:TPU:4, one launch (start us, length us, event | category | flops | bytes accessed | tf_op | source)
XLA Modules:
  0.0 184.9 jit_solution(14790857525291936898)
XLA Ops:
  1.4 7.6 %shard_map.85 = (f32[512,1]{1,0:T(8,128)}, bf16[512,512]{1,0:T(8,128)(2,1)}, bf16[512,1024]{1,0:T(8,128)(2,1)}, bf16[512,3072]{1,0:T(8,128)(2,1)}) custom-call(s32[16]{0:T(128)} %stack.67.table, bf16[512,8192]{1,0:T(8,128)(2,1)} %own_same.3, bf16[512,512]{1,0:T(8,128)(2,1)} %cot.1), custom_call_target="tpu_custom_call" | custom-call | flops 12582912 | bytes 12582912 | tf_op jit(solution)/shard_map/pallas_call | solution.py:88
  9.6 7.5 %collective-permute-done.21.cot_t_sibling = bf16[512,512]{1,0:T(8,128)(2,1)S(1)} collective-permute-done((bf16[512,512]{1,0:T(8,128)(2,1)}, bf16[512,512]{1,0:T(8,128)(2,1)S(1)}, u32[]{:S(2)}, u32[]{:S(2)}) %collective-permute-start.21) | collective-permute-done | bytes 524320 | tf_op jit(solution)/shard_map/ppermute | solution.py:31
  17.9 1.0 copy-done.1
  18.9 4.9 %shard_map.88 = (bf16[512,256]{1,0:T(8,128)(2,1)}, bf16[512,256]{1,0:T(8,128)(2,1)}, bf16[512,256]{1,0:T(8,128)(2,1)}, bf16[512,256]{1,0:T(8,128)(2,1)}) custom-call(s32[16]{0:T(128)} %stack.67.table, bf16[512,8192]{1,0:T(8,128)(2,1)} %own_same.3, bf16[512,8192]{1,0:T(8,128)(2,1)} %own_same.3, bf16[512,1024]{1,0:T(8,128)(2,1)} %copy-done.1, ...), custom_call_target="tpu_custom_call" | custom-call | flops 1073741824 | bytes 3145728 | tf_op jit(solution)/shard_map/pallas_call | solution.py:130
  23.8 2.2 %collective-permute-start.26 = (bf16[512,256]{1,0:T(8,128)(2,1)}, bf16[512,256]{1,0:T(8,128)(2,1)S(1)}, u32[]{:S(2)}, u32[]{:S(2)}) collective-permute-start(bf16[512,256]{1,0:T(8,128)(2,1)} %get-tuple-element.40), channel_id=1, source_target_pairs={{0,16},{1,17},{2,18},{3,19},{4,20},{5,21},{6,22},{7,23},{8,24},{9,... | collective-permute-start | bytes 786440 | tf_op jit(solution)/shard_map/ppermute | solution.py:31
  26.0 1.3 collective-permute-start.25
  27.3 7.3 %collective-permute-done.26 = bf16[512,256]{1,0:T(8,128)(2,1)S(1)} collective-permute-done((bf16[512,256]{1,0:T(8,128)(2,1)}, bf16[512,256]{1,0:T(8,128)(2,1)S(1)}, u32[]{:S(2)}, u32[]{:S(2)}) %collective-permute-start.26) | collective-permute-done | bytes 262176 | tf_op jit(solution)/shard_map/ppermute | solution.py:31
  34.6 1.0 add_convert_fusion.5
  35.7 2.0 %collective-permute-start.27 = (bf16[256,256]{1,0:T(8,128)(2,1)S(1)}, bf16[256,256]{1,0:T(8,128)(2,1)S(1)}, u32[]{:S(2)}, u32[]{:S(2)}) collective-permute-start(bf16[256,256]{1,0:T(8,128)(2,1)S(1)} %get-tuple-element.59), channel_id=1, source_target_pairs={{0,2},{1,3},{2,4},{3,5},{4,6},{5,7},{6,8},{7,9},{8,10},{9,11},{10,... | collective-permute-start | bytes 393224 | tf_op jit(solution)/shard_map/ppermute | solution.py:31
  37.7 4.0 %collective-permute-start.34 = (bf16[256,256]{1,0:T(8,128)(2,1)S(1)}, bf16[256,256]{1,0:T(8,128)(2,1)S(1)}, u32[]{:S(2)}, u32[]{:S(2)}) collective-permute-start(bf16[256,256]{1,0:T(8,128)(2,1)S(1)} %get-tuple-element.60), channel_id=1, source_target_pairs={{0,14},{1,15},{2,0},{3,1},{4,2},{5,3},{6,4},{7,5},{8,6},{9,7},{10,... | collective-permute-start | bytes 393224 | tf_op jit(solution)/shard_map/ppermute | solution.py:31
  41.7 1.6 copy-done
  43.4 9.9 %shard_map.87 = (bf16[512,256]{1,0:T(8,128)(2,1)}, bf16[512,256]{1,0:T(8,128)(2,1)}, bf16[512,256]{1,0:T(8,128)(2,1)}, bf16[512,256]{1,0:T(8,128)(2,1)}, bf16[51...) custom-call(s32[16]{0:T(128)} %stack.67.table, ...), custom_call_target="tpu_custom_call" | custom-call | flops 3221225472 | bytes 9437184 | tf_op jit(solution)/shard_map/pallas_call | solution.py:130
  54.1 3.1 %collective-permute-start.24 = (bf16[512,256]{1,0:T(8,128)(2,1)}, bf16[512,256]{1,0:T(8,128)(2,1)S(1)}, u32[]{:S(2)}, u32[]{:S(2)}) collective-permute-start(bf16[512,256]{1,0:T(8,128)(2,1)} %get-tuple-element.36), channel_id=1, source_target_pairs={{0,16},{1,17},{2,18},{3,19},{4,20},{5,21},{6,22},{7,23},{8,24},{9,... | collective-permute-start | bytes 786440 | tf_op jit(solution)/shard_map/ppermute | solution.py:31
  57.7 6.6 %collective-permute-done.33 = bf16[512,256]{1,0:T(8,128)(2,1)S(1)} collective-permute-done((bf16[512,256]{1,0:T(8,128)(2,1)}, bf16[512,256]{1,0:T(8,128)(2,1)S(1)}, u32[]{:S(2)}, u32[]{:S(2)}) %collective-permute-start.33) | collective-permute-done | bytes 262176 | tf_op jit(solution)/shard_map/ppermute | solution.py:31
  64.3 1.1 add_convert_fusion.7
  65.4 2.0 %collective-permute-start.35 = (bf16[512,256]{1,0:T(8,128)(2,1)S(1)}, bf16[512,256]{1,0:T(8,128)(2,1)S(1)}, u32[]{:S(2)}, u32[]{:S(2)}) collective-permute-start(bf16[512,256]{1,0:T(8,128)(2,1)S(1)} %pad_maximum_fusion.1), channel_id=1, source_target_pairs={{0,14},{1,15},{2,0},{3,1},{4,2},{5,3},{6,4},{7,5},{8,6},{9,7},{10,... | collective-permute-start | bytes 786440 | tf_op jit(solution)/shard_map/ppermute | solution.py:31
  67.4 3.5 %collective-permute-start.31 = (bf16[512,256]{1,0:T(8,128)(2,1)}, bf16[512,256]{1,0:T(8,128)(2,1)S(1)}, u32[]{:S(2)}, u32[]{:S(2)}) collective-permute-start(bf16[512,256]{1,0:T(8,128)(2,1)} %get-tuple-element.42), channel_id=1, source_target_pairs={{0,16},{1,17},{2,18},{3,19},{4,20},{5,21},{6,22},{7,23},{8,24},{9,... | collective-permute-start | bytes 786440 | tf_op jit(solution)/shard_map/ppermute | solution.py:31
  71.0 1.1 add_convert_fusion.4
  72.2 3.3 %collective-permute-done.32 = bf16[512,256]{1,0:T(8,128)(2,1)S(1)} collective-permute-done((bf16[512,256]{1,0:T(8,128)(2,1)}, bf16[512,256]{1,0:T(8,128)(2,1)S(1)}, u32[]{:S(2)}, u32[]{:S(2)}) %collective-permute-start.32) | collective-permute-done | bytes 262176 | tf_op jit(solution)/shard_map/ppermute | solution.py:31
  75.7 2.2 %collective-permute-start.36 = (bf16[512,256]{1,0:T(8,128)(2,1)S(1)}, bf16[512,256]{1,0:T(8,128)(2,1)S(1)}, u32[]{:S(2)}, u32[]{:S(2)}) collective-permute-start(bf16[512,256]{1,0:T(8,128)(2,1)S(1)} %add_convert_fusion.2), channel_id=1, source_target_pairs={{0,14},{1,15},{2,0},{3,1},{4,2},{5,3},{6,4},{7,5},{8,6},{9,7},{10,... | collective-permute-start | bytes 786440 | tf_op jit(solution)/shard_map/ppermute | solution.py:31
  77.9 3.3 %collective-permute-done.23 = bf16[512,256]{1,0:T(8,128)(2,1)S(1)} collective-permute-done((bf16[512,256]{1,0:T(8,128)(2,1)}, bf16[512,256]{1,0:T(8,128)(2,1)S(1)}, u32[]{:S(2)}, u32[]{:S(2)}) %collective-permute-start.23) | collective-permute-done | bytes 262176 | tf_op jit(solution)/shard_map/ppermute | solution.py:31
  81.4 5.4 %collective-permute-done.31 = bf16[512,256]{1,0:T(8,128)(2,1)S(1)} collective-permute-done((bf16[512,256]{1,0:T(8,128)(2,1)}, bf16[512,256]{1,0:T(8,128)(2,1)S(1)}, u32[]{:S(2)}, u32[]{:S(2)}) %collective-permute-start.31) | collective-permute-done | bytes 262176 | tf_op jit(solution)/shard_map/ppermute | solution.py:31
  86.9 1.7 collective-permute-start.37
  88.6 1.0 collective-permute-done.22
  89.6 3.7 %collective-permute-done.37 = bf16[512,256]{1,0:T(8,128)(2,1)S(1)} collective-permute-done((bf16[512,256]{1,0:T(8,128)(2,1)S(1)}, bf16[512,256]{1,0:T(8,128)(2,1)S(1)}, u32[]{:S(2)}, u32[]{:S(2)}) %collective-permute-start.37) | collective-permute-done | bytes 262176 | tf_op jit(solution)/shard_map/ppermute | solution.py:31
  93.5 3.7 %collective-permute-start.38 = (bf16[512,256]{1,0:T(8,128)(2,1)S(1)}, bf16[512,256]{1,0:T(8,128)(2,1)S(1)}, u32[]{:S(2)}, u32[]{:S(2)}) collective-permute-start(bf16[512,256]{1,0:T(8,128)(2,1)S(1)} %add_convert_fusion), channel_id=1, source_target_pairs={{0,224},{1,225},{2,226},{3,227},{4,228},{5,229},{6,230},{7,231},{8... | collective-permute-start | bytes 786440 | tf_op jit(solution)/shard_map/ppermute | solution.py:55
  97.3 5.1 %collective-permute-done.38 = bf16[512,256]{1,0:T(8,128)(2,1)S(1)} collective-permute-done((bf16[512,256]{1,0:T(8,128)(2,1)S(1)}, bf16[512,256]{1,0:T(8,128)(2,1)S(1)}, u32[]{:S(2)}, u32[]{:S(2)}) %collective-permute-start.38) | collective-permute-done | bytes 262176 | tf_op jit(solution)/shard_map/ppermute | solution.py:55
  102.6 1.2 collective-permute-start.2
  103.8 1.3 collective-permute-start.11
  105.0 7.8 %collective-permute-done.2 = bf16[256,512]{0,1:T(8,128)(2,1)S(1)} collective-permute-done((bf16[256,512]{0,1:T(8,128)(2,1)S(1)}, bf16[256,512]{0,1:T(8,128)(2,1)S(1)}, u32[]{:S(2)}, u32[]{:S(2)}) %collective-permute-start.2) | collective-permute-done | bytes 262176 | tf_op jit(solution)/shard_map/ppermute | solution.py:55
  112.9 3.2 %collective-permute-start.7 = (bf16[256,512]{0,1:T(8,128)(2,1)S(1)}, bf16[256,512]{0,1:T(8,128)(2,1)S(1)}, u32[]{:S(2)}, u32[]{:S(2)}) collective-permute-start(bf16[256,512]{0,1:T(8,128)(2,1)S(1)} %collective-permute-done.2), channel_id=1, source_target_pairs={{0,14},{1,15},{2,0},{3,1},{4,2},{5,3},{6,4},{7,5},{8,6},{9,7},{10,... | collective-permute-start | bytes 786440 | tf_op jit(solution)/shard_map/ppermute | solution.py:31
  116.1 3.3 %collective-permute-start.16 = (bf16[256,512]{0,1:T(8,128)(2,1)S(1)}, bf16[256,512]{0,1:T(8,128)(2,1)S(1)}, u32[]{:S(2)}, u32[]{:S(2)}) collective-permute-start(bf16[256,512]{0,1:T(8,128)(2,1)S(1)} %collective-permute-done.11), channel_id=1, source_target_pairs={{0,14},{1,15},{2,0},{3,1},{4,2},{5,3},{6,4},{7,5},{8,6},{9,7},{10,... | collective-permute-start | bytes 786440 | tf_op jit(solution)/shard_map/ppermute | solution.py:31
  119.4 3.9 %collective-permute-done.3 = bf16[256,512]{0,1:T(8,128)(2,1)S(1)} collective-permute-done((bf16[256,512]{0,1:T(8,128)(2,1)S(1)}, bf16[256,512]{0,1:T(8,128)(2,1)S(1)}, u32[]{:S(2)}, u32[]{:S(2)}) %collective-permute-start.3) | collective-permute-done | bytes 262176 | tf_op jit(solution)/shard_map/ppermute | solution.py:31
  123.2 3.3 %collective-permute-start.8 = (bf16[256,512]{0,1:T(8,128)(2,1)S(1)}, bf16[256,512]{0,1:T(8,128)(2,1)S(1)}, u32[]{:S(2)}, u32[]{:S(2)}) collective-permute-start(bf16[256,512]{0,1:T(8,128)(2,1)S(1)} %collective-permute-done.7), channel_id=1, source_target_pairs={{0,14},{1,15},{2,0},{3,1},{4,2},{5,3},{6,4},{7,5},{8,6},{9,7},{10,... | collective-permute-start | bytes 786440 | tf_op jit(solution)/shard_map/ppermute | solution.py:31
  126.5 2.3 %collective-permute-done.12 = bf16[256,512]{0,1:T(8,128)(2,1)S(1)} collective-permute-done((bf16[256,512]{0,1:T(8,128)(2,1)S(1)}, bf16[256,512]{0,1:T(8,128)(2,1)S(1)}, u32[]{:S(2)}, u32[]{:S(2)}) %collective-permute-start.12) | collective-permute-done | bytes 262176 | tf_op jit(solution)/shard_map/ppermute | solution.py:31
  128.8 3.3 %collective-permute-start.17 = (bf16[256,512]{0,1:T(8,128)(2,1)S(1)}, bf16[256,512]{0,1:T(8,128)(2,1)S(1)}, u32[]{:S(2)}, u32[]{:S(2)}) collective-permute-start(bf16[256,512]{0,1:T(8,128)(2,1)S(1)} %collective-permute-done.16), channel_id=1, source_target_pairs={{0,14},{1,15},{2,0},{3,1},{4,2},{5,3},{6,4},{7,5},{8,6},{9,7},{10,... | collective-permute-start | bytes 786440 | tf_op jit(solution)/shard_map/ppermute | solution.py:31
  132.1 2.3 %collective-permute-done.4 = bf16[256,512]{0,1:T(8,128)(2,1)S(1)} collective-permute-done((bf16[256,512]{0,1:T(8,128)(2,1)S(1)}, bf16[256,512]{0,1:T(8,128)(2,1)S(1)}, u32[]{:S(2)}, u32[]{:S(2)}) %collective-permute-start.4) | collective-permute-done | bytes 262176 | tf_op jit(solution)/shard_map/ppermute | solution.py:31
  134.4 3.2 %collective-permute-start.9 = (bf16[256,512]{0,1:T(8,128)(2,1)S(1)}, bf16[256,512]{0,1:T(8,128)(2,1)S(1)}, u32[]{:S(2)}, u32[]{:S(2)}) collective-permute-start(bf16[256,512]{0,1:T(8,128)(2,1)S(1)} %collective-permute-done.8), channel_id=1, source_target_pairs={{0,14},{1,15},{2,0},{3,1},{4,2},{5,3},{6,4},{7,5},{8,6},{9,7},{10,... | collective-permute-start | bytes 786440 | tf_op jit(solution)/shard_map/ppermute | solution.py:31
  138.0 3.2 %collective-permute-start.18 = (bf16[256,512]{0,1:T(8,128)(2,1)S(1)}, bf16[256,512]{0,1:T(8,128)(2,1)S(1)}, u32[]{:S(2)}, u32[]{:S(2)}) collective-permute-start(bf16[256,512]{0,1:T(8,128)(2,1)S(1)} %collective-permute-done.17), channel_id=1, source_target_pairs={{0,14},{1,15},{2,0},{3,1},{4,2},{5,3},{6,4},{7,5},{8,6},{9,7},{10,... | collective-permute-start | bytes 786440 | tf_op jit(solution)/shard_map/ppermute | solution.py:31
  143.6 3.2 %collective-permute-start.10 = (bf16[128,512]{0,1:T(8,128)(2,1)}, bf16[128,512]{0,1:T(8,128)(2,1)}, u32[]{:S(2)}, u32[]{:S(2)}) collective-permute-start(bf16[128,512]{0,1:T(8,128)(2,1)} %slice.57), channel_id=1, source_target_pairs={{0,14},{1,15},{2,0},{3,1},{4,2},{5,3},{6,4},{7,5},{8,6},{9,7},{10,... | collective-permute-start | bytes 393224 | tf_op jit(solution)/shard_map/ppermute | solution.py:31
  148.2 3.2 %collective-permute-start.19 = (bf16[128,512]{0,1:T(8,128)(2,1)}, bf16[128,512]{0,1:T(8,128)(2,1)}, u32[]{:S(2)}, u32[]{:S(2)}) collective-permute-start(bf16[128,512]{0,1:T(8,128)(2,1)} %slice.59), channel_id=1, source_target_pairs={{0,14},{1,15},{2,0},{3,1},{4,2},{5,3},{6,4},{7,5},{8,6},{9,7},{10,... | collective-permute-start | bytes 393224 | tf_op jit(solution)/shard_map/ppermute | solution.py:31
  157.4 1.8 copy.40.refs_27_
  165.1 1.7 copy.32.refs_19_
  166.8 1.7 copy.33.refs_20_
  168.4 1.7 copy.34.refs_21_
  170.1 10.8 %shard_map.86 = (f32[512,512]{1,0:T(8,128)}, f32[512,512]{1,0:T(8,128)}) custom-call(s32[16]{0:T(128)} %stack.67.table, bf16[512,8192]{1,0:T(8,128)(2,1)} %own_same.3, bf16[512,8192]{1,0:T(8,128)(2,1)} %own_same.3, bf16[512,8192]{1,0:T(8,128)(2,1)} %own_same.3, bf16[512,8192]{1,0:T(8,128)(2,1)} %own_same.3, bf16[512,8192]{1,0:T(8,128)(2,1)} %own_same.3, ...), custom_call_target="tpu_custom_call" | custom-call | flops 4294967296 | bytes 12582912 | tf_op jit(solution)/shard_map/pallas_call | solution.py:187
  181.3 1.1 reduce
  182.4 1.0 copy.50
  (111 shorter events, 22.1 us)
Async XLA Ops:
  9.0 32.7 %collective-permute-start.1 = (bf16[512,3072]{1,0:T(8,128)(2,1)}, bf16[512,3072]{1,0:T(8,128)(2,1)S(1)}, u32[]{:S(2)}, u32[]{:S(2)}) collective-permute-start(bf16[512,3072]{1,0:T(8,128)(2,1)} %get-tuple-element.26), channel_id=1, source_target_pairs={{0,1},{1,0},{2,3},{3,2},{4,5},{5,4},{6,7},{7,6},{8,9},{9,8},{10,11... | collective-permute-start | bytes 9437192 | tf_op jit(solution)/shard_map/ppermute | solution.py:31
  9.0 8.1 %collective-permute-start = (bf16[512,1024]{1,0:T(8,128)(2,1)}, bf16[512,1024]{1,0:T(8,128)(2,1)S(1)}, u32[]{:S(2)}, u32[]{:S(2)}) collective-permute-start(bf16[512,1024]{1,0:T(8,128)(2,1)} %get-tuple-element.25), channel_id=1, source_target_pairs={{0,1},{1,0},{2,3},{3,2},{4,5},{5,4},{6,7},{7,6},{8,9},{9,8},{10,11... | collective-permute-start | bytes 3145736 | tf_op jit(solution)/shard_map/ppermute | solution.py:31
  9.5 7.6 %collective-permute-start.21 = (bf16[512,512]{1,0:T(8,128)(2,1)}, bf16[512,512]{1,0:T(8,128)(2,1)S(1)}, u32[]{:S(2)}, u32[]{:S(2)}) collective-permute-start(bf16[512,512]{1,0:T(8,128)(2,1)} %get-tuple-element.30.cot_t), channel_id=1, source_target_pairs={{0,1},{1,0},{2,3},{3,2},{4,5},{5,4},{6,7},{7,6},{8,9},{9,8},{10,11... | collective-permute-start | bytes 1572872 | tf_op jit(solution)/shard_map/ppermute | solution.py:31
  23.8 10.9 %collective-permute-start.26 = (bf16[512,256]{1,0:T(8,128)(2,1)}, bf16[512,256]{1,0:T(8,128)(2,1)S(1)}, u32[]{:S(2)}, u32[]{:S(2)}) collective-permute-start(bf16[512,256]{1,0:T(8,128)(2,1)} %get-tuple-element.40), channel_id=1, source_target_pairs={{0,16},{1,17},{2,18},{3,19},{4,20},{5,21},{6,22},{7,23},{8,24},{9,... | collective-permute-start | bytes 786440 | tf_op jit(solution)/shard_map/ppermute | solution.py:31
  26.0 27.9 %collective-permute-start.25 = (bf16[512,256]{1,0:T(8,128)(2,1)}, bf16[512,256]{1,0:T(8,128)(2,1)S(1)}, u32[]{:S(2)}, u32[]{:S(2)}) collective-permute-start(bf16[512,256]{1,0:T(8,128)(2,1)} %get-tuple-element.38), channel_id=1, source_target_pairs={{0,16},{1,17},{2,18},{3,19},{4,20},{5,21},{6,22},{7,23},{8,24},{9,... | collective-permute-start | bytes 786440 | tf_op jit(solution)/shard_map/ppermute | solution.py:31
  35.7 18.2 %collective-permute-start.27 = (bf16[256,256]{1,0:T(8,128)(2,1)S(1)}, bf16[256,256]{1,0:T(8,128)(2,1)S(1)}, u32[]{:S(2)}, u32[]{:S(2)}) collective-permute-start(bf16[256,256]{1,0:T(8,128)(2,1)S(1)} %get-tuple-element.59), channel_id=1, source_target_pairs={{0,2},{1,3},{2,4},{3,5},{4,6},{5,7},{6,8},{7,9},{8,10},{9,11},{10,... | collective-permute-start | bytes 393224 | tf_op jit(solution)/shard_map/ppermute | solution.py:31
  37.7 16.2 %copy-start.6 = (bf16[512,256]{1,0:T(8,128)(2,1)S(1)}, bf16[512,256]{1,0:T(8,128)(2,1)}, u32[]{:S(2)}) copy-start(bf16[512,256]{1,0:T(8,128)(2,1)} %get-tuple-element.37) | copy-start | bytes 786436
  37.7 20.0 %collective-permute-start.34 = (bf16[256,256]{1,0:T(8,128)(2,1)S(1)}, bf16[256,256]{1,0:T(8,128)(2,1)S(1)}, u32[]{:S(2)}, u32[]{:S(2)}) collective-permute-start(bf16[256,256]{1,0:T(8,128)(2,1)S(1)} %get-tuple-element.60), channel_id=1, source_target_pairs={{0,14},{1,15},{2,0},{3,1},{4,2},{5,3},{6,4},{7,5},{8,6},{9,7},{10,... | collective-permute-start | bytes 393224 | tf_op jit(solution)/shard_map/ppermute | solution.py:31
  53.2 22.3 %copy-start.13 = (bf16[512,256]{1,0:T(8,128)(2,1)S(1)}, bf16[512,256]{1,0:T(8,128)(2,1)}, u32[]{:S(2)}) copy-start(bf16[512,256]{1,0:T(8,128)(2,1)} %get-tuple-element.43) | copy-start | bytes 786436
  53.3 24.6 %copy-start.16 = (bf16[512,256]{1,0:T(8,128)(2,1)S(1)}, bf16[512,256]{1,0:T(8,128)(2,1)}, u32[]{:S(2)}) copy-start(bf16[512,256]{1,0:T(8,128)(2,1)} %get-tuple-element.32) | copy-start | bytes 786436
  53.3 27.9 %copy-start.12 = (bf16[512,256]{1,0:T(8,128)(2,1)S(1)}, bf16[512,256]{1,0:T(8,128)(2,1)}, u32[]{:S(2)}) copy-start(bf16[512,256]{1,0:T(8,128)(2,1)} %get-tuple-element.33) | copy-start | bytes 786436
  53.3 33.5 %copy-start.11 = (bf16[512,256]{1,0:T(8,128)(2,1)S(1)}, bf16[512,256]{1,0:T(8,128)(2,1)}, u32[]{:S(2)}) copy-start(bf16[512,256]{1,0:T(8,128)(2,1)} %get-tuple-element.41) | copy-start | bytes 786436
  53.3 11.0 %collective-permute-start.33 = (bf16[512,256]{1,0:T(8,128)(2,1)}, bf16[512,256]{1,0:T(8,128)(2,1)S(1)}, u32[]{:S(2)}, u32[]{:S(2)}) collective-permute-start(bf16[512,256]{1,0:T(8,128)(2,1)} %get-tuple-element.46), channel_id=1, source_target_pairs={{0,16},{1,17},{2,18},{3,19},{4,20},{5,21},{6,22},{7,23},{8,24},{9,... | collective-permute-start | bytes 786440 | tf_op jit(solution)/shard_map/ppermute | solution.py:31
  54.0 39.4 %copy-start.5 = (bf16[512,256]{1,0:T(8,128)(2,1)S(1)}, bf16[512,256]{1,0:T(8,128)(2,1)}, u32[]{:S(2)}) copy-start(bf16[512,256]{1,0:T(8,128)(2,1)} %get-tuple-element.31) | copy-start | bytes 786436
  54.0 13.5 %collective-permute-start.28 = (bf16[512,256]{1,0:T(8,128)(2,1)S(1)}, bf16[512,256]{1,0:T(8,128)(2,1)S(1)}, u32[]{:S(2)}, u32[]{:S(2)}) collective-permute-start(bf16[512,256]{1,0:T(8,128)(2,1)S(1)} %pad_maximum_fusion), channel_id=1, source_target_pairs={{0,2},{1,3},{2,4},{3,5},{4,6},{5,7},{6,8},{7,9},{8,10},{9,11},{10,... | collective-permute-start | bytes 786440 | tf_op jit(solution)/shard_map/ppermute | solution.py:31
  54.1 16.9 %collective-permute-start.24 = (bf16[512,256]{1,0:T(8,128)(2,1)}, bf16[512,256]{1,0:T(8,128)(2,1)S(1)}, u32[]{:S(2)}, u32[]{:S(2)}) collective-permute-start(bf16[512,256]{1,0:T(8,128)(2,1)} %get-tuple-element.36), channel_id=1, source_target_pairs={{0,16},{1,17},{2,18},{3,19},{4,20},{5,21},{6,22},{7,23},{8,24},{9,... | collective-permute-start | bytes 786440 | tf_op jit(solution)/shard_map/ppermute | solution.py:31
  57.2 18.3 %collective-permute-start.32 = (bf16[512,256]{1,0:T(8,128)(2,1)}, bf16[512,256]{1,0:T(8,128)(2,1)S(1)}, u32[]{:S(2)}, u32[]{:S(2)}) collective-permute-start(bf16[512,256]{1,0:T(8,128)(2,1)} %get-tuple-element.44), channel_id=1, source_target_pairs={{0,16},{1,17},{2,18},{3,19},{4,20},{5,21},{6,22},{7,23},{8,24},{9,... | collective-permute-start | bytes 786440 | tf_op jit(solution)/shard_map/ppermute | solution.py:31
  65.4 31.8 %copy-start.15 = (bf16[1,256]{1,0:T(2,128)(2,1)S(1)}, bf16[1,256]{1,0:T(2,128)(2,1)}, u32[]{:S(2)}) copy-start(bf16[1,256]{1,0:T(2,128)(2,1)} %param.7) | copy-start | bytes 1540
  65.4 31.8 %copy-start.7 = (bf16[1,256,512]{2,1,0:T(8,128)(2,1)S(1)}, bf16[1,256,512]{2,1,0:T(8,128)(2,1)}, u32[]{:S(2)}) copy-start(bf16[1,256,512]{2,1,0:T(8,128)(2,1)} %param.8) | copy-start | bytes 786436
  65.4 10.1 %collective-permute-start.35 = (bf16[512,256]{1,0:T(8,128)(2,1)S(1)}, bf16[512,256]{1,0:T(8,128)(2,1)S(1)}, u32[]{:S(2)}, u32[]{:S(2)}) collective-permute-start(bf16[512,256]{1,0:T(8,128)(2,1)S(1)} %pad_maximum_fusion.1), channel_id=1, source_target_pairs={{0,14},{1,15},{2,0},{3,1},{4,2},{5,3},{6,4},{7,5},{8,6},{9,7},{10,... | collective-permute-start | bytes 786440 | tf_op jit(solution)/shard_map/ppermute | solution.py:31
  67.4 13.7 %collective-permute-start.23 = (bf16[512,256]{1,0:T(8,128)(2,1)}, bf16[512,256]{1,0:T(8,128)(2,1)S(1)}, u32[]{:S(2)}, u32[]{:S(2)}) collective-permute-start(bf16[512,256]{1,0:T(8,128)(2,1)} %get-tuple-element.34), channel_id=1, source_target_pairs={{0,16},{1,17},{2,18},{3,19},{4,20},{5,21},{6,22},{7,23},{8,24},{9,... | collective-permute-start | bytes 786440 | tf_op jit(solution)/shard_map/ppermute | solution.py:31
  67.4 19.3 %collective-permute-start.31 = (bf16[512,256]{1,0:T(8,128)(2,1)}, bf16[512,256]{1,0:T(8,128)(2,1)S(1)}, u32[]{:S(2)}, u32[]{:S(2)}) collective-permute-start(bf16[512,256]{1,0:T(8,128)(2,1)} %get-tuple-element.42), channel_id=1, source_target_pairs={{0,16},{1,17},{2,18},{3,19},{4,20},{5,21},{6,22},{7,23},{8,24},{9,... | collective-permute-start | bytes 786440 | tf_op jit(solution)/shard_map/ppermute | solution.py:31
  72.0 9.1 %collective-permute-start.29 = (bf16[512,256]{1,0:T(8,128)(2,1)S(1)}, bf16[512,256]{1,0:T(8,128)(2,1)S(1)}, u32[]{:S(2)}, u32[]{:S(2)}) collective-permute-start(bf16[512,256]{1,0:T(8,128)(2,1)S(1)} %add_convert_fusion.4), channel_id=1, source_target_pairs={{0,2},{1,3},{2,4},{3,5},{4,6},{5,7},{6,8},{7,9},{8,10},{9,11},{10,... | collective-permute-start | bytes 786440 | tf_op jit(solution)/shard_map/ppermute | solution.py:31
  75.7 11.1 %collective-permute-start.36 = (bf16[512,256]{1,0:T(8,128)(2,1)S(1)}, bf16[512,256]{1,0:T(8,128)(2,1)S(1)}, u32[]{:S(2)}, u32[]{:S(2)}) collective-permute-start(bf16[512,256]{1,0:T(8,128)(2,1)S(1)} %add_convert_fusion.2), channel_id=1, source_target_pairs={{0,14},{1,15},{2,0},{3,1},{4,2},{5,3},{6,4},{7,5},{8,6},{9,7},{10,... | collective-permute-start | bytes 786440 | tf_op jit(solution)/shard_map/ppermute | solution.py:31
  77.9 11.7 %collective-permute-start.22 = (bf16[512,256]{1,0:T(8,128)(2,1)S(1)}, bf16[512,256]{1,0:T(8,128)(2,1)S(1)}, u32[]{:S(2)}, u32[]{:S(2)}) collective-permute-start(bf16[512,256]{1,0:T(8,128)(2,1)S(1)} %copy-done.16), channel_id=1, source_target_pairs={{0,16},{1,17},{2,18},{3,19},{4,20},{5,21},{6,22},{7,23},{8,24},{9,... | collective-permute-start | bytes 786440 | tf_op jit(solution)/shard_map/ppermute | solution.py:31
  81.3 8.3 %collective-permute-start.30 = (bf16[512,256]{1,0:T(8,128)(2,1)S(1)}, bf16[512,256]{1,0:T(8,128)(2,1)S(1)}, u32[]{:S(2)}, u32[]{:S(2)}) collective-permute-start(bf16[512,256]{1,0:T(8,128)(2,1)S(1)} %add_convert_fusion.3), channel_id=1, source_target_pairs={{0,2},{1,3},{2,4},{3,5},{4,6},{5,7},{6,8},{7,9},{8,10},{9,11},{10,... | collective-permute-start | bytes 786440 | tf_op jit(solution)/shard_map/ppermute | solution.py:31
  86.9 6.5 %collective-permute-start.37 = (bf16[512,256]{1,0:T(8,128)(2,1)S(1)}, bf16[512,256]{1,0:T(8,128)(2,1)S(1)}, u32[]{:S(2)}, u32[]{:S(2)}) collective-permute-start(bf16[512,256]{1,0:T(8,128)(2,1)S(1)} %add_convert_fusion.1), channel_id=1, source_target_pairs={{0,14},{1,15},{2,0},{3,1},{4,2},{5,3},{6,4},{7,5},{8,6},{9,7},{10,... | collective-permute-start | bytes 786440 | tf_op jit(solution)/shard_map/ppermute | solution.py:31
  93.5 9.0 %collective-permute-start.38 = (bf16[512,256]{1,0:T(8,128)(2,1)S(1)}, bf16[512,256]{1,0:T(8,128)(2,1)S(1)}, u32[]{:S(2)}, u32[]{:S(2)}) collective-permute-start(bf16[512,256]{1,0:T(8,128)(2,1)S(1)} %add_convert_fusion), channel_id=1, source_target_pairs={{0,224},{1,225},{2,226},{3,227},{4,228},{5,229},{6,230},{7,231},{8... | collective-permute-start | bytes 786440 | tf_op jit(solution)/shard_map/ppermute | solution.py:55
  102.6 10.3 %collective-permute-start.2 = (bf16[256,512]{0,1:T(8,128)(2,1)S(1)}, bf16[256,512]{0,1:T(8,128)(2,1)S(1)}, u32[]{:S(2)}, u32[]{:S(2)}) collective-permute-start(bf16[256,512]{0,1:T(8,128)(2,1)S(1)} %get-tuple-element.58), channel_id=1, source_target_pairs={{0,48},{1,49},{2,50},{3,51},{4,52},{5,53},{6,54},{7,55},{8,56},{9,... | collective-permute-start | bytes 786440 | tf_op jit(solution)/shard_map/ppermute | solution.py:55
  103.8 12.3 %collective-permute-start.11 = (bf16[256,512]{0,1:T(8,128)(2,1)S(1)}, bf16[256,512]{0,1:T(8,128)(2,1)S(1)}, u32[]{:S(2)}, u32[]{:S(2)}) collective-permute-start(bf16[256,512]{0,1:T(8,128)(2,1)S(1)} %get-tuple-element.58), channel_id=1, source_target_pairs={{0,32},{1,33},{2,34},{3,35},{4,36},{5,37},{6,38},{7,39},{8,40},{9,... | collective-permute-start | bytes 786440 | tf_op jit(solution)/shard_map/ppermute | solution.py:55
  112.9 10.3 %collective-permute-start.3 = (bf16[256,512]{0,1:T(8,128)(2,1)S(1)}, bf16[256,512]{0,1:T(8,128)(2,1)S(1)}, u32[]{:S(2)}, u32[]{:S(2)}) collective-permute-start(bf16[256,512]{0,1:T(8,128)(2,1)S(1)} %collective-permute-done.2), channel_id=1, source_target_pairs={{0,2},{1,3},{2,4},{3,5},{4,6},{5,7},{6,8},{7,9},{8,10},{9,11},{10,... | collective-permute-start | bytes 786440 | tf_op jit(solution)/shard_map/ppermute | solution.py:31
  112.9 10.3 %collective-permute-start.7 = (bf16[256,512]{0,1:T(8,128)(2,1)S(1)}, bf16[256,512]{0,1:T(8,128)(2,1)S(1)}, u32[]{:S(2)}, u32[]{:S(2)}) collective-permute-start(bf16[256,512]{0,1:T(8,128)(2,1)S(1)} %collective-permute-done.2), channel_id=1, source_target_pairs={{0,14},{1,15},{2,0},{3,1},{4,2},{5,3},{6,4},{7,5},{8,6},{9,7},{10,... | collective-permute-start | bytes 786440 | tf_op jit(solution)/shard_map/ppermute | solution.py:31
  116.1 12.7 %collective-permute-start.12 = (bf16[256,512]{0,1:T(8,128)(2,1)S(1)}, bf16[256,512]{0,1:T(8,128)(2,1)S(1)}, u32[]{:S(2)}, u32[]{:S(2)}) collective-permute-start(bf16[256,512]{0,1:T(8,128)(2,1)S(1)} %collective-permute-done.11), channel_id=1, source_target_pairs={{0,2},{1,3},{2,4},{3,5},{4,6},{5,7},{6,8},{7,9},{8,10},{9,11},{10,... | collective-permute-start | bytes 786440 | tf_op jit(solution)/shard_map/ppermute | solution.py:31
  116.1 12.7 %collective-permute-start.16 = (bf16[256,512]{0,1:T(8,128)(2,1)S(1)}, bf16[256,512]{0,1:T(8,128)(2,1)S(1)}, u32[]{:S(2)}, u32[]{:S(2)}) collective-permute-start(bf16[256,512]{0,1:T(8,128)(2,1)S(1)} %collective-permute-done.11), channel_id=1, source_target_pairs={{0,14},{1,15},{2,0},{3,1},{4,2},{5,3},{6,4},{7,5},{8,6},{9,7},{10,... | collective-permute-start | bytes 786440 | tf_op jit(solution)/shard_map/ppermute | solution.py:31
  123.2 11.2 %collective-permute-start.4 = (bf16[256,512]{0,1:T(8,128)(2,1)S(1)}, bf16[256,512]{0,1:T(8,128)(2,1)S(1)}, u32[]{:S(2)}, u32[]{:S(2)}) collective-permute-start(bf16[256,512]{0,1:T(8,128)(2,1)S(1)} %collective-permute-done.3), channel_id=1, source_target_pairs={{0,2},{1,3},{2,4},{3,5},{4,6},{5,7},{6,8},{7,9},{8,10},{9,11},{10,... | collective-permute-start | bytes 786440 | tf_op jit(solution)/shard_map/ppermute | solution.py:31
  123.2 11.2 %collective-permute-start.8 = (bf16[256,512]{0,1:T(8,128)(2,1)S(1)}, bf16[256,512]{0,1:T(8,128)(2,1)S(1)}, u32[]{:S(2)}, u32[]{:S(2)}) collective-permute-start(bf16[256,512]{0,1:T(8,128)(2,1)S(1)} %collective-permute-done.7), channel_id=1, source_target_pairs={{0,14},{1,15},{2,0},{3,1},{4,2},{5,3},{6,4},{7,5},{8,6},{9,7},{10,... | collective-permute-start | bytes 786440 | tf_op jit(solution)/shard_map/ppermute | solution.py:31
  128.8 9.2 %collective-permute-start.13 = (bf16[256,512]{0,1:T(8,128)(2,1)S(1)}, bf16[256,512]{0,1:T(8,128)(2,1)S(1)}, u32[]{:S(2)}, u32[]{:S(2)}) collective-permute-start(bf16[256,512]{0,1:T(8,128)(2,1)S(1)} %collective-permute-done.12), channel_id=1, source_target_pairs={{0,2},{1,3},{2,4},{3,5},{4,6},{5,7},{6,8},{7,9},{8,10},{9,11},{10,... | collective-permute-start | bytes 786440 | tf_op jit(solution)/shard_map/ppermute | solution.py:31
  128.8 9.2 %collective-permute-start.17 = (bf16[256,512]{0,1:T(8,128)(2,1)S(1)}, bf16[256,512]{0,1:T(8,128)(2,1)S(1)}, u32[]{:S(2)}, u32[]{:S(2)}) collective-permute-start(bf16[256,512]{0,1:T(8,128)(2,1)S(1)} %collective-permute-done.16), channel_id=1, source_target_pairs={{0,14},{1,15},{2,0},{3,1},{4,2},{5,3},{6,4},{7,5},{8,6},{9,7},{10,... | collective-permute-start | bytes 786440 | tf_op jit(solution)/shard_map/ppermute | solution.py:31
  134.4 7.8 %collective-permute-start.5 = (bf16[256,512]{0,1:T(8,128)(2,1)S(1)}, bf16[256,512]{0,1:T(8,128)(2,1)S(1)}, u32[]{:S(2)}, u32[]{:S(2)}) collective-permute-start(bf16[256,512]{0,1:T(8,128)(2,1)S(1)} %collective-permute-done.4), channel_id=1, source_target_pairs={{0,2},{1,3},{2,4},{3,5},{4,6},{5,7},{6,8},{7,9},{8,10},{9,11},{10,... | collective-permute-start | bytes 786440 | tf_op jit(solution)/shard_map/ppermute | solution.py:31
  134.4 8.5 %collective-permute-start.9 = (bf16[256,512]{0,1:T(8,128)(2,1)S(1)}, bf16[256,512]{0,1:T(8,128)(2,1)S(1)}, u32[]{:S(2)}, u32[]{:S(2)}) collective-permute-start(bf16[256,512]{0,1:T(8,128)(2,1)S(1)} %collective-permute-done.8), channel_id=1, source_target_pairs={{0,14},{1,15},{2,0},{3,1},{4,2},{5,3},{6,4},{7,5},{8,6},{9,7},{10,... | collective-permute-start | bytes 786440 | tf_op jit(solution)/shard_map/ppermute | solution.py:31
  138.0 8.8 %collective-permute-start.14 = (bf16[256,512]{0,1:T(8,128)(2,1)S(1)}, bf16[256,512]{0,1:T(8,128)(2,1)S(1)}, u32[]{:S(2)}, u32[]{:S(2)}) collective-permute-start(bf16[256,512]{0,1:T(8,128)(2,1)S(1)} %collective-permute-done.13), channel_id=1, source_target_pairs={{0,2},{1,3},{2,4},{3,5},{4,6},{5,7},{6,8},{7,9},{8,10},{9,11},{10,... | collective-permute-start | bytes 786440 | tf_op jit(solution)/shard_map/ppermute | solution.py:31
  138.0 9.5 %collective-permute-start.18 = (bf16[256,512]{0,1:T(8,128)(2,1)S(1)}, bf16[256,512]{0,1:T(8,128)(2,1)S(1)}, u32[]{:S(2)}, u32[]{:S(2)}) collective-permute-start(bf16[256,512]{0,1:T(8,128)(2,1)S(1)} %collective-permute-done.17), channel_id=1, source_target_pairs={{0,14},{1,15},{2,0},{3,1},{4,2},{5,3},{6,4},{7,5},{8,6},{9,7},{10,... | collective-permute-start | bytes 786440 | tf_op jit(solution)/shard_map/ppermute | solution.py:31
  142.9 21.4 %collective-permute-start.6 = (bf16[128,512]{0,1:T(8,128)(2,1)}, bf16[128,512]{0,1:T(8,128)(2,1)S(1)}, u32[]{:S(2)}, u32[]{:S(2)}) collective-permute-start(bf16[128,512]{0,1:T(8,128)(2,1)} %slice.56), channel_id=1, source_target_pairs={{0,2},{1,3},{2,4},{3,5},{4,6},{5,7},{6,8},{7,9},{8,10},{9,11},{10,... | collective-permute-start | bytes 393224 | tf_op jit(solution)/shard_map/ppermute | solution.py:31
  143.6 21.5 %collective-permute-start.10 = (bf16[128,512]{0,1:T(8,128)(2,1)}, bf16[128,512]{0,1:T(8,128)(2,1)}, u32[]{:S(2)}, u32[]{:S(2)}) collective-permute-start(bf16[128,512]{0,1:T(8,128)(2,1)} %slice.57), channel_id=1, source_target_pairs={{0,14},{1,15},{2,0},{3,1},{4,2},{5,3},{6,4},{7,5},{8,6},{9,7},{10,... | collective-permute-start | bytes 393224 | tf_op jit(solution)/shard_map/ppermute | solution.py:31
  147.5 19.3 %collective-permute-start.15 = (bf16[128,512]{0,1:T(8,128)(2,1)}, bf16[128,512]{0,1:T(8,128)(2,1)}, u32[]{:S(2)}, u32[]{:S(2)}) collective-permute-start(bf16[128,512]{0,1:T(8,128)(2,1)} %slice.58), channel_id=1, source_target_pairs={{0,2},{1,3},{2,4},{3,5},{4,6},{5,7},{6,8},{7,9},{8,10},{9,11},{10,... | collective-permute-start | bytes 393224 | tf_op jit(solution)/shard_map/ppermute | solution.py:31
  148.2 20.3 %collective-permute-start.19 = (bf16[128,512]{0,1:T(8,128)(2,1)}, bf16[128,512]{0,1:T(8,128)(2,1)}, u32[]{:S(2)}, u32[]{:S(2)}) collective-permute-start(bf16[128,512]{0,1:T(8,128)(2,1)} %slice.59), channel_id=1, source_target_pairs={{0,14},{1,15},{2,0},{3,1},{4,2},{5,3},{6,4},{7,5},{8,6},{9,7},{10,... | collective-permute-start | bytes 393224 | tf_op jit(solution)/shard_map/ppermute | solution.py:31
  170.1 10.9 %copy-start.4 = (f32[1,256,512]{2,1,0:T(8,128)S(1)}, f32[1,256,512]{2,1,0:T(8,128)}, u32[]{:S(2)}) copy-start(f32[1,256,512]{2,1,0:T(8,128)} %param.10) | copy-start | bytes 1572868
  180.9 3.0 %collective-permute-start.20 = (f32[512,512]{1,0:T(8,128)}, f32[512,512]{1,0:T(8,128)S(1)}, u32[]{:S(2)}, u32[]{:S(2)}) collective-permute-start(f32[512,512]{1,0:T(8,128)} %get-tuple-element.28), channel_id=1, source_target_pairs={{0,1},{1,0},{2,3},{3,2},{4,5},{5,4},{6,7},{7,6},{8,9},{9,8},{10,11... | collective-permute-start | bytes 3145736 | tf_op jit(solution)/shard_map/ppermute | solution.py:31
  (8 other events, 36.5 us)

commit v2 on v1

--- a/solution.py
+++ b/solution.py
@@ -5,7 +5,7 @@
 from jax import lax
 from jax.experimental import pallas as pl
 from jax.experimental.pallas import tpu as pltpu
-from jax.sharding import PartitionSpec as P
+from jax.sharding import Mesh, PartitionSpec as P
 
 NX, NZ, NC = 2, 8, 2
 NB = 8
@@ -28,7 +28,7 @@
         for z in range(NZ)
         for c in range(NC)
     ]
-    return lax.ppermute(value, "fsdp", pairs)
+    return lax.ppermute(value, ("x", "z", "core"), pairs)
 
 
 def along_z(value, steps):
@@ -52,14 +52,14 @@
         for z in range(NZ)
         for c in range(NC)
     ]
-    return lax.ppermute(value, ("blk", "fsdp"), pairs)
+    return lax.ppermute(value, ("blk", "x", "z", "core"), pairs)
 
 
 def params(**more):
     return pltpu.CompilerParams(vmem_limit_bytes=VMEM_LIMIT, **more)
 
 
-def prepare_kernel(width, table, hidden, cot, scale, cot_t, send_a, send_b):
+def prepare_kernel(width, table, hidden, cot, after, scale, cot_t, send_a, send_b):
     rows = hidden.shape[0]
     total = jnp.zeros((rows, width), F32)
     for j in range(hidden.shape[1] // width):
@@ -79,7 +79,7 @@
             send_b[:, j * width:(j + 1) * width] = part
 
 
-def prepare(table, hidden, cot, width):
+def prepare(table, hidden, cot, after, width):
     tokens, features = hidden.shape
     values = cot.shape[1]
     step = 128
@@ -90,7 +90,7 @@
         grid_spec=pltpu.PrefetchScalarGridSpec(
             num_scalar_prefetch=1,
             grid=(tokens // step,),
-            in_specs=[pl.BlockSpec((step, features), row), pl.BlockSpec((step, values), row)],
+            in_specs=[pl.BlockSpec((step, features), row), pl.BlockSpec((step, values), row), pl.BlockSpec(memory_space=pl.ANY)],
             out_specs=[
                 pl.BlockSpec((step, 1), row),
                 pl.BlockSpec((values, step), lambda i, table: (0, i)),
@@ -106,7 +106,7 @@
         ],
         compiler_params=params(),
         cost_estimate=pl.CostEstimate(flops=3 * tokens * features, bytes_accessed=3 * tokens * features, transcendentals=0),
-    )(table, hidden, cot)
+    )(table, hidden, cot, after)
 
 
 def gradient_kernel(count, width, table, own_other, own_same, visiting, cot_t, cot_t_sibling, *outs):
@@ -150,54 +150,84 @@
     return outs[0::2], outs[1::2]
 
 
-def project_kernel(blocks, width, table, *refs):
-    own = refs[:blocks]
-    visit_a, visit_b = refs[blocks:blocks + 2]
-    weights = refs[blocks + 2:-2]
-    mine, theirs = refs[-2:]
-    total = jnp.zeros(mine.shape, F32)
-    total_theirs = jnp.zeros(theirs.shape, F32)
-    at = 0
-    for i in range(blocks):
-        if i < 2 * FIRST:
-            visitor = visit_a[:, i * width:(i + 1) * width]
-        else:
-            j = i - 2 * FIRST
-            visitor = visit_b[:, j * width:(j + 1) * width]
-        first = 0
-        while first < width:
-            weight = weights[at][...]
-            last = first + weight.shape[0]
-            total += jnp.dot(own[i][:, first:last], weight, preferred_element_type=F32)
-            total_theirs += jnp.dot(visitor[:, first:last], weight, preferred_element_type=F32)
-            first, at = last, at + 1
-    mine[...] = total
-    theirs[...] = total_theirs
+def project_kernel(width, table, own_other, own_same, visit_a, visit_b, weights, mine, theirs):
+    step = pl.program_id(0)
+
+    @pl.when(step == 0)
+    def _():
+        mine[...] = jnp.zeros_like(mine)
+        theirs[...] = jnp.zeros_like(theirs)
+
+    other, same = weights[0, 1], weights[0, 0]
+    mine[...] += jnp.dot(own_other[...], other, preferred_element_type=F32) + jnp.dot(own_same[...], same, preferred_element_type=F32)
+
+    def visitors(visit):
+        theirs[...] += jnp.dot(visit[:, :width], other, preferred_element_type=F32) + jnp.dot(visit[:, width:], same, preferred_element_type=F32)
+
+    pl.when(step < FIRST)(lambda: visitors(visit_a))
+    pl.when(step >= FIRST)(lambda: visitors(visit_b))
 
 
 def project(table, hidden, visit_a, visit_b, weights, width):
     tokens = hidden.shape[0]
-    values = weights[0].shape[1]
-    blocks = 2 * len(OFFSETS)
-    step = 256 if tokens % 256 == 0 else tokens
-    row = lambda t, table: (t, 0)
-    specs = [pl.BlockSpec((step, width), lambda t, table, i=i: (t, table[i])) for i in range(blocks)]
-    specs += [pl.BlockSpec((step, v.shape[1]), row) for v in (visit_a, visit_b)]
-    specs += [pl.BlockSpec(w.shape, lambda t, table: (0, 0)) for w in weights]
+    values = weights.shape[-1]
+    count = len(OFFSETS)
+    blocks = 2 * count
+    out = pl.BlockSpec((tokens, values), lambda i, table: (0, 0))
     return pl.pallas_call(
-        functools.partial(project_kernel, blocks, width),
+        functools.partial(project_kernel, width),
         grid_spec=pltpu.PrefetchScalarGridSpec(
             num_scalar_prefetch=1,
-            grid=(tokens // step,),
-            in_specs=specs,
-            out_specs=[pl.BlockSpec((step, values), row)] * 2,
+            grid=(count,),
+            in_specs=[
+                pl.BlockSpec((tokens, width), lambda i, table: (0, table[2 * i])),
+                pl.BlockSpec((tokens, width), lambda i, table: (0, table[2 * i + 1])),
+                pl.BlockSpec((tokens, 2 * width), lambda i, table: (0, jnp.minimum(i, FIRST - 1))),
+                pl.BlockSpec((tokens, 2 * width), lambda i, table: (0, jnp.maximum(i - FIRST, 0))),
+                pl.BlockSpec((1, 2, width, values), lambda i, table: ((table[2 * i] // NC) % NZ, 0, 0, 0)),
+            ],
+            out_specs=[out, out],
         ),
         out_shape=[jax.ShapeDtypeStruct((tokens, values), F32)] * 2,
         compiler_params=params(),
         cost_estimate=pl.CostEstimate(
             flops=4 * tokens * blocks * width * values, bytes_accessed=4 * tokens * blocks * width + 2 * blocks * width * values, transcendentals=0
         ),
-    )(table, *([hidden] * blocks), visit_a, visit_b, *weights)
+    )(table, hidden, hidden, visit_a, visit_b, weights)
+
+
+def diagonal(width):
+    return lax.broadcasted_iota(jnp.int32, (width, width), 0) == lax.broadcasted_iota(jnp.int32, (width, width), 1)
+
+
+def as_column(row):
+    return jnp.sum(jnp.where(diagonal(row.shape[1]), row, 0.0), axis=1, keepdims=True)
+
+
+def as_row(column):
+    return jnp.sum(jnp.where(diagonal(column.shape[0]), column, 0.0), axis=0, keepdims=True)
+
+
+def scale_kernel(gain, weight, out):
+    out[...] = (weight[0].astype(F32) * as_column(gain[...].astype(F32))).astype(BF16)
+
+
+def scale_weight(gain, weight):
+    return pl.pallas_call(scale_kernel, out_shape=jax.ShapeDtypeStruct(weight.shape[1:], BF16), compiler_params=params())(gain, weight)
+
+
+def finish_kernel(total, gain, weight, grad_weight_in, grad_gain_in, grad_weight, grad_gain):
+    summed = total[...].astype(F32).T
+    grad_weight[0] = grad_weight_in[0] + as_column(gain[...].astype(F32)) * summed
+    grad_gain[...] = grad_gain_in[...] + as_row(jnp.sum(weight[0].astype(F32) * summed, axis=1, keepdims=True))
+
+
+def finish(total, gain, weight, grad_weight_in, grad_gain_in):
+    return pl.pallas_call(
+        finish_kernel,
+        out_shape=[jax.ShapeDtypeStruct(a.shape, F32) for a in (grad_weight_in, grad_gain_in)],
+        compiler_params=params(),
+    )(total, gain, weight, grad_weight_in, grad_gain_in)
 
 
 def add(*terms):
@@ -205,19 +235,17 @@
 
 
 def per_device(hidden, gain, value_weight, cotangent, grad_weight_in, grad_gain_in):
-    weight = value_weight[0].astype(F32)
-    gains = gain[0].astype(F32)
-    width = weight.shape[0]
-    place = lax.axis_index("fsdp")
-    core, z, x = place % NC, (place // NC) % NZ, place // (NC * NZ)
+    width = value_weight.shape[1]
+    x, z, core = (lax.axis_index(a) for a in ("x", "z", "core"))
     table = jnp.stack(
         [fsdp_index(x ^ flip, (z + off + NZ) % NZ, core) for off in OFFSETS for flip in (1, 0)]
     ).astype(jnp.int32)
 
-    scaled_weight = (weight * gains[:, None]).astype(BF16)
-    layer = [along_blk(scaled_weight, 1, 0), along_blk(scaled_weight, 1, 1)]
-
-    scale, cot_t, send_a, send_b = prepare(table, hidden, cotangent, width)
+    scaled_weight = scale_weight(gain, value_weight)
+    layer = jnp.stack([along_blk(scaled_weight, 1, 0), along_blk(scaled_weight, 1, 1)])
+    weights = lax.all_gather(layer, "z", axis=0)
+
+    scale, cot_t, send_a, send_b = prepare(table, hidden, cotangent, scaled_weight, width)
     visit_a = swap_core(send_a)
     cot_t_sibling = swap_core(cot_t)
     visit_b = swap_core(send_b)
@@ -240,35 +268,25 @@
             sum_up, sum_down = add(*mine[off], up), add(*mine[-off], down)
     total = along_blk(add(*mine[0], up, down), -1, 0)
 
-    blocks = {(0, flip): [layer[flip]] for flip in (0, 1)}
-    for flip in (0, 1):
-        from_below, from_above = layer[flip], layer[flip]
-        for step in (1, 2, 3):
-            from_below, from_above = along_z(from_below, 1), along_z(from_above, -1)
-            blocks[-step, flip], blocks[step, flip] = [from_below], [from_above]
-        blocks[4, flip] = [along_z(from_below[:width // 2], 1), along_z(from_above[width // 2:], -1)]
-    weights = [w for off in OFFSETS for flip in (1, 0) for w in blocks[off, flip]]
     product, product_sibling = project(table, hidden, visit_a, visit_b, weights, width)
     values = ((product + swap_core(product_sibling)) * scale).astype(BF16)
 
-    summed = total.astype(F32).T
-    grad_weight = grad_weight_in + (gains[:, None] * summed)[None]
-    grad_gain = grad_gain_in + jnp.sum(weight * summed, axis=1)[None]
-    return values, grad_weight, grad_gain
+    return values, *finish(total, gain, value_weight, grad_weight_in, grad_gain_in)
 
 
 def solution(mesh):
+    fsdp = ("x", "z", "core")
     return jax.shard_map(
         per_device,
-        mesh=mesh,
+        mesh=Mesh(mesh.devices.reshape(NB, NX, NZ, NC), ("blk", *fsdp)),
         in_specs=(
-            P(("blk", "fsdp"), None),
-            P("blk", "fsdp"),
-            P("blk", "fsdp", None),
-            P(("blk", "fsdp"), None),
-            P("blk", "fsdp", None),
-            P("blk", "fsdp"),
-        ),
-        out_specs=(P(("blk", "fsdp"), None), P("blk", "fsdp", None), P("blk", "fsdp")),
+            P(("blk", *fsdp), None),
+            P("blk", fsdp),
+            P("blk", fsdp, None),
+            P(("blk", *fsdp), None),
+            P("blk", fsdp, None),
+            P("blk", fsdp),
+        ),
+        out_specs=(P(("blk", *fsdp), None), P("blk", fsdp, None), P("blk", fsdp)),
         check_vma=False,
     )

time: 189 us -> 154 us (0.81); the launches traced: 185 us -> 152 us
  starting transfers between devices: 56.4 us -> 34 us
  local copies, waits for them, and re-layouts: 26.8 us -> 4.99 us
  between operations: 1.04 us -> 14.3 us
  waiting for transfers between devices: 61 us -> 49.8 us
  Pallas kernels: 33.1 us -> 39 us
  other arithmetic: 6.5 us -> 9.95 us
    ppermute x39 -> x23, starting transfers between devices: 56.4 us -> 34 us  [the longest x20 31 us: move(): return lax.ppermute(value, ('x', 'z', 'core'), pairs)]
    ppermute x18 -> x0, local copies, waits for them, and re-layouts: 18.7 us -> none  [the longest x16 17 us: move(): return lax.ppermute(value, 'fsdp', pairs)]
    ppermute x39 -> x23, waiting for transfers between devices: 61 us -> 49.8 us  [the longest x20 29.3 us: move(): return lax.ppermute(value, ('x', 'z', 'core'), pairs)]
    pallas_call x1 -> x3, Pallas kernels: 10.8 us -> 16.7 us  [the longest x1 12.6 us: project(): pl.pallas_call(functools.partial(project_kernel, width), grid_spec=pltpu....]
    convert_element_type x8, other arithmetic: 3.66 us -> 7.98 us  [add(): return sum((t.astype(F32) for t in terms)).astype(BF16)]
    slice x4 -> x0, local copies, waits for them, and re-layouts: 2.7 us -> none  [the longest x2 1.36 us: per_device(): from_below[:width // 2]]
    unnamed x37 -> x20, local copies, waits for them, and re-layouts: 4.79 us -> 4.28 us
  transfers between devices with their start and end apart: 39 -> 24, of which waited for: 15 -> 9; matrix products, arithmetic and copies ran while one was open for 14% -> 6% of each run, Pallas kernels for 8% -> 24%
where the time goes in v2:
time: 154 us; the launch traced here: 152 us
  waiting for transfers between devices  49.8 us (32%)
  Pallas kernels  39 us (25%)
  starting transfers between devices  34 us (22%)
  between operations  14.3 us (9%)
  other arithmetic  9.95 us (6%)
  local copies, waits for them, and re-layouts  4.99 us (3%)
    ppermute x20, starting transfers between devices, move(): return lax.ppermute(value, ('x', 'z', 'core'), pairs)  31 us
    ppermute x20, waiting for transfers between devices, move(): return lax.ppermute(value, ('x', 'z', 'core'), pairs)  29.3 us
    ppermute x3, waiting for transfers between devices, along_blk(): return lax.ppermute(value, ('blk', 'x', 'z', 'core'), pairs)  20.5 us
    pallas_call x2, Pallas kernels, gradient(): pl.pallas_call(functools.partial(gradient_kernel, count, width), grid_spe...  14.7 us
    pallas_call x1, Pallas kernels, project(): pl.pallas_call(functools.partial(project_kernel, width), grid_spec=pltpu....  12.6 us
    convert_element_type x8, other arithmetic, add(): return sum((t.astype(F32) for t in terms)).astype(BF16)  7.98 us
    pallas_call x1, Pallas kernels, prepare(): pl.pallas_call(functools.partial(prepare_kernel, width), grid_spec=pltpu....  7.58 us
    unnamed x20, local copies, waits for them, and re-layouts  4.28 us
  transfers between devices with their start and end apart: 24, of which 9 were waited for; matrix products, arithmetic and copies ran while one was open for 6% of the time, Pallas kernels for 24%

profile of v2, /device:TPU:4, one launch (start us, length us, event | category | flops | bytes accessed | tf_op | source)
XLA Modules:
  0.0 152.1 jit_solution(13634824112654819505)
XLA Ops:
  7.2 1.8 %shard_map.85.after = bf16[256,512]{1,0:T(8,128)(2,1)} custom-call(bf16[1,256]{1,0:T(2,128)(2,1)} %gain.3, bf16[1,256,512]{2,1,0:T(8,128)(2,1)} %weight.3), custom_call_target="tpu_custom_call" | custom-call | tf_op jit(solution)/shard_map/pallas_call | solution.py:216
  9.0 0.5 collective-permute-start.3
  9.6 2.2 %collective-permute-start.2 = (bf16[256,512]{1,0:T(8,128)(2,1)}, bf16[256,512]{1,0:T(8,128)(2,1)S(1)}, u32[]{:S(2)}, u32[]{:S(2)}) collective-permute-start(bf16[256,512]{1,0:T(8,128)(2,1)} %shard_map.85.after), channel_id=1, source_target_pairs={{0,32},{1,33},{2,34},{3,35},{4,36},{5,37},{6,38},{7,39},{8,40},{9,... | collective-permute-start | bytes 786440 | tf_op jit(solution)/shard_map/ppermute | solution.py:55
  11.7 13.0 %collective-permute-done.3 = bf16[256,512]{1,0:T(8,128)(2,1)S(1)} collective-permute-done((bf16[256,512]{1,0:T(8,128)(2,1)}, bf16[256,512]{1,0:T(8,128)(2,1)S(1)}, u32[]{:S(2)}, u32[]{:S(2)}) %collective-permute-start.3) | collective-permute-done | bytes 262176 | tf_op jit(solution)/shard_map/ppermute | solution.py:55
  24.7 0.3 collective-permute-done.2
  25.0 0.8 pad_maximum_fusion
  26.0 0.7 stack.76.table
  26.7 7.6 %shard_map.86 = (f32[512,1]{1,0:T(8,128)}, bf16[512,512]{1,0:T(8,128)(2,1)}, bf16[512,1024]{1,0:T(8,128)(2,1)}, bf16[512,3072]{1,0:T(8,128)(2,1)}) custom-call(s32[16]{0:T(128)} %stack.76.table, bf16[512,8192]{1,0:T(8,128)(2,1)} %own_same.5, bf16[512,512]{1,0:T(8,128)(2,1)} %cot.1, bf16[256,512]{1,0:T(8,128)(2,1)} %shard_map.85.after), custom_call_target="tpu_custom_call" | custom-call | flops 12582912 | bytes 12582912 | tf_op jit(solution)/shard_map/pallas_call | solution.py:88
  34.3 0.5 collective-permute-start
  34.8 0.1 collective-permute-start.5
  34.8 7.5 %collective-permute-done.5.cot_t_sibling = bf16[512,512]{1,0:T(8,128)(2,1)S(1)} collective-permute-done((bf16[512,512]{1,0:T(8,128)(2,1)}, bf16[512,512]{1,0:T(8,128)(2,1)S(1)}, u32[]{:S(2)}, u32[]{:S(2)}) %collective-permute-start.5) | collective-permute-done | bytes 524320 | tf_op jit(solution)/shard_map/ppermute | solution.py:31
  42.4 0.8 copy-done.2
  43.2 1.1 copy-done.1
  44.3 4.9 %shard_map.89 = (bf16[512,256]{1,0:T(8,128)(2,1)}, bf16[512,256]{1,0:T(8,128)(2,1)}, bf16[512,256]{1,0:T(8,128)(2,1)}, bf16[512,256]{1,0:T(8,128)(2,1)}) custom-call(s32[16]{0:T(128)} %stack.76.table, bf16[512,8192]{1,0:T(8,128)(2,1)} %own_same.5, bf16[512,8192]{1,0:T(8,128)(2,1)} %own_same.5, bf16[512,1024]{1,0:T(8,128)(2,1)} %copy-done.1, ...), custom_call_target="tpu_custom_call" | custom-call | flops 1073741824 | bytes 3145728 | tf_op jit(solution)/shard_map/pallas_call | solution.py:130
  49.1 1.9 %collective-permute-start.10 = (bf16[512,256]{1,0:T(8,128)(2,1)}, bf16[512,256]{1,0:T(8,128)(2,1)S(1)}, u32[]{:S(2)}, u32[]{:S(2)}) collective-permute-start(bf16[512,256]{1,0:T(8,128)(2,1)} %get-tuple-element.42), channel_id=1, source_target_pairs={{0,16},{1,17},{2,18},{3,19},{4,20},{5,21},{6,22},{7,23},{8,24},{9,... | collective-permute-start | bytes 786440 | tf_op jit(solution)/shard_map/ppermute | solution.py:31
  51.0 1.7 %collective-permute-start.9 = (bf16[512,256]{1,0:T(8,128)(2,1)}, bf16[512,256]{1,0:T(8,128)(2,1)S(1)}, u32[]{:S(2)}, u32[]{:S(2)}) collective-permute-start(bf16[512,256]{1,0:T(8,128)(2,1)} %get-tuple-element.40), channel_id=1, source_target_pairs={{0,16},{1,17},{2,18},{3,19},{4,20},{5,21},{6,22},{7,23},{8,24},{9,... | collective-permute-start | bytes 786440 | tf_op jit(solution)/shard_map/ppermute | solution.py:31
  52.7 7.3 %collective-permute-done.10 = bf16[512,256]{1,0:T(8,128)(2,1)S(1)} collective-permute-done((bf16[512,256]{1,0:T(8,128)(2,1)}, bf16[512,256]{1,0:T(8,128)(2,1)S(1)}, u32[]{:S(2)}, u32[]{:S(2)}) %collective-permute-start.10) | collective-permute-done | bytes 262176 | tf_op jit(solution)/shard_map/ppermute | solution.py:31
  60.0 1.0 add_convert_fusion.5
  61.1 5.9 %collective-permute-start.18 = (bf16[256,256]{1,0:T(8,128)(2,1)S(1)}, bf16[256,256]{1,0:T(8,128)(2,1)S(1)}, u32[]{:S(2)}, u32[]{:S(2)}) collective-permute-start(bf16[256,256]{1,0:T(8,128)(2,1)S(1)} %get-tuple-element.56), channel_id=1, source_target_pairs={{0,14},{1,15},{2,0},{3,1},{4,2},{5,3},{6,4},{7,5},{8,6},{9,7},{10,... | collective-permute-start | bytes 393224 | tf_op jit(solution)/shard_map/ppermute | solution.py:31
  67.0 1.6 %copy-done = bf16[512,3072]{1,0:T(8,128)(2,1)} copy-done((bf16[512,3072]{1,0:T(8,128)(2,1)}, bf16[512,3072]{1,0:T(8,128)(2,1)S(1)}, u32[]{:S(2)}) %copy-start) | copy-done | bytes 3145752
  68.6 9.9 %shard_map.88 = (bf16[512,256]{1,0:T(8,128)(2,1)}, bf16[512,256]{1,0:T(8,128)(2,1)}, bf16[512,256]{1,0:T(8,128)(2,1)}, bf16[512,256]{1,0:T(8,128)(2,1)}, bf16[51...) custom-call(s32[16]{0:T(128)} %stack.76.table, ...), custom_call_target="tpu_custom_call" | custom-call | flops 3221225472 | bytes 9437184 | tf_op jit(solution)/shard_map/pallas_call | solution.py:130
  78.5 1.9 %collective-permute-start.17 = (bf16[512,256]{1,0:T(8,128)(2,1)}, bf16[512,256]{1,0:T(8,128)(2,1)S(1)}, u32[]{:S(2)}, u32[]{:S(2)}) collective-permute-start(bf16[512,256]{1,0:T(8,128)(2,1)} %get-tuple-element.48), channel_id=1, source_target_pairs={{0,16},{1,17},{2,18},{3,19},{4,20},{5,21},{6,22},{7,23},{8,24},{9,... | collective-permute-start | bytes 786440 | tf_op jit(solution)/shard_map/ppermute | solution.py:31
  80.6 1.8 %collective-permute-start.16 = (bf16[512,256]{1,0:T(8,128)(2,1)}, bf16[512,256]{1,0:T(8,128)(2,1)S(1)}, u32[]{:S(2)}, u32[]{:S(2)}) collective-permute-start(bf16[512,256]{1,0:T(8,128)(2,1)} %get-tuple-element.46), channel_id=1, source_target_pairs={{0,16},{1,17},{2,18},{3,19},{4,20},{5,21},{6,22},{7,23},{8,24},{9,... | collective-permute-start | bytes 786440 | tf_op jit(solution)/shard_map/ppermute | solution.py:31
  82.4 1.9 %collective-permute-start.8 = (bf16[512,256]{1,0:T(8,128)(2,1)}, bf16[512,256]{1,0:T(8,128)(2,1)S(1)}, u32[]{:S(2)}, u32[]{:S(2)}) collective-permute-start(bf16[512,256]{1,0:T(8,128)(2,1)} %get-tuple-element.38), channel_id=1, source_target_pairs={{0,16},{1,17},{2,18},{3,19},{4,20},{5,21},{6,22},{7,23},{8,24},{9,... | collective-permute-start | bytes 786440 | tf_op jit(solution)/shard_map/ppermute | solution.py:31
  84.2 5.3 %collective-permute-done.17 = bf16[512,256]{1,0:T(8,128)(2,1)S(1)} collective-permute-done((bf16[512,256]{1,0:T(8,128)(2,1)}, bf16[512,256]{1,0:T(8,128)(2,1)S(1)}, u32[]{:S(2)}, u32[]{:S(2)}) %collective-permute-start.17) | collective-permute-done | bytes 262176 | tf_op jit(solution)/shard_map/ppermute | solution.py:31
  89.5 1.1 add_convert_fusion.7
  90.6 3.3 %collective-permute-start.19 = (bf16[512,256]{1,0:T(8,128)(2,1)S(1)}, bf16[512,256]{1,0:T(8,128)(2,1)S(1)}, u32[]{:S(2)}, u32[]{:S(2)}) collective-permute-start(bf16[512,256]{1,0:T(8,128)(2,1)S(1)} %pad_maximum_fusion.2), channel_id=1, source_target_pairs={{0,14},{1,15},{2,0},{3,1},{4,2},{5,3},{6,4},{7,5},{8,6},{9,7},{10,... | collective-permute-start | bytes 786440 | tf_op jit(solution)/shard_map/ppermute | solution.py:31
  93.9 1.9 %collective-permute-start.15 = (bf16[512,256]{1,0:T(8,128)(2,1)}, bf16[512,256]{1,0:T(8,128)(2,1)S(1)}, u32[]{:S(2)}, u32[]{:S(2)}) collective-permute-start(bf16[512,256]{1,0:T(8,128)(2,1)} %get-tuple-element.44), channel_id=1, source_target_pairs={{0,16},{1,17},{2,18},{3,19},{4,20},{5,21},{6,22},{7,23},{8,24},{9,... | collective-permute-start | bytes 786440 | tf_op jit(solution)/shard_map/ppermute | solution.py:31
  95.7 1.7 %collective-permute-start.7 = (bf16[512,256]{1,0:T(8,128)(2,1)}, bf16[512,256]{1,0:T(8,128)(2,1)S(1)}, u32[]{:S(2)}, u32[]{:S(2)}) collective-permute-start(bf16[512,256]{1,0:T(8,128)(2,1)} %get-tuple-element.36), channel_id=1, source_target_pairs={{0,16},{1,17},{2,18},{3,19},{4,20},{5,21},{6,22},{7,23},{8,24},{9,... | collective-permute-start | bytes 786440 | tf_op jit(solution)/shard_map/ppermute | solution.py:31
  97.4 3.3 %collective-permute-done.8 = bf16[512,256]{1,0:T(8,128)(2,1)S(1)} collective-permute-done((bf16[512,256]{1,0:T(8,128)(2,1)}, bf16[512,256]{1,0:T(8,128)(2,1)S(1)}, u32[]{:S(2)}, u32[]{:S(2)}) %collective-permute-start.8) | collective-permute-done | bytes 262176 | tf_op jit(solution)/shard_map/ppermute | solution.py:31
  100.7 1.9 %collective-permute-start.6 = (bf16[512,256]{1,0:T(8,128)(2,1)}, bf16[512,256]{1,0:T(8,128)(2,1)S(1)}, u32[]{:S(2)}, u32[]{:S(2)}) collective-permute-start(bf16[512,256]{1,0:T(8,128)(2,1)} %get-tuple-element.34), channel_id=1, source_target_pairs={{0,16},{1,17},{2,18},{3,19},{4,20},{5,21},{6,22},{7,23},{8,24},{9,... | collective-permute-start | bytes 786440 | tf_op jit(solution)/shard_map/ppermute | solution.py:31
  102.6 1.8 %add_convert_fusion.4 = bf16[512,256]{1,0:T(8,128)(2,1)} fusion(bf16[512,256]{1,0:T(8,128)(2,1)S(1)} %collective-permute-done.12, bf16[512,256]{1,0:T(8,128)(2,1)S(1)} %collective-permute-done.8, bf16[512,256]{1,0:T(8,128)(2,1)} %get-tuple-element.37), kind=kLoop, calls=%fused_computation.6 | loop fusion | flops 786432 | bytes 1048576 | tf_op jit(solution)/shard_map/convert_element_type | solution.py:234
  104.4 1.8 %add_convert_fusion.2 = bf16[512,256]{1,0:T(8,128)(2,1)} fusion(bf16[512,256]{1,0:T(8,128)(2,1)S(1)} %collective-permute-done.19, bf16[512,256]{1,0:T(8,128)(2,1)S(1)} %collective-permute-done.16, bf16[512,256]{1,0:T(8,128)(2,1)} %get-tuple-element.45), kind=kLoop, calls=%fused_computation.4 | loop fusion | flops 786432 | bytes 1048576 | tf_op jit(solution)/shard_map/convert_element_type | solution.py:234
  106.1 3.2 %collective-permute-start.20 = (bf16[512,256]{1,0:T(8,128)(2,1)}, bf16[512,256]{1,0:T(8,128)(2,1)}, u32[]{:S(2)}, u32[]{:S(2)}) collective-permute-start(bf16[512,256]{1,0:T(8,128)(2,1)} %add_convert_fusion.2), channel_id=1, source_target_pairs={{0,14},{1,15},{2,0},{3,1},{4,2},{5,3},{6,4},{7,5},{8,6},{9,7},{10,... | collective-permute-start | bytes 786440 | tf_op jit(solution)/shard_map/ppermute | solution.py:31
  109.4 12.6 %shard_map.87 = (f32[512,512]{1,0:T(8,128)}, f32[512,512]{1,0:T(8,128)}) custom-call(s32[16]{0:T(128)} %stack.76.table, bf16[512,8192]{1,0:T(8,128)(2,1)} %own_same.5, bf16[512,8192]{1,0:T(8,128)(2,1)} %own_same.5, bf16[512,1024]{1,0:T(8,128)(2,1)} %copy-done.1, bf16[512,3072]{1,0:T(8,128)(2,1)} %copy-done, bf16[8,2,256,512]{3,2,1,0:T(8,128)(2,1)} %bitcast.19), custom_call_target="tpu_custom_call" | custom-call | flops 4294967296 | bytes 12582912 | tf_op jit(solution)/shard_map/pallas_call | solution.py:177
  122.0 0.1 collective-permute-start.4
  122.2 1.1 add_convert_fusion.3
  123.4 1.0 add_convert_fusion.1
  124.4 3.3 %collective-permute-start.21 = (bf16[512,256]{1,0:T(8,128)(2,1)S(1)}, bf16[512,256]{1,0:T(8,128)(2,1)S(1)}, u32[]{:S(2)}, u32[]{:S(2)}) collective-permute-start(bf16[512,256]{1,0:T(8,128)(2,1)S(1)} %add_convert_fusion.1), channel_id=1, source_target_pairs={{0,14},{1,15},{2,0},{3,1},{4,2},{5,3},{6,4},{7,5},{8,6},{9,7},{10,... | collective-permute-start | bytes 786440 | tf_op jit(solution)/shard_map/ppermute | solution.py:31
  127.7 5.5 %collective-permute-done.14 = bf16[512,256]{1,0:T(8,128)(2,1)S(1)} collective-permute-done((bf16[512,256]{1,0:T(8,128)(2,1)S(1)}, bf16[512,256]{1,0:T(8,128)(2,1)S(1)}, u32[]{:S(2)}, u32[]{:S(2)}) %collective-permute-start.14) | collective-permute-done | bytes 262176 | tf_op jit(solution)/shard_map/ppermute | solution.py:31
  133.2 0.4 collective-permute-done.21
  133.6 0.1 add_convert_fusion
  133.7 0.3 collective-permute-start.22
  134.0 0.1 reduce
  134.2 7.2 %collective-permute-done.22.total = bf16[512,256]{1,0:T(8,128)(2,1)S(1)} collective-permute-done((bf16[512,256]{1,0:T(8,128)(2,1)S(1)}, bf16[512,256]{1,0:T(8,128)(2,1)S(1)}, u32[]{:S(2)}, u32[]{:S(2)}) %collective-permute-start.22) | collective-permute-done | bytes 262176 | tf_op jit(solution)/shard_map/ppermute | solution.py:55
  141.4 0.7 copy-done.9
  142.1 2.3 %shard_map.90 = (f32[1,256,512]{2,1,0:T(8,128)}, f32[1,256]{1,0:T(1,128)}) custom-call(bf16[512,256]{1,0:T(8,128)(2,1)} %copy-done.9, bf16[1,256]{1,0:T(2,128)(2,1)} %gain.3, bf16[1,256,512]{2,1,0:T(8,128)(2,1)} %weight.3, f32[1,256,512]{2,1,0:T(8,128)} %grad_weight_in.1, f32[1,256]{1,0:T(1,128)} %grad_gain_in.1), custom_call_target="tpu_custom_call" | custom-call | tf_op jit(solution)/shard_map/pallas_call | solution.py:226
  144.3 0.9 multiply_convert_fusion
  (42 shorter events, 0.4 us)
Async XLA Ops:
  7.2 102.2 %all-gather.3.cloned.1.call-start = ((), (), s32[]{:S(2)}) async-start(), calls=%async_computation | async-start | bytes 4718592 | tf_op jit(solution)/shard_map/all_gather | solution.py:246
  9.0 15.7 %collective-permute-start.3 = (bf16[256,512]{1,0:T(8,128)(2,1)}, bf16[256,512]{1,0:T(8,128)(2,1)S(1)}, u32[]{:S(2)}, u32[]{:S(2)}) collective-permute-start(bf16[256,512]{1,0:T(8,128)(2,1)} %shard_map.85.after), channel_id=1, source_target_pairs={{0,48},{1,49},{2,50},{3,51},{4,52},{5,53},{6,54},{7,55},{8,56},{9,... | collective-permute-start | bytes 786440 | tf_op jit(solution)/shard_map/ppermute | solution.py:55
  9.6 15.4 %collective-permute-start.2 = (bf16[256,512]{1,0:T(8,128)(2,1)}, bf16[256,512]{1,0:T(8,128)(2,1)S(1)}, u32[]{:S(2)}, u32[]{:S(2)}) collective-permute-start(bf16[256,512]{1,0:T(8,128)(2,1)} %shard_map.85.after), channel_id=1, source_target_pairs={{0,32},{1,33},{2,34},{3,35},{4,36},{5,37},{6,38},{7,39},{8,40},{9,... | collective-permute-start | bytes 786440 | tf_op jit(solution)/shard_map/ppermute | solution.py:55
  34.2 32.7 %collective-permute-start.1 = (bf16[512,3072]{1,0:T(8,128)(2,1)}, bf16[512,3072]{1,0:T(8,128)(2,1)S(1)}, u32[]{:S(2)}, u32[]{:S(2)}) collective-permute-start(bf16[512,3072]{1,0:T(8,128)(2,1)} %get-tuple-element.28), channel_id=1, source_target_pairs={{0,1},{1,0},{2,3},{3,2},{4,5},{5,4},{6,7},{7,6},{8,9},{9,8},{10,11... | collective-permute-start | bytes 9437192 | tf_op jit(solution)/shard_map/ppermute | solution.py:31
  34.3 8.1 %collective-permute-start = (bf16[512,1024]{1,0:T(8,128)(2,1)}, bf16[512,1024]{1,0:T(8,128)(2,1)S(1)}, u32[]{:S(2)}, u32[]{:S(2)}) collective-permute-start(bf16[512,1024]{1,0:T(8,128)(2,1)} %get-tuple-element.27), channel_id=1, source_target_pairs={{0,1},{1,0},{2,3},{3,2},{4,5},{5,4},{6,7},{7,6},{8,9},{9,8},{10,11... | collective-permute-start | bytes 3145736 | tf_op jit(solution)/shard_map/ppermute | solution.py:31
  34.8 7.6 %collective-permute-start.5 = (bf16[512,512]{1,0:T(8,128)(2,1)}, bf16[512,512]{1,0:T(8,128)(2,1)S(1)}, u32[]{:S(2)}, u32[]{:S(2)}) collective-permute-start(bf16[512,512]{1,0:T(8,128)(2,1)} %get-tuple-element.32.cot_t), channel_id=1, source_target_pairs={{0,1},{1,0},{2,3},{3,2},{4,5},{5,4},{6,7},{7,6},{8,9},{9,8},{10,11... | collective-permute-start | bytes 1572872 | tf_op jit(solution)/shard_map/ppermute | solution.py:31
  42.4 0.8 copy-start.2
  43.2 1.1 copy-start.1
  49.1 10.9 %collective-permute-start.10 = (bf16[512,256]{1,0:T(8,128)(2,1)}, bf16[512,256]{1,0:T(8,128)(2,1)S(1)}, u32[]{:S(2)}, u32[]{:S(2)}) collective-permute-start(bf16[512,256]{1,0:T(8,128)(2,1)} %get-tuple-element.42), channel_id=1, source_target_pairs={{0,16},{1,17},{2,18},{3,19},{4,20},{5,21},{6,22},{7,23},{8,24},{9,... | collective-permute-start | bytes 786440 | tf_op jit(solution)/shard_map/ppermute | solution.py:31
  51.0 29.4 %collective-permute-start.9 = (bf16[512,256]{1,0:T(8,128)(2,1)}, bf16[512,256]{1,0:T(8,128)(2,1)S(1)}, u32[]{:S(2)}, u32[]{:S(2)}) collective-permute-start(bf16[512,256]{1,0:T(8,128)(2,1)} %get-tuple-element.40), channel_id=1, source_target_pairs={{0,16},{1,17},{2,18},{3,19},{4,20},{5,21},{6,22},{7,23},{8,24},{9,... | collective-permute-start | bytes 786440 | tf_op jit(solution)/shard_map/ppermute | solution.py:31
  61.1 23.2 %collective-permute-start.18 = (bf16[256,256]{1,0:T(8,128)(2,1)S(1)}, bf16[256,256]{1,0:T(8,128)(2,1)S(1)}, u32[]{:S(2)}, u32[]{:S(2)}) collective-permute-start(bf16[256,256]{1,0:T(8,128)(2,1)S(1)} %get-tuple-element.56), channel_id=1, source_target_pairs={{0,14},{1,15},{2,0},{3,1},{4,2},{5,3},{6,4},{7,5},{8,6},{9,7},{10,... | collective-permute-start | bytes 393224 | tf_op jit(solution)/shard_map/ppermute | solution.py:31
  67.0 13.4 %copy-start.5 = (bf16[512,256]{1,0:T(8,128)(2,1)S(1)}, bf16[512,256]{1,0:T(8,128)(2,1)}, u32[]{:S(2)}) copy-start(bf16[512,256]{1,0:T(8,128)(2,1)} %get-tuple-element.39) | copy-start | bytes 786436
  67.0 13.4 %collective-permute-start.11 = (bf16[256,256]{1,0:T(8,128)(2,1)S(1)}, bf16[256,256]{1,0:T(8,128)(2,1)S(1)}, u32[]{:S(2)}, u32[]{:S(2)}) collective-permute-start(bf16[256,256]{1,0:T(8,128)(2,1)S(1)} %get-tuple-element.55), channel_id=1, source_target_pairs={{0,2},{1,3},{2,4},{3,5},{4,6},{5,7},{6,8},{7,9},{8,10},{9,11},{10,... | collective-permute-start | bytes 393224 | tf_op jit(solution)/shard_map/ppermute | solution.py:31
  67.0 1.6 %copy-start = (bf16[512,3072]{1,0:T(8,128)(2,1)}, bf16[512,3072]{1,0:T(8,128)(2,1)S(1)}, u32[]{:S(2)}) copy-start(bf16[512,3072]{1,0:T(8,128)(2,1)S(1)} %collective-permute-done.1.visit_b.visiting) | copy-start | bytes 9437188
  78.5 11.0 %collective-permute-start.17 = (bf16[512,256]{1,0:T(8,128)(2,1)}, bf16[512,256]{1,0:T(8,128)(2,1)S(1)}, u32[]{:S(2)}, u32[]{:S(2)}) collective-permute-start(bf16[512,256]{1,0:T(8,128)(2,1)} %get-tuple-element.48), channel_id=1, source_target_pairs={{0,16},{1,17},{2,18},{3,19},{4,20},{5,21},{6,22},{7,23},{8,24},{9,... | collective-permute-start | bytes 786440 | tf_op jit(solution)/shard_map/ppermute | solution.py:31
  80.5 15.2 %collective-permute-start.12 = (bf16[512,256]{1,0:T(8,128)(2,1)S(1)}, bf16[512,256]{1,0:T(8,128)(2,1)S(1)}, u32[]{:S(2)}, u32[]{:S(2)}) collective-permute-start(bf16[512,256]{1,0:T(8,128)(2,1)S(1)} %pad_maximum_fusion.1), channel_id=1, source_target_pairs={{0,2},{1,3},{2,4},{3,5},{4,6},{5,7},{6,8},{7,9},{8,10},{9,11},{10,... | collective-permute-start | bytes 786440 | tf_op jit(solution)/shard_map/ppermute | solution.py:31
  80.6 23.8 %collective-permute-start.16 = (bf16[512,256]{1,0:T(8,128)(2,1)}, bf16[512,256]{1,0:T(8,128)(2,1)S(1)}, u32[]{:S(2)}, u32[]{:S(2)}) collective-permute-start(bf16[512,256]{1,0:T(8,128)(2,1)} %get-tuple-element.46), channel_id=1, source_target_pairs={{0,16},{1,17},{2,18},{3,19},{4,20},{5,21},{6,22},{7,23},{8,24},{9,... | collective-permute-start | bytes 786440 | tf_op jit(solution)/shard_map/ppermute | solution.py:31
  82.4 18.4 %collective-permute-start.8 = (bf16[512,256]{1,0:T(8,128)(2,1)}, bf16[512,256]{1,0:T(8,128)(2,1)S(1)}, u32[]{:S(2)}, u32[]{:S(2)}) collective-permute-start(bf16[512,256]{1,0:T(8,128)(2,1)} %get-tuple-element.38), channel_id=1, source_target_pairs={{0,16},{1,17},{2,18},{3,19},{4,20},{5,21},{6,22},{7,23},{8,24},{9,... | collective-permute-start | bytes 786440 | tf_op jit(solution)/shard_map/ppermute | solution.py:31
  90.6 13.8 %collective-permute-start.19 = (bf16[512,256]{1,0:T(8,128)(2,1)S(1)}, bf16[512,256]{1,0:T(8,128)(2,1)S(1)}, u32[]{:S(2)}, u32[]{:S(2)}) collective-permute-start(bf16[512,256]{1,0:T(8,128)(2,1)S(1)} %pad_maximum_fusion.2), channel_id=1, source_target_pairs={{0,14},{1,15},{2,0},{3,1},{4,2},{5,3},{6,4},{7,5},{8,6},{9,7},{10,... | collective-permute-start | bytes 786440 | tf_op jit(solution)/shard_map/ppermute | solution.py:31
  93.9 29.5 %collective-permute-start.15 = (bf16[512,256]{1,0:T(8,128)(2,1)}, bf16[512,256]{1,0:T(8,128)(2,1)S(1)}, u32[]{:S(2)}, u32[]{:S(2)}) collective-permute-start(bf16[512,256]{1,0:T(8,128)(2,1)} %get-tuple-element.44), channel_id=1, source_target_pairs={{0,16},{1,17},{2,18},{3,19},{4,20},{5,21},{6,22},{7,23},{8,24},{9,... | collective-permute-start | bytes 786440 | tf_op jit(solution)/shard_map/ppermute | solution.py:31
  95.7 26.3 %collective-permute-start.7 = (bf16[512,256]{1,0:T(8,128)(2,1)}, bf16[512,256]{1,0:T(8,128)(2,1)S(1)}, u32[]{:S(2)}, u32[]{:S(2)}) collective-permute-start(bf16[512,256]{1,0:T(8,128)(2,1)} %get-tuple-element.36), channel_id=1, source_target_pairs={{0,16},{1,17},{2,18},{3,19},{4,20},{5,21},{6,22},{7,23},{8,24},{9,... | collective-permute-start | bytes 786440 | tf_op jit(solution)/shard_map/ppermute | solution.py:31
  100.7 27.0 %collective-permute-start.6 = (bf16[512,256]{1,0:T(8,128)(2,1)}, bf16[512,256]{1,0:T(8,128)(2,1)S(1)}, u32[]{:S(2)}, u32[]{:S(2)}) collective-permute-start(bf16[512,256]{1,0:T(8,128)(2,1)} %get-tuple-element.34), channel_id=1, source_target_pairs={{0,16},{1,17},{2,18},{3,19},{4,20},{5,21},{6,22},{7,23},{8,24},{9,... | collective-permute-start | bytes 786440 | tf_op jit(solution)/shard_map/ppermute | solution.py:31
  104.4 17.8 %collective-permute-start.13 = (bf16[512,256]{1,0:T(8,128)(2,1)}, bf16[512,256]{1,0:T(8,128)(2,1)}, u32[]{:S(2)}, u32[]{:S(2)}) collective-permute-start(bf16[512,256]{1,0:T(8,128)(2,1)} %add_convert_fusion.4), channel_id=1, source_target_pairs={{0,2},{1,3},{2,4},{3,5},{4,6},{5,7},{6,8},{7,9},{8,10},{9,11},{10,... | collective-permute-start | bytes 786440 | tf_op jit(solution)/shard_map/ppermute | solution.py:31
  106.1 17.2 %collective-permute-start.20 = (bf16[512,256]{1,0:T(8,128)(2,1)}, bf16[512,256]{1,0:T(8,128)(2,1)}, u32[]{:S(2)}, u32[]{:S(2)}) collective-permute-start(bf16[512,256]{1,0:T(8,128)(2,1)} %add_convert_fusion.2), channel_id=1, source_target_pairs={{0,14},{1,15},{2,0},{3,1},{4,2},{5,3},{6,4},{7,5},{8,6},{9,7},{10,... | collective-permute-start | bytes 786440 | tf_op jit(solution)/shard_map/ppermute | solution.py:31
  109.4 12.8 %copy-start.8 = (bf16[512,256]{1,0:T(8,128)(2,1)S(1)}, bf16[512,256]{1,0:T(8,128)(2,1)}, u32[]{:S(2)}) copy-start(bf16[512,256]{1,0:T(8,128)(2,1)} %get-tuple-element.35) | copy-start | bytes 786436
  109.4 14.0 %copy-start.7 = (bf16[512,256]{1,0:T(8,128)(2,1)S(1)}, bf16[512,256]{1,0:T(8,128)(2,1)}, u32[]{:S(2)}) copy-start(bf16[512,256]{1,0:T(8,128)(2,1)} %get-tuple-element.43) | copy-start | bytes 786436
  109.4 24.2 %copy-start.4 = (bf16[512,256]{1,0:T(8,128)(2,1)S(1)}, bf16[512,256]{1,0:T(8,128)(2,1)}, u32[]{:S(2)}) copy-start(bf16[512,256]{1,0:T(8,128)(2,1)} %get-tuple-element.33) | copy-start | bytes 786436
  109.4 24.6 %copy-start.6 = (f32[512,1]{1,0:T(8,128)S(1)}, f32[512,1]{1,0:T(8,128)}, u32[]{:S(2)}) copy-start(f32[512,1]{1,0:T(8,128)} %get-tuple-element.31) | copy-start | bytes 6148
  122.0 22.3 %copy-start.3 = (f32[512,512]{1,0:T(8,128)S(1)}, f32[512,512]{1,0:T(8,128)}, u32[]{:S(2)}) copy-start(f32[512,512]{1,0:T(8,128)} %get-tuple-element.29) | copy-start | bytes 3145732
  122.0 22.3 %collective-permute-start.4 = (f32[512,512]{1,0:T(8,128)}, f32[512,512]{1,0:T(8,128)S(1)}, u32[]{:S(2)}, u32[]{:S(2)}) collective-permute-start(f32[512,512]{1,0:T(8,128)} %get-tuple-element.30), channel_id=1, source_target_pairs={{0,1},{1,0},{2,3},{3,2},{4,5},{5,4},{6,7},{7,6},{8,9},{9,8},{10,11... | collective-permute-start | bytes 3145736 | tf_op jit(solution)/shard_map/ppermute | solution.py:31
  123.3 9.9 %collective-permute-start.14 = (bf16[512,256]{1,0:T(8,128)(2,1)S(1)}, bf16[512,256]{1,0:T(8,128)(2,1)S(1)}, u32[]{:S(2)}, u32[]{:S(2)}) collective-permute-start(bf16[512,256]{1,0:T(8,128)(2,1)S(1)} %add_convert_fusion.3), channel_id=1, source_target_pairs={{0,2},{1,3},{2,4},{3,5},{4,6},{5,7},{6,8},{7,9},{8,10},{9,11},{10,... | collective-permute-start | bytes 786440 | tf_op jit(solution)/shard_map/ppermute | solution.py:31
  124.4 9.2 %collective-permute-start.21 = (bf16[512,256]{1,0:T(8,128)(2,1)S(1)}, bf16[512,256]{1,0:T(8,128)(2,1)S(1)}, u32[]{:S(2)}, u32[]{:S(2)}) collective-permute-start(bf16[512,256]{1,0:T(8,128)(2,1)S(1)} %add_convert_fusion.1), channel_id=1, source_target_pairs={{0,14},{1,15},{2,0},{3,1},{4,2},{5,3},{6,4},{7,5},{8,6},{9,7},{10,... | collective-permute-start | bytes 786440 | tf_op jit(solution)/shard_map/ppermute | solution.py:31
  133.7 7.6 %collective-permute-start.22 = (bf16[512,256]{1,0:T(8,128)(2,1)S(1)}, bf16[512,256]{1,0:T(8,128)(2,1)S(1)}, u32[]{:S(2)}, u32[]{:S(2)}) collective-permute-start(bf16[512,256]{1,0:T(8,128)(2,1)S(1)} %add_convert_fusion), channel_id=1, source_target_pairs={{0,224},{1,225},{2,226},{3,227},{4,228},{5,229},{6,230},{7,231},{8... | collective-permute-start | bytes 786440 | tf_op jit(solution)/shard_map/ppermute | solution.py:55
  141.3 0.7 copy-start.9
Sparse Core Ops, SparseCore 0:
  26.0 60.9 all-gather.2

commit v3 on v2

v3 whole, which is shorter than its diff:
```python
import functools

import jax
import jax.numpy as jnp
from jax import lax
from jax.experimental import pallas as pl
from jax.experimental.pallas import tpu as pltpu
from jax.sharding import Mesh, PartitionSpec as P

NX, NZ, NC = 2, 8, 2
NB = 8
EPS = 1e-05
BF16 = jnp.bfloat16
F32 = jnp.float32
OFFSETS = (4, 3, -3, 2, -2, 1, -1, 0)
FIRST = 2
VMEM_LIMIT = 16 * 1024 * 1024
LOAD_LIMIT = 47 * 1024 * 1024


def fsdp_index(x, z, core):
    return (x * NZ + z) * NC + core


def move(value, change):
    pairs = [
        (fsdp_index(x, z, c), fsdp_index(*change(x, z, c)))
        for x in range(NX)
        for z in range(NZ)
        for c in range(NC)
    ]
    return lax.ppermute(value, ("x", "z", "core"), pairs)


def along_z(value, steps):
    return move(value, lambda x, z, c: (x, (z + steps) % NZ, c))


def swap_x(value):
    return move(value, lambda x, z, c: (1 - x, z, c))


def swap_core(value):
    return move(value, lambda x, z, c: (x, z, 1 - c))


def along_blk(value, steps, flip_x):
    size = NX * NZ * NC
    pairs = [
        (b * size + fsdp_index(x, z, c), ((b + steps) % NB) * size + fsdp_index(x ^ flip_x, z, c))
        for b in range(NB)
        for x in range(NX)
        for z in range(NZ)
        for c in range(NC)
    ]
    return lax.ppermute(value, ("blk", "x", "z", "core"), pairs)


def params(limit=VMEM_LIMIT):
    return pltpu.CompilerParams(vmem_limit_bytes=limit)


def cost(flops, size):
    return pl.CostEstimate(flops=flops, bytes_accessed=size, transcendentals=0)


IN_VMEM = pl.BlockSpec(memory_space=pltpu.VMEM)
IN_SMEM = pl.BlockSpec(memory_space=pltpu.SMEM)
ANYWHERE = pl.BlockSpec(memory_space=pl.ANY)
IN_HBM = pl.BlockSpec(memory_space=pltpu.HBM)


def block(ref, index, width):
    return ref[:, pl.ds(pl.multiple_of(index * width, width), width)]


def prepare_kernel(width, steps, table, hidden, cot, after, scale, cot_t, send_a, send_b, held, arrivals):
    step = hidden.shape[0] // steps
    lanes = 128
    copies = []
    for at in range(steps):
        rows = pl.ds(at * step, step)
        copy = pltpu.make_async_copy(hidden.at[rows, :], held.at[rows, :], arrivals.at[at])
        copy.start()
        copies.append(copy)
    first = send_a.shape[1] // width
    for at in range(steps):
        copies[at].wait()
        rows = slice(at * step, (at + 1) * step)
        total = jnp.zeros((step, lanes), F32)
        for j in range(hidden.shape[1] // lanes):
            part = held[rows, j * lanes:(j + 1) * lanes].astype(F32)
            total += part * part
        inverse = lax.rsqrt(jnp.sum(total, axis=1, keepdims=True) * (1.0 / hidden.shape[1]) + EPS)
        scale[rows, :] = inverse
        cot_t[:, rows] = (cot[rows, :].astype(F32) * inverse).T.astype(BF16)
        for i in range(first + send_b.shape[1] // width):
            out, j = (send_a, i) if i < first else (send_b, i - first)
            start = pl.multiple_of((table[i] ^ 1) * width, width)
            out[rows, j * width:(j + 1) * width] = held[rows, pl.ds(start, width)]


def prepare(table, hidden, cot, after, width):
    tokens, features = hidden.shape
    values = cot.shape[1]
    steps = 4
    return pl.pallas_call(
        functools.partial(prepare_kernel, width, steps),
        in_specs=[IN_SMEM, IN_HBM, IN_VMEM, ANYWHERE],
        out_specs=[IN_VMEM] * 4,
        out_shape=[
            jax.ShapeDtypeStruct((tokens, 1), F32),
            jax.ShapeDtypeStruct((values, tokens), BF16),
            jax.ShapeDtypeStruct((tokens, 2 * FIRST * width), BF16),
            jax.ShapeDtypeStruct((tokens, 2 * (len(OFFSETS) - FIRST) * width), BF16),
        ],
        scratch_shapes=[pltpu.VMEM((tokens, features), BF16), pltpu.SemaphoreType.DMA((steps,))],
        compiler_params=params(LOAD_LIMIT),
        cost_estimate=cost(0, tokens),
    )(table, hidden, cot, after)


def gradient_kernel(base, width, table, hidden, visiting, cot_t, cot_t_sibling, *outs):
    for i, out in enumerate(outs):
        total = jnp.dot(cot_t[...], block(hidden, table[2 * base + i], width), preferred_element_type=F32)
        theirs = visiting[:, i * width:(i + 1) * width]
        out[...] = (total + jnp.dot(cot_t_sibling[...], theirs, preferred_element_type=F32)).astype(BF16)


def gradient(table, hidden, visiting, cot_t, cot_t_sibling, base, count, width):
    tokens = hidden.shape[0]
    values = cot_t.shape[0]
    outs = pl.pallas_call(
        functools.partial(gradient_kernel, base, width),
        in_specs=[IN_SMEM] + [IN_VMEM] * 4,
        out_specs=[IN_VMEM] * (2 * count),
        out_shape=[jax.ShapeDtypeStruct((values, width), BF16)] * (2 * count),
        compiler_params=params(),
        cost_estimate=cost(8 * count * tokens * values * width, 8 * count * tokens * width + 4 * count * values * width),
    )(table, hidden, visiting, cot_t, cot_t_sibling)
    return outs[0::2], outs[1::2]


def project_kernel(width, table, hidden, visit_a, visit_b, weights, mine, theirs):
    for i in range(0, len(OFFSETS), 2):
        near, far = ((table[2 * j] // NC) % NZ for j in (i, i + 1))
        weight = jnp.concatenate([weights[z].reshape(2 * width, mine.shape[1]) for z in (near, far)], axis=0)
        own = jnp.concatenate([block(hidden, table[2 * i + j], width) for j in range(4)], axis=1)
        visit, at = (visit_a, 2 * i * width) if i < FIRST else (visit_b, 2 * (i - FIRST) * width)
        product = jnp.dot(own, weight, preferred_element_type=F32)
        product_theirs = jnp.dot(visit[:, at:at + 4 * width], weight, preferred_element_type=F32)
        if i:
            mine[...] += product
            theirs[...] += product_theirs
        else:
            mine[...] = product
            theirs[...] = product_theirs


def project(table, hidden, visit_a, visit_b, weights, width):
    tokens = hidden.shape[0]
    values = weights.shape[-1]
    size = weights.size
    return pl.pallas_call(
        functools.partial(project_kernel, width),
        in_specs=[IN_SMEM] + [IN_VMEM] * 4,
        out_specs=[IN_VMEM, IN_VMEM],
        out_shape=[jax.ShapeDtypeStruct((tokens, values), F32)] * 2,
        compiler_params=params(),
        cost_estimate=cost(4 * tokens * size, 2 * size),
    )(table, hidden, visit_a, visit_b, weights)


def pair_kernel(one, other, after, out):
    out[0] = one[...]
    out[1] = other[...]


def pair(one, other, after):
    return pl.pallas_call(
        pair_kernel,
        in_specs=[IN_VMEM, IN_VMEM, ANYWHERE],
        out_specs=IN_VMEM,
        out_shape=jax.ShapeDtypeStruct((2, *one.shape), one.dtype),
        compiler_params=params(),
        cost_estimate=cost(0, 8 * one.size),
    )(one, other, after)


def halves_kernel(one, other, after, upper, lower):
    half = upper.shape[0]
    upper[...] = (one[:half].astype(F32) + other[:half].astype(F32)).astype(BF16)
    lower[...] = (one[half:].astype(F32) + other[half:].astype(F32)).astype(BF16)


def halves(one, other, after):
    half = jax.ShapeDtypeStruct((one.shape[0] // 2, one.shape[1]), BF16)
    return pl.pallas_call(
        halves_kernel,
        in_specs=[IN_VMEM, IN_VMEM, ANYWHERE],
        out_specs=[IN_VMEM, IN_VMEM],
        out_shape=[half, half],
        compiler_params=params(),
        cost_estimate=cost(one.size, 6 * one.size),
    )(one, other, after)


def diagonal(width):
    return lax.broadcasted_iota(jnp.int32, (width, width), 0) == lax.broadcasted_iota(jnp.int32, (width, width), 1)


def as_column(row):
    return jnp.sum(jnp.where(diagonal(row.shape[1]), row, 0.0), axis=1, keepdims=True)


def as_row(column):
    return jnp.sum(jnp.where(diagonal(column.shape[0]), column, 0.0), axis=0, keepdims=True)


def scale_kernel(gain, weight, out):
    out[...] = (weight[0].astype(F32) * as_column(gain[...].astype(F32))).astype(BF16)


def scale_weight(gain, weight):
    return pl.pallas_call(scale_kernel, out_shape=jax.ShapeDtypeStruct(weight.shape[1:], BF16), compiler_params=params())(gain, weight)


def finish_kernel(total, gain, weight, grad_weight_in, grad_gain_in, grad_weight, grad_gain):
    summed = total[...].astype(F32).T
    grad_weight[0] = grad_weight_in[0] + as_column(gain[...].astype(F32)) * summed
    grad_gain[...] = grad_gain_in[...] + as_row(jnp.sum(weight[0].astype(F32) * summed, axis=1, keepdims=True))


def finish(total, gain, weight, grad_weight_in, grad_gain_in):
    return pl.pallas_call(
        finish_kernel,
        out_shape=[jax.ShapeDtypeStruct(a.shape, F32) for a in (grad_weight_in, grad_gain_in)],
        compiler_params=params(),
    )(total, gain, weight, grad_weight_in, grad_gain_in)


def add(*terms):
    return sum(t.astype(F32) for t in terms).astype(BF16)


def per_device(hidden, gain, value_weight, cotangent, grad_weight_in, grad_gain_in):
    width = value_weight.shape[1]
    x, z, core = (lax.axis_index(a) for a in ("x", "z", "core"))
    table = jnp.stack(
        [fsdp_index(x ^ flip, (z + off + NZ) % NZ, core) for off in OFFSETS for flip in (0, 1)]
    ).astype(jnp.int32)

    scaled_weight = scale_weight(gain, value_weight)
    layer = [along_blk(scaled_weight, 1, flip) for flip in (0, 1)]

    rest = len(OFFSETS) - FIRST
    scale, cot_t, send_a, send_b = prepare(table, hidden, cotangent, scaled_weight, width)
    cot_t_sibling, visit_a, visit_b = (swap_core(a) for a in (cot_t, send_a, send_b))
    weights = lax.all_gather(pair(*layer, cot_t), "z", axis=0)

    keep_1, send_1 = gradient(table, hidden, visit_a, cot_t, cot_t_sibling, 0, FIRST, width)
    keep_2, send_2 = gradient(table, hidden, visit_b, cot_t, cot_t_sibling, FIRST, rest, width)
    sends, keeps = [*send_1, *send_2], [*keep_1, *keep_2]
    arrived = [swap_x(s) for s in sends]
    mine = {off: (keeps[i], arrived[i]) for i, off in enumerate(OFFSETS)}

    half = sends[0].shape[0] // 2
    upper, lower = halves(*mine[4], send_2[-1])
    up, down = along_z(upper, 1), along_z(lower, -1)
    sum_up = jnp.concatenate([add(mine[3][0][:half], mine[3][1][:half], up), add(mine[3][0][half:], mine[3][1][half:])], axis=0)
    sum_down = jnp.concatenate([add(mine[-3][0][:half], mine[-3][1][:half]), add(mine[-3][0][half:], mine[-3][1][half:], down)], axis=0)
    for off in (2, 1, 0):
        up, down = along_z(sum_up, 1), along_z(sum_down, -1)
        if off:
            sum_up, sum_down = add(*mine[off], up), add(*mine[-off], down)
    total = along_blk(add(*mine[0], up, down), -1, 0)

    product, product_sibling = project(table, hidden, visit_a, visit_b, weights, width)
    values = ((product + swap_core(product_sibling)) * scale).astype(BF16)

    return values, *finish(total, gain, value_weight, grad_weight_in, grad_gain_in)


def solution(mesh):
    fsdp = ("x", "z", "core")
    return jax.shard_map(
        per_device,
        mesh=Mesh(mesh.devices.reshape(NB, NX, NZ, NC), ("blk", *fsdp)),
        in_specs=(
            P(("blk", *fsdp), None),
            P("blk", fsdp),
            P("blk", fsdp, None),
            P(("blk", *fsdp), None),
            P("blk", fsdp, None),
            P("blk", fsdp),
        ),
        out_specs=(P(("blk", *fsdp), None), P("blk", fsdp, None), P("blk", fsdp)),
        check_vma=False,
    )
```

time: 154 us -> 144 us (0.935)
  Pallas kernels: 39 us -> 19.7 us
  local copies, waits for them, and re-layouts: 4.99 us -> 18.2 us
  waiting for transfers between devices: 49.8 us -> 46.8 us
  other arithmetic: 9.95 us -> 7.28 us
  starting transfers between devices: 34 us -> 35.9 us
    pallas_call x4 -> x6, Pallas kernels: 35 us -> 18.5 us  [the longest x2 6.44 us: gradient(): pl.pallas_call(functools.partial(gradient_kernel, base, width), in_specs=...]
    unnamed x20 -> x52, local copies, waits for them, and re-layouts: 4.28 us -> 18.2 us
    all_gather x1, waiting for transfers between devices: 0.01 us -> 11.9 us  [per_device(): weights = lax.all_gather(pair(*layer, cot_t), 'z', axis=0)]
    ppermute x3, waiting for transfers between devices: 20.5 us -> 10.7 us  [along_blk(): return lax.ppermute(value, ('blk', 'x', 'z', 'core'), pairs)]
    ppermute x20, waiting for transfers between devices: 29.3 us -> 24.2 us  [move(): return lax.ppermute(value, ('x', 'z', 'core'), pairs)]
    convert_element_type x8 -> x7, other arithmetic: 7.98 us -> 5.2 us  [add(): return sum((t.astype(F32) for t in terms)).astype(BF16)]
    ppermute x3, starting transfers between devices: 2.97 us -> 5.59 us  [along_blk(): return lax.ppermute(value, ('blk', 'x', 'z', 'core'), pairs)]
    pallas_call x1, Pallas kernels: 1.81 us -> 0.12 us  [scale_weight(): pl.pallas_call(scale_kernel, out_shape=jax.ShapeDtypeStruct(weight.shape[...]
  transfers between devices with their start and end apart: 24 -> 24, of which waited for: 9 -> 11; matrix products, arithmetic and copies ran while one was open for 6% -> 5% of each run, Pallas kernels for 24% -> 13%
where the time goes in v3:
time: 144 us; the launch traced here: 142 us
  waiting for transfers between devices  46.8 us (32%)
  starting transfers between devices  35.9 us (25%)
  Pallas kernels  19.7 us (14%)
  local copies, waits for them, and re-layouts  18.2 us (13%)
  between operations  14.3 us (10%)
  other arithmetic  7.28 us (5%)
    ppermute x20, starting transfers between devices, move(): return lax.ppermute(value, ('x', 'z', 'core'), pairs)  30.3 us
    ppermute x20, waiting for transfers between devices, move(): return lax.ppermute(value, ('x', 'z', 'core'), pairs)  24.2 us
    unnamed x52, local copies, waits for them, and re-layouts  18.2 us
    all_gather x1, waiting for transfers between devices, per_device(): weights = lax.all_gather(pair(*layer, cot_t), 'z', axis=0)  11.9 us
    ppermute x3, waiting for transfers between devices, along_blk(): return lax.ppermute(value, ('blk', 'x', 'z', 'core'), pairs)  10.7 us
    pallas_call x2, Pallas kernels, gradient(): pl.pallas_call(functools.partial(gradient_kernel, base, width), in_specs=...  6.44 us
    pallas_call x1, Pallas kernels, project(): pl.pallas_call(functools.partial(project_kernel, width), in_specs=[IN_SME...  6.05 us
    ppermute x3, starting transfers between devices, along_blk(): return lax.ppermute(value, ('blk', 'x', 'z', 'core'), pairs)  5.59 us
  transfers between devices with their start and end apart: 24, of which 11 were waited for; matrix products, arithmetic and copies ran while one was open for 5% of the time, Pallas kernels for 13%

profile of v3, /device:TPU:4, one launch (start us, length us, event | category | flops | bytes accessed | tf_op | source)
XLA Modules:
  0.0 142.2 jit_solution(17122724200401267273)
XLA Ops:
  7.2 0.9 copy-done.10
  9.0 1.3 collective-permute-start.2
  10.2 0.9 collective-permute-start.3
  11.2 1.0 copy-done.12
  12.3 5.1 %shard_map.86 = (f32[512,1]{1,0:T(8,128)S(1)}, bf16[512,512]{1,0:T(8,128)(2,1)S(1)}, bf16[512,1024]{1,0:T(8,128)(2,1)S(1)}, bf16[512,3072]{1,0:T(8,128)(2,1)S(1)}) custom-call(s32[16]{0:T(128)S(1)} %stack.67.table, bf16[512,8192]{1,0:T(8,128)(2,1)} %hidden.7, bf16[512,512]{1,0:T(8,128)(2,1)S(1)} %copy-done.12, bf16[256,512]{1,0:T(8,128)(2,1)S(1)} %shard_map.85.after), custom_call_target="tpu_custom_call" | custom-call | bytes 512 | tf_op jit(solution)/shard_map/pallas_call | solution.py:107
  17.4 0.7 copy-done.16
  18.1 5.8 %collective-permute-done.2.one = bf16[256,512]{1,0:T(8,128)(2,1)S(1)} collective-permute-done((bf16[256,512]{1,0:T(8,128)(2,1)S(1)}, bf16[256,512]{1,0:T(8,128)(2,1)S(1)}, u32[]{:S(2)}, u32[]{:S(2)}) %collective-permute-start.2) | collective-permute-done | bytes 262176 | tf_op jit(solution)/shard_map/ppermute | solution.py:56
  23.9 0.9 collective-permute-done.3.other
  24.8 0.8 shard_map.87
  25.7 0.8 copy-done.2
  27.2 7.5 %collective-permute-done.5.cot_t_sibling = bf16[512,512]{1,0:T(8,128)(2,1)S(1)} collective-permute-done((bf16[512,512]{1,0:T(8,128)(2,1)}, bf16[512,512]{1,0:T(8,128)(2,1)S(1)}, u32[]{:S(2)}, u32[]{:S(2)}) %collective-permute-start.5) | collective-permute-done | bytes 524320 | tf_op jit(solution)/shard_map/ppermute | solution.py:32
  34.7 3.4 %copy-done = bf16[512,8192]{1,0:T(8,128)(2,1)S(1)} copy-done((bf16[512,8192]{1,0:T(8,128)(2,1)S(1)}, bf16[512,8192]{1,0:T(8,128)(2,1)}, u32[]{:S(2)}) %copy-start) | copy-done | bytes 8388632
  38.1 1.0 copy-done.3
  39.1 1.8 %shard_map.90 = (bf16[512,256]{1,0:T(8,128)(2,1)S(1)}, bf16[512,256]{1,0:T(8,128)(2,1)S(1)}, bf16[512,256]{1,0:T(8,128)(2,1)S(1)}, bf16[512,256]{1,0:T(8,128)(2,1)S(1)}) custom-call(s32[16]{0:T(128)S(1)} %stack.67.table, bf16[512,8192]{1,0:T(8,128)(2,1)S(1)} %copy-done, bf16[512,1024]{1,0:T(8,128)(2,1)S(1)} %collective-permute-done.visit_a.visiting, ...), custom_call_target="tpu_custom_call" | custom-call | flops 1073741824 | bytes 3145728 | tf_op jit(solution)/shard_map/pallas_call | solution.py:133
  41.6 2.9 %collective-permute-start.9 = (bf16[512,256]{1,0:T(8,128)(2,1)S(1)}, bf16[512,256]{1,0:T(8,128)(2,1)S(1)}, u32[]{:S(2)}, u32[]{:S(2)}) collective-permute-start(bf16[512,256]{1,0:T(8,128)(2,1)S(1)} %get-tuple-element.42), channel_id=1, source_target_pairs={{0,16},{1,17},{2,18},{3,19},{4,20},{5,21},{6,22},{7,23},{8,24},{9,... | collective-permute-start | bytes 786440 | tf_op jit(solution)/shard_map/ppermute | solution.py:32
  44.5 4.7 %shard_map.89 = (bf16[512,256]{1,0:T(8,128)(2,1)S(1)}, bf16[512,256]{1,0:T(8,128)(2,1)S(1)}, bf16[512,256]{1,0:T(8,128)(2,1)S(1)}, bf16[512,256]{1,0:T(8,128)(2,...) custom-call(s32[16]{0:T(128)S(1)} %stack.67.table, ...), custom_call_target="tpu_custom_call" | custom-call | flops 3221225472 | bytes 9437184 | tf_op jit(solution)/shard_map/pallas_call | solution.py:133
  49.2 0.7 copy-done.14
  49.9 1.7 %collective-permute-done.10.other = bf16[512,256]{1,0:T(8,128)(2,1)S(1)} collective-permute-done((bf16[512,256]{1,0:T(8,128)(2,1)S(1)}, bf16[512,256]{1,0:T(8,128)(2,1)S(1)}, u32[]{:S(2)}, u32[]{:S(2)}) %collective-permute-start.10) | collective-permute-done | bytes 262176 | tf_op jit(solution)/shard_map/ppermute | solution.py:32
  51.7 2.0 %collective-permute-start.11 = (bf16[256,256]{1,0:T(8,128)(2,1)S(1)}, bf16[256,256]{1,0:T(8,128)(2,1)S(1)}, u32[]{:S(2)}, u32[]{:S(2)}) collective-permute-start(bf16[256,256]{1,0:T(8,128)(2,1)S(1)} %get-tuple-element.45), channel_id=1, source_target_pairs={{0,2},{1,3},{2,4},{3,5},{4,6},{5,7},{6,8},{7,9},{8,10},{9,11},{10,... | collective-permute-start | bytes 393224 | tf_op jit(solution)/shard_map/ppermute | solution.py:32
  54.3 4.2 %collective-permute-start.18 = (bf16[256,256]{1,0:T(8,128)(2,1)S(1)}, bf16[256,256]{1,0:T(8,128)(2,1)S(1)}, u32[]{:S(2)}, u32[]{:S(2)}) collective-permute-start(bf16[256,256]{1,0:T(8,128)(2,1)S(1)} %get-tuple-element.52), channel_id=1, source_target_pairs={{0,14},{1,15},{2,0},{3,1},{4,2},{5,3},{6,4},{7,5},{8,6},{9,7},{10,... | collective-permute-start | bytes 393224 | tf_op jit(solution)/shard_map/ppermute | solution.py:32
  58.5 2.9 %collective-permute-start.16 = (bf16[512,256]{1,0:T(8,128)(2,1)S(1)}, bf16[512,256]{1,0:T(8,128)(2,1)S(1)}, u32[]{:S(2)}, u32[]{:S(2)}) collective-permute-start(bf16[512,256]{1,0:T(8,128)(2,1)S(1)} %get-tuple-element.49), channel_id=1, source_target_pairs={{0,16},{1,17},{2,18},{3,19},{4,20},{5,21},{6,22},{7,23},{8,24},{9,... | collective-permute-start | bytes 786440 | tf_op jit(solution)/shard_map/ppermute | solution.py:32
  62.1 2.2 %collective-permute-done.11 = bf16[256,256]{1,0:T(8,128)(2,1)S(1)} collective-permute-done((bf16[256,256]{1,0:T(8,128)(2,1)S(1)}, bf16[256,256]{1,0:T(8,128)(2,1)S(1)}, u32[]{:S(2)}, u32[]{:S(2)}) %collective-permute-start.11) | collective-permute-done | bytes 131104 | tf_op jit(solution)/shard_map/ppermute | solution.py:32
  64.6 4.5 %collective-permute-start.19 = (bf16[512,256]{1,0:T(8,128)(2,1)S(1)}, bf16[512,256]{1,0:T(8,128)(2,1)S(1)}, u32[]{:S(2)}, u32[]{:S(2)}) collective-permute-start(bf16[512,256]{1,0:T(8,128)(2,1)S(1)} %pad_maximum_fusion.1), channel_id=1, source_target_pairs={{0,14},{1,15},{2,0},{3,1},{4,2},{5,3},{6,4},{7,5},{8,6},{9,7},{10,... | collective-permute-start | bytes 786440 | tf_op jit(solution)/shard_map/ppermute | solution.py:32
  69.1 0.9 collective-permute-start.6
  70.1 4.7 %collective-permute-done.8 = bf16[512,256]{1,0:T(8,128)(2,1)S(1)} collective-permute-done((bf16[512,256]{1,0:T(8,128)(2,1)S(1)}, bf16[512,256]{1,0:T(8,128)(2,1)S(1)}, u32[]{:S(2)}, u32[]{:S(2)}) %collective-permute-start.8) | collective-permute-done | bytes 262176 | tf_op jit(solution)/shard_map/ppermute | solution.py:32
  74.8 2.6 %collective-permute-start.15 = (bf16[512,256]{1,0:T(8,128)(2,1)}, bf16[512,256]{1,0:T(8,128)(2,1)}, u32[]{:S(2)}, u32[]{:S(2)}) collective-permute-start(bf16[512,256]{1,0:T(8,128)(2,1)} %get-tuple-element.47), channel_id=1, source_target_pairs={{0,16},{1,17},{2,18},{3,19},{4,20},{5,21},{6,22},{7,23},{8,24},{9,... | collective-permute-start | bytes 786440 | tf_op jit(solution)/shard_map/ppermute | solution.py:32
  77.4 2.1 %collective-permute-done.12 = bf16[512,256]{1,0:T(8,128)(2,1)S(1)} collective-permute-done((bf16[512,256]{1,0:T(8,128)(2,1)S(1)}, bf16[512,256]{1,0:T(8,128)(2,1)S(1)}, u32[]{:S(2)}, u32[]{:S(2)}) %collective-permute-start.12) | collective-permute-done | bytes 262176 | tf_op jit(solution)/shard_map/ppermute | solution.py:32
  80.1 0.8 add_convert_fusion.4
  80.9 1.0 collective-permute-start.13
  82.0 0.8 add_convert_fusion.2
  82.8 2.5 %collective-permute-start.20 = (bf16[512,256]{1,0:T(8,128)(2,1)}, bf16[512,256]{1,0:T(8,128)(2,1)}, u32[]{:S(2)}, u32[]{:S(2)}) collective-permute-start(bf16[512,256]{1,0:T(8,128)(2,1)} %add_convert_fusion.2), channel_id=1, source_target_pairs={{0,14},{1,15},{2,0},{3,1},{4,2},{5,3},{6,4},{7,5},{8,6},{9,7},{10,... | collective-permute-start | bytes 786440 | tf_op jit(solution)/shard_map/ppermute | solution.py:32
  85.3 11.9 %all-gather.3.cloned.1.call-done = bf16[16,256,512]{2,1,0:T(8,128)(2,1)} async-done(((bf16[2,256,512]{2,1,0:T(8,128)(2,1)}), bf16[16,256,512]{2,1,0:T(8,128)(2,1)}) %all-gather.3.cloned.1.call-update) | async-done | bytes 4194320 | tf_op jit(solution)/shard_map/all_gather | solution.py:259
  97.2 3.4 %copy-done.1 = bf16[512,8192]{1,0:T(8,128)(2,1)S(1)} copy-done((bf16[512,8192]{1,0:T(8,128)(2,1)S(1)}, bf16[512,8192]{1,0:T(8,128)(2,1)}, u32[]{:S(2)}) %copy-start.1) | copy-done | bytes 8388632
  100.6 2.2 %copy-done.5 = bf16[16,256,512]{2,1,0:T(8,128)(2,1)S(1)} copy-done((bf16[16,256,512]{2,1,0:T(8,128)(2,1)S(1)}, bf16[16,256,512]{2,1,0:T(8,128)(2,1)}, u32[]{:S(2)}) %copy-start.5) | copy-done | bytes 4194328
  102.8 1.2 copy-done.7
  104.0 6.1 %shard_map.88 = (f32[512,512]{1,0:T(8,128)S(1)}, f32[512,512]{1,0:T(8,128)}) custom-call(s32[16]{0:T(128)S(1)} %stack.67.table, bf16[512,8192]{1,0:T(8,128)(2,1)S(1)} %copy-done.1, bf16[512,1024]{1,0:T(8,128)(2,1)S(1)} %copy-done.7, bf16[512,3072]{1,0:T(8,128)(2,1)S(1)} %collective-permute-done.1.visit_b.visiting, bf16[8,2,256,512]{3,2,1,0:T(8,128)(2,1)S(1)} %bitcast.17), custom_call_target="tpu_custom_call" | custom-call | flops 4294967296 | bytes 4194304 | tf_op jit(solution)/shard_map/pallas_call | solution.py:164
  110.1 1.0 copy-done.8
  111.1 1.2 add_convert_fusion.3
  112.4 1.1 add_convert_fusion.1
  113.6 3.3 %collective-permute-start.21 = (bf16[512,256]{1,0:T(8,128)(2,1)S(1)}, bf16[512,256]{1,0:T(8,128)(2,1)S(1)}, u32[]{:S(2)}, u32[]{:S(2)}) collective-permute-start(bf16[512,256]{1,0:T(8,128)(2,1)S(1)} %add_convert_fusion.1), channel_id=1, source_target_pairs={{0,14},{1,15},{2,0},{3,1},{4,2},{5,3},{6,4},{7,5},{8,6},{9,7},{10,... | collective-permute-start | bytes 786440 | tf_op jit(solution)/shard_map/ppermute | solution.py:32
  116.9 5.4 %collective-permute-done.14 = bf16[512,256]{1,0:T(8,128)(2,1)S(1)} collective-permute-done((bf16[512,256]{1,0:T(8,128)(2,1)S(1)}, bf16[512,256]{1,0:T(8,128)(2,1)S(1)}, u32[]{:S(2)}, u32[]{:S(2)}) %collective-permute-start.14) | collective-permute-done | bytes 262176 | tf_op jit(solution)/shard_map/ppermute | solution.py:32
  122.7 1.1 add_convert_fusion
  123.8 3.4 %collective-permute-start.22 = (bf16[512,256]{1,0:T(8,128)(2,1)S(1)}, bf16[512,256]{1,0:T(8,128)(2,1)S(1)}, u32[]{:S(2)}, u32[]{:S(2)}) collective-permute-start(bf16[512,256]{1,0:T(8,128)(2,1)S(1)} %add_convert_fusion), channel_id=1, source_target_pairs={{0,224},{1,225},{2,226},{3,227},{4,228},{5,229},{6,230},{7,231},{8... | collective-permute-start | bytes 786440 | tf_op jit(solution)/shard_map/ppermute | solution.py:56
  127.3 1.1 reduce
  128.4 4.0 %collective-permute-done.22.total = bf16[512,256]{1,0:T(8,128)(2,1)S(1)} collective-permute-done((bf16[512,256]{1,0:T(8,128)(2,1)S(1)}, bf16[512,256]{1,0:T(8,128)(2,1)S(1)}, u32[]{:S(2)}, u32[]{:S(2)}) %collective-permute-start.22) | collective-permute-done | bytes 262176 | tf_op jit(solution)/shard_map/ppermute | solution.py:56
  132.3 1.0 copy-done.13
  133.4 1.1 shard_map.92
  134.4 0.9 multiply_convert_fusion
  (73 shorter events, 5.2 us)
Async XLA Ops:
  7.2 90.0 %all-gather.3.cloned.1.call-start = ((), (), s32[]{:S(2)}) async-start(), calls=%async_computation | async-start | bytes 4718592 | tf_op jit(solution)/shard_map/all_gather | solution.py:259
  7.2 1.0 copy-start.10
  9.0 14.9 %collective-permute-start.2 = (bf16[256,512]{1,0:T(8,128)(2,1)S(1)}, bf16[256,512]{1,0:T(8,128)(2,1)S(1)}, u32[]{:S(2)}, u32[]{:S(2)}) collective-permute-start(bf16[256,512]{1,0:T(8,128)(2,1)S(1)} %shard_map.85.after), channel_id=1, source_target_pairs={{0,32},{1,33},{2,34},{3,35},{4,36},{5,37},{6,38},{7,39},{8,40},{9,... | collective-permute-start | bytes 786440 | tf_op jit(solution)/shard_map/ppermute | solution.py:56
  10.2 14.6 %collective-permute-start.3 = (bf16[256,512]{1,0:T(8,128)(2,1)S(1)}, bf16[256,512]{1,0:T(8,128)(2,1)S(1)}, u32[]{:S(2)}, u32[]{:S(2)}) collective-permute-start(bf16[256,512]{1,0:T(8,128)(2,1)S(1)} %shard_map.85.after), channel_id=1, source_target_pairs={{0,48},{1,49},{2,50},{3,51},{4,52},{5,53},{6,54},{7,55},{8,56},{9,... | collective-permute-start | bytes 786440 | tf_op jit(solution)/shard_map/ppermute | solution.py:56
  11.2 1.0 copy-start.12
  18.1 6.8 %copy-start.24 = (bf16[512,3072]{1,0:T(8,128)(2,1)}, bf16[512,3072]{1,0:T(8,128)(2,1)S(1)}, u32[]{:S(2)}) copy-start(bf16[512,3072]{1,0:T(8,128)(2,1)S(1)} %get-tuple-element.30) | copy-start | bytes 9437188
  18.1 6.8 %copy-start.25 = (bf16[512,1024]{1,0:T(8,128)(2,1)}, bf16[512,1024]{1,0:T(8,128)(2,1)S(1)}, u32[]{:S(2)}) copy-start(bf16[512,1024]{1,0:T(8,128)(2,1)S(1)} %get-tuple-element.29) | copy-start | bytes 3145732
  25.7 0.8 copy-start.2
  26.5 18.1 %collective-permute-start.1 = (bf16[512,3072]{1,0:T(8,128)(2,1)}, bf16[512,3072]{1,0:T(8,128)(2,1)S(1)}, u32[]{:S(2)}, u32[]{:S(2)}) collective-permute-start(bf16[512,3072]{1,0:T(8,128)(2,1)} %copy-done.24), channel_id=1, source_target_pairs={{0,1},{1,0},{2,3},{3,2},{4,5},{5,4},{6,7},{7,6},{8,9},{9,8},{10,11... | collective-permute-start | bytes 9437192 | tf_op jit(solution)/shard_map/ppermute | solution.py:32
  26.6 8.1 %collective-permute-start = (bf16[512,1024]{1,0:T(8,128)(2,1)}, bf16[512,1024]{1,0:T(8,128)(2,1)S(1)}, u32[]{:S(2)}, u32[]{:S(2)}) collective-permute-start(bf16[512,1024]{1,0:T(8,128)(2,1)} %copy-done.25), channel_id=1, source_target_pairs={{0,1},{1,0},{2,3},{3,2},{4,5},{5,4},{6,7},{7,6},{8,9},{9,8},{10,11... | collective-permute-start | bytes 3145736 | tf_op jit(solution)/shard_map/ppermute | solution.py:32
  27.1 7.6 %collective-permute-start.5 = (bf16[512,512]{1,0:T(8,128)(2,1)}, bf16[512,512]{1,0:T(8,128)(2,1)S(1)}, u32[]{:S(2)}, u32[]{:S(2)}) collective-permute-start(bf16[512,512]{1,0:T(8,128)(2,1)} %copy-done.2), channel_id=1, source_target_pairs={{0,1},{1,0},{2,3},{3,2},{4,5},{5,4},{6,7},{7,6},{8,9},{9,8},{10,11... | collective-permute-start | bytes 1572872 | tf_op jit(solution)/shard_map/ppermute | solution.py:32
  34.7 3.4 %copy-start = (bf16[512,8192]{1,0:T(8,128)(2,1)S(1)}, bf16[512,8192]{1,0:T(8,128)(2,1)}, u32[]{:S(2)}) copy-start(bf16[512,8192]{1,0:T(8,128)(2,1)} %hidden.7) | copy-start | bytes 25165828
  38.1 1.0 copy-start.3
  39.1 1.8 %copy-start.6 = (bf16[512,1024]{1,0:T(8,128)(2,1)}, bf16[512,1024]{1,0:T(8,128)(2,1)S(1)}, u32[]{:S(2)}) copy-start(bf16[512,1024]{1,0:T(8,128)(2,1)S(1)} %collective-permute-done.visit_a.visiting) | copy-start | bytes 3145732
  39.1 5.4 %copy-start.4 = (bf16[512,512]{1,0:T(8,128)(2,1)S(1)}, bf16[512,512]{1,0:T(8,128)(2,1)}, u32[]{:S(2)}) copy-start(bf16[512,512]{1,0:T(8,128)(2,1)} %copy-done.2) | copy-start | bytes 1572868
  40.9 10.7 %collective-permute-start.10 = (bf16[512,256]{1,0:T(8,128)(2,1)S(1)}, bf16[512,256]{1,0:T(8,128)(2,1)S(1)}, u32[]{:S(2)}, u32[]{:S(2)}) collective-permute-start(bf16[512,256]{1,0:T(8,128)(2,1)S(1)} %get-tuple-element.44), channel_id=1, source_target_pairs={{0,16},{1,17},{2,18},{3,19},{4,20},{5,21},{6,22},{7,23},{8,24},{9,... | collective-permute-start | bytes 786440 | tf_op jit(solution)/shard_map/ppermute | solution.py:32
  41.6 19.9 %collective-permute-start.9 = (bf16[512,256]{1,0:T(8,128)(2,1)S(1)}, bf16[512,256]{1,0:T(8,128)(2,1)S(1)}, u32[]{:S(2)}, u32[]{:S(2)}) collective-permute-start(bf16[512,256]{1,0:T(8,128)(2,1)S(1)} %get-tuple-element.42), channel_id=1, source_target_pairs={{0,16},{1,17},{2,18},{3,19},{4,20},{5,21},{6,22},{7,23},{8,24},{9,... | collective-permute-start | bytes 786440 | tf_op jit(solution)/shard_map/ppermute | solution.py:32
  49.2 0.7 copy-start.14
  49.9 14.7 %copy-start.17 = (bf16[512,256]{1,0:T(8,128)(2,1)}, bf16[512,256]{1,0:T(8,128)(2,1)S(1)}, u32[]{:S(2)}) copy-start(bf16[512,256]{1,0:T(8,128)(2,1)S(1)} %get-tuple-element.46) | copy-start | bytes 786436
  49.9 14.7 %copy-start.19 = (bf16[512,256]{1,0:T(8,128)(2,1)}, bf16[512,256]{1,0:T(8,128)(2,1)S(1)}, u32[]{:S(2)}) copy-start(bf16[512,256]{1,0:T(8,128)(2,1)S(1)} %get-tuple-element.37) | copy-start | bytes 786436
  51.7 12.5 %collective-permute-start.11 = (bf16[256,256]{1,0:T(8,128)(2,1)S(1)}, bf16[256,256]{1,0:T(8,128)(2,1)S(1)}, u32[]{:S(2)}, u32[]{:S(2)}) collective-permute-start(bf16[256,256]{1,0:T(8,128)(2,1)S(1)} %get-tuple-element.45), channel_id=1, source_target_pairs={{0,2},{1,3},{2,4},{3,5},{4,6},{5,7},{6,8},{7,9},{8,10},{9,11},{10,... | collective-permute-start | bytes 393224 | tf_op jit(solution)/shard_map/ppermute | solution.py:32
  53.7 10.8 %collective-permute-start.17 = (bf16[512,256]{1,0:T(8,128)(2,1)S(1)}, bf16[512,256]{1,0:T(8,128)(2,1)S(1)}, u32[]{:S(2)}, u32[]{:S(2)}) collective-permute-start(bf16[512,256]{1,0:T(8,128)(2,1)S(1)} %get-tuple-element.51), channel_id=1, source_target_pairs={{0,16},{1,17},{2,18},{3,19},{4,20},{5,21},{6,22},{7,23},{8,24},{9,... | collective-permute-start | bytes 786440 | tf_op jit(solution)/shard_map/ppermute | solution.py:32
  54.3 10.2 %collective-permute-start.18 = (bf16[256,256]{1,0:T(8,128)(2,1)S(1)}, bf16[256,256]{1,0:T(8,128)(2,1)S(1)}, u32[]{:S(2)}, u32[]{:S(2)}) collective-permute-start(bf16[256,256]{1,0:T(8,128)(2,1)S(1)} %get-tuple-element.52), channel_id=1, source_target_pairs={{0,14},{1,15},{2,0},{3,1},{4,2},{5,3},{6,4},{7,5},{8,6},{9,7},{10,... | collective-permute-start | bytes 393224 | tf_op jit(solution)/shard_map/ppermute | solution.py:32
  58.5 22.4 %collective-permute-start.16 = (bf16[512,256]{1,0:T(8,128)(2,1)S(1)}, bf16[512,256]{1,0:T(8,128)(2,1)S(1)}, u32[]{:S(2)}, u32[]{:S(2)}) collective-permute-start(bf16[512,256]{1,0:T(8,128)(2,1)S(1)} %get-tuple-element.49), channel_id=1, source_target_pairs={{0,16},{1,17},{2,18},{3,19},{4,20},{5,21},{6,22},{7,23},{8,24},{9,... | collective-permute-start | bytes 786440 | tf_op jit(solution)/shard_map/ppermute | solution.py:32
  61.5 13.3 %collective-permute-start.8 = (bf16[512,256]{1,0:T(8,128)(2,1)S(1)}, bf16[512,256]{1,0:T(8,128)(2,1)S(1)}, u32[]{:S(2)}, u32[]{:S(2)}) collective-permute-start(bf16[512,256]{1,0:T(8,128)(2,1)S(1)} %get-tuple-element.40), channel_id=1, source_target_pairs={{0,16},{1,17},{2,18},{3,19},{4,20},{5,21},{6,22},{7,23},{8,24},{9,... | collective-permute-start | bytes 786440 | tf_op jit(solution)/shard_map/ppermute | solution.py:32
  64.4 15.1 %collective-permute-start.12 = (bf16[512,256]{1,0:T(8,128)(2,1)S(1)}, bf16[512,256]{1,0:T(8,128)(2,1)S(1)}, u32[]{:S(2)}, u32[]{:S(2)}) collective-permute-start(bf16[512,256]{1,0:T(8,128)(2,1)S(1)} %pad_maximum_fusion), channel_id=1, source_target_pairs={{0,2},{1,3},{2,4},{3,5},{4,6},{5,7},{6,8},{7,9},{8,10},{9,11},{10,... | collective-permute-start | bytes 786440 | tf_op jit(solution)/shard_map/ppermute | solution.py:32
  64.6 17.3 %collective-permute-start.19 = (bf16[512,256]{1,0:T(8,128)(2,1)S(1)}, bf16[512,256]{1,0:T(8,128)(2,1)S(1)}, u32[]{:S(2)}, u32[]{:S(2)}) collective-permute-start(bf16[512,256]{1,0:T(8,128)(2,1)S(1)} %pad_maximum_fusion.1), channel_id=1, source_target_pairs={{0,14},{1,15},{2,0},{3,1},{4,2},{5,3},{6,4},{7,5},{8,6},{9,7},{10,... | collective-permute-start | bytes 786440 | tf_op jit(solution)/shard_map/ppermute | solution.py:32
  69.1 47.7 %collective-permute-start.6 = (bf16[512,256]{1,0:T(8,128)(2,1)}, bf16[512,256]{1,0:T(8,128)(2,1)}, u32[]{:S(2)}, u32[]{:S(2)}) collective-permute-start(bf16[512,256]{1,0:T(8,128)(2,1)} %get-tuple-element.36.after), channel_id=1, source_target_pairs={{0,16},{1,17},{2,18},{3,19},{4,20},{5,21},{6,22},{7,23},{8,24},{9,... | collective-permute-start | bytes 786440 | tf_op jit(solution)/shard_map/ppermute | solution.py:32
  74.8 37.6 %collective-permute-start.15 = (bf16[512,256]{1,0:T(8,128)(2,1)}, bf16[512,256]{1,0:T(8,128)(2,1)}, u32[]{:S(2)}, u32[]{:S(2)}) collective-permute-start(bf16[512,256]{1,0:T(8,128)(2,1)} %get-tuple-element.47), channel_id=1, source_target_pairs={{0,16},{1,17},{2,18},{3,19},{4,20},{5,21},{6,22},{7,23},{8,24},{9,... | collective-permute-start | bytes 786440 | tf_op jit(solution)/shard_map/ppermute | solution.py:32
  79.5 31.6 %collective-permute-start.7 = (bf16[512,256]{1,0:T(8,128)(2,1)}, bf16[512,256]{1,0:T(8,128)(2,1)}, u32[]{:S(2)}, u32[]{:S(2)}) collective-permute-start(bf16[512,256]{1,0:T(8,128)(2,1)} %get-tuple-element.38), channel_id=1, source_target_pairs={{0,16},{1,17},{2,18},{3,19},{4,20},{5,21},{6,22},{7,23},{8,24},{9,... | collective-permute-start | bytes 786440 | tf_op jit(solution)/shard_map/ppermute | solution.py:32
  80.9 30.2 %collective-permute-start.13 = (bf16[512,256]{1,0:T(8,128)(2,1)}, bf16[512,256]{1,0:T(8,128)(2,1)}, u32[]{:S(2)}, u32[]{:S(2)}) collective-permute-start(bf16[512,256]{1,0:T(8,128)(2,1)} %add_convert_fusion.4), channel_id=1, source_target_pairs={{0,2},{1,3},{2,4},{3,5},{4,6},{5,7},{6,8},{7,9},{8,10},{9,11},{10,... | collective-permute-start | bytes 786440 | tf_op jit(solution)/shard_map/ppermute | solution.py:32
  82.8 29.6 %collective-permute-start.20 = (bf16[512,256]{1,0:T(8,128)(2,1)}, bf16[512,256]{1,0:T(8,128)(2,1)}, u32[]{:S(2)}, u32[]{:S(2)}) collective-permute-start(bf16[512,256]{1,0:T(8,128)(2,1)} %add_convert_fusion.2), channel_id=1, source_target_pairs={{0,14},{1,15},{2,0},{3,1},{4,2},{5,3},{6,4},{7,5},{8,6},{9,7},{10,... | collective-permute-start | bytes 786440 | tf_op jit(solution)/shard_map/ppermute | solution.py:32
  97.2 3.4 %copy-start.1 = (bf16[512,8192]{1,0:T(8,128)(2,1)S(1)}, bf16[512,8192]{1,0:T(8,128)(2,1)}, u32[]{:S(2)}) copy-start(bf16[512,8192]{1,0:T(8,128)(2,1)} %hidden.7) | copy-start | bytes 25165828
  100.6 2.2 %copy-start.5 = (bf16[16,256,512]{2,1,0:T(8,128)(2,1)S(1)}, bf16[16,256,512]{2,1,0:T(8,128)(2,1)}, u32[]{:S(2)}) copy-start(bf16[16,256,512]{2,1,0:T(8,128)(2,1)} %all-gather.3.cloned.1.call-done) | copy-start | bytes 12582916
  102.8 1.2 copy-start.7
  104.0 7.1 %copy-start.20 = (bf16[512,256]{1,0:T(8,128)(2,1)S(1)}, bf16[512,256]{1,0:T(8,128)(2,1)}, u32[]{:S(2)}) copy-start(bf16[512,256]{1,0:T(8,128)(2,1)} %copy-done.19) | copy-start | bytes 786436
  104.0 8.4 %copy-start.18 = (bf16[512,256]{1,0:T(8,128)(2,1)S(1)}, bf16[512,256]{1,0:T(8,128)(2,1)}, u32[]{:S(2)}) copy-start(bf16[512,256]{1,0:T(8,128)(2,1)} %copy-done.17) | copy-start | bytes 786436
  104.0 18.7 %copy-start.15 = (bf16[512,256]{1,0:T(8,128)(2,1)S(1)}, bf16[512,256]{1,0:T(8,128)(2,1)}, u32[]{:S(2)}) copy-start(bf16[512,256]{1,0:T(8,128)(2,1)} %copy-done.14) | copy-start | bytes 786436
  104.0 28.3 %copy-start.11 = (bf16[1,256,512]{2,1,0:T(8,128)(2,1)S(1)}, bf16[1,256,512]{2,1,0:T(8,128)(2,1)}, u32[]{:S(2)}) copy-start(bf16[1,256,512]{2,1,0:T(8,128)(2,1)} %weight.3) | copy-start | bytes 786436
  104.0 28.3 %copy-start.22 = (bf16[1,256]{1,0:T(2,128)(2,1)S(1)}, bf16[1,256]{1,0:T(2,128)(2,1)}, u32[]{:S(2)}) copy-start(bf16[1,256]{1,0:T(2,128)(2,1)} %gain.3) | copy-start | bytes 1540
  104.0 28.3 %copy-start.23 = (f32[1,256]{1,0:T(1,128)S(1)}, f32[1,256]{1,0:T(1,128)}, u32[]{:S(2)}) copy-start(f32[1,256]{1,0:T(1,128)} %grad_gain_in.1) | copy-start | bytes 3076
  110.1 1.0 copy-start.8
  111.1 23.4 %copy-start.9 = (f32[512,512]{1,0:T(8,128)S(1)}, f32[512,512]{1,0:T(8,128)}, u32[]{:S(2)}) copy-start(f32[512,512]{1,0:T(8,128)} %copy-done.8) | copy-start | bytes 3145732
  111.1 23.4 %collective-permute-start.4 = (f32[512,512]{1,0:T(8,128)}, f32[512,512]{1,0:T(8,128)S(1)}, u32[]{:S(2)}, u32[]{:S(2)}) collective-permute-start(f32[512,512]{1,0:T(8,128)} %get-tuple-element.33), channel_id=1, source_target_pairs={{0,1},{1,0},{2,3},{3,2},{4,5},{5,4},{6,7},{7,6},{8,9},{9,8},{10,11... | collective-permute-start | bytes 3145736 | tf_op jit(solution)/shard_map/ppermute | solution.py:32
  112.3 9.9 %collective-permute-start.14 = (bf16[512,256]{1,0:T(8,128)(2,1)S(1)}, bf16[512,256]{1,0:T(8,128)(2,1)S(1)}, u32[]{:S(2)}, u32[]{:S(2)}) collective-permute-start(bf16[512,256]{1,0:T(8,128)(2,1)S(1)} %add_convert_fusion.3), channel_id=1, source_target_pairs={{0,2},{1,3},{2,4},{3,5},{4,6},{5,7},{6,8},{7,9},{8,10},{9,11},{10,... | collective-permute-start | bytes 786440 | tf_op jit(solution)/shard_map/ppermute | solution.py:32
  113.6 9.2 %collective-permute-start.21 = (bf16[512,256]{1,0:T(8,128)(2,1)S(1)}, bf16[512,256]{1,0:T(8,128)(2,1)S(1)}, u32[]{:S(2)}, u32[]{:S(2)}) collective-permute-start(bf16[512,256]{1,0:T(8,128)(2,1)S(1)} %add_convert_fusion.1), channel_id=1, source_target_pairs={{0,14},{1,15},{2,0},{3,1},{4,2},{5,3},{6,4},{7,5},{8,6},{9,7},{10,... | collective-permute-start | bytes 786440 | tf_op jit(solution)/shard_map/ppermute | solution.py:32
  123.8 8.5 %collective-permute-start.22 = (bf16[512,256]{1,0:T(8,128)(2,1)S(1)}, bf16[512,256]{1,0:T(8,128)(2,1)S(1)}, u32[]{:S(2)}, u32[]{:S(2)}) collective-permute-start(bf16[512,256]{1,0:T(8,128)(2,1)S(1)} %add_convert_fusion), channel_id=1, source_target_pairs={{0,224},{1,225},{2,226},{3,227},{4,228},{5,229},{6,230},{7,231},{8... | collective-permute-start | bytes 786440 | tf_op jit(solution)/shard_map/ppermute | solution.py:56
  132.3 1.0 copy-start.13
  (2 other events, 1.4 us)
Sparse Core Ops, SparseCore 0:
  26.6 70.5 all-gather.2

commit v4 on v3

v4 whole, which is shorter than its diff:
```python
import functools

import jax
import jax.numpy as jnp
from jax import lax
from jax.experimental import pallas as pl
from jax.experimental.pallas import tpu as pltpu
from jax.sharding import Mesh, PartitionSpec as P

NX, NZ, NC = 2, 8, 2
NB = 8
EPS = 1e-05
BF16 = jnp.bfloat16
F32 = jnp.float32
OFFSETS = (4, 3, -3, 2, -2, 1, -1, 0)
FIRST = 2
VMEM_LIMIT = 16 * 1024 * 1024
LOAD_LIMIT = 36 * 1024 * 1024


def fsdp_index(x, z, core):
    return (x * NZ + z) * NC + core


def move(value, change):
    pairs = [
        (fsdp_index(x, z, c), fsdp_index(*change(x, z, c)))
        for x in range(NX)
        for z in range(NZ)
        for c in range(NC)
    ]
    return lax.ppermute(value, ("x", "z", "core"), pairs)


def along_z(value, steps):
    return move(value, lambda x, z, c: (x, (z + steps) % NZ, c))


def swap_x(value):
    return move(value, lambda x, z, c: (1 - x, z, c))


def swap_core(value):
    return move(value, lambda x, z, c: (x, z, 1 - c))


def along_blk(value, steps, flip_x):
    size = NX * NZ * NC
    pairs = [
        (b * size + fsdp_index(x, z, c), ((b + steps) % NB) * size + fsdp_index(x ^ flip_x, z, c))
        for b in range(NB)
        for x in range(NX)
        for z in range(NZ)
        for c in range(NC)
    ]
    return lax.ppermute(value, ("blk", "x", "z", "core"), pairs)


def params(limit=VMEM_LIMIT):
    return pltpu.CompilerParams(vmem_limit_bytes=limit)


def cost(flops, size):
    return pl.CostEstimate(flops=flops, bytes_accessed=size, transcendentals=0)


IN_VMEM = pl.BlockSpec(memory_space=pltpu.VMEM)
IN_SMEM = pl.BlockSpec(memory_space=pltpu.SMEM)
ANYWHERE = pl.BlockSpec(memory_space=pl.ANY)
IN_HBM = pl.BlockSpec(memory_space=pltpu.HBM)


def block(ref, index, width):
    return ref[:, pl.ds(pl.multiple_of(index * width, width), width)]


def prepare_kernel(width, steps, table, hidden, cot, after, held, scale, cot_t, send_a, send_b, arrivals):
    step = hidden.shape[0] // steps
    lanes = 128
    copies = []
    for at in range(steps):
        rows = pl.ds(at * step, step)
        copy = pltpu.make_async_copy(hidden.at[rows, :], held.at[rows, :], arrivals.at[at])
        copy.start()
        copies.append(copy)
    first = send_a.shape[1] // width
    for at in range(steps):
        copies[at].wait()
        rows = slice(at * step, (at + 1) * step)
        total = jnp.zeros((step, lanes), F32)
        for j in range(hidden.shape[1] // lanes):
            part = held[rows, j * lanes:(j + 1) * lanes].astype(F32)
            total += part * part
        inverse = lax.rsqrt(jnp.sum(total, axis=1, keepdims=True) * (1.0 / hidden.shape[1]) + EPS)
        scale[rows, :] = inverse
        cot_t[:, rows] = (cot[rows, :].astype(F32) * inverse).T.astype(BF16)
        for i in range(first + send_b.shape[1] // width):
            out, j = (send_a, i) if i < first else (send_b, i - first)
            start = pl.multiple_of((table[i] ^ 1) * width, width)
            out[rows, j * width:(j + 1) * width] = held[rows, pl.ds(start, width)]


def prepare(table, hidden, cot, after, width):
    tokens, features = hidden.shape
    values = cot.shape[1]
    steps = 4
    return pl.pallas_call(
        functools.partial(prepare_kernel, width, steps),
        in_specs=[IN_SMEM, IN_HBM, IN_VMEM, ANYWHERE],
        out_specs=[IN_VMEM] * 5,
        out_shape=[
            jax.ShapeDtypeStruct((tokens, features), BF16),
            jax.ShapeDtypeStruct((tokens, 1), F32),
            jax.ShapeDtypeStruct((values, tokens), BF16),
            jax.ShapeDtypeStruct((tokens, 2 * FIRST * width), BF16),
            jax.ShapeDtypeStruct((tokens, 2 * (len(OFFSETS) - FIRST) * width), BF16),
        ],
        scratch_shapes=[pltpu.SemaphoreType.DMA((steps,))],
        compiler_params=params(LOAD_LIMIT),
        cost_estimate=cost(0, tokens),
    )(table, hidden, cot, after)


def gradient_kernel(base, groups, width, table, hidden, visiting, cot_t, cot_t_sibling, *outs):
    at = base
    sends = iter(outs[:len(groups)])
    keeps = iter(outs[len(groups):])
    for size in groups:
        send = next(sends)
        for j in range(size):
            for flip in (1, 0):
                total = jnp.dot(cot_t[...], block(hidden, table[2 * at + flip], width), preferred_element_type=F32)
                i = 2 * (at - base) + flip
                theirs = visiting[:, i * width:(i + 1) * width]
                total = (total + jnp.dot(cot_t_sibling[...], theirs, preferred_element_type=F32)).astype(BF16)
                if flip:
                    send[j] = total
                else:
                    next(keeps)[...] = total
            at += 1


def gradient(table, hidden, visiting, cot_t, cot_t_sibling, base, groups, width):
    tokens = hidden.shape[0]
    values = cot_t.shape[0]
    count = sum(groups)
    outs = pl.pallas_call(
        functools.partial(gradient_kernel, base, groups, width),
        in_specs=[IN_SMEM] + [IN_VMEM] * 4,
        out_specs=[IN_VMEM] * (len(groups) + count),
        out_shape=[jax.ShapeDtypeStruct((size, values, width), BF16) for size in groups]
        + [jax.ShapeDtypeStruct((values, width), BF16)] * count,
        compiler_params=params(),
        cost_estimate=cost(8 * count * tokens * values * width, 8 * count * tokens * width + 4 * count * values * width),
    )(table, hidden, visiting, cot_t, cot_t_sibling)
    return outs[:len(groups)], outs[len(groups):]


def project_kernel(offsets, sizes, more, width, table, hidden, visit_a, visit_b, *refs):
    mine, theirs = refs[-2:]
    start = refs[-4:-2] if more else None
    refs = iter(refs)
    weights = [[next(refs) for _ in range(size)] for size in sizes]
    product = product_theirs = None
    for at in range(0, len(offsets), 2):
        chosen = [OFFSETS.index(off) for off in offsets[at:at + 2]]
        weight = [ref[...].reshape(-1, mine.shape[1]) for group in weights[at:at + 2] for ref in group]
        weight = jnp.concatenate(weight, axis=0)
        own = jnp.concatenate([block(hidden, table[2 * i + flip], width) for i in chosen for flip in (0, 1)], axis=1)
        visitors = []
        for i in chosen:
            visit, j = (visit_a, i) if i < FIRST else (visit_b, i - FIRST)
            visitors.append(visit[:, 2 * j * width:2 * (j + 1) * width])
        visitors = jnp.concatenate(visitors, axis=1)
        product = jnp.dot(own, weight, preferred_element_type=F32)
        product_theirs = jnp.dot(visitors, weight, preferred_element_type=F32)
        if at:
            mine[...] += product
            theirs[...] += product_theirs
        elif more:
            mine[...] = start[0][...] + product
            theirs[...] = start[1][...] + product_theirs
        else:
            mine[...] = product
            theirs[...] = product_theirs


def project(table, hidden, visit_a, visit_b, weights, start, width):
    tokens = hidden.shape[0]
    values = hidden.shape[0] if start is None else start[0].shape[1]
    arrays = [w for group in weights.values() for w in group]
    values = arrays[0].shape[-1]
    size = sum(w.size for w in arrays)
    more = [] if start is None else list(start)
    return pl.pallas_call(
        functools.partial(project_kernel, tuple(weights), [len(g) for g in weights.values()], bool(more), width),
        in_specs=[IN_SMEM] + [IN_VMEM] * (3 + len(arrays) + len(more)),
        out_specs=[IN_VMEM, IN_VMEM],
        out_shape=[jax.ShapeDtypeStruct((tokens, values), F32)] * 2,
        compiler_params=params(),
        cost_estimate=cost(4 * tokens * size, 2 * size),
    )(table, hidden, visit_a, visit_b, *arrays, *more)


def small(kernel, inputs, after, shapes, dtype=BF16):
    def body(*refs):
        kernel(*refs[:len(inputs)], *refs[len(inputs) + len(after):])

    return pl.pallas_call(
        body,
        in_specs=[IN_VMEM] * len(inputs) + [ANYWHERE] * len(after),
        out_specs=[IN_VMEM] * len(shapes),
        out_shape=[jax.ShapeDtypeStruct(shape, dtype) for shape in shapes],
        compiler_params=params(),
        cost_estimate=cost(0, sum(a.size * a.dtype.itemsize for a in inputs)),
    )(*inputs, *after)


def pair(one, other, after):
    def kernel(one, other, out):
        out[0] = one[...]
        out[1] = other[...]

    return small(kernel, [one, other], after, [(2, *one.shape)])[0]


def split(pair_up, pair_down):
    def kernel(up, down, out_up, out_down):
        out_up[...] = up[0]
        out_down[...] = down[1]

    return small(kernel, [pair_up, pair_down], [], [pair_up.shape[1:]] * 2)


def total_of(terms, rows=slice(None)):
    return sum(t[rows].astype(F32) for t in terms).astype(BF16)


def begin(terms, places, after):
    values, width = terms[0].shape
    half = values // 2

    def kernel(keep, arrived, upper, lower):
        parts = (keep, arrived.at[places[0]])
        upper[...] = total_of(parts, slice(0, half))
        lower[...] = total_of(parts, slice(half, values))

    return small(kernel, terms, after, [(half, width)] * 2)


def carry(ups, downs, places, after):
    values, width = ups[0].shape

    def kernel(keep_up, arrived_up, up, keep_down, arrived_down, down, out_up, out_down):
        up_parts = (keep_up, arrived_up.at[places[0]])
        down_parts = (keep_down, arrived_down.at[places[1]])
        if up.shape[0] == values:
            out_up[...] = total_of((*up_parts, up))
            out_down[...] = total_of((*down_parts, down))
        else:
            half = values // 2
            upper, lower = slice(0, half), slice(half, values)
            out_up[upper, :] = (sum(t[upper].astype(F32) for t in up_parts) + up[...].astype(F32)).astype(BF16)
            out_up[lower, :] = total_of(up_parts, lower)
            out_down[upper, :] = total_of(down_parts, upper)
            out_down[lower, :] = (sum(t[lower].astype(F32) for t in down_parts) + down[...].astype(F32)).astype(BF16)

    return small(kernel, [*ups, *downs], after, [(values, width)] * 2)


def end(terms, place):
    def kernel(keep, arrived, up, down, out):
        out[...] = total_of((keep, arrived.at[place], up, down))

    return small(kernel, terms, [], [terms[0].shape])[0]


def scaled_values(product, arrived, scale):
    def kernel(product, arrived, scale, out):
        out[...] = ((product[...] + arrived[...]) * scale[...]).astype(BF16)

    return small(kernel, [product, arrived, scale], [], [product.shape])[0]


def diagonal(width):
    return lax.broadcasted_iota(jnp.int32, (width, width), 0) == lax.broadcasted_iota(jnp.int32, (width, width), 1)


def as_column(row):
    return jnp.sum(jnp.where(diagonal(row.shape[1]), row, 0.0), axis=1, keepdims=True)


def as_row(column):
    return jnp.sum(jnp.where(diagonal(column.shape[0]), column, 0.0), axis=0, keepdims=True)


def scale_kernel(gain, weight, out):
    out[...] = (weight[0].astype(F32) * as_column(gain[...].astype(F32))).astype(BF16)


def scale_weight(gain, weight):
    return pl.pallas_call(scale_kernel, out_shape=jax.ShapeDtypeStruct(weight.shape[1:], BF16), compiler_params=params())(gain, weight)


def finish_kernel(total, gain, weight, grad_weight_in, grad_gain_in, grad_weight, grad_gain):
    summed = total[...].astype(F32).T
    grad_weight[0] = grad_weight_in[0] + as_column(gain[...].astype(F32)) * summed
    grad_gain[...] = grad_gain_in[...] + as_row(jnp.sum(weight[0].astype(F32) * summed, axis=1, keepdims=True))


def finish(total, gain, weight, grad_weight_in, grad_gain_in):
    return pl.pallas_call(
        finish_kernel,
        out_shape=[jax.ShapeDtypeStruct(a.shape, F32) for a in (grad_weight_in, grad_gain_in)],
        compiler_params=params(),
    )(total, gain, weight, grad_weight_in, grad_gain_in)


def per_device(hidden, gain, value_weight, cotangent, grad_weight_in, grad_gain_in):
    width = value_weight.shape[1]
    x, z, core = (lax.axis_index(a) for a in ("x", "z", "core"))
    table = jnp.stack(
        [fsdp_index(x ^ flip, (z + off + NZ) % NZ, core) for off in OFFSETS for flip in (0, 1)]
    ).astype(jnp.int32)

    scaled_weight = scale_weight(gain, value_weight)
    layer = [along_blk(scaled_weight, 1, flip) for flip in (0, 1)]

    rest = len(OFFSETS) - FIRST
    held, scale, cot_t, send_a, send_b = prepare(table, hidden, cotangent, scaled_weight, width)
    cot_t_sibling, visit_a, visit_b = (swap_core(a) for a in (cot_t, send_a, send_b))

    pairs = (len(OFFSETS) - FIRST) // 2
    sends_1, keeps_1 = gradient(table, held, visit_a, cot_t, cot_t_sibling, 0, (1,) * FIRST, width)
    sends_2, keeps_2 = gradient(table, held, visit_b, cot_t, cot_t_sibling, FIRST, (2,) * pairs, width)
    arrived = [swap_x(send) for send in (*sends_1, *sends_2)]
    keeps = [*keeps_1, *keeps_2]
    places = [(i, 0) for i in range(FIRST)] + [(FIRST + i, j) for i in range(pairs) for j in (0, 1)]
    mine = {off: (keeps[i], arrived[places[i][0]]) for i, off in enumerate(OFFSETS)}
    place = {off: places[i][1] for i, off in enumerate(OFFSETS)}

    layer = pair(*layer, [cot_t])
    up, down = begin(mine[4], (place[4],), [sends_2[-1]])
    weights = {0: [layer]}
    layer_up = layer_down = layer
    for step in (1, 2, 3):
        layer_up, layer_down = along_z(layer_up, 1), along_z(layer_down, -1)
        weights[-step], weights[step] = [layer_up], [layer_down]
        off = 4 - step
        up, down = along_z(up, 1), along_z(down, -1)
        up, down = carry((*mine[off], up), (*mine[-off], down), (place[off], place[-off]), [layer_up, layer_down])
    far_up, far_down = split(layer_up, layer_down)
    weights[4] = [along_z(far_up, 1), along_z(far_down, -1)]
    up, down = along_z(up, 1), along_z(down, -1)
    total = along_blk(end((*mine[0], up, down), place[0]), -1, 0)

    near = {off: weights[off] for off in (0, -1, 1, -2, 2)}
    far = {off: weights[off] for off in (-3, 3, 4)}
    products = project(table, held, visit_a, visit_b, near, None, width)
    product, product_sibling = project(table, held, visit_a, visit_b, far, products, width)
    values = scaled_values(product, swap_core(product_sibling), scale)

    return values, *finish(total, gain, value_weight, grad_weight_in, grad_gain_in)


def solution(mesh):
    fsdp = ("x", "z", "core")
    return jax.shard_map(
        per_device,
        mesh=Mesh(mesh.devices.reshape(NB, NX, NZ, NC), ("blk", *fsdp)),
        in_specs=(
            P(("blk", *fsdp), None),
            P("blk", fsdp),
            P("blk", fsdp, None),
            P(("blk", *fsdp), None),
            P("blk", fsdp, None),
            P("blk", fsdp),
        ),
        out_specs=(P(("blk", *fsdp), None), P("blk", fsdp, None), P("blk", fsdp)),
        check_vma=False,
    )
```

time: 144 us -> 123 us (0.85)
  waiting for transfers between devices: 46.8 us -> 63.1 us
  local copies, waits for them, and re-layouts: 18.2 us -> 2.79 us
  between operations: 14.3 us -> 0.94 us
  other arithmetic: 7.28 us -> 0 us
    ppermute x20 -> x25, waiting for transfers between devices: 24.2 us -> 43.5 us  [move(): return lax.ppermute(value, ('x', 'z', 'core'), pairs)]
    unnamed x52 -> x14, local copies, waits for them, and re-layouts: 18.2 us -> 2.69 us
    all_gather x1 -> x0, waiting for transfers between devices: 11.9 us -> none  [per_device(): weights = lax.all_gather(pair(*layer, cot_t), 'z', axis=0)]
    ppermute x3, waiting for transfers between devices: 10.7 us -> 19.6 us  [along_blk(): return lax.ppermute(value, ('blk', 'x', 'z', 'core'), pairs)]
    convert_element_type x8 -> x0, other arithmetic: 6.15 us -> none  [the longest x7 5.2 us: add(): return sum((t.astype(F32) for t in terms)).astype(BF16)]
    ppermute x20 -> x25, starting transfers between devices: 30.3 us -> 33.8 us  [move(): return lax.ppermute(value, ('x', 'z', 'core'), pairs)]
    ppermute x3, starting transfers between devices: 5.59 us -> 2.24 us  [along_blk(): return lax.ppermute(value, ('blk', 'x', 'z', 'core'), pairs)]
    pallas_call x5 -> x12, Pallas kernels: 13.4 us -> 13.3 us  [the longest x2 5.76 us: project(): pl.pallas_call(functools.partial(project_kernel, tuple(weights), [len(g)...]
  transfers between devices with their start and end apart: 24 -> 28, of which waited for: 11 -> 13; matrix products, arithmetic and copies ran while one was open for 5% -> 0% of each run, Pallas kernels for 13% -> 11%
where the time goes in v4:
time: 123 us; the launch traced here: 122 us
  waiting for transfers between devices  63.1 us (51%)
  starting transfers between devices  36 us (29%)
  Pallas kernels  19.6 us (16%)
  local copies, waits for them, and re-layouts  2.79 us (2%)
    ppermute x25, waiting for transfers between devices, move(): return lax.ppermute(value, ('x', 'z', 'core'), pairs)  43.5 us
    ppermute x25, starting transfers between devices, move(): return lax.ppermute(value, ('x', 'z', 'core'), pairs)  33.8 us
    ppermute x3, waiting for transfers between devices, along_blk(): return lax.ppermute(value, ('blk', 'x', 'z', 'core'), pairs)  19.6 us
    pallas_call x2, Pallas kernels, project(): pl.pallas_call(functools.partial(project_kernel, tuple(weights), [len(g)...  5.76 us
    pallas_call x2, Pallas kernels, gradient(): pl.pallas_call(functools.partial(gradient_kernel, base, groups, width), i...  5.75 us
    pallas_call x1, Pallas kernels, prepare(): pl.pallas_call(functools.partial(prepare_kernel, width, steps), in_specs=...  5.08 us
    unnamed x14, local copies, waits for them, and re-layouts  2.69 us
  transfers between devices with their start and end apart: 28, of which 13 were waited for; matrix products, arithmetic and copies ran while one was open for 0% of the time, Pallas kernels for 11%

profile of v4, /device:TPU:4, one launch (start us, length us, event | category | flops | bytes accessed | tf_op | source)
XLA Modules:
  0.0 122.4 jit_solution(839706094166546296)
XLA Ops:
  0.7 0.9 copy-done
  1.7 0.7 copy-done.4
  2.4 0.1 shard_map.85.after
  2.6 1.0 copy-done.2
  3.6 5.1 %shard_map.86 = (bf16[512,8192]{1,0:T(8,128)(2,1)S(1)}, f32[512,1]{1,0:T(8,128)S(1)}, bf16[512,512]{1,0:T(8,128)(2,1)S(1)}, bf16[512,1024]{1,0:T(8,128)(2,1)S(1)}, bf16[512,3072]{1,0:T(8,128)(2,1)S(1)}) custom-call(s32[16]{0:T(128)S(1)} %stack.67.table, bf16[512,8192]{1,0:T(8,128)(2,1)} %hidden.1, bf16[512,512]{1,0:T(8,128)(2,1)S(1)} %copy-done.2, ...), custom_call_target="tpu_custom_call" | custom-call | bytes 512 | tf_op jit(solution)/shard_map/pallas_call | solution.py:107
  8.8 1.3 %collective-permute-start.2 = (bf16[256,512]{1,0:T(8,128)(2,1)S(1)}, bf16[256,512]{1,0:T(8,128)(2,1)S(1)}, u32[]{:S(2)}, u32[]{:S(2)}) collective-permute-start(bf16[256,512]{1,0:T(8,128)(2,1)S(1)} %shard_map.85.after), channel_id=1, source_target_pairs={{0,32},{1,33},{2,34},{3,35},{4,36},{5,37},{6,38},{7,39},{8,40},{9,... | collective-permute-start | bytes 786440 | tf_op jit(solution)/shard_map/ppermute | solution.py:56
  10.1 0.9 collective-permute-start.3
  11.0 13.4 %collective-permute-done.2.refs_0_ = bf16[256,512]{1,0:T(8,128)(2,1)S(1)} collective-permute-done((bf16[256,512]{1,0:T(8,128)(2,1)S(1)}, bf16[256,512]{1,0:T(8,128)(2,1)S(1)}, u32[]{:S(2)}, u32[]{:S(2)}) %collective-permute-start.2) | collective-permute-done | bytes 262176 | tf_op jit(solution)/shard_map/ppermute | solution.py:56
  24.4 0.9 collective-permute-done.3.refs_1_
  25.3 2.0 %collective-permute-start.4 = (bf16[2,256,512]{2,1,0:T(8,128)(2,1)S(1)}, bf16[2,256,512]{2,1,0:T(8,128)(2,1)S(1)}, u32[]{:S(2)}, u32[]{:S(2)}) collective-permute-start(bf16[2,256,512]{2,1,0:T(8,128)(2,1)S(1)} %shard_map.87.refs_0_), channel_id=1, source_target_pairs={{0,2},{1,3},{2,4},{3,5},{4,6},{5,7},{6,8},{7,9},{8,10},{9,11},{10,... | collective-permute-start | bytes 1572872 | tf_op jit(solution)/shard_map/ppermute | solution.py:32
  27.3 4.0 %collective-permute-start.7 = (bf16[2,256,512]{2,1,0:T(8,128)(2,1)S(1)}, bf16[2,256,512]{2,1,0:T(8,128)(2,1)S(1)}, u32[]{:S(2)}, u32[]{:S(2)}) collective-permute-start(bf16[2,256,512]{2,1,0:T(8,128)(2,1)S(1)} %shard_map.87.refs_0_), channel_id=1, source_target_pairs={{0,14},{1,15},{2,0},{3,1},{4,2},{5,3},{6,4},{7,5},{8,6},{9,7},{10,... | collective-permute-start | bytes 1572872 | tf_op jit(solution)/shard_map/ppermute | solution.py:32
  31.3 11.0 %collective-permute-done.4.refs_1_.refs_6_ = bf16[2,256,512]{2,1,0:T(8,128)(2,1)S(1)} collective-permute-done((bf16[2,256,512]{2,1,0:T(8,128)(2,1)S(1)}, bf16[2,256,512]{2,1,0:T(8,128)(2,1)S(1)}, u32[]{:S(2)}, u32[]{:S(2)}) %collective-permute-start.4) | collective-permute-done | bytes 524320 | tf_op jit(solution)/shard_map/ppermute | solution.py:32
  42.4 3.2 %collective-permute-start.8 = (bf16[2,256,512]{2,1,0:T(8,128)(2,1)S(1)}, bf16[2,256,512]{2,1,0:T(8,128)(2,1)S(1)}, u32[]{:S(2)}, u32[]{:S(2)}) collective-permute-start(bf16[2,256,512]{2,1,0:T(8,128)(2,1)S(1)} %collective-permute-done.7.refs_2_.refs_7_), channel_id=1, source_target_pairs={{0,14},{1,15},{2,0},{3,1},{4,2},{5,3},{6,4},{7,5},{8,6},{9,7},{10,... | collective-permute-start | bytes 1572872 | tf_op jit(solution)/shard_map/ppermute | solution.py:32
  45.6 1.8 %shard_map.93 = (bf16[1,512,256]{2,1,0:T(8,128)(2,1)S(1)}, bf16[1,512,256]{2,1,0:T(8,128)(2,1)S(1)}, bf16[512,256]{1,0:T(8,128)(2,1)S(1)}, bf16[512,256]{1,0:T(8,128)(2,1)S(1)}) custom-call(s32[16]{0:T(128)S(1)} %stack.67.table, bf16[512,8192]{1,0:T(8,128)(2,1)S(1)} %get-tuple-element.37.hidden, bf16[512,1024]{1,0:T(8,128)(2,1)S(1)} %collective-permute-done.visit_a.visiting, ...), custom_call_target="tpu_custom_call" | custom-call | flops 1073741824 | bytes 3145728 | tf_op jit(solution)/shard_map/pallas_call | solution.py:147
  47.4 0.7 collective-permute-start.18
  48.1 7.7 %collective-permute-done.5.refs_3_.refs_6_ = bf16[2,256,512]{2,1,0:T(8,128)(2,1)S(1)} collective-permute-done((bf16[2,256,512]{2,1,0:T(8,128)(2,1)S(1)}, bf16[2,256,512]{2,1,0:T(8,128)(2,1)S(1)}, u32[]{:S(2)}, u32[]{:S(2)}) %collective-permute-start.5) | collective-permute-done | bytes 524320 | tf_op jit(solution)/shard_map/ppermute | solution.py:32
  55.8 3.2 %collective-permute-start.9 = (bf16[2,256,512]{2,1,0:T(8,128)(2,1)S(1)}, bf16[2,256,512]{2,1,0:T(8,128)(2,1)S(1)}, u32[]{:S(2)}, u32[]{:S(2)}) collective-permute-start(bf16[2,256,512]{2,1,0:T(8,128)(2,1)S(1)} %collective-permute-done.8.refs_4_.refs_7_), channel_id=1, source_target_pairs={{0,14},{1,15},{2,0},{3,1},{4,2},{5,3},{6,4},{7,5},{8,6},{9,7},{10,... | collective-permute-start | bytes 1572872 | tf_op jit(solution)/shard_map/ppermute | solution.py:32
  59.0 4.0 %shard_map.92 = (bf16[2,512,256]{2,1,0:T(8,128)(2,1)S(1)}, bf16[2,512,256]{2,1,0:T(8,128)(2,1)S(1)}, bf16[2,512,256]{2,1,0:T(8,128)(2,1)S(1)}, bf16[512,256]{1,0...) custom-call(s32[16]{0:T(128)S(1)} %stack.67.table, ...), custom_call_target="tpu_custom_call" | custom-call | flops 3221225472 | bytes 9437184 | tf_op jit(solution)/shard_map/pallas_call | solution.py:147
  63.0 0.7 collective-permute-start.16
  63.7 2.9 %collective-permute-start.17 = (bf16[1,512,256]{2,1,0:T(8,128)(2,1)S(1)}, bf16[1,512,256]{2,1,0:T(8,128)(2,1)S(1)}, u32[]{:S(2)}, u32[]{:S(2)}) collective-permute-start(bf16[1,512,256]{2,1,0:T(8,128)(2,1)S(1)} %get-tuple-element.55), channel_id=1, source_target_pairs={{0,16},{1,17},{2,18},{3,19},{4,20},{5,21},{6,22},{7,23},{8,24},{9,... | collective-permute-start | bytes 786440 | tf_op jit(solution)/shard_map/ppermute | solution.py:32
  66.8 2.8 %collective-permute-done.6.refs_0_.refs_6_ = bf16[2,256,512]{2,1,0:T(8,128)(2,1)S(1)} collective-permute-done((bf16[2,256,512]{2,1,0:T(8,128)(2,1)S(1)}, bf16[2,256,512]{2,1,0:T(8,128)(2,1)S(1)}, u32[]{:S(2)}, u32[]{:S(2)}) %collective-permute-start.6) | collective-permute-done | bytes 524320 | tf_op jit(solution)/shard_map/ppermute | solution.py:32
  69.7 3.2 %collective-permute-start.11 = (bf16[256,512]{1,0:T(8,128)(2,1)S(1)}, bf16[256,512]{1,0:T(8,128)(2,1)S(1)}, u32[]{:S(2)}, u32[]{:S(2)}) collective-permute-start(bf16[256,512]{1,0:T(8,128)(2,1)S(1)} %get-tuple-element.42), channel_id=1, source_target_pairs={{0,14},{1,15},{2,0},{3,1},{4,2},{5,3},{6,4},{7,5},{8,6},{9,7},{10,... | collective-permute-start | bytes 786440 | tf_op jit(solution)/shard_map/ppermute | solution.py:32
  72.9 8.1 %collective-permute-done.17.refs_1_ = bf16[1,512,256]{2,1,0:T(8,128)(2,1)S(1)} collective-permute-done((bf16[1,512,256]{2,1,0:T(8,128)(2,1)S(1)}, bf16[1,512,256]{2,1,0:T(8,128)(2,1)S(1)}, u32[]{:S(2)}, u32[]{:S(2)}) %collective-permute-start.17) | collective-permute-done | bytes 262176 | tf_op jit(solution)/shard_map/ppermute | solution.py:32
  81.0 0.3 collective-permute-start.20
  81.3 0.6 collective-permute-start.15
  81.9 3.4 %shard_map.89 = (f32[512,512]{1,0:T(8,128)S(1)}, f32[512,512]{1,0:T(8,128)S(1)}) custom-call(s32[16]{0:T(128)S(1)} %stack.67.table, bf16[512,8192]{1,0:T(8,128)(2,1)S(1)} %get-tuple-element.37.hidden, bf16[512,1024]{1,0:T(8,128)(2,1)S(1)} %collective-permute-done.visit_a.visiting, bf16[512,3072]{1,0:T(8,128)(2,1)S(1)} %collective-permute-done.1.visit_b.visiting, ...), custom_call_target="tpu_custom_call" | custom-call | flops 2684354560 | bytes 2621440 | tf_op jit(solution)/shard_map/pallas_call | solution.py:195
  85.3 0.7 collective-permute-done.20.refs_5_
  86.0 2.4 %collective-permute-start.14 = (bf16[2,512,256]{2,1,0:T(8,128)(2,1)S(1)}, bf16[2,512,256]{2,1,0:T(8,128)(2,1)S(1)}, u32[]{:S(2)}, u32[]{:S(2)}) collective-permute-start(bf16[2,512,256]{2,1,0:T(8,128)(2,1)S(1)} %get-tuple-element.49.refs_2_), channel_id=1, source_target_pairs={{0,16},{1,17},{2,18},{3,19},{4,20},{5,21},{6,22},{7,23},{8,24},{9,... | collective-permute-start | bytes 1572872 | tf_op jit(solution)/shard_map/ppermute | solution.py:32
  88.3 0.2 shard_map.95
  88.5 1.8 %collective-permute-start.21 = (bf16[512,256]{1,0:T(8,128)(2,1)S(1)}, bf16[512,256]{1,0:T(8,128)(2,1)S(1)}, u32[]{:S(2)}, u32[]{:S(2)}) collective-permute-start(bf16[512,256]{1,0:T(8,128)(2,1)S(1)} %get-tuple-element.61), channel_id=1, source_target_pairs={{0,2},{1,3},{2,4},{3,5},{4,6},{5,7},{6,8},{7,9},{8,10},{9,11},{10,... | collective-permute-start | bytes 786440 | tf_op jit(solution)/shard_map/ppermute | solution.py:32
  90.3 1.5 %collective-permute-start.22 = (bf16[512,256]{1,0:T(8,128)(2,1)S(1)}, bf16[512,256]{1,0:T(8,128)(2,1)S(1)}, u32[]{:S(2)}, u32[]{:S(2)}) collective-permute-start(bf16[512,256]{1,0:T(8,128)(2,1)S(1)} %get-tuple-element.63), channel_id=1, source_target_pairs={{0,14},{1,15},{2,0},{3,1},{4,2},{5,3},{6,4},{7,5},{8,6},{9,7},{10,... | collective-permute-start | bytes 786440 | tf_op jit(solution)/shard_map/ppermute | solution.py:32
  91.8 2.3 %shard_map.90 = (f32[512,512]{1,0:T(8,128)S(1)}, f32[512,512]{1,0:T(8,128)S(1)}) custom-call(s32[16]{0:T(128)S(1)} %stack.67.table, bf16[512,8192]{1,0:T(8,128)(2,1)S(1)} %get-tuple-element.37.hidden, bf16[512,1024]{1,0:T(8,128)(2,1)S(1)} %collective-permute-done.visit_a.visiting, bf16[512,3072]{1,0:T(8,128)(2,1)S(1)} %collective-permute-done.1.visit_b.visiting, ...), custom_call_target="tpu_custom_call" | custom-call | flops 1610612736 | bytes 1572864 | tf_op jit(solution)/shard_map/pallas_call | solution.py:195
  94.2 0.3 collective-permute-start.12
  94.5 3.1 %collective-permute-done.15.refs_4_.refs_1_ = bf16[2,512,256]{2,1,0:T(8,128)(2,1)S(1)} collective-permute-done((bf16[2,512,256]{2,1,0:T(8,128)(2,1)S(1)}, bf16[2,512,256]{2,1,0:T(8,128)(2,1)S(1)}, u32[]{:S(2)}, u32[]{:S(2)}) %collective-permute-start.15) | collective-permute-done | bytes 524320 | tf_op jit(solution)/shard_map/ppermute | solution.py:32
  97.6 0.2 shard_map.96
  97.8 1.8 %collective-permute-start.23 = (bf16[512,256]{1,0:T(8,128)(2,1)S(1)}, bf16[512,256]{1,0:T(8,128)(2,1)S(1)}, u32[]{:S(2)}, u32[]{:S(2)}) collective-permute-start(bf16[512,256]{1,0:T(8,128)(2,1)S(1)} %get-tuple-element.64), channel_id=1, source_target_pairs={{0,2},{1,3},{2,4},{3,5},{4,6},{5,7},{6,8},{7,9},{8,10},{9,11},{10,... | collective-permute-start | bytes 786440 | tf_op jit(solution)/shard_map/ppermute | solution.py:32
  99.7 1.5 %collective-permute-start.24 = (bf16[512,256]{1,0:T(8,128)(2,1)S(1)}, bf16[512,256]{1,0:T(8,128)(2,1)S(1)}, u32[]{:S(2)}, u32[]{:S(2)}) collective-permute-start(bf16[512,256]{1,0:T(8,128)(2,1)S(1)} %get-tuple-element.66), channel_id=1, source_target_pairs={{0,14},{1,15},{2,0},{3,1},{4,2},{5,3},{6,4},{7,5},{8,6},{9,7},{10,... | collective-permute-start | bytes 786440 | tf_op jit(solution)/shard_map/ppermute | solution.py:32
  101.2 2.7 %collective-permute-done.14.refs_4_.refs_1_ = bf16[2,512,256]{2,1,0:T(8,128)(2,1)S(1)} collective-permute-done((bf16[2,512,256]{2,1,0:T(8,128)(2,1)S(1)}, bf16[2,512,256]{2,1,0:T(8,128)(2,1)S(1)}, u32[]{:S(2)}, u32[]{:S(2)}) %collective-permute-start.14) | collective-permute-done | bytes 524320 | tf_op jit(solution)/shard_map/ppermute | solution.py:32
  103.9 1.6 %collective-permute-done.23.refs_2_ = bf16[512,256]{1,0:T(8,128)(2,1)S(1)} collective-permute-done((bf16[512,256]{1,0:T(8,128)(2,1)S(1)}, bf16[512,256]{1,0:T(8,128)(2,1)S(1)}, u32[]{:S(2)}, u32[]{:S(2)}) %collective-permute-start.23) | collective-permute-done | bytes 262176 | tf_op jit(solution)/shard_map/ppermute | solution.py:32
  105.5 1.4 %collective-permute-done.24.refs_5_ = bf16[512,256]{1,0:T(8,128)(2,1)S(1)} collective-permute-done((bf16[512,256]{1,0:T(8,128)(2,1)S(1)}, bf16[512,256]{1,0:T(8,128)(2,1)S(1)}, u32[]{:S(2)}, u32[]{:S(2)}) %collective-permute-start.24) | collective-permute-done | bytes 262176 | tf_op jit(solution)/shard_map/ppermute | solution.py:32
  106.9 0.2 shard_map.97
  107.1 0.1 collective-permute-start.25
  107.2 3.2 %collective-permute-start.26 = (bf16[512,256]{1,0:T(8,128)(2,1)S(1)}, bf16[512,256]{1,0:T(8,128)(2,1)S(1)}, u32[]{:S(2)}, u32[]{:S(2)}) collective-permute-start(bf16[512,256]{1,0:T(8,128)(2,1)S(1)} %get-tuple-element.68), channel_id=1, source_target_pairs={{0,14},{1,15},{2,0},{3,1},{4,2},{5,3},{6,4},{7,5},{8,6},{9,7},{10,... | collective-permute-start | bytes 786440 | tf_op jit(solution)/shard_map/ppermute | solution.py:32
  110.4 4.3 %collective-permute-done.25.refs_2_ = bf16[512,256]{1,0:T(8,128)(2,1)S(1)} collective-permute-done((bf16[512,256]{1,0:T(8,128)(2,1)S(1)}, bf16[512,256]{1,0:T(8,128)(2,1)S(1)}, u32[]{:S(2)}, u32[]{:S(2)}) %collective-permute-start.25) | collective-permute-done | bytes 262176 | tf_op jit(solution)/shard_map/ppermute | solution.py:32
  114.8 0.1 shard_map.98
  115.0 1.0 shard_map.91
  116.0 5.4 %collective-permute-done.27.total = bf16[512,256]{1,0:T(8,128)(2,1)S(1)} collective-permute-done((bf16[512,256]{1,0:T(8,128)(2,1)S(1)}, bf16[512,256]{1,0:T(8,128)(2,1)S(1)}, u32[]{:S(2)}, u32[]{:S(2)}) %collective-permute-start.27) | collective-permute-done | bytes 262176 | tf_op jit(solution)/shard_map/ppermute | solution.py:56
  121.4 1.1 shard_map.99
  (38 shorter events, 0.7 us)
Async XLA Ops:
  0.7 1.0 copy-start
  1.7 0.7 copy-start.4
  2.6 1.0 copy-start.2
  8.7 50.3 %collective-permute-start.1 = (bf16[512,3072]{1,0:T(8,128)(2,1)S(1)}, bf16[512,3072]{1,0:T(8,128)(2,1)S(1)}, u32[]{:S(2)}, u32[]{:S(2)}) collective-permute-start(bf16[512,3072]{1,0:T(8,128)(2,1)S(1)} %get-tuple-element.39), channel_id=1, source_target_pairs={{0,1},{1,0},{2,3},{3,2},{4,5},{5,4},{6,7},{7,6},{8,9},{9,8},{10,11... | collective-permute-start | bytes 9437192 | tf_op jit(solution)/shard_map/ppermute | solution.py:32
  8.8 15.5 %collective-permute-start.2 = (bf16[256,512]{1,0:T(8,128)(2,1)S(1)}, bf16[256,512]{1,0:T(8,128)(2,1)S(1)}, u32[]{:S(2)}, u32[]{:S(2)}) collective-permute-start(bf16[256,512]{1,0:T(8,128)(2,1)S(1)} %shard_map.85.after), channel_id=1, source_target_pairs={{0,32},{1,33},{2,34},{3,35},{4,36},{5,37},{6,38},{7,39},{8,40},{9,... | collective-permute-start | bytes 786440 | tf_op jit(solution)/shard_map/ppermute | solution.py:56
  10.1 15.2 %collective-permute-start.3 = (bf16[256,512]{1,0:T(8,128)(2,1)S(1)}, bf16[256,512]{1,0:T(8,128)(2,1)S(1)}, u32[]{:S(2)}, u32[]{:S(2)}) collective-permute-start(bf16[256,512]{1,0:T(8,128)(2,1)S(1)} %shard_map.85.after), channel_id=1, source_target_pairs={{0,48},{1,49},{2,50},{3,51},{4,52},{5,53},{6,54},{7,55},{8,56},{9,... | collective-permute-start | bytes 786440 | tf_op jit(solution)/shard_map/ppermute | solution.py:56
  11.0 34.6 %collective-permute-start = (bf16[512,1024]{1,0:T(8,128)(2,1)S(1)}, bf16[512,1024]{1,0:T(8,128)(2,1)S(1)}, u32[]{:S(2)}, u32[]{:S(2)}) collective-permute-start(bf16[512,1024]{1,0:T(8,128)(2,1)S(1)} %get-tuple-element.38), channel_id=1, source_target_pairs={{0,1},{1,0},{2,3},{3,2},{4,5},{5,4},{6,7},{7,6},{8,9},{9,8},{10,11... | collective-permute-start | bytes 3145736 | tf_op jit(solution)/shard_map/ppermute | solution.py:32
  25.3 17.0 %collective-permute-start.4 = (bf16[2,256,512]{2,1,0:T(8,128)(2,1)S(1)}, bf16[2,256,512]{2,1,0:T(8,128)(2,1)S(1)}, u32[]{:S(2)}, u32[]{:S(2)}) collective-permute-start(bf16[2,256,512]{2,1,0:T(8,128)(2,1)S(1)} %shard_map.87.refs_0_), channel_id=1, source_target_pairs={{0,2},{1,3},{2,4},{3,5},{4,6},{5,7},{6,8},{7,9},{8,10},{9,11},{10,... | collective-permute-start | bytes 1572872 | tf_op jit(solution)/shard_map/ppermute | solution.py:32
  27.3 15.1 %collective-permute-start.7 = (bf16[2,256,512]{2,1,0:T(8,128)(2,1)S(1)}, bf16[2,256,512]{2,1,0:T(8,128)(2,1)S(1)}, u32[]{:S(2)}, u32[]{:S(2)}) collective-permute-start(bf16[2,256,512]{2,1,0:T(8,128)(2,1)S(1)} %shard_map.87.refs_0_), channel_id=1, source_target_pairs={{0,14},{1,15},{2,0},{3,1},{4,2},{5,3},{6,4},{7,5},{8,6},{9,7},{10,... | collective-permute-start | bytes 1572872 | tf_op jit(solution)/shard_map/ppermute | solution.py:32
  31.3 14.3 %collective-permute-start.13 = (bf16[512,512]{1,0:T(8,128)(2,1)S(1)}, bf16[512,512]{1,0:T(8,128)(2,1)S(1)}, u32[]{:S(2)}, u32[]{:S(2)}) collective-permute-start(bf16[512,512]{1,0:T(8,128)(2,1)S(1)} %get-tuple-element.40.refs_2_.cot_t), channel_id=1, source_target_pairs={{0,1},{1,0},{2,3},{3,2},{4,5},{5,4},{6,7},{7,6},{8,9},{9,8},{10,11... | collective-permute-start | bytes 1572872 | tf_op jit(solution)/shard_map/ppermute | solution.py:32
  42.4 13.4 %collective-permute-start.5 = (bf16[2,256,512]{2,1,0:T(8,128)(2,1)S(1)}, bf16[2,256,512]{2,1,0:T(8,128)(2,1)S(1)}, u32[]{:S(2)}, u32[]{:S(2)}) collective-permute-start(bf16[2,256,512]{2,1,0:T(8,128)(2,1)S(1)} %collective-permute-done.4.refs_1_.refs_6_), channel_id=1, source_target_pairs={{0,2},{1,3},{2,4},{3,5},{4,6},{5,7},{6,8},{7,9},{8,10},{9,11},{10,... | collective-permute-start | bytes 1572872 | tf_op jit(solution)/shard_map/ppermute | solution.py:32
  42.4 13.4 %collective-permute-start.8 = (bf16[2,256,512]{2,1,0:T(8,128)(2,1)S(1)}, bf16[2,256,512]{2,1,0:T(8,128)(2,1)S(1)}, u32[]{:S(2)}, u32[]{:S(2)}) collective-permute-start(bf16[2,256,512]{2,1,0:T(8,128)(2,1)S(1)} %collective-permute-done.7.refs_2_.refs_7_), channel_id=1, source_target_pairs={{0,14},{1,15},{2,0},{3,1},{4,2},{5,3},{6,4},{7,5},{8,6},{9,7},{10,... | collective-permute-start | bytes 1572872 | tf_op jit(solution)/shard_map/ppermute | solution.py:32
  47.4 19.2 %collective-permute-start.18 = (bf16[1,512,256]{2,1,0:T(8,128)(2,1)S(1)}, bf16[1,512,256]{2,1,0:T(8,128)(2,1)S(1)}, u32[]{:S(2)}, u32[]{:S(2)}) collective-permute-start(bf16[1,512,256]{2,1,0:T(8,128)(2,1)S(1)} %get-tuple-element.57), channel_id=1, source_target_pairs={{0,16},{1,17},{2,18},{3,19},{4,20},{5,21},{6,22},{7,23},{8,24},{9,... | collective-permute-start | bytes 786440 | tf_op jit(solution)/shard_map/ppermute | solution.py:32
  55.8 13.8 %collective-permute-start.6 = (bf16[2,256,512]{2,1,0:T(8,128)(2,1)S(1)}, bf16[2,256,512]{2,1,0:T(8,128)(2,1)S(1)}, u32[]{:S(2)}, u32[]{:S(2)}) collective-permute-start(bf16[2,256,512]{2,1,0:T(8,128)(2,1)S(1)} %collective-permute-done.5.refs_3_.refs_6_), channel_id=1, source_target_pairs={{0,2},{1,3},{2,4},{3,5},{4,6},{5,7},{6,8},{7,9},{8,10},{9,11},{10,... | collective-permute-start | bytes 1572872 | tf_op jit(solution)/shard_map/ppermute | solution.py:32
  55.8 13.8 %collective-permute-start.9 = (bf16[2,256,512]{2,1,0:T(8,128)(2,1)S(1)}, bf16[2,256,512]{2,1,0:T(8,128)(2,1)S(1)}, u32[]{:S(2)}, u32[]{:S(2)}) collective-permute-start(bf16[2,256,512]{2,1,0:T(8,128)(2,1)S(1)} %collective-permute-done.8.refs_4_.refs_7_), channel_id=1, source_target_pairs={{0,14},{1,15},{2,0},{3,1},{4,2},{5,3},{6,4},{7,5},{8,6},{9,7},{10,... | collective-permute-start | bytes 1572872 | tf_op jit(solution)/shard_map/ppermute | solution.py:32
  63.0 25.3 %collective-permute-start.16 = (bf16[2,512,256]{2,1,0:T(8,128)(2,1)S(1)}, bf16[2,512,256]{2,1,0:T(8,128)(2,1)S(1)}, u32[]{:S(2)}, u32[]{:S(2)}) collective-permute-start(bf16[2,512,256]{2,1,0:T(8,128)(2,1)S(1)} %get-tuple-element.53), channel_id=1, source_target_pairs={{0,16},{1,17},{2,18},{3,19},{4,20},{5,21},{6,22},{7,23},{8,24},{9,... | collective-permute-start | bytes 1572872 | tf_op jit(solution)/shard_map/ppermute | solution.py:32
  63.7 17.3 %collective-permute-start.17 = (bf16[1,512,256]{2,1,0:T(8,128)(2,1)S(1)}, bf16[1,512,256]{2,1,0:T(8,128)(2,1)S(1)}, u32[]{:S(2)}, u32[]{:S(2)}) collective-permute-start(bf16[1,512,256]{2,1,0:T(8,128)(2,1)S(1)} %get-tuple-element.55), channel_id=1, source_target_pairs={{0,16},{1,17},{2,18},{3,19},{4,20},{5,21},{6,22},{7,23},{8,24},{9,... | collective-permute-start | bytes 786440 | tf_op jit(solution)/shard_map/ppermute | solution.py:32
  66.7 14.6 %collective-permute-start.19 = (bf16[256,256]{1,0:T(8,128)(2,1)S(1)}, bf16[256,256]{1,0:T(8,128)(2,1)S(1)}, u32[]{:S(2)}, u32[]{:S(2)}) collective-permute-start(bf16[256,256]{1,0:T(8,128)(2,1)S(1)} %get-tuple-element.58), channel_id=1, source_target_pairs={{0,2},{1,3},{2,4},{3,5},{4,6},{5,7},{6,8},{7,9},{8,10},{9,11},{10,... | collective-permute-start | bytes 393224 | tf_op jit(solution)/shard_map/ppermute | solution.py:32
  69.6 20.7 %collective-permute-start.10 = (bf16[256,512]{1,0:T(8,128)(2,1)S(1)}, bf16[256,512]{1,0:T(8,128)(2,1)S(1)}, u32[]{:S(2)}, u32[]{:S(2)}) collective-permute-start(bf16[256,512]{1,0:T(8,128)(2,1)S(1)} %get-tuple-element.41), channel_id=1, source_target_pairs={{0,2},{1,3},{2,4},{3,5},{4,6},{5,7},{6,8},{7,9},{8,10},{9,11},{10,... | collective-permute-start | bytes 786440 | tf_op jit(solution)/shard_map/ppermute | solution.py:32
  69.7 22.1 %collective-permute-start.11 = (bf16[256,512]{1,0:T(8,128)(2,1)S(1)}, bf16[256,512]{1,0:T(8,128)(2,1)S(1)}, u32[]{:S(2)}, u32[]{:S(2)}) collective-permute-start(bf16[256,512]{1,0:T(8,128)(2,1)S(1)} %get-tuple-element.42), channel_id=1, source_target_pairs={{0,14},{1,15},{2,0},{3,1},{4,2},{5,3},{6,4},{7,5},{8,6},{9,7},{10,... | collective-permute-start | bytes 786440 | tf_op jit(solution)/shard_map/ppermute | solution.py:32
  81.0 5.0 %collective-permute-start.20 = (bf16[256,256]{1,0:T(8,128)(2,1)S(1)}, bf16[256,256]{1,0:T(8,128)(2,1)S(1)}, u32[]{:S(2)}, u32[]{:S(2)}) collective-permute-start(bf16[256,256]{1,0:T(8,128)(2,1)S(1)} %get-tuple-element.60), channel_id=1, source_target_pairs={{0,14},{1,15},{2,0},{3,1},{4,2},{5,3},{6,4},{7,5},{8,6},{9,7},{10,... | collective-permute-start | bytes 393224 | tf_op jit(solution)/shard_map/ppermute | solution.py:32
  81.3 16.4 %collective-permute-start.15 = (bf16[2,512,256]{2,1,0:T(8,128)(2,1)S(1)}, bf16[2,512,256]{2,1,0:T(8,128)(2,1)S(1)}, u32[]{:S(2)}, u32[]{:S(2)}) collective-permute-start(bf16[2,512,256]{2,1,0:T(8,128)(2,1)S(1)} %get-tuple-element.51), channel_id=1, source_target_pairs={{0,16},{1,17},{2,18},{3,19},{4,20},{5,21},{6,22},{7,23},{8,24},{9,... | collective-permute-start | bytes 1572872 | tf_op jit(solution)/shard_map/ppermute | solution.py:32
  86.0 17.9 %collective-permute-start.14 = (bf16[2,512,256]{2,1,0:T(8,128)(2,1)S(1)}, bf16[2,512,256]{2,1,0:T(8,128)(2,1)S(1)}, u32[]{:S(2)}, u32[]{:S(2)}) collective-permute-start(bf16[2,512,256]{2,1,0:T(8,128)(2,1)S(1)} %get-tuple-element.49.refs_2_), channel_id=1, source_target_pairs={{0,16},{1,17},{2,18},{3,19},{4,20},{5,21},{6,22},{7,23},{8,24},{9,... | collective-permute-start | bytes 1572872 | tf_op jit(solution)/shard_map/ppermute | solution.py:32
  88.5 9.1 %collective-permute-start.21 = (bf16[512,256]{1,0:T(8,128)(2,1)S(1)}, bf16[512,256]{1,0:T(8,128)(2,1)S(1)}, u32[]{:S(2)}, u32[]{:S(2)}) collective-permute-start(bf16[512,256]{1,0:T(8,128)(2,1)S(1)} %get-tuple-element.61), channel_id=1, source_target_pairs={{0,2},{1,3},{2,4},{3,5},{4,6},{5,7},{6,8},{7,9},{8,10},{9,11},{10,... | collective-permute-start | bytes 786440 | tf_op jit(solution)/shard_map/ppermute | solution.py:32
  90.3 7.3 %collective-permute-start.22 = (bf16[512,256]{1,0:T(8,128)(2,1)S(1)}, bf16[512,256]{1,0:T(8,128)(2,1)S(1)}, u32[]{:S(2)}, u32[]{:S(2)}) collective-permute-start(bf16[512,256]{1,0:T(8,128)(2,1)S(1)} %get-tuple-element.63), channel_id=1, source_target_pairs={{0,14},{1,15},{2,0},{3,1},{4,2},{5,3},{6,4},{7,5},{8,6},{9,7},{10,... | collective-permute-start | bytes 786440 | tf_op jit(solution)/shard_map/ppermute | solution.py:32
  94.2 27.2 %copy-start.1 = (bf16[1,256,512]{2,1,0:T(8,128)(2,1)S(1)}, bf16[1,256,512]{2,1,0:T(8,128)(2,1)}, u32[]{:S(2)}) copy-start(bf16[1,256,512]{2,1,0:T(8,128)(2,1)} %weight.3) | copy-start | bytes 786436
  94.2 27.2 %copy-start.3 = (f32[1,256,512]{2,1,0:T(8,128)S(1)}, f32[1,256,512]{2,1,0:T(8,128)}, u32[]{:S(2)}) copy-start(f32[1,256,512]{2,1,0:T(8,128)} %grad_weight_in.1) | copy-start | bytes 1572868
  94.2 27.2 %copy-start.5 = (bf16[1,256]{1,0:T(2,128)(2,1)S(1)}, bf16[1,256]{1,0:T(2,128)(2,1)}, u32[]{:S(2)}) copy-start(bf16[1,256]{1,0:T(2,128)(2,1)} %gain.3) | copy-start | bytes 1540
  94.2 27.2 %copy-start.6 = (f32[1,256]{1,0:T(1,128)S(1)}, f32[1,256]{1,0:T(1,128)}, u32[]{:S(2)}) copy-start(f32[1,256]{1,0:T(1,128)} %grad_gain_in.1) | copy-start | bytes 3076
  94.2 20.8 %collective-permute-start.12 = (f32[512,512]{1,0:T(8,128)S(1)}, f32[512,512]{1,0:T(8,128)S(1)}, u32[]{:S(2)}, u32[]{:S(2)}) collective-permute-start(f32[512,512]{1,0:T(8,128)S(1)} %get-tuple-element.46), channel_id=1, source_target_pairs={{0,1},{1,0},{2,3},{3,2},{4,5},{5,4},{6,7},{7,6},{8,9},{9,8},{10,11... | collective-permute-start | bytes 3145736 | tf_op jit(solution)/shard_map/ppermute | solution.py:32
  97.8 7.7 %collective-permute-start.23 = (bf16[512,256]{1,0:T(8,128)(2,1)S(1)}, bf16[512,256]{1,0:T(8,128)(2,1)S(1)}, u32[]{:S(2)}, u32[]{:S(2)}) collective-permute-start(bf16[512,256]{1,0:T(8,128)(2,1)S(1)} %get-tuple-element.64), channel_id=1, source_target_pairs={{0,2},{1,3},{2,4},{3,5},{4,6},{5,7},{6,8},{7,9},{8,10},{9,11},{10,... | collective-permute-start | bytes 786440 | tf_op jit(solution)/shard_map/ppermute | solution.py:32
  99.7 7.2 %collective-permute-start.24 = (bf16[512,256]{1,0:T(8,128)(2,1)S(1)}, bf16[512,256]{1,0:T(8,128)(2,1)S(1)}, u32[]{:S(2)}, u32[]{:S(2)}) collective-permute-start(bf16[512,256]{1,0:T(8,128)(2,1)S(1)} %get-tuple-element.66), channel_id=1, source_target_pairs={{0,14},{1,15},{2,0},{3,1},{4,2},{5,3},{6,4},{7,5},{8,6},{9,7},{10,... | collective-permute-start | bytes 786440 | tf_op jit(solution)/shard_map/ppermute | solution.py:32
  107.1 7.7 %collective-permute-start.25 = (bf16[512,256]{1,0:T(8,128)(2,1)S(1)}, bf16[512,256]{1,0:T(8,128)(2,1)S(1)}, u32[]{:S(2)}, u32[]{:S(2)}) collective-permute-start(bf16[512,256]{1,0:T(8,128)(2,1)S(1)} %get-tuple-element.67), channel_id=1, source_target_pairs={{0,2},{1,3},{2,4},{3,5},{4,6},{5,7},{6,8},{7,9},{8,10},{9,11},{10,... | collective-permute-start | bytes 786440 | tf_op jit(solution)/shard_map/ppermute | solution.py:32
  107.2 7.5 %collective-permute-start.26 = (bf16[512,256]{1,0:T(8,128)(2,1)S(1)}, bf16[512,256]{1,0:T(8,128)(2,1)S(1)}, u32[]{:S(2)}, u32[]{:S(2)}) collective-permute-start(bf16[512,256]{1,0:T(8,128)(2,1)S(1)} %get-tuple-element.68), channel_id=1, source_target_pairs={{0,14},{1,15},{2,0},{3,1},{4,2},{5,3},{6,4},{7,5},{8,6},{9,7},{10,... | collective-permute-start | bytes 786440 | tf_op jit(solution)/shard_map/ppermute | solution.py:32
  114.9 6.4 %collective-permute-start.27 = (bf16[512,256]{1,0:T(8,128)(2,1)S(1)}, bf16[512,256]{1,0:T(8,128)(2,1)S(1)}, u32[]{:S(2)}, u32[]{:S(2)}) collective-permute-start(bf16[512,256]{1,0:T(8,128)(2,1)S(1)} %shard_map.98), channel_id=1, source_target_pairs={{0,224},{1,225},{2,226},{3,227},{4,228},{5,229},{6,230},{7,231},{8... | collective-permute-start | bytes 786440 | tf_op jit(solution)/shard_map/ppermute | solution.py:56

commit v5 on v4

--- a/solution.py
+++ b/solution.py
@@ -13,7 +13,9 @@
 BF16 = jnp.bfloat16
 F32 = jnp.float32
 OFFSETS = (4, 3, -3, 2, -2, 1, -1, 0)
-FIRST = 2
+GROUPS = ((1, 2), (2, 2, 1))
+FIRST = sum(GROUPS[0])
+SWAPS = (3, 2, 3)
 VMEM_LIMIT = 16 * 1024 * 1024
 LOAD_LIMIT = 36 * 1024 * 1024
 
@@ -74,7 +76,15 @@
     return ref[:, pl.ds(pl.multiple_of(index * width, width), width)]
 
 
-def prepare_kernel(width, steps, table, hidden, cot, after, held, scale, cot_t, send_a, send_b, arrivals):
+def swapped(visits, index, width):
+    for visit, size in zip(visits, SWAPS):
+        if index < size:
+            return visit[:, 2 * index * width:2 * (index + 1) * width]
+        index -= size
+
+
+def prepare_kernel(width, steps, table, hidden, cot, after, held, scale, cot_t, *rest):
+    sends, arrivals = rest[:-1], rest[-1]
     step = hidden.shape[0] // steps
     lanes = 128
     copies = []
@@ -83,7 +93,6 @@
         copy = pltpu.make_async_copy(hidden.at[rows, :], held.at[rows, :], arrivals.at[at])
         copy.start()
         copies.append(copy)
-    first = send_a.shape[1] // width
     for at in range(steps):
         copies[at].wait()
         rows = slice(at * step, (at + 1) * step)
@@ -93,113 +102,116 @@
             total += part * part
         inverse = lax.rsqrt(jnp.sum(total, axis=1, keepdims=True) * (1.0 / hidden.shape[1]) + EPS)
         scale[rows, :] = inverse
-        cot_t[:, rows] = (cot[rows, :].astype(F32) * inverse).T.astype(BF16)
-        for i in range(first + send_b.shape[1] // width):
-            out, j = (send_a, i) if i < first else (send_b, i - first)
-            start = pl.multiple_of((table[i] ^ 1) * width, width)
-            out[rows, j * width:(j + 1) * width] = held[rows, pl.ds(start, width)]
+        columns = (cot[rows, :].astype(F32) * inverse).T.astype(BF16)
+        cot_t[:, rows] = columns
+        sends[0][:, pl.ds(2 * SWAPS[0] * width + at * step, step)] = columns
+        i = 0
+        for send, size in zip(sends, SWAPS):
+            for j in range(2 * size):
+                start = pl.multiple_of((table[i] ^ 1) * width, width)
+                send[rows, j * width:(j + 1) * width] = held[rows, pl.ds(start, width)]
+                i += 1
 
 
 def prepare(table, hidden, cot, after, width):
     tokens, features = hidden.shape
     values = cot.shape[1]
     steps = 4
+    columns = [2 * size * width for size in SWAPS]
+    columns[0] += tokens
     return pl.pallas_call(
         functools.partial(prepare_kernel, width, steps),
         in_specs=[IN_SMEM, IN_HBM, IN_VMEM, ANYWHERE],
-        out_specs=[IN_VMEM] * 5,
+        out_specs=[IN_VMEM] * (3 + len(columns)),
         out_shape=[
             jax.ShapeDtypeStruct((tokens, features), BF16),
             jax.ShapeDtypeStruct((tokens, 1), F32),
             jax.ShapeDtypeStruct((values, tokens), BF16),
-            jax.ShapeDtypeStruct((tokens, 2 * FIRST * width), BF16),
-            jax.ShapeDtypeStruct((tokens, 2 * (len(OFFSETS) - FIRST) * width), BF16),
-        ],
+        ] + [jax.ShapeDtypeStruct((tokens, count), BF16) for count in columns],
         scratch_shapes=[pltpu.SemaphoreType.DMA((steps,))],
         compiler_params=params(LOAD_LIMIT),
-        cost_estimate=cost(0, tokens),
+        cost_estimate=cost(0, 4 * tokens * features),
     )(table, hidden, cot, after)
 
 
-def gradient_kernel(base, groups, width, table, hidden, visiting, cot_t, cot_t_sibling, *outs):
-    at = base
+def gradient_kernel(base, groups, width, table, hidden, cot_t, *refs):
+    visits, outs = refs[:len(SWAPS)], refs[len(SWAPS) + 1:]
     sends = iter(outs[:len(groups)])
     keeps = iter(outs[len(groups):])
+    at = base
     for size in groups:
         send = next(sends)
         for j in range(size):
+            theirs = swapped(visits, at, width)
             for flip in (1, 0):
                 total = jnp.dot(cot_t[...], block(hidden, table[2 * at + flip], width), preferred_element_type=F32)
-                i = 2 * (at - base) + flip
-                theirs = visiting[:, i * width:(i + 1) * width]
-                total = (total + jnp.dot(cot_t_sibling[...], theirs, preferred_element_type=F32)).astype(BF16)
+                total += jnp.dot(
+                    visits[0][:, 2 * SWAPS[0] * width:], theirs[:, flip * width:(flip + 1) * width], preferred_element_type=F32
+                )
                 if flip:
-                    send[j] = total
+                    send[j] = total.astype(BF16)
                 else:
-                    next(keeps)[...] = total
+                    next(keeps)[...] = total.astype(BF16)
             at += 1
 
 
-def gradient(table, hidden, visiting, cot_t, cot_t_sibling, base, groups, width):
+def gradient(table, hidden, cot_t, visits, after, base, groups, width):
     tokens = hidden.shape[0]
     values = cot_t.shape[0]
     count = sum(groups)
     outs = pl.pallas_call(
         functools.partial(gradient_kernel, base, groups, width),
-        in_specs=[IN_SMEM] + [IN_VMEM] * 4,
+        in_specs=[IN_SMEM] + [IN_VMEM] * (2 + len(SWAPS)) + [ANYWHERE],
         out_specs=[IN_VMEM] * (len(groups) + count),
         out_shape=[jax.ShapeDtypeStruct((size, values, width), BF16) for size in groups]
         + [jax.ShapeDtypeStruct((values, width), BF16)] * count,
         compiler_params=params(),
-        cost_estimate=cost(8 * count * tokens * values * width, 8 * count * tokens * width + 4 * count * values * width),
-    )(table, hidden, visiting, cot_t, cot_t_sibling)
+        cost_estimate=cost(0, tokens),
+    )(table, hidden, cot_t, *visits, after)
     return outs[:len(groups)], outs[len(groups):]
 
 
-def project_kernel(offsets, sizes, more, width, table, hidden, visit_a, visit_b, *refs):
-    mine, theirs = refs[-2:]
-    start = refs[-4:-2] if more else None
+def project_kernel(offsets, sizes, more, extra, width, table, hidden, *refs):
+    visits, refs = refs[:len(SWAPS)], refs[len(SWAPS):]
+    outs = refs[-3:] if more else refs[-2:]
+    start = refs[-5 - extra:-3 - extra] if more else None
     refs = iter(refs)
     weights = [[next(refs) for _ in range(size)] for size in sizes]
-    product = product_theirs = None
+    totals = [ref[...] for ref in start] if more else []
     for at in range(0, len(offsets), 2):
         chosen = [OFFSETS.index(off) for off in offsets[at:at + 2]]
-        weight = [ref[...].reshape(-1, mine.shape[1]) for group in weights[at:at + 2] for ref in group]
+        weight = [ref[...].reshape(-1, outs[0].shape[1]) for group in weights[at:at + 2] for ref in group]
         weight = jnp.concatenate(weight, axis=0)
         own = jnp.concatenate([block(hidden, table[2 * i + flip], width) for i in chosen for flip in (0, 1)], axis=1)
-        visitors = []
-        for i in chosen:
-            visit, j = (visit_a, i) if i < FIRST else (visit_b, i - FIRST)
-            visitors.append(visit[:, 2 * j * width:2 * (j + 1) * width])
-        visitors = jnp.concatenate(visitors, axis=1)
-        product = jnp.dot(own, weight, preferred_element_type=F32)
-        product_theirs = jnp.dot(visitors, weight, preferred_element_type=F32)
-        if at:
-            mine[...] += product
-            theirs[...] += product_theirs
-        elif more:
-            mine[...] = start[0][...] + product
-            theirs[...] = start[1][...] + product_theirs
-        else:
-            mine[...] = product
-            theirs[...] = product_theirs
-
-
-def project(table, hidden, visit_a, visit_b, weights, start, width):
+        visitors = jnp.concatenate([swapped(visits, i, width) for i in chosen], axis=1)
+        products = [jnp.dot(rows, weight, preferred_element_type=F32) for rows in (own, visitors)]
+        totals = [t + p for t, p in zip(totals, products)] if totals else products
+    outs[0][...] = totals[0]
+    if more:
+        half = outs[1].shape[0]
+        outs[1][...] = totals[1][:half].astype(BF16)
+        outs[2][...] = totals[1][half:].astype(BF16)
+    else:
+        outs[1][...] = totals[1]
+
+
+def project(table, hidden, visits, weights, start, after, width):
     tokens = hidden.shape[0]
-    values = hidden.shape[0] if start is None else start[0].shape[1]
     arrays = [w for group in weights.values() for w in group]
     values = arrays[0].shape[-1]
     size = sum(w.size for w in arrays)
     more = [] if start is None else list(start)
+    whole = jax.ShapeDtypeStruct((tokens, values), F32)
+    half = jax.ShapeDtypeStruct((tokens // 2, values), BF16)
+    out_shape = [whole, half, half] if more else [whole, whole]
     return pl.pallas_call(
-        functools.partial(project_kernel, tuple(weights), [len(g) for g in weights.values()], bool(more), width),
-        in_specs=[IN_SMEM] + [IN_VMEM] * (3 + len(arrays) + len(more)),
-        out_specs=[IN_VMEM, IN_VMEM],
-        out_shape=[jax.ShapeDtypeStruct((tokens, values), F32)] * 2,
+        functools.partial(project_kernel, tuple(weights), [len(g) for g in weights.values()], bool(more), len(after), width),
+        in_specs=[IN_SMEM] + [IN_VMEM] * (1 + len(SWAPS) + len(arrays) + len(more)) + [ANYWHERE] * len(after),
+        out_specs=[IN_VMEM] * len(out_shape),
+        out_shape=out_shape,
         compiler_params=params(),
-        cost_estimate=cost(4 * tokens * size, 2 * size),
-    )(table, hidden, visit_a, visit_b, *arrays, *more)
+        cost_estimate=cost(4 * tokens * size, 0),
+    )(table, hidden, *visits, *arrays, *more, *after)
 
 
 def small(kernel, inputs, after, shapes, dtype=BF16):
@@ -212,8 +224,21 @@
         out_specs=[IN_VMEM] * len(shapes),
         out_shape=[jax.ShapeDtypeStruct(shape, dtype) for shape in shapes],
         compiler_params=params(),
-        cost_estimate=cost(0, sum(a.size * a.dtype.itemsize for a in inputs)),
+        cost_estimate=cost(0, inputs[0].shape[0]),
     )(*inputs, *after)
+
+
+def tie(arrays, after):
+    count = len(arrays)
+    return pl.pallas_call(
+        lambda *refs: None,
+        in_specs=[ANYWHERE] * (count + len(after)),
+        out_specs=[ANYWHERE] * count,
+        out_shape=[jax.ShapeDtypeStruct(a.shape, a.dtype) for a in arrays],
+        input_output_aliases={i: i for i in range(count)},
+        compiler_params=params(),
+        cost_estimate=cost(0, 1),
+    )(*arrays, *after)
 
 
 def pair(one, other, after):
@@ -224,12 +249,12 @@
     return small(kernel, [one, other], after, [(2, *one.shape)])[0]
 
 
-def split(pair_up, pair_down):
+def split(pair_up, pair_down, after):
     def kernel(up, down, out_up, out_down):
         out_up[...] = up[0]
         out_down[...] = down[1]
 
-    return small(kernel, [pair_up, pair_down], [], [pair_up.shape[1:]] * 2)
+    return small(kernel, [pair_up, pair_down], after, [pair_up.shape[1:]] * 2)
 
 
 def total_of(terms, rows=slice(None)):
@@ -268,18 +293,20 @@
     return small(kernel, [*ups, *downs], after, [(values, width)] * 2)
 
 
-def end(terms, place):
+def end(terms, place, after):
     def kernel(keep, arrived, up, down, out):
         out[...] = total_of((keep, arrived.at[place], up, down))
 
-    return small(kernel, terms, [], [terms[0].shape])[0]
-
-
-def scaled_values(product, arrived, scale):
-    def kernel(product, arrived, scale, out):
-        out[...] = ((product[...] + arrived[...]) * scale[...]).astype(BF16)
-
-    return small(kernel, [product, arrived, scale], [], [product.shape])[0]
+    return small(kernel, terms, after, [terms[0].shape])[0]
+
+
+def scaled_values(product, upper, lower, scale):
+    def kernel(product, upper, lower, scale, out):
+        half = upper.shape[0]
+        for arrived, rows in ((upper, slice(0, half)), (lower, slice(half, 2 * half))):
+            out[rows, :] = ((product[rows, :] + arrived[...].astype(F32)) * scale[rows, :]).astype(BF16)
+
+    return small(kernel, [product, upper, lower, scale], [], [product.shape])[0]
 
 
 def diagonal(width):
@@ -326,39 +353,42 @@
     scaled_weight = scale_weight(gain, value_weight)
     layer = [along_blk(scaled_weight, 1, flip) for flip in (0, 1)]
 
-    rest = len(OFFSETS) - FIRST
-    held, scale, cot_t, send_a, send_b = prepare(table, hidden, cotangent, scaled_weight, width)
-    cot_t_sibling, visit_a, visit_b = (swap_core(a) for a in (cot_t, send_a, send_b))
-
-    pairs = (len(OFFSETS) - FIRST) // 2
-    sends_1, keeps_1 = gradient(table, held, visit_a, cot_t, cot_t_sibling, 0, (1,) * FIRST, width)
-    sends_2, keeps_2 = gradient(table, held, visit_b, cot_t, cot_t_sibling, FIRST, (2,) * pairs, width)
+    held, scale, cot_t, *sends = prepare(table, hidden, cotangent, scaled_weight, width)
+    visits = [swap_core(send) for send in sends]
+
+    early = [visits[0]] * len(SWAPS)
+    sends_1, keeps_1 = gradient(table, held, cot_t, early, cot_t, 0, GROUPS[0], width)
+    sends_2, keeps_2 = gradient(table, held, cot_t, visits, sends_1[-1], FIRST, GROUPS[1], width)
     arrived = [swap_x(send) for send in (*sends_1, *sends_2)]
     keeps = [*keeps_1, *keeps_2]
-    places = [(i, 0) for i in range(FIRST)] + [(FIRST + i, j) for i in range(pairs) for j in (0, 1)]
+    places = [(i, j) for i, size in enumerate(GROUPS[0] + GROUPS[1]) for j in range(size)]
     mine = {off: (keeps[i], arrived[places[i][0]]) for i, off in enumerate(OFFSETS)}
     place = {off: places[i][1] for i, off in enumerate(OFFSETS)}
 
-    layer = pair(*layer, [cot_t])
+    layer = pair(*layer, [sends_1[-1]])
     up, down = begin(mine[4], (place[4],), [sends_2[-1]])
     weights = {0: [layer]}
     layer_up = layer_down = layer
     for step in (1, 2, 3):
         layer_up, layer_down = along_z(layer_up, 1), along_z(layer_down, -1)
+        if step < 3:
+            layer_up, layer_down = tie([layer_up, layer_down], [up, down, mine[4 - step][1]])
+        else:
+            far_up, far_down = split(layer_up, layer_down, [up, down, mine[1][1]])
         weights[-step], weights[step] = [layer_up], [layer_down]
         off = 4 - step
         up, down = along_z(up, 1), along_z(down, -1)
-        up, down = carry((*mine[off], up), (*mine[-off], down), (place[off], place[-off]), [layer_up, layer_down])
-    far_up, far_down = split(layer_up, layer_down)
+        ready = [layer_up, layer_down] if step < 3 else [mine[0][1]]
+        up, down = carry((*mine[off], up), (*mine[-off], down), (place[off], place[-off]), ready)
     weights[4] = [along_z(far_up, 1), along_z(far_down, -1)]
-    up, down = along_z(up, 1), along_z(down, -1)
-    total = along_blk(end((*mine[0], up, down), place[0]), -1, 0)
 
     near = {off: weights[off] for off in (0, -1, 1, -2, 2)}
     far = {off: weights[off] for off in (-3, 3, 4)}
-    products = project(table, held, visit_a, visit_b, near, None, width)
-    product, product_sibling = project(table, held, visit_a, visit_b, far, products, width)
-    values = scaled_values(product, swap_core(product_sibling), scale)
+    products = project(table, held, visits, near, None, [up], width)
+    product, *products = project(table, held, visits, far, products, [], width)
+    up, down = along_z(up, 1), along_z(down, -1)
+    total = along_blk(end((*mine[0], up, down), place[0], []), -1, 0)
+    values = scaled_values(product, *(swap_core(p) for p in products), scale)
 
     return values, *finish(total, gain, value_weight, grad_weight_in, grad_gain_in)
 

time: 123 us -> 118 us (0.959)
  waiting for transfers between devices: 63.1 us -> 58.3 us
    ppermute x3, waiting for transfers between devices: 19.6 us -> 13.2 us  [along_blk(): return lax.ppermute(value, ('blk', 'x', 'z', 'core'), pairs)]
    ppermute x25 -> x26, waiting for transfers between devices: 43.5 us -> 45.1 us  [move(): return lax.ppermute(value, ('x', 'z', 'core'), pairs)]
    ppermute x25 -> x26, starting transfers between devices: 33.8 us -> 33.8 us  [move(): return lax.ppermute(value, ('x', 'z', 'core'), pairs)]
  transfers between devices with their start and end apart: 28 -> 29, of which waited for: 13 -> 11; matrix products, arithmetic and copies ran while one was open for 0% -> 0% of each run, Pallas kernels for 11% -> 11%
where the time goes in v5:
time: 118 us
  waiting for transfers between devices  58.3 us (49%)
  starting transfers between devices  36 us (31%)
  Pallas kernels  19.6 us (17%)
  local copies, waits for them, and re-layouts  2.78 us (2%)
    ppermute x26, waiting for transfers between devices, move(): return lax.ppermute(value, ('x', 'z', 'core'), pairs)  45.1 us
    ppermute x26, starting transfers between devices, move(): return lax.ppermute(value, ('x', 'z', 'core'), pairs)  33.8 us
    ppermute x3, waiting for transfers between devices, along_blk(): return lax.ppermute(value, ('blk', 'x', 'z', 'core'), pairs)  13.2 us
    pallas_call x2, Pallas kernels, gradient(): pl.pallas_call(functools.partial(gradient_kernel, base, groups, width), i...  5.75 us
    pallas_call x2, Pallas kernels, project(): pl.pallas_call(functools.partial(project_kernel, tuple(weights), [len(g)...  5.74 us
    pallas_call x1, Pallas kernels, prepare(): pl.pallas_call(functools.partial(prepare_kernel, width, steps), in_specs=...  5.17 us
    unnamed x14, local copies, waits for them, and re-layouts  2.68 us
  transfers between devices with their start and end apart: 29, of which 11 were waited for; matrix products, arithmetic and copies ran while one was open for 0% of the time, Pallas kernels for 11%

profile of v5, /device:TPU:4, one launch (start us, length us, event | category | flops | bytes accessed | tf_op | source)
XLA Modules:
  0.0 117.7 jit_solution(2984022019286385887)
XLA Ops:
  0.7 0.9 copy-done
  1.7 0.7 copy-done.4
  2.4 0.1 shard_map.85.after
  2.5 0.1 stack.67.table
  2.6 1.0 copy-done.2
  3.6 5.2 %shard_map.86 = (bf16[512,8192]{1,0:T(8,128)(2,1)S(1)}, f32[512,1]{1,0:T(8,128)S(1)}, bf16[512,512]{1,0:T(8,128)(2,1)S(1)}, bf16[512,2048]{1,0:T(8,128)(2,1)S(1)...) custom-call(s32[16]{0:T(128)S(1)} %stack.67.table, bf16[512,8192]{1,0:T(8,128)(2,1)} %hidden.1, ...), custom_call_target="tpu_custom_call" | custom-call | bytes 16777216 | tf_op jit(solution)/shard_map/pallas_call | solution.py:122
  8.8 0.1 collective-permute-start
  8.9 0.5 collective-permute-start.2
  9.4 0.1 collective-permute-start.1
  9.5 1.2 %collective-permute-start.3 = (bf16[256,512]{1,0:T(8,128)(2,1)S(1)}, bf16[256,512]{1,0:T(8,128)(2,1)S(1)}, u32[]{:S(2)}, u32[]{:S(2)}) collective-permute-start(bf16[256,512]{1,0:T(8,128)(2,1)S(1)} %shard_map.85.after), channel_id=1, source_target_pairs={{0,32},{1,33},{2,34},{3,35},{4,36},{5,37},{6,38},{7,39},{8,40},{9,... | collective-permute-start | bytes 786440 | tf_op jit(solution)/shard_map/ppermute | solution.py:58
  10.7 0.9 collective-permute-start.4
  11.6 1.5 %collective-permute-done.refs_0_.refs_1_.refs_2_ = bf16[512,2048]{1,0:T(8,128)(2,1)S(1)} collective-permute-done((bf16[512,2048]{1,0:T(8,128)(2,1)S(1)}, bf16[512,2048]{1,0:T(8,128)(2,1)S(1)}, u32[]{:S(2)}, u32[]{:S(2)}) %collective-permute-start) | collective-permute-done | bytes 2097184 | tf_op jit(solution)/shard_map/ppermute | solution.py:34
  13.1 2.3 %shard_map.87 = (bf16[1,512,256]{2,1,0:T(8,128)(2,1)S(1)}, bf16[2,512,256]{2,1,0:T(8,128)(2,1)S(1)}, bf16[512,256]{1,0:T(8,128)(2,1)S(1)}, bf16[512,256]{1,0:T(8,128)(2,1)S(1)}, bf16[512,256]{1,0:T(8,128)(2,1)S(1)}) custom-call(s32[16]{0:T(128)S(1)} %stack.67.table, bf16[512,8192]{1,0:T(8,128)(2,1)S(1)} %get-tuple-element.43.hidden, ...), custom_call_target="tpu_custom_call" | custom-call | bytes 512 | tf_op jit(solution)/shard_map/pallas_call | solution.py:162
  15.4 9.6 %collective-permute-done.3.refs_0_ = bf16[256,512]{1,0:T(8,128)(2,1)S(1)} collective-permute-done((bf16[256,512]{1,0:T(8,128)(2,1)S(1)}, bf16[256,512]{1,0:T(8,128)(2,1)S(1)}, u32[]{:S(2)}, u32[]{:S(2)}) %collective-permute-start.3) | collective-permute-done | bytes 262176 | tf_op jit(solution)/shard_map/ppermute | solution.py:58
  25.0 0.9 collective-permute-done.4.refs_1_
  25.9 2.0 %collective-permute-start.5 = (bf16[2,256,512]{2,1,0:T(8,128)(2,1)S(1)}, bf16[2,256,512]{2,1,0:T(8,128)(2,1)S(1)}, u32[]{:S(2)}, u32[]{:S(2)}) collective-permute-start(bf16[2,256,512]{2,1,0:T(8,128)(2,1)S(1)} %shard_map.88.refs_3_), channel_id=1, source_target_pairs={{0,2},{1,3},{2,4},{3,5},{4,6},{5,7},{6,8},{7,9},{8,10},{9,11},{10,... | collective-permute-start | bytes 1572872 | tf_op jit(solution)/shard_map/ppermute | solution.py:34
  27.9 4.0 %collective-permute-start.6 = (bf16[2,256,512]{2,1,0:T(8,128)(2,1)S(1)}, bf16[2,256,512]{2,1,0:T(8,128)(2,1)S(1)}, u32[]{:S(2)}, u32[]{:S(2)}) collective-permute-start(bf16[2,256,512]{2,1,0:T(8,128)(2,1)S(1)} %shard_map.88.refs_3_), channel_id=1, source_target_pairs={{0,14},{1,15},{2,0},{3,1},{4,2},{5,3},{6,4},{7,5},{8,6},{9,7},{10,... | collective-permute-start | bytes 1572872 | tf_op jit(solution)/shard_map/ppermute | solution.py:34
  31.9 0.6 collective-permute-start.8
  32.5 3.0 %collective-permute-start.7 = (bf16[1,512,256]{2,1,0:T(8,128)(2,1)S(1)}, bf16[1,512,256]{2,1,0:T(8,128)(2,1)S(1)}, u32[]{:S(2)}, u32[]{:S(2)}) collective-permute-start(bf16[1,512,256]{2,1,0:T(8,128)(2,1)S(1)} %get-tuple-element.50), channel_id=1, source_target_pairs={{0,16},{1,17},{2,18},{3,19},{4,20},{5,21},{6,22},{7,23},{8,24},{9,... | collective-permute-start | bytes 786440 | tf_op jit(solution)/shard_map/ppermute | solution.py:34
  35.4 3.4 %shard_map.89 = (bf16[2,512,256]{2,1,0:T(8,128)(2,1)S(1)}, bf16[2,512,256]{2,1,0:T(8,128)(2,1)S(1)}, bf16[1,512,256]{2,1,0:T(8,128)(2,1)S(1)}, bf16[512,256]{1,0...) custom-call(s32[16]{0:T(128)S(1)} %stack.67.table, ...), custom_call_target="tpu_custom_call" | custom-call | bytes 512 | tf_op jit(solution)/shard_map/pallas_call | solution.py:162
  38.9 0.8 collective-permute-start.13
  39.7 14.2 %collective-permute-done.7.refs_1_ = bf16[1,512,256]{2,1,0:T(8,128)(2,1)S(1)} collective-permute-done((bf16[1,512,256]{2,1,0:T(8,128)(2,1)S(1)}, bf16[1,512,256]{2,1,0:T(8,128)(2,1)S(1)}, u32[]{:S(2)}, u32[]{:S(2)}) %collective-permute-start.7) | collective-permute-done | bytes 262176 | tf_op jit(solution)/shard_map/ppermute | solution.py:34
  54.0 2.0 %collective-permute-start.10 = (bf16[2,256,512]{2,1,0:T(8,128)(2,1)S(1)}, bf16[2,256,512]{2,1,0:T(8,128)(2,1)S(1)}, u32[]{:S(2)}, u32[]{:S(2)}) collective-permute-start(bf16[2,256,512]{2,1,0:T(8,128)(2,1)S(1)} %get-tuple-element.55.refs_7_.refs_5_), channel_id=1, source_target_pairs={{0,14},{1,15},{2,0},{3,1},{4,2},{5,3},{6,4},{7,5},{8,6},{9,7},{10,... | collective-permute-start | bytes 1572872 | tf_op jit(solution)/shard_map/ppermute | solution.py:34
  56.1 3.2 %collective-permute-start.12 = (bf16[256,256]{1,0:T(8,128)(2,1)S(1)}, bf16[256,256]{1,0:T(8,128)(2,1)S(1)}, u32[]{:S(2)}, u32[]{:S(2)}) collective-permute-start(bf16[256,256]{1,0:T(8,128)(2,1)S(1)} %get-tuple-element.53.refs_3_), channel_id=1, source_target_pairs={{0,14},{1,15},{2,0},{3,1},{4,2},{5,3},{6,4},{7,5},{8,6},{9,7},{10,... | collective-permute-start | bytes 393224 | tf_op jit(solution)/shard_map/ppermute | solution.py:34
  59.3 11.3 %collective-permute-done.11.refs_2_ = bf16[256,256]{1,0:T(8,128)(2,1)S(1)} collective-permute-done((bf16[256,256]{1,0:T(8,128)(2,1)S(1)}, bf16[256,256]{1,0:T(8,128)(2,1)S(1)}, u32[]{:S(2)}, u32[]{:S(2)}) %collective-permute-start.11) | collective-permute-done | bytes 131104 | tf_op jit(solution)/shard_map/ppermute | solution.py:34
  70.7 0.2 shard_map.92
  70.9 3.2 %collective-permute-start.17 = (bf16[512,256]{1,0:T(8,128)(2,1)S(1)}, bf16[512,256]{1,0:T(8,128)(2,1)S(1)}, u32[]{:S(2)}, u32[]{:S(2)}) collective-permute-start(bf16[512,256]{1,0:T(8,128)(2,1)S(1)} %get-tuple-element.59.refs_3_), channel_id=1, source_target_pairs={{0,14},{1,15},{2,0},{3,1},{4,2},{5,3},{6,4},{7,5},{8,6},{9,7},{10,... | collective-permute-start | bytes 786440 | tf_op jit(solution)/shard_map/ppermute | solution.py:34
  74.1 0.6 collective-permute-start.23
  74.7 3.0 %collective-permute-start.18 = (bf16[2,512,256]{2,1,0:T(8,128)(2,1)S(1)}, bf16[2,512,256]{2,1,0:T(8,128)(2,1)S(1)}, u32[]{:S(2)}, u32[]{:S(2)}) collective-permute-start(bf16[2,512,256]{2,1,0:T(8,128)(2,1)S(1)} %get-tuple-element.67), channel_id=1, source_target_pairs={{0,16},{1,17},{2,18},{3,19},{4,20},{5,21},{6,22},{7,23},{8,24},{9,... | collective-permute-start | bytes 1572872 | tf_op jit(solution)/shard_map/ppermute | solution.py:34
  77.7 3.7 %collective-permute-done.16.refs_2_ = bf16[512,256]{1,0:T(8,128)(2,1)S(1)} collective-permute-done((bf16[512,256]{1,0:T(8,128)(2,1)S(1)}, bf16[512,256]{1,0:T(8,128)(2,1)S(1)}, u32[]{:S(2)}, u32[]{:S(2)}) %collective-permute-start.16) | collective-permute-done | bytes 262176 | tf_op jit(solution)/shard_map/ppermute | solution.py:34
  81.4 0.2 shard_map.94
  81.6 2.1 %collective-permute-start.21 = (bf16[512,256]{1,0:T(8,128)(2,1)S(1)}, bf16[512,256]{1,0:T(8,128)(2,1)S(1)}, u32[]{:S(2)}, u32[]{:S(2)}) collective-permute-start(bf16[512,256]{1,0:T(8,128)(2,1)S(1)} %get-tuple-element.65.refs_2_), channel_id=1, source_target_pairs={{0,2},{1,3},{2,4},{3,5},{4,6},{5,7},{6,8},{7,9},{8,10},{9,11},{10,... | collective-permute-start | bytes 786440 | tf_op jit(solution)/shard_map/ppermute | solution.py:34
  83.7 1.3 %collective-permute-start.22 = (bf16[512,256]{1,0:T(8,128)(2,1)S(1)}, bf16[512,256]{1,0:T(8,128)(2,1)S(1)}, u32[]{:S(2)}, u32[]{:S(2)}) collective-permute-start(bf16[512,256]{1,0:T(8,128)(2,1)S(1)} %get-tuple-element.66.refs_3_), channel_id=1, source_target_pairs={{0,14},{1,15},{2,0},{3,1},{4,2},{5,3},{6,4},{7,5},{8,6},{9,7},{10,... | collective-permute-start | bytes 786440 | tf_op jit(solution)/shard_map/ppermute | solution.py:34
  85.0 2.7 %collective-permute-done.18.refs_4_.refs_1_ = bf16[2,512,256]{2,1,0:T(8,128)(2,1)S(1)} collective-permute-done((bf16[2,512,256]{2,1,0:T(8,128)(2,1)S(1)}, bf16[2,512,256]{2,1,0:T(8,128)(2,1)S(1)}, u32[]{:S(2)}, u32[]{:S(2)}) %collective-permute-start.18) | collective-permute-done | bytes 524320 | tf_op jit(solution)/shard_map/ppermute | solution.py:34
  87.6 6.5 %collective-permute-done.21.refs_2_ = bf16[512,256]{1,0:T(8,128)(2,1)S(1)} collective-permute-done((bf16[512,256]{1,0:T(8,128)(2,1)S(1)}, bf16[512,256]{1,0:T(8,128)(2,1)S(1)}, u32[]{:S(2)}, u32[]{:S(2)}) %collective-permute-start.21) | collective-permute-done | bytes 262176 | tf_op jit(solution)/shard_map/ppermute | solution.py:34
  94.1 4.6 %collective-permute-done.22.refs_5_ = bf16[512,256]{1,0:T(8,128)(2,1)S(1)} collective-permute-done((bf16[512,256]{1,0:T(8,128)(2,1)S(1)}, bf16[512,256]{1,0:T(8,128)(2,1)S(1)}, u32[]{:S(2)}, u32[]{:S(2)}) %collective-permute-start.22) | collective-permute-done | bytes 262176 | tf_op jit(solution)/shard_map/ppermute | solution.py:34
  98.7 0.2 shard_map.96
  99.0 3.2 %collective-permute-start.27 = (bf16[512,256]{1,0:T(8,128)(2,1)S(1)}, bf16[512,256]{1,0:T(8,128)(2,1)S(1)}, u32[]{:S(2)}, u32[]{:S(2)}) collective-permute-start(bf16[512,256]{1,0:T(8,128)(2,1)S(1)} %get-tuple-element.80), channel_id=1, source_target_pairs={{0,14},{1,15},{2,0},{3,1},{4,2},{5,3},{6,4},{7,5},{8,6},{9,7},{10,... | collective-permute-start | bytes 786440 | tf_op jit(solution)/shard_map/ppermute | solution.py:34
  102.4 3.2 %collective-permute-start.20 = (bf16[256,512]{1,0:T(8,128)(2,1)S(1)}, bf16[256,512]{1,0:T(8,128)(2,1)S(1)}, u32[]{:S(2)}, u32[]{:S(2)}) collective-permute-start(bf16[256,512]{1,0:T(8,128)(2,1)S(1)} %get-tuple-element.69), channel_id=1, source_target_pairs={{0,14},{1,15},{2,0},{3,1},{4,2},{5,3},{6,4},{7,5},{8,6},{9,7},{10,... | collective-permute-start | bytes 786440 | tf_op jit(solution)/shard_map/ppermute | solution.py:34
  105.6 3.4 %shard_map.97 = (f32[512,512]{1,0:T(8,128)S(1)}, f32[512,512]{1,0:T(8,128)S(1)}) custom-call(s32[16]{0:T(128)S(1)} %stack.67.table, bf16[512,8192]{1,0:T(8,128)(2,1)S(1)} %get-tuple-element.43.hidden, bf16[512,2048]{1,0:T(8,128)(2,1)S(1)} %collective-permute-done.refs_0_.refs_1_.refs_2_, bf16[512,1024]{1,0:T(8,128)(2,1)S(1)} %collective-permute-done.1.refs_1_, ...), custom_call_target="tpu_custom_call" | custom-call | flops 2684354560 | tf_op jit(solution)/shard_map/pallas_call | solution.py:207
  109.0 0.1 shard_map.100
  109.2 0.7 collective-permute-done.19.refs_5_
  110.0 2.3 %shard_map.98 = (f32[512,512]{1,0:T(8,128)S(1)}, bf16[256,512]{1,0:T(8,128)(2,1)S(1)}, bf16[256,512]{1,0:T(8,128)(2,1)S(1)}) custom-call(s32[16]{0:T(128)S(1)} %stack.67.table, bf16[512,8192]{1,0:T(8,128)(2,1)S(1)} %get-tuple-element.43.hidden, bf16[512,2048]{1,0:T(8,128)(2,1)S(1)} %collective-permute-done.refs_0_.refs_1_.refs_2_, ...), custom_call_target="tpu_custom_call" | custom-call | flops 1610612736 | tf_op jit(solution)/shard_map/pallas_call | solution.py:207
  112.3 0.1 collective-permute-start.24
  112.4 0.5 collective-permute-start.25
  112.9 2.7 %collective-permute-done.28.total = bf16[512,256]{1,0:T(8,128)(2,1)S(1)} collective-permute-done((bf16[512,256]{1,0:T(8,128)(2,1)S(1)}, bf16[512,256]{1,0:T(8,128)(2,1)S(1)}, u32[]{:S(2)}, u32[]{:S(2)}) %collective-permute-start.28) | collective-permute-done | bytes 262176 | tf_op jit(solution)/shard_map/ppermute | solution.py:58
  115.6 1.1 shard_map.101
  116.7 1.0 shard_map.99
  (42 shorter events, 0.7 us)
Async XLA Ops:
  0.7 1.0 copy-start
  1.7 0.7 copy-start.4
  2.6 1.0 copy-start.2
  8.8 4.2 %collective-permute-start = (bf16[512,2048]{1,0:T(8,128)(2,1)S(1)}, bf16[512,2048]{1,0:T(8,128)(2,1)S(1)}, u32[]{:S(2)}, u32[]{:S(2)}) collective-permute-start(bf16[512,2048]{1,0:T(8,128)(2,1)S(1)} %get-tuple-element.44), channel_id=1, source_target_pairs={{0,1},{1,0},{2,3},{3,2},{4,5},{5,4},{6,7},{7,6},{8,9},{9,8},{10,11... | collective-permute-start | bytes 6291464 | tf_op jit(solution)/shard_map/ppermute | solution.py:34
  8.9 26.5 %collective-permute-start.2 = (bf16[512,1536]{1,0:T(8,128)(2,1)S(1)}, bf16[512,1536]{1,0:T(8,128)(2,1)S(1)}, u32[]{:S(2)}, u32[]{:S(2)}) collective-permute-start(bf16[512,1536]{1,0:T(8,128)(2,1)S(1)} %get-tuple-element.46), channel_id=1, source_target_pairs={{0,1},{1,0},{2,3},{3,2},{4,5},{5,4},{6,7},{7,6},{8,9},{9,8},{10,11... | collective-permute-start | bytes 4718600 | tf_op jit(solution)/shard_map/ppermute | solution.py:34
  9.4 23.1 %collective-permute-start.1 = (bf16[512,1024]{1,0:T(8,128)(2,1)S(1)}, bf16[512,1024]{1,0:T(8,128)(2,1)S(1)}, u32[]{:S(2)}, u32[]{:S(2)}) collective-permute-start(bf16[512,1024]{1,0:T(8,128)(2,1)S(1)} %get-tuple-element.45), channel_id=1, source_target_pairs={{0,1},{1,0},{2,3},{3,2},{4,5},{5,4},{6,7},{7,6},{8,9},{9,8},{10,11... | collective-permute-start | bytes 3145736 | tf_op jit(solution)/shard_map/ppermute | solution.py:34
  9.5 15.4 %collective-permute-start.3 = (bf16[256,512]{1,0:T(8,128)(2,1)S(1)}, bf16[256,512]{1,0:T(8,128)(2,1)S(1)}, u32[]{:S(2)}, u32[]{:S(2)}) collective-permute-start(bf16[256,512]{1,0:T(8,128)(2,1)S(1)} %shard_map.85.after), channel_id=1, source_target_pairs={{0,32},{1,33},{2,34},{3,35},{4,36},{5,37},{6,38},{7,39},{8,40},{9,... | collective-permute-start | bytes 786440 | tf_op jit(solution)/shard_map/ppermute | solution.py:58
  10.7 15.2 %collective-permute-start.4 = (bf16[256,512]{1,0:T(8,128)(2,1)S(1)}, bf16[256,512]{1,0:T(8,128)(2,1)S(1)}, u32[]{:S(2)}, u32[]{:S(2)}) collective-permute-start(bf16[256,512]{1,0:T(8,128)(2,1)S(1)} %shard_map.85.after), channel_id=1, source_target_pairs={{0,48},{1,49},{2,50},{3,51},{4,52},{5,53},{6,54},{7,55},{8,56},{9,... | collective-permute-start | bytes 786440 | tf_op jit(solution)/shard_map/ppermute | solution.py:58
  25.9 28.0 %collective-permute-start.5 = (bf16[2,256,512]{2,1,0:T(8,128)(2,1)S(1)}, bf16[2,256,512]{2,1,0:T(8,128)(2,1)S(1)}, u32[]{:S(2)}, u32[]{:S(2)}) collective-permute-start(bf16[2,256,512]{2,1,0:T(8,128)(2,1)S(1)} %shard_map.88.refs_3_), channel_id=1, source_target_pairs={{0,2},{1,3},{2,4},{3,5},{4,6},{5,7},{6,8},{7,9},{8,10},{9,11},{10,... | collective-permute-start | bytes 1572872 | tf_op jit(solution)/shard_map/ppermute | solution.py:34
  27.9 26.1 %collective-permute-start.6 = (bf16[2,256,512]{2,1,0:T(8,128)(2,1)S(1)}, bf16[2,256,512]{2,1,0:T(8,128)(2,1)S(1)}, u32[]{:S(2)}, u32[]{:S(2)}) collective-permute-start(bf16[2,256,512]{2,1,0:T(8,128)(2,1)S(1)} %shard_map.88.refs_3_), channel_id=1, source_target_pairs={{0,14},{1,15},{2,0},{3,1},{4,2},{5,3},{6,4},{7,5},{8,6},{9,7},{10,... | collective-permute-start | bytes 1572872 | tf_op jit(solution)/shard_map/ppermute | solution.py:34
  31.9 22.1 %collective-permute-start.8 = (bf16[2,512,256]{2,1,0:T(8,128)(2,1)S(1)}, bf16[2,512,256]{2,1,0:T(8,128)(2,1)S(1)}, u32[]{:S(2)}, u32[]{:S(2)}) collective-permute-start(bf16[2,512,256]{2,1,0:T(8,128)(2,1)S(1)} %get-tuple-element.48.refs_2_.refs_3_), channel_id=1, source_target_pairs={{0,16},{1,17},{2,18},{3,19},{4,20},{5,21},{6,22},{7,23},{8,24},{9,... | collective-permute-start | bytes 1572872 | tf_op jit(solution)/shard_map/ppermute | solution.py:34
  32.5 21.4 %collective-permute-start.7 = (bf16[1,512,256]{2,1,0:T(8,128)(2,1)S(1)}, bf16[1,512,256]{2,1,0:T(8,128)(2,1)S(1)}, u32[]{:S(2)}, u32[]{:S(2)}) collective-permute-start(bf16[1,512,256]{2,1,0:T(8,128)(2,1)S(1)} %get-tuple-element.50), channel_id=1, source_target_pairs={{0,16},{1,17},{2,18},{3,19},{4,20},{5,21},{6,22},{7,23},{8,24},{9,... | collective-permute-start | bytes 786440 | tf_op jit(solution)/shard_map/ppermute | solution.py:34
  38.9 35.3 %collective-permute-start.13 = (bf16[2,512,256]{2,1,0:T(8,128)(2,1)S(1)}, bf16[2,512,256]{2,1,0:T(8,128)(2,1)S(1)}, u32[]{:S(2)}, u32[]{:S(2)}) collective-permute-start(bf16[2,512,256]{2,1,0:T(8,128)(2,1)S(1)} %get-tuple-element.60), channel_id=1, source_target_pairs={{0,16},{1,17},{2,18},{3,19},{4,20},{5,21},{6,22},{7,23},{8,24},{9,... | collective-permute-start | bytes 1572872 | tf_op jit(solution)/shard_map/ppermute | solution.py:34
  54.0 20.7 %collective-permute-start.10 = (bf16[2,256,512]{2,1,0:T(8,128)(2,1)S(1)}, bf16[2,256,512]{2,1,0:T(8,128)(2,1)S(1)}, u32[]{:S(2)}, u32[]{:S(2)}) collective-permute-start(bf16[2,256,512]{2,1,0:T(8,128)(2,1)S(1)} %get-tuple-element.55.refs_7_.refs_5_), channel_id=1, source_target_pairs={{0,14},{1,15},{2,0},{3,1},{4,2},{5,3},{6,4},{7,5},{8,6},{9,7},{10,... | collective-permute-start | bytes 1572872 | tf_op jit(solution)/shard_map/ppermute | solution.py:34
  56.0 21.7 %collective-permute-start.9 = (bf16[2,256,512]{2,1,0:T(8,128)(2,1)S(1)}, bf16[2,256,512]{2,1,0:T(8,128)(2,1)S(1)}, u32[]{:S(2)}, u32[]{:S(2)}) collective-permute-start(bf16[2,256,512]{2,1,0:T(8,128)(2,1)S(1)} %get-tuple-element.54.refs_6_.refs_4_), channel_id=1, source_target_pairs={{0,2},{1,3},{2,4},{3,5},{4,6},{5,7},{6,8},{7,9},{8,10},{9,11},{10,... | collective-permute-start | bytes 1572872 | tf_op jit(solution)/shard_map/ppermute | solution.py:34
  56.1 14.6 %collective-permute-start.11 = (bf16[256,256]{1,0:T(8,128)(2,1)S(1)}, bf16[256,256]{1,0:T(8,128)(2,1)S(1)}, u32[]{:S(2)}, u32[]{:S(2)}) collective-permute-start(bf16[256,256]{1,0:T(8,128)(2,1)S(1)} %get-tuple-element.52.refs_2_), channel_id=1, source_target_pairs={{0,2},{1,3},{2,4},{3,5},{4,6},{5,7},{6,8},{7,9},{8,10},{9,11},{10,... | collective-permute-start | bytes 393224 | tf_op jit(solution)/shard_map/ppermute | solution.py:34
  56.1 14.5 %collective-permute-start.12 = (bf16[256,256]{1,0:T(8,128)(2,1)S(1)}, bf16[256,256]{1,0:T(8,128)(2,1)S(1)}, u32[]{:S(2)}, u32[]{:S(2)}) collective-permute-start(bf16[256,256]{1,0:T(8,128)(2,1)S(1)} %get-tuple-element.53.refs_3_), channel_id=1, source_target_pairs={{0,14},{1,15},{2,0},{3,1},{4,2},{5,3},{6,4},{7,5},{8,6},{9,7},{10,... | collective-permute-start | bytes 393224 | tf_op jit(solution)/shard_map/ppermute | solution.py:34
  70.8 10.5 %collective-permute-start.16 = (bf16[512,256]{1,0:T(8,128)(2,1)S(1)}, bf16[512,256]{1,0:T(8,128)(2,1)S(1)}, u32[]{:S(2)}, u32[]{:S(2)}) collective-permute-start(bf16[512,256]{1,0:T(8,128)(2,1)S(1)} %get-tuple-element.58.refs_2_), channel_id=1, source_target_pairs={{0,2},{1,3},{2,4},{3,5},{4,6},{5,7},{6,8},{7,9},{8,10},{9,11},{10,... | collective-permute-start | bytes 786440 | tf_op jit(solution)/shard_map/ppermute | solution.py:34
  70.9 10.4 %collective-permute-start.17 = (bf16[512,256]{1,0:T(8,128)(2,1)S(1)}, bf16[512,256]{1,0:T(8,128)(2,1)S(1)}, u32[]{:S(2)}, u32[]{:S(2)}) collective-permute-start(bf16[512,256]{1,0:T(8,128)(2,1)S(1)} %get-tuple-element.59.refs_3_), channel_id=1, source_target_pairs={{0,14},{1,15},{2,0},{3,1},{4,2},{5,3},{6,4},{7,5},{8,6},{9,7},{10,... | collective-permute-start | bytes 786440 | tf_op jit(solution)/shard_map/ppermute | solution.py:34
  74.1 9.5 %collective-permute-start.23 = (bf16[1,512,256]{2,1,0:T(8,128)(2,1)S(1)}, bf16[1,512,256]{2,1,0:T(8,128)(2,1)S(1)}, u32[]{:S(2)}, u32[]{:S(2)}) collective-permute-start(bf16[1,512,256]{2,1,0:T(8,128)(2,1)S(1)} %get-tuple-element.51.refs_2_), channel_id=1, source_target_pairs={{0,16},{1,17},{2,18},{3,19},{4,20},{5,21},{6,22},{7,23},{8,24},{9,... | collective-permute-start | bytes 786440 | tf_op jit(solution)/shard_map/ppermute | solution.py:34
  74.7 12.9 %collective-permute-start.18 = (bf16[2,512,256]{2,1,0:T(8,128)(2,1)S(1)}, bf16[2,512,256]{2,1,0:T(8,128)(2,1)S(1)}, u32[]{:S(2)}, u32[]{:S(2)}) collective-permute-start(bf16[2,512,256]{2,1,0:T(8,128)(2,1)S(1)} %get-tuple-element.67), channel_id=1, source_target_pairs={{0,16},{1,17},{2,18},{3,19},{4,20},{5,21},{6,22},{7,23},{8,24},{9,... | collective-permute-start | bytes 1572872 | tf_op jit(solution)/shard_map/ppermute | solution.py:34
  77.7 24.5 %collective-permute-start.14 = (bf16[2,256,512]{2,1,0:T(8,128)(2,1)S(1)}, bf16[2,256,512]{2,1,0:T(8,128)(2,1)S(1)}, u32[]{:S(2)}, u32[]{:S(2)}) collective-permute-start(bf16[2,256,512]{2,1,0:T(8,128)(2,1)S(1)} %get-tuple-element.61.refs_6_), channel_id=1, source_target_pairs={{0,2},{1,3},{2,4},{3,5},{4,6},{5,7},{6,8},{7,9},{8,10},{9,11},{10,... | collective-permute-start | bytes 1572872 | tf_op jit(solution)/shard_map/ppermute | solution.py:34
  81.4 20.9 %collective-permute-start.15 = (bf16[2,256,512]{2,1,0:T(8,128)(2,1)S(1)}, bf16[2,256,512]{2,1,0:T(8,128)(2,1)S(1)}, u32[]{:S(2)}, u32[]{:S(2)}) collective-permute-start(bf16[2,256,512]{2,1,0:T(8,128)(2,1)S(1)} %get-tuple-element.62.refs_7_), channel_id=1, source_target_pairs={{0,14},{1,15},{2,0},{3,1},{4,2},{5,3},{6,4},{7,5},{8,6},{9,7},{10,... | collective-permute-start | bytes 1572872 | tf_op jit(solution)/shard_map/ppermute | solution.py:34
  81.6 12.6 %collective-permute-start.21 = (bf16[512,256]{1,0:T(8,128)(2,1)S(1)}, bf16[512,256]{1,0:T(8,128)(2,1)S(1)}, u32[]{:S(2)}, u32[]{:S(2)}) collective-permute-start(bf16[512,256]{1,0:T(8,128)(2,1)S(1)} %get-tuple-element.65.refs_2_), channel_id=1, source_target_pairs={{0,2},{1,3},{2,4},{3,5},{4,6},{5,7},{6,8},{7,9},{8,10},{9,11},{10,... | collective-permute-start | bytes 786440 | tf_op jit(solution)/shard_map/ppermute | solution.py:34
  83.7 15.0 %collective-permute-start.22 = (bf16[512,256]{1,0:T(8,128)(2,1)S(1)}, bf16[512,256]{1,0:T(8,128)(2,1)S(1)}, u32[]{:S(2)}, u32[]{:S(2)}) collective-permute-start(bf16[512,256]{1,0:T(8,128)(2,1)S(1)} %get-tuple-element.66.refs_3_), channel_id=1, source_target_pairs={{0,14},{1,15},{2,0},{3,1},{4,2},{5,3},{6,4},{7,5},{8,6},{9,7},{10,... | collective-permute-start | bytes 786440 | tf_op jit(solution)/shard_map/ppermute | solution.py:34
  98.9 10.1 %collective-permute-start.26 = (bf16[512,256]{1,0:T(8,128)(2,1)S(1)}, bf16[512,256]{1,0:T(8,128)(2,1)S(1)}, u32[]{:S(2)}, u32[]{:S(2)}) collective-permute-start(bf16[512,256]{1,0:T(8,128)(2,1)S(1)} %get-tuple-element.72.refs_8_), channel_id=1, source_target_pairs={{0,2},{1,3},{2,4},{3,5},{4,6},{5,7},{6,8},{7,9},{8,10},{9,11},{10,... | collective-permute-start | bytes 786440 | tf_op jit(solution)/shard_map/ppermute | solution.py:34
  99.0 10.0 %collective-permute-start.27 = (bf16[512,256]{1,0:T(8,128)(2,1)S(1)}, bf16[512,256]{1,0:T(8,128)(2,1)S(1)}, u32[]{:S(2)}, u32[]{:S(2)}) collective-permute-start(bf16[512,256]{1,0:T(8,128)(2,1)S(1)} %get-tuple-element.80), channel_id=1, source_target_pairs={{0,14},{1,15},{2,0},{3,1},{4,2},{5,3},{6,4},{7,5},{8,6},{9,7},{10,... | collective-permute-start | bytes 786440 | tf_op jit(solution)/shard_map/ppermute | solution.py:34
  102.3 7.7 %collective-permute-start.19 = (bf16[256,512]{1,0:T(8,128)(2,1)S(1)}, bf16[256,512]{1,0:T(8,128)(2,1)S(1)}, u32[]{:S(2)}, u32[]{:S(2)}) collective-permute-start(bf16[256,512]{1,0:T(8,128)(2,1)S(1)} %get-tuple-element.68), channel_id=1, source_target_pairs={{0,2},{1,3},{2,4},{3,5},{4,6},{5,7},{6,8},{7,9},{8,10},{9,11},{10,... | collective-permute-start | bytes 786440 | tf_op jit(solution)/shard_map/ppermute | solution.py:34
  102.4 7.6 %collective-permute-start.20 = (bf16[256,512]{1,0:T(8,128)(2,1)S(1)}, bf16[256,512]{1,0:T(8,128)(2,1)S(1)}, u32[]{:S(2)}, u32[]{:S(2)}) collective-permute-start(bf16[256,512]{1,0:T(8,128)(2,1)S(1)} %get-tuple-element.69), channel_id=1, source_target_pairs={{0,14},{1,15},{2,0},{3,1},{4,2},{5,3},{6,4},{7,5},{8,6},{9,7},{10,... | collective-permute-start | bytes 786440 | tf_op jit(solution)/shard_map/ppermute | solution.py:34
  109.1 6.4 %collective-permute-start.28 = (bf16[512,256]{1,0:T(8,128)(2,1)S(1)}, bf16[512,256]{1,0:T(8,128)(2,1)S(1)}, u32[]{:S(2)}, u32[]{:S(2)}) collective-permute-start(bf16[512,256]{1,0:T(8,128)(2,1)S(1)} %shard_map.100), channel_id=1, source_target_pairs={{0,224},{1,225},{2,226},{3,227},{4,228},{5,229},{6,230},{7,231},{8... | collective-permute-start | bytes 786440 | tf_op jit(solution)/shard_map/ppermute | solution.py:58
  109.9 5.7 %copy-start.1 = (bf16[1,256,512]{2,1,0:T(8,128)(2,1)S(1)}, bf16[1,256,512]{2,1,0:T(8,128)(2,1)}, u32[]{:S(2)}) copy-start(bf16[1,256,512]{2,1,0:T(8,128)(2,1)} %weight.3) | copy-start | bytes 786436
  109.9 5.7 %copy-start.3 = (f32[1,256,512]{2,1,0:T(8,128)S(1)}, f32[1,256,512]{2,1,0:T(8,128)}, u32[]{:S(2)}) copy-start(f32[1,256,512]{2,1,0:T(8,128)} %grad_weight_in.1) | copy-start | bytes 1572868
  109.9 5.7 %copy-start.5 = (bf16[1,256]{1,0:T(2,128)(2,1)S(1)}, bf16[1,256]{1,0:T(2,128)(2,1)}, u32[]{:S(2)}) copy-start(bf16[1,256]{1,0:T(2,128)(2,1)} %gain.3) | copy-start | bytes 1540
  109.9 5.7 %copy-start.6 = (f32[1,256]{1,0:T(1,128)S(1)}, f32[1,256]{1,0:T(1,128)}, u32[]{:S(2)}) copy-start(f32[1,256]{1,0:T(1,128)} %grad_gain_in.1) | copy-start | bytes 3076
  112.3 4.4 %collective-permute-start.24 = (bf16[256,512]{1,0:T(8,128)(2,1)S(1)}, bf16[256,512]{1,0:T(8,128)(2,1)S(1)}, u32[]{:S(2)}, u32[]{:S(2)}) collective-permute-start(bf16[256,512]{1,0:T(8,128)(2,1)S(1)} %get-tuple-element.76), channel_id=1, source_target_pairs={{0,1},{1,0},{2,3},{3,2},{4,5},{5,4},{6,7},{7,6},{8,9},{9,8},{10,11... | collective-permute-start | bytes 786440 | tf_op jit(solution)/shard_map/ppermute | solution.py:34
  112.4 4.3 %collective-permute-start.25 = (bf16[256,512]{1,0:T(8,128)(2,1)S(1)}, bf16[256,512]{1,0:T(8,128)(2,1)S(1)}, u32[]{:S(2)}, u32[]{:S(2)}) collective-permute-start(bf16[256,512]{1,0:T(8,128)(2,1)S(1)} %get-tuple-element.77), channel_id=1, source_target_pairs={{0,1},{1,0},{2,3},{3,2},{4,5},{5,4},{6,7},{7,6},{8,9},{9,8},{10,11... | collective-permute-start | bytes 786440 | tf_op jit(solution)/shard_map/ppermute | solution.py:34

commit v6 on v5

--- a/solution.py
+++ b/solution.py
@@ -365,21 +365,21 @@
     mine = {off: (keeps[i], arrived[places[i][0]]) for i, off in enumerate(OFFSETS)}
     place = {off: places[i][1] for i, off in enumerate(OFFSETS)}
 
-    layer = pair(*layer, [sends_1[-1]])
-    up, down = begin(mine[4], (place[4],), [sends_2[-1]])
+    layer = pair(*layer, [arrived[0]])
+    up, down = begin(mine[4], (place[4],), [])
     weights = {0: [layer]}
     layer_up = layer_down = layer
     for step in (1, 2, 3):
         layer_up, layer_down = along_z(layer_up, 1), along_z(layer_down, -1)
-        if step < 3:
-            layer_up, layer_down = tie([layer_up, layer_down], [up, down, mine[4 - step][1]])
-        else:
-            far_up, far_down = split(layer_up, layer_down, [up, down, mine[1][1]])
-        weights[-step], weights[step] = [layer_up], [layer_down]
         off = 4 - step
         up, down = along_z(up, 1), along_z(down, -1)
-        ready = [layer_up, layer_down] if step < 3 else [mine[0][1]]
+        ready = [mine[0][1]] if step == 3 else []
         up, down = carry((*mine[off], up), (*mine[-off], down), (place[off], place[-off]), ready)
+        if step < 3:
+            layer_up, layer_down = tie([layer_up, layer_down], [up, down])
+        else:
+            far_up, far_down = split(layer_up, layer_down, [up, down])
+        weights[-step], weights[step] = [layer_up], [layer_down]
     weights[4] = [along_z(far_up, 1), along_z(far_down, -1)]
 
     near = {off: weights[off] for off in (0, -1, 1, -2, 2)}

time: 118 us -> 128 us (1.085)
  the two profiles are of different devices: /device:TPU:4 before, /device:TPU:83 now
where the time goes in v6:
time: 128 us
  waiting for transfers between devices  61.7 us (48%)
  starting transfers between devices  42.8 us (33%)
  Pallas kernels  19.7 us (15%)
  local copies, waits for them, and re-layouts  2.79 us (2%)
    ppermute x26, waiting for transfers between devices, move(): return lax.ppermute(value, ('x', 'z', 'core'), pairs)  45 us
    ppermute x26, starting transfers between devices, move(): return lax.ppermute(value, ('x', 'z', 'core'), pairs)  30.9 us
    ppermute x3, waiting for transfers between devices, along_blk(): return lax.ppermute(value, ('blk', 'x', 'z', 'core'), pairs)  16.7 us
    ppermute x3, starting transfers between devices, along_blk(): return lax.ppermute(value, ('blk', 'x', 'z', 'core'), pairs)  11.9 us
    pallas_call x2, Pallas kernels, gradient(): pl.pallas_call(functools.partial(gradient_kernel, base, groups, width), i...  5.82 us
    pallas_call x2, Pallas kernels, project(): pl.pallas_call(functools.partial(project_kernel, tuple(weights), [len(g)...  5.78 us
    pallas_call x1, Pallas kernels, prepare(): pl.pallas_call(functools.partial(prepare_kernel, width, steps), in_specs=...  5.16 us
    unnamed x14, local copies, waits for them, and re-layouts  2.69 us
  transfers between devices with their start and end apart: 29, of which 13 were waited for; matrix products, arithmetic and copies ran while one was open for 0% of the time, Pallas kernels for 11%

profile of v6, /device:TPU:83, one launch (start us, length us, event | category | flops | bytes accessed | tf_op | source)
XLA Modules:
  0.0 128.1 jit_solution(3918547740532977624)
XLA Ops:
  0.7 0.9 copy-done
  1.7 0.7 copy-done.4
  2.4 0.1 shard_map.85.after
  2.5 0.1 stack.67.table
  2.6 1.0 copy-done.2
  3.6 5.2 %shard_map.86 = (bf16[512,8192]{1,0:T(8,128)(2,1)S(1)}, f32[512,1]{1,0:T(8,128)S(1)}, bf16[512,512]{1,0:T(8,128)(2,1)S(1)}, bf16[512,2048]{1,0:T(8,128)(2,1)S(1)...) custom-call(s32[16]{0:T(128)S(1)} %stack.67.table, bf16[512,8192]{1,0:T(8,128)(2,1)} %hidden.1, ...), custom_call_target="tpu_custom_call" | custom-call | bytes 16777216 | tf_op jit(solution)/shard_map/pallas_call | solution.py:122
  8.8 0.8 collective-permute-start
  9.6 0.1 collective-permute-start.2
  9.7 0.4 collective-permute-start.1
  10.1 1.0 collective-permute-start.3
  11.1 1.9 %collective-permute-start.4 = (bf16[256,512]{1,0:T(8,128)(2,1)S(1)}, bf16[256,512]{1,0:T(8,128)(2,1)S(1)}, u32[]{:S(2)}, u32[]{:S(2)}) collective-permute-start(bf16[256,512]{1,0:T(8,128)(2,1)S(1)} %shard_map.85.after), channel_id=1, source_target_pairs={{0,48},{1,49},{2,50},{3,51},{4,52},{5,53},{6,54},{7,55},{8,56},{9,... | collective-permute-start | bytes 786440 | tf_op jit(solution)/shard_map/ppermute | solution.py:58
  12.9 0.4 collective-permute-done.refs_0_.refs_1_.refs_2_
  13.4 2.4 %shard_map.87 = (bf16[1,512,256]{2,1,0:T(8,128)(2,1)S(1)}, bf16[2,512,256]{2,1,0:T(8,128)(2,1)S(1)}, bf16[512,256]{1,0:T(8,128)(2,1)S(1)}, bf16[512,256]{1,0:T(8,128)(2,1)S(1)}, bf16[512,256]{1,0:T(8,128)(2,1)S(1)}) custom-call(s32[16]{0:T(128)S(1)} %stack.67.table, bf16[512,8192]{1,0:T(8,128)(2,1)S(1)} %get-tuple-element.43.hidden, ...), custom_call_target="tpu_custom_call" | custom-call | bytes 512 | tf_op jit(solution)/shard_map/pallas_call | solution.py:162
  15.7 1.9 %collective-permute-start.5 = (bf16[1,512,256]{2,1,0:T(8,128)(2,1)S(1)}, bf16[1,512,256]{2,1,0:T(8,128)(2,1)S(1)}, u32[]{:S(2)}, u32[]{:S(2)}) collective-permute-start(bf16[1,512,256]{2,1,0:T(8,128)(2,1)S(1)} %get-tuple-element.48), channel_id=1, source_target_pairs={{0,16},{1,17},{2,18},{3,19},{4,20},{5,21},{6,22},{7,23},{8,24},{9,... | collective-permute-start | bytes 786440 | tf_op jit(solution)/shard_map/ppermute | solution.py:34
  17.7 1.4 %collective-permute-done.3.refs_0_ = bf16[256,512]{1,0:T(8,128)(2,1)S(1)} collective-permute-done((bf16[256,512]{1,0:T(8,128)(2,1)S(1)}, bf16[256,512]{1,0:T(8,128)(2,1)S(1)}, u32[]{:S(2)}, u32[]{:S(2)}) %collective-permute-start.3) | collective-permute-done | bytes 262176 | tf_op jit(solution)/shard_map/ppermute | solution.py:58
  19.0 3.0 %collective-permute-start.8 = (bf16[2,512,256]{2,1,0:T(8,128)(2,1)S(1)}, bf16[2,512,256]{2,1,0:T(8,128)(2,1)S(1)}, u32[]{:S(2)}, u32[]{:S(2)}) collective-permute-start(bf16[2,512,256]{2,1,0:T(8,128)(2,1)S(1)} %get-tuple-element.50.refs_3_), channel_id=1, source_target_pairs={{0,16},{1,17},{2,18},{3,19},{4,20},{5,21},{6,22},{7,23},{8,24},{9,... | collective-permute-start | bytes 1572872 | tf_op jit(solution)/shard_map/ppermute | solution.py:34
  22.1 15.3 %collective-permute-done.4.refs_1_ = bf16[256,512]{1,0:T(8,128)(2,1)S(1)} collective-permute-done((bf16[256,512]{1,0:T(8,128)(2,1)S(1)}, bf16[256,512]{1,0:T(8,128)(2,1)S(1)}, u32[]{:S(2)}, u32[]{:S(2)}) %collective-permute-start.4) | collective-permute-done | bytes 262176 | tf_op jit(solution)/shard_map/ppermute | solution.py:58
  37.5 1.7 %collective-permute-start.6 = (bf16[2,256,512]{2,1,0:T(8,128)(2,1)S(1)}, bf16[2,256,512]{2,1,0:T(8,128)(2,1)S(1)}, u32[]{:S(2)}, u32[]{:S(2)}) collective-permute-start(bf16[2,256,512]{2,1,0:T(8,128)(2,1)S(1)} %shard_map.88.refs_3_), channel_id=1, source_target_pairs={{0,2},{1,3},{2,4},{3,5},{4,6},{5,7},{6,8},{7,9},{8,10},{9,11},{10,... | collective-permute-start | bytes 1572872 | tf_op jit(solution)/shard_map/ppermute | solution.py:34
  39.2 0.3 collective-permute-start.10
  39.5 3.5 %shard_map.92 = (bf16[2,512,256]{2,1,0:T(8,128)(2,1)S(1)}, bf16[2,512,256]{2,1,0:T(8,128)(2,1)S(1)}, bf16[1,512,256]{2,1,0:T(8,128)(2,1)S(1)}, bf16[512,256]{1,0...) custom-call(s32[16]{0:T(128)S(1)} %stack.67.table, ...), custom_call_target="tpu_custom_call" | custom-call | bytes 512 | tf_op jit(solution)/shard_map/pallas_call | solution.py:162
  43.1 12.6 %collective-permute-done.10.refs_5_ = bf16[256,256]{1,0:T(8,128)(2,1)S(1)} collective-permute-done((bf16[256,256]{1,0:T(8,128)(2,1)S(1)}, bf16[256,256]{1,0:T(8,128)(2,1)S(1)}, u32[]{:S(2)}, u32[]{:S(2)}) %collective-permute-start.10) | collective-permute-done | bytes 131104 | tf_op jit(solution)/shard_map/ppermute | solution.py:34
  55.6 2.4 %collective-permute-start.9 = (bf16[256,256]{1,0:T(8,128)(2,1)S(1)}, bf16[256,256]{1,0:T(8,128)(2,1)S(1)}, u32[]{:S(2)}, u32[]{:S(2)}) collective-permute-start(bf16[256,256]{1,0:T(8,128)(2,1)S(1)} %get-tuple-element.52), channel_id=1, source_target_pairs={{0,2},{1,3},{2,4},{3,5},{4,6},{5,7},{6,8},{7,9},{8,10},{9,11},{10,... | collective-permute-start | bytes 393224 | tf_op jit(solution)/shard_map/ppermute | solution.py:34
  58.0 1.9 %collective-permute-done.9.refs_2_ = bf16[256,256]{1,0:T(8,128)(2,1)S(1)} collective-permute-done((bf16[256,256]{1,0:T(8,128)(2,1)S(1)}, bf16[256,256]{1,0:T(8,128)(2,1)S(1)}, u32[]{:S(2)}, u32[]{:S(2)}) %collective-permute-start.9) | collective-permute-done | bytes 131104 | tf_op jit(solution)/shard_map/ppermute | solution.py:34
  60.0 0.2 shard_map.90
  60.1 1.9 %collective-permute-start.11 = (bf16[2,256,512]{2,1,0:T(8,128)(2,1)S(1)}, bf16[2,256,512]{2,1,0:T(8,128)(2,1)S(1)}, u32[]{:S(2)}, u32[]{:S(2)}) collective-permute-start(bf16[2,256,512]{2,1,0:T(8,128)(2,1)S(1)} %get-tuple-element.57.refs_4_), channel_id=1, source_target_pairs={{0,2},{1,3},{2,4},{3,5},{4,6},{5,7},{6,8},{7,9},{8,10},{9,11},{10,... | collective-permute-start | bytes 1572872 | tf_op jit(solution)/shard_map/ppermute | solution.py:34
  62.1 1.5 %collective-permute-start.14 = (bf16[512,256]{1,0:T(8,128)(2,1)S(1)}, bf16[512,256]{1,0:T(8,128)(2,1)S(1)}, u32[]{:S(2)}, u32[]{:S(2)}) collective-permute-start(bf16[512,256]{1,0:T(8,128)(2,1)S(1)} %get-tuple-element.55.refs_2_), channel_id=1, source_target_pairs={{0,2},{1,3},{2,4},{3,5},{4,6},{5,7},{6,8},{7,9},{8,10},{9,11},{10,... | collective-permute-start | bytes 786440 | tf_op jit(solution)/shard_map/ppermute | solution.py:34
  63.6 12.3 %collective-permute-done.14.refs_2_ = bf16[512,256]{1,0:T(8,128)(2,1)S(1)} collective-permute-done((bf16[512,256]{1,0:T(8,128)(2,1)S(1)}, bf16[512,256]{1,0:T(8,128)(2,1)S(1)}, u32[]{:S(2)}, u32[]{:S(2)}) %collective-permute-start.14) | collective-permute-done | bytes 262176 | tf_op jit(solution)/shard_map/ppermute | solution.py:34
  75.9 1.3 collective-permute-done.15.refs_5_
  77.2 0.2 shard_map.93
  77.4 3.2 %collective-permute-start.16 = (bf16[2,256,512]{2,1,0:T(8,128)(2,1)S(1)}, bf16[2,256,512]{2,1,0:T(8,128)(2,1)S(1)}, u32[]{:S(2)}, u32[]{:S(2)}) collective-permute-start(bf16[2,256,512]{2,1,0:T(8,128)(2,1)S(1)} %get-tuple-element.64.refs_6_), channel_id=1, source_target_pairs={{0,2},{1,3},{2,4},{3,5},{4,6},{5,7},{6,8},{7,9},{8,10},{9,11},{10,... | collective-permute-start | bytes 1572872 | tf_op jit(solution)/shard_map/ppermute | solution.py:34
  80.6 1.5 %collective-permute-start.19 = (bf16[512,256]{1,0:T(8,128)(2,1)S(1)}, bf16[512,256]{1,0:T(8,128)(2,1)S(1)}, u32[]{:S(2)}, u32[]{:S(2)}) collective-permute-start(bf16[512,256]{1,0:T(8,128)(2,1)S(1)} %get-tuple-element.62.refs_2_), channel_id=1, source_target_pairs={{0,2},{1,3},{2,4},{3,5},{4,6},{5,7},{6,8},{7,9},{8,10},{9,11},{10,... | collective-permute-start | bytes 786440 | tf_op jit(solution)/shard_map/ppermute | solution.py:34
  82.1 0.6 collective-permute-done.21.refs_6_.refs_1_
  82.6 0.9 collective-permute-start.20
  83.6 9.5 %collective-permute-done.19.refs_2_ = bf16[512,256]{1,0:T(8,128)(2,1)S(1)} collective-permute-done((bf16[512,256]{1,0:T(8,128)(2,1)S(1)}, bf16[512,256]{1,0:T(8,128)(2,1)S(1)}, u32[]{:S(2)}, u32[]{:S(2)}) %collective-permute-start.19) | collective-permute-done | bytes 262176 | tf_op jit(solution)/shard_map/ppermute | solution.py:34
  93.1 1.9 %collective-permute-done.20.refs_5_ = bf16[512,256]{1,0:T(8,128)(2,1)S(1)} collective-permute-done((bf16[512,256]{1,0:T(8,128)(2,1)S(1)}, bf16[512,256]{1,0:T(8,128)(2,1)S(1)}, u32[]{:S(2)}, u32[]{:S(2)}) %collective-permute-start.20) | collective-permute-done | bytes 262176 | tf_op jit(solution)/shard_map/ppermute | solution.py:34
  95.0 0.2 shard_map.95
  95.2 1.7 %collective-permute-start.26 = (bf16[512,256]{1,0:T(8,128)(2,1)S(1)}, bf16[512,256]{1,0:T(8,128)(2,1)S(1)}, u32[]{:S(2)}, u32[]{:S(2)}) collective-permute-start(bf16[512,256]{1,0:T(8,128)(2,1)S(1)} %get-tuple-element.70.refs_2_.refs_8_), channel_id=1, source_target_pairs={{0,2},{1,3},{2,4},{3,5},{4,6},{5,7},{6,8},{7,9},{8,10},{9,11},{10,... | collective-permute-start | bytes 786440 | tf_op jit(solution)/shard_map/ppermute | solution.py:34
  97.0 1.5 %collective-permute-start.22 = (bf16[256,512]{1,0:T(8,128)(2,1)S(1)}, bf16[256,512]{1,0:T(8,128)(2,1)S(1)}, u32[]{:S(2)}, u32[]{:S(2)}) collective-permute-start(bf16[256,512]{1,0:T(8,128)(2,1)S(1)} %get-tuple-element.72), channel_id=1, source_target_pairs={{0,2},{1,3},{2,4},{3,5},{4,6},{5,7},{6,8},{7,9},{8,10},{9,11},{10,... | collective-permute-start | bytes 786440 | tf_op jit(solution)/shard_map/ppermute | solution.py:34
  98.6 2.2 %collective-permute-done.26.refs_2_ = bf16[512,256]{1,0:T(8,128)(2,1)S(1)} collective-permute-done((bf16[512,256]{1,0:T(8,128)(2,1)S(1)}, bf16[512,256]{1,0:T(8,128)(2,1)S(1)}, u32[]{:S(2)}, u32[]{:S(2)}) %collective-permute-start.26) | collective-permute-done | bytes 262176 | tf_op jit(solution)/shard_map/ppermute | solution.py:34
  100.8 1.9 %collective-permute-done.27.refs_3_ = bf16[512,256]{1,0:T(8,128)(2,1)S(1)} collective-permute-done((bf16[512,256]{1,0:T(8,128)(2,1)S(1)}, bf16[512,256]{1,0:T(8,128)(2,1)S(1)}, u32[]{:S(2)}, u32[]{:S(2)}) %collective-permute-start.27) | collective-permute-done | bytes 262176 | tf_op jit(solution)/shard_map/ppermute | solution.py:34
  102.7 0.1 shard_map.100
  102.8 9.1 %collective-permute-start.28 = (bf16[512,256]{1,0:T(8,128)(2,1)S(1)}, bf16[512,256]{1,0:T(8,128)(2,1)S(1)}, u32[]{:S(2)}, u32[]{:S(2)}) collective-permute-start(bf16[512,256]{1,0:T(8,128)(2,1)S(1)} %shard_map.100), channel_id=1, source_target_pairs={{0,224},{1,225},{2,226},{3,227},{4,228},{5,229},{6,230},{7,231},{8... | collective-permute-start | bytes 786440 | tf_op jit(solution)/shard_map/ppermute | solution.py:58
  111.9 3.4 %shard_map.97 = (f32[512,512]{1,0:T(8,128)S(1)}, f32[512,512]{1,0:T(8,128)S(1)}) custom-call(s32[16]{0:T(128)S(1)} %stack.67.table, bf16[512,8192]{1,0:T(8,128)(2,1)S(1)} %get-tuple-element.43.hidden, bf16[512,2048]{1,0:T(8,128)(2,1)S(1)} %collective-permute-done.refs_0_.refs_1_.refs_2_, bf16[512,1024]{1,0:T(8,128)(2,1)S(1)} %collective-permute-done.1.refs_1_, ...), custom_call_target="tpu_custom_call" | custom-call | flops 2684354560 | tf_op jit(solution)/shard_map/pallas_call | solution.py:207
  115.4 2.3 %shard_map.98 = (f32[512,512]{1,0:T(8,128)S(1)}, bf16[256,512]{1,0:T(8,128)(2,1)S(1)}, bf16[256,512]{1,0:T(8,128)(2,1)S(1)}) custom-call(s32[16]{0:T(128)S(1)} %stack.67.table, bf16[512,8192]{1,0:T(8,128)(2,1)S(1)} %get-tuple-element.43.hidden, bf16[512,2048]{1,0:T(8,128)(2,1)S(1)} %collective-permute-done.refs_0_.refs_1_.refs_2_, ...), custom_call_target="tpu_custom_call" | custom-call | flops 1610612736 | tf_op jit(solution)/shard_map/pallas_call | solution.py:207
  117.7 7.9 %collective-permute-start.24 = (bf16[256,512]{1,0:T(8,128)(2,1)S(1)}, bf16[256,512]{1,0:T(8,128)(2,1)S(1)}, u32[]{:S(2)}, u32[]{:S(2)}) collective-permute-start(bf16[256,512]{1,0:T(8,128)(2,1)S(1)} %get-tuple-element.77), channel_id=1, source_target_pairs={{0,1},{1,0},{2,3},{3,2},{4,5},{5,4},{6,7},{7,6},{8,9},{9,8},{10,11... | collective-permute-start | bytes 786440 | tf_op jit(solution)/shard_map/ppermute | solution.py:34
  125.7 1.1 shard_map.101
  126.8 0.3 collective-permute-done.25.refs_2_
  127.1 1.0 shard_map.99
  (42 shorter events, 0.4 us)
Async XLA Ops:
  0.7 1.0 copy-start
  1.7 0.7 copy-start.4
  2.6 1.0 copy-start.2
  8.8 4.5 %collective-permute-start = (bf16[512,2048]{1,0:T(8,128)(2,1)S(1)}, bf16[512,2048]{1,0:T(8,128)(2,1)S(1)}, u32[]{:S(2)}, u32[]{:S(2)}) collective-permute-start(bf16[512,2048]{1,0:T(8,128)(2,1)S(1)} %get-tuple-element.44), channel_id=1, source_target_pairs={{0,1},{1,0},{2,3},{3,2},{4,5},{5,4},{6,7},{7,6},{8,9},{9,8},{10,11... | collective-permute-start | bytes 6291464 | tf_op jit(solution)/shard_map/ppermute | solution.py:34
  9.6 29.9 %collective-permute-start.2 = (bf16[512,1536]{1,0:T(8,128)(2,1)S(1)}, bf16[512,1536]{1,0:T(8,128)(2,1)S(1)}, u32[]{:S(2)}, u32[]{:S(2)}) collective-permute-start(bf16[512,1536]{1,0:T(8,128)(2,1)S(1)} %get-tuple-element.46), channel_id=1, source_target_pairs={{0,1},{1,0},{2,3},{3,2},{4,5},{5,4},{6,7},{7,6},{8,9},{9,8},{10,11... | collective-permute-start | bytes 4718600 | tf_op jit(solution)/shard_map/ppermute | solution.py:34
  9.7 29.5 %collective-permute-start.1 = (bf16[512,1024]{1,0:T(8,128)(2,1)S(1)}, bf16[512,1024]{1,0:T(8,128)(2,1)S(1)}, u32[]{:S(2)}, u32[]{:S(2)}) collective-permute-start(bf16[512,1024]{1,0:T(8,128)(2,1)S(1)} %get-tuple-element.45), channel_id=1, source_target_pairs={{0,1},{1,0},{2,3},{3,2},{4,5},{5,4},{6,7},{7,6},{8,9},{9,8},{10,11... | collective-permute-start | bytes 3145736 | tf_op jit(solution)/shard_map/ppermute | solution.py:34
  10.1 9.0 %collective-permute-start.3 = (bf16[256,512]{1,0:T(8,128)(2,1)S(1)}, bf16[256,512]{1,0:T(8,128)(2,1)S(1)}, u32[]{:S(2)}, u32[]{:S(2)}) collective-permute-start(bf16[256,512]{1,0:T(8,128)(2,1)S(1)} %shard_map.85.after), channel_id=1, source_target_pairs={{0,32},{1,33},{2,34},{3,35},{4,36},{5,37},{6,38},{7,39},{8,40},{9,... | collective-permute-start | bytes 786440 | tf_op jit(solution)/shard_map/ppermute | solution.py:58
  11.1 26.3 %collective-permute-start.4 = (bf16[256,512]{1,0:T(8,128)(2,1)S(1)}, bf16[256,512]{1,0:T(8,128)(2,1)S(1)}, u32[]{:S(2)}, u32[]{:S(2)}) collective-permute-start(bf16[256,512]{1,0:T(8,128)(2,1)S(1)} %shard_map.85.after), channel_id=1, source_target_pairs={{0,48},{1,49},{2,50},{3,51},{4,52},{5,53},{6,54},{7,55},{8,56},{9,... | collective-permute-start | bytes 786440 | tf_op jit(solution)/shard_map/ppermute | solution.py:58
  15.7 21.7 %collective-permute-start.5 = (bf16[1,512,256]{2,1,0:T(8,128)(2,1)S(1)}, bf16[1,512,256]{2,1,0:T(8,128)(2,1)S(1)}, u32[]{:S(2)}, u32[]{:S(2)}) collective-permute-start(bf16[1,512,256]{2,1,0:T(8,128)(2,1)S(1)} %get-tuple-element.48), channel_id=1, source_target_pairs={{0,16},{1,17},{2,18},{3,19},{4,20},{5,21},{6,22},{7,23},{8,24},{9,... | collective-permute-start | bytes 786440 | tf_op jit(solution)/shard_map/ppermute | solution.py:34
  19.0 40.9 %collective-permute-start.8 = (bf16[2,512,256]{2,1,0:T(8,128)(2,1)S(1)}, bf16[2,512,256]{2,1,0:T(8,128)(2,1)S(1)}, u32[]{:S(2)}, u32[]{:S(2)}) collective-permute-start(bf16[2,512,256]{2,1,0:T(8,128)(2,1)S(1)} %get-tuple-element.50.refs_3_), channel_id=1, source_target_pairs={{0,16},{1,17},{2,18},{3,19},{4,20},{5,21},{6,22},{7,23},{8,24},{9,... | collective-permute-start | bytes 1572872 | tf_op jit(solution)/shard_map/ppermute | solution.py:34
  37.5 22.7 %collective-permute-start.6 = (bf16[2,256,512]{2,1,0:T(8,128)(2,1)S(1)}, bf16[2,256,512]{2,1,0:T(8,128)(2,1)S(1)}, u32[]{:S(2)}, u32[]{:S(2)}) collective-permute-start(bf16[2,256,512]{2,1,0:T(8,128)(2,1)S(1)} %shard_map.88.refs_3_), channel_id=1, source_target_pairs={{0,2},{1,3},{2,4},{3,5},{4,6},{5,7},{6,8},{7,9},{8,10},{9,11},{10,... | collective-permute-start | bytes 1572872 | tf_op jit(solution)/shard_map/ppermute | solution.py:34
  39.1 21.0 %collective-permute-start.7 = (bf16[2,256,512]{2,1,0:T(8,128)(2,1)S(1)}, bf16[2,256,512]{2,1,0:T(8,128)(2,1)S(1)}, u32[]{:S(2)}, u32[]{:S(2)}) collective-permute-start(bf16[2,256,512]{2,1,0:T(8,128)(2,1)S(1)} %shard_map.88.refs_3_), channel_id=1, source_target_pairs={{0,14},{1,15},{2,0},{3,1},{4,2},{5,3},{6,4},{7,5},{8,6},{9,7},{10,... | collective-permute-start | bytes 1572872 | tf_op jit(solution)/shard_map/ppermute | solution.py:34
  39.2 16.4 %collective-permute-start.10 = (bf16[256,256]{1,0:T(8,128)(2,1)S(1)}, bf16[256,256]{1,0:T(8,128)(2,1)S(1)}, u32[]{:S(2)}, u32[]{:S(2)}) collective-permute-start(bf16[256,256]{1,0:T(8,128)(2,1)S(1)} %get-tuple-element.54), channel_id=1, source_target_pairs={{0,14},{1,15},{2,0},{3,1},{4,2},{5,3},{6,4},{7,5},{8,6},{9,7},{10,... | collective-permute-start | bytes 393224 | tf_op jit(solution)/shard_map/ppermute | solution.py:34
  43.0 20.6 %collective-permute-start.13 = (bf16[2,512,256]{2,1,0:T(8,128)(2,1)S(1)}, bf16[2,512,256]{2,1,0:T(8,128)(2,1)S(1)}, u32[]{:S(2)}, u32[]{:S(2)}) collective-permute-start(bf16[2,512,256]{2,1,0:T(8,128)(2,1)S(1)} %get-tuple-element.60), channel_id=1, source_target_pairs={{0,16},{1,17},{2,18},{3,19},{4,20},{5,21},{6,22},{7,23},{8,24},{9,... | collective-permute-start | bytes 1572872 | tf_op jit(solution)/shard_map/ppermute | solution.py:34
  55.6 4.3 %collective-permute-start.9 = (bf16[256,256]{1,0:T(8,128)(2,1)S(1)}, bf16[256,256]{1,0:T(8,128)(2,1)S(1)}, u32[]{:S(2)}, u32[]{:S(2)}) collective-permute-start(bf16[256,256]{1,0:T(8,128)(2,1)S(1)} %get-tuple-element.52), channel_id=1, source_target_pairs={{0,2},{1,3},{2,4},{3,5},{4,6},{5,7},{6,8},{7,9},{8,10},{9,11},{10,... | collective-permute-start | bytes 393224 | tf_op jit(solution)/shard_map/ppermute | solution.py:34
  60.1 17.2 %collective-permute-start.11 = (bf16[2,256,512]{2,1,0:T(8,128)(2,1)S(1)}, bf16[2,256,512]{2,1,0:T(8,128)(2,1)S(1)}, u32[]{:S(2)}, u32[]{:S(2)}) collective-permute-start(bf16[2,256,512]{2,1,0:T(8,128)(2,1)S(1)} %get-tuple-element.57.refs_4_), channel_id=1, source_target_pairs={{0,2},{1,3},{2,4},{3,5},{4,6},{5,7},{6,8},{7,9},{8,10},{9,11},{10,... | collective-permute-start | bytes 1572872 | tf_op jit(solution)/shard_map/ppermute | solution.py:34
  62.1 15.3 %collective-permute-start.12 = (bf16[2,256,512]{2,1,0:T(8,128)(2,1)S(1)}, bf16[2,256,512]{2,1,0:T(8,128)(2,1)S(1)}, u32[]{:S(2)}, u32[]{:S(2)}) collective-permute-start(bf16[2,256,512]{2,1,0:T(8,128)(2,1)S(1)} %get-tuple-element.58.refs_5_), channel_id=1, source_target_pairs={{0,14},{1,15},{2,0},{3,1},{4,2},{5,3},{6,4},{7,5},{8,6},{9,7},{10,... | collective-permute-start | bytes 1572872 | tf_op jit(solution)/shard_map/ppermute | solution.py:34
  62.1 13.8 %collective-permute-start.14 = (bf16[512,256]{1,0:T(8,128)(2,1)S(1)}, bf16[512,256]{1,0:T(8,128)(2,1)S(1)}, u32[]{:S(2)}, u32[]{:S(2)}) collective-permute-start(bf16[512,256]{1,0:T(8,128)(2,1)S(1)} %get-tuple-element.55.refs_2_), channel_id=1, source_target_pairs={{0,2},{1,3},{2,4},{3,5},{4,6},{5,7},{6,8},{7,9},{8,10},{9,11},{10,... | collective-permute-start | bytes 786440 | tf_op jit(solution)/shard_map/ppermute | solution.py:34
  63.6 13.6 %collective-permute-start.15 = (bf16[512,256]{1,0:T(8,128)(2,1)S(1)}, bf16[512,256]{1,0:T(8,128)(2,1)S(1)}, u32[]{:S(2)}, u32[]{:S(2)}) collective-permute-start(bf16[512,256]{1,0:T(8,128)(2,1)S(1)} %get-tuple-element.56.refs_3_), channel_id=1, source_target_pairs={{0,14},{1,15},{2,0},{3,1},{4,2},{5,3},{6,4},{7,5},{8,6},{9,7},{10,... | collective-permute-start | bytes 786440 | tf_op jit(solution)/shard_map/ppermute | solution.py:34
  63.6 20.0 %collective-permute-start.18 = (bf16[2,512,256]{2,1,0:T(8,128)(2,1)S(1)}, bf16[2,512,256]{2,1,0:T(8,128)(2,1)S(1)}, u32[]{:S(2)}, u32[]{:S(2)}) collective-permute-start(bf16[2,512,256]{2,1,0:T(8,128)(2,1)S(1)} %get-tuple-element.67), channel_id=1, source_target_pairs={{0,16},{1,17},{2,18},{3,19},{4,20},{5,21},{6,22},{7,23},{8,24},{9,... | collective-permute-start | bytes 1572872 | tf_op jit(solution)/shard_map/ppermute | solution.py:34
  75.9 6.7 %collective-permute-start.21 = (bf16[1,512,256]{2,1,0:T(8,128)(2,1)S(1)}, bf16[1,512,256]{2,1,0:T(8,128)(2,1)S(1)}, u32[]{:S(2)}, u32[]{:S(2)}) collective-permute-start(bf16[1,512,256]{2,1,0:T(8,128)(2,1)S(1)} %get-tuple-element.69), channel_id=1, source_target_pairs={{0,16},{1,17},{2,18},{3,19},{4,20},{5,21},{6,22},{7,23},{8,24},{9,... | collective-permute-start | bytes 786440 | tf_op jit(solution)/shard_map/ppermute | solution.py:34
  77.4 19.6 %collective-permute-start.16 = (bf16[2,256,512]{2,1,0:T(8,128)(2,1)S(1)}, bf16[2,256,512]{2,1,0:T(8,128)(2,1)S(1)}, u32[]{:S(2)}, u32[]{:S(2)}) collective-permute-start(bf16[2,256,512]{2,1,0:T(8,128)(2,1)S(1)} %get-tuple-element.64.refs_6_), channel_id=1, source_target_pairs={{0,2},{1,3},{2,4},{3,5},{4,6},{5,7},{6,8},{7,9},{8,10},{9,11},{10,... | collective-permute-start | bytes 1572872 | tf_op jit(solution)/shard_map/ppermute | solution.py:34
  80.6 16.4 %collective-permute-start.17 = (bf16[2,256,512]{2,1,0:T(8,128)(2,1)S(1)}, bf16[2,256,512]{2,1,0:T(8,128)(2,1)S(1)}, u32[]{:S(2)}, u32[]{:S(2)}) collective-permute-start(bf16[2,256,512]{2,1,0:T(8,128)(2,1)S(1)} %get-tuple-element.65.refs_7_), channel_id=1, source_target_pairs={{0,14},{1,15},{2,0},{3,1},{4,2},{5,3},{6,4},{7,5},{8,6},{9,7},{10,... | collective-permute-start | bytes 1572872 | tf_op jit(solution)/shard_map/ppermute | solution.py:34
  80.6 12.5 %collective-permute-start.19 = (bf16[512,256]{1,0:T(8,128)(2,1)S(1)}, bf16[512,256]{1,0:T(8,128)(2,1)S(1)}, u32[]{:S(2)}, u32[]{:S(2)}) collective-permute-start(bf16[512,256]{1,0:T(8,128)(2,1)S(1)} %get-tuple-element.62.refs_2_), channel_id=1, source_target_pairs={{0,2},{1,3},{2,4},{3,5},{4,6},{5,7},{6,8},{7,9},{8,10},{9,11},{10,... | collective-permute-start | bytes 786440 | tf_op jit(solution)/shard_map/ppermute | solution.py:34
  82.6 12.4 %collective-permute-start.20 = (bf16[512,256]{1,0:T(8,128)(2,1)S(1)}, bf16[512,256]{1,0:T(8,128)(2,1)S(1)}, u32[]{:S(2)}, u32[]{:S(2)}) collective-permute-start(bf16[512,256]{1,0:T(8,128)(2,1)S(1)} %get-tuple-element.63.refs_3_), channel_id=1, source_target_pairs={{0,14},{1,15},{2,0},{3,1},{4,2},{5,3},{6,4},{7,5},{8,6},{9,7},{10,... | collective-permute-start | bytes 786440 | tf_op jit(solution)/shard_map/ppermute | solution.py:34
  95.2 5.5 %collective-permute-start.26 = (bf16[512,256]{1,0:T(8,128)(2,1)S(1)}, bf16[512,256]{1,0:T(8,128)(2,1)S(1)}, u32[]{:S(2)}, u32[]{:S(2)}) collective-permute-start(bf16[512,256]{1,0:T(8,128)(2,1)S(1)} %get-tuple-element.70.refs_2_.refs_8_), channel_id=1, source_target_pairs={{0,2},{1,3},{2,4},{3,5},{4,6},{5,7},{6,8},{7,9},{8,10},{9,11},{10,... | collective-permute-start | bytes 786440 | tf_op jit(solution)/shard_map/ppermute | solution.py:34
  97.0 5.7 %collective-permute-start.27 = (bf16[512,256]{1,0:T(8,128)(2,1)S(1)}, bf16[512,256]{1,0:T(8,128)(2,1)S(1)}, u32[]{:S(2)}, u32[]{:S(2)}) collective-permute-start(bf16[512,256]{1,0:T(8,128)(2,1)S(1)} %get-tuple-element.71.refs_3_), channel_id=1, source_target_pairs={{0,14},{1,15},{2,0},{3,1},{4,2},{5,3},{6,4},{7,5},{8,6},{9,7},{10,... | collective-permute-start | bytes 786440 | tf_op jit(solution)/shard_map/ppermute | solution.py:34
  97.0 18.3 %collective-permute-start.22 = (bf16[256,512]{1,0:T(8,128)(2,1)S(1)}, bf16[256,512]{1,0:T(8,128)(2,1)S(1)}, u32[]{:S(2)}, u32[]{:S(2)}) collective-permute-start(bf16[256,512]{1,0:T(8,128)(2,1)S(1)} %get-tuple-element.72), channel_id=1, source_target_pairs={{0,2},{1,3},{2,4},{3,5},{4,6},{5,7},{6,8},{7,9},{8,10},{9,11},{10,... | collective-permute-start | bytes 786440 | tf_op jit(solution)/shard_map/ppermute | solution.py:34
  98.5 16.8 %collective-permute-start.23 = (bf16[256,512]{1,0:T(8,128)(2,1)S(1)}, bf16[256,512]{1,0:T(8,128)(2,1)S(1)}, u32[]{:S(2)}, u32[]{:S(2)}) collective-permute-start(bf16[256,512]{1,0:T(8,128)(2,1)S(1)} %get-tuple-element.73), channel_id=1, source_target_pairs={{0,14},{1,15},{2,0},{3,1},{4,2},{5,3},{6,4},{7,5},{8,6},{9,7},{10,... | collective-permute-start | bytes 786440 | tf_op jit(solution)/shard_map/ppermute | solution.py:34
  102.8 22.9 %collective-permute-start.28 = (bf16[512,256]{1,0:T(8,128)(2,1)S(1)}, bf16[512,256]{1,0:T(8,128)(2,1)S(1)}, u32[]{:S(2)}, u32[]{:S(2)}) collective-permute-start(bf16[512,256]{1,0:T(8,128)(2,1)S(1)} %shard_map.100), channel_id=1, source_target_pairs={{0,224},{1,225},{2,226},{3,227},{4,228},{5,229},{6,230},{7,231},{8... | collective-permute-start | bytes 786440 | tf_op jit(solution)/shard_map/ppermute | solution.py:58
  115.3 10.4 %copy-start.1 = (bf16[1,256,512]{2,1,0:T(8,128)(2,1)S(1)}, bf16[1,256,512]{2,1,0:T(8,128)(2,1)}, u32[]{:S(2)}) copy-start(bf16[1,256,512]{2,1,0:T(8,128)(2,1)} %weight.3) | copy-start | bytes 786436
  115.3 10.3 %copy-start.3 = (f32[1,256,512]{2,1,0:T(8,128)S(1)}, f32[1,256,512]{2,1,0:T(8,128)}, u32[]{:S(2)}) copy-start(f32[1,256,512]{2,1,0:T(8,128)} %grad_weight_in.1) | copy-start | bytes 1572868
  115.3 10.3 %copy-start.5 = (bf16[1,256]{1,0:T(2,128)(2,1)S(1)}, bf16[1,256]{1,0:T(2,128)(2,1)}, u32[]{:S(2)}) copy-start(bf16[1,256]{1,0:T(2,128)(2,1)} %gain.3) | copy-start | bytes 1540
  115.4 10.3 %copy-start.6 = (f32[1,256]{1,0:T(1,128)S(1)}, f32[1,256]{1,0:T(1,128)}, u32[]{:S(2)}) copy-start(f32[1,256]{1,0:T(1,128)} %grad_gain_in.1) | copy-start | bytes 3076
  117.7 9.1 %collective-permute-start.24 = (bf16[256,512]{1,0:T(8,128)(2,1)S(1)}, bf16[256,512]{1,0:T(8,128)(2,1)S(1)}, u32[]{:S(2)}, u32[]{:S(2)}) collective-permute-start(bf16[256,512]{1,0:T(8,128)(2,1)S(1)} %get-tuple-element.77), channel_id=1, source_target_pairs={{0,1},{1,0},{2,3},{3,2},{4,5},{5,4},{6,7},{7,6},{8,9},{9,8},{10,11... | collective-permute-start | bytes 786440 | tf_op jit(solution)/shard_map/ppermute | solution.py:34
  125.6 1.5 %collective-permute-start.25 = (bf16[256,512]{1,0:T(8,128)(2,1)S(1)}, bf16[256,512]{1,0:T(8,128)(2,1)S(1)}, u32[]{:S(2)}, u32[]{:S(2)}) collective-permute-start(bf16[256,512]{1,0:T(8,128)(2,1)S(1)} %get-tuple-element.78), channel_id=1, source_target_pairs={{0,1},{1,0},{2,3},{3,2},{4,5},{5,4},{6,7},{7,6},{8,9},{9,8},{10,11... | collective-permute-start | bytes 786440 | tf_op jit(solution)/shard_map/ppermute | solution.py:34

commit v7 on v6

--- a/solution.py
+++ b/solution.py
@@ -13,9 +13,9 @@
 BF16 = jnp.bfloat16
 F32 = jnp.float32
 OFFSETS = (4, 3, -3, 2, -2, 1, -1, 0)
-GROUPS = ((1, 2), (2, 2, 1))
+GROUPS = ((1,), (2, 2, 2, 1))
 FIRST = sum(GROUPS[0])
-SWAPS = (3, 2, 3)
+SWAPS = (2, 2, 2, 2)
 VMEM_LIMIT = 16 * 1024 * 1024
 LOAD_LIMIT = 36 * 1024 * 1024
 
@@ -148,10 +148,12 @@
                 total += jnp.dot(
                     visits[0][:, 2 * SWAPS[0] * width:], theirs[:, flip * width:(flip + 1) * width], preferred_element_type=F32
                 )
+                half = total.shape[0] // 2
+                total = jnp.concatenate([total[:half], total[half:]], axis=1).astype(BF16)
                 if flip:
-                    send[j] = total.astype(BF16)
+                    send[j] = total
                 else:
-                    next(keeps)[...] = total.astype(BF16)
+                    next(keeps)[...] = total
             at += 1
 
 
@@ -163,25 +165,24 @@
         functools.partial(gradient_kernel, base, groups, width),
         in_specs=[IN_SMEM] + [IN_VMEM] * (2 + len(SWAPS)) + [ANYWHERE],
         out_specs=[IN_VMEM] * (len(groups) + count),
-        out_shape=[jax.ShapeDtypeStruct((size, values, width), BF16) for size in groups]
-        + [jax.ShapeDtypeStruct((values, width), BF16)] * count,
+        out_shape=[jax.ShapeDtypeStruct((size, values // 2, 2 * width), BF16) for size in groups]
+        + [jax.ShapeDtypeStruct((values // 2, 2 * width), BF16)] * count,
         compiler_params=params(),
         cost_estimate=cost(0, tokens),
     )(table, hidden, cot_t, *visits, after)
     return outs[:len(groups)], outs[len(groups):]
 
 
-def project_kernel(offsets, sizes, more, extra, width, table, hidden, *refs):
+def project_kernel(offsets, rows, more, extra, width, table, hidden, *refs):
     visits, refs = refs[:len(SWAPS)], refs[len(SWAPS):]
     outs = refs[-3:] if more else refs[-2:]
     start = refs[-5 - extra:-3 - extra] if more else None
     refs = iter(refs)
-    weights = [[next(refs) for _ in range(size)] for size in sizes]
+    weights = [[next(refs)[:count] for count in group] for group in rows]
     totals = [ref[...] for ref in start] if more else []
     for at in range(0, len(offsets), 2):
         chosen = [OFFSETS.index(off) for off in offsets[at:at + 2]]
-        weight = [ref[...].reshape(-1, outs[0].shape[1]) for group in weights[at:at + 2] for ref in group]
-        weight = jnp.concatenate(weight, axis=0)
+        weight = jnp.concatenate([part for group in weights[at:at + 2] for part in group], axis=0)
         own = jnp.concatenate([block(hidden, table[2 * i + flip], width) for i in chosen for flip in (0, 1)], axis=1)
         visitors = jnp.concatenate([swapped(visits, i, width) for i in chosen], axis=1)
         products = [jnp.dot(rows, weight, preferred_element_type=F32) for rows in (own, visitors)]
@@ -197,15 +198,16 @@
 
 def project(table, hidden, visits, weights, start, after, width):
     tokens = hidden.shape[0]
-    arrays = [w for group in weights.values() for w in group]
+    arrays = [w for group in weights.values() for w, _ in group]
+    rows = [[count for _, count in group] for group in weights.values()]
     values = arrays[0].shape[-1]
-    size = sum(w.size for w in arrays)
+    size = values * sum(map(sum, rows))
     more = [] if start is None else list(start)
     whole = jax.ShapeDtypeStruct((tokens, values), F32)
     half = jax.ShapeDtypeStruct((tokens // 2, values), BF16)
     out_shape = [whole, half, half] if more else [whole, whole]
     return pl.pallas_call(
-        functools.partial(project_kernel, tuple(weights), [len(g) for g in weights.values()], bool(more), len(after), width),
+        functools.partial(project_kernel, tuple(weights), rows, bool(more), len(after), width),
         in_specs=[IN_SMEM] + [IN_VMEM] * (1 + len(SWAPS) + len(arrays) + len(more)) + [ANYWHERE] * len(after),
         out_specs=[IN_VMEM] * len(out_shape),
         out_shape=out_shape,
@@ -241,63 +243,60 @@
     )(*arrays, *after)
 
 
-def pair(one, other, after):
-    def kernel(one, other, out):
-        out[0] = one[...]
-        out[1] = other[...]
-
-    return small(kernel, [one, other], after, [(2, *one.shape)])[0]
-
-
-def split(pair_up, pair_down, after):
-    def kernel(up, down, out_up, out_down):
-        out_up[...] = up[0]
-        out_down[...] = down[1]
-
-    return small(kernel, [pair_up, pair_down], after, [pair_up.shape[1:]] * 2)
-
-
-def total_of(terms, rows=slice(None)):
-    return sum(t[rows].astype(F32) for t in terms).astype(BF16)
-
-
-def begin(terms, places, after):
-    values, width = terms[0].shape
-    half = values // 2
-
-    def kernel(keep, arrived, upper, lower):
-        parts = (keep, arrived.at[places[0]])
-        upper[...] = total_of(parts, slice(0, half))
-        lower[...] = total_of(parts, slice(half, values))
-
-    return small(kernel, terms, after, [(half, width)] * 2)
-
-
-def carry(ups, downs, places, after):
-    values, width = ups[0].shape
-
-    def kernel(keep_up, arrived_up, up, keep_down, arrived_down, down, out_up, out_down):
-        up_parts = (keep_up, arrived_up.at[places[0]])
-        down_parts = (keep_down, arrived_down.at[places[1]])
-        if up.shape[0] == values:
-            out_up[...] = total_of((*up_parts, up))
-            out_down[...] = total_of((*down_parts, down))
+def summed(terms):
+    return sum(t.astype(F32) for t in terms).astype(BF16)
+
+
+def begin(layer, far, ring, after):
+    keep, arrived, place = far
+    width, values = layer.shape
+    part = width // 4
+
+    def kernel(layer, keep, arrived, up, down):
+        for i, out in enumerate((up, down)):
+            rows = slice((2 * ring + i) * part, (2 * ring + i + 1) * part)
+            out[:width] = layer[...]
+            out[width:] = summed((keep[rows], arrived[place, rows]))
+
+    return small(kernel, [layer, keep, arrived], after, [(width + part, values)] * 2)
+
+
+def advance(up, down, above, below, ring, width, step, after):
+    values = up.shape[1]
+    half = width // 2
+    rows = slice(ring * half, (ring + 1) * half)
+    layer_rows = half if step == 3 else width
+
+    def kernel(up, keep_up, arrived_up, down, keep_down, arrived_down, next_up, next_down):
+        next_up[:layer_rows] = up[:layer_rows]
+        next_down[:layer_rows] = down[width - layer_rows:width]
+        mine_up = keep_up[rows].astype(F32) + arrived_up[above[2], rows].astype(F32)
+        mine_down = keep_down[rows].astype(F32) + arrived_down[below[2], rows].astype(F32)
+        came_up, came_down = up[width:].astype(F32), down[width:].astype(F32)
+        if step == 1:
+            part = half // 2
+            mine_up = jnp.concatenate([mine_up[:part] + came_up, mine_up[part:]], axis=0)
+            mine_down = jnp.concatenate([mine_down[:part], mine_down[part:] + came_down], axis=0)
         else:
-            half = values // 2
-            upper, lower = slice(0, half), slice(half, values)
-            out_up[upper, :] = (sum(t[upper].astype(F32) for t in up_parts) + up[...].astype(F32)).astype(BF16)
-            out_up[lower, :] = total_of(up_parts, lower)
-            out_down[upper, :] = total_of(down_parts, upper)
-            out_down[lower, :] = (sum(t[lower].astype(F32) for t in down_parts) + down[...].astype(F32)).astype(BF16)
-
-    return small(kernel, [*ups, *downs], after, [(values, width)] * 2)
-
-
-def end(terms, place, after):
-    def kernel(keep, arrived, up, down, out):
-        out[...] = total_of((keep, arrived.at[place], up, down))
-
-    return small(kernel, terms, after, [terms[0].shape])[0]
+            mine_up += came_up
+            mine_down += came_down
+        next_up[layer_rows:] = mine_up.astype(BF16)
+        next_down[layer_rows:] = mine_down.astype(BF16)
+
+    return small(kernel, [up, *above[:2], down, *below[:2]], after, [(layer_rows + half, values)] * 2)
+
+
+def end(rings, own):
+    keep, arrived, place = own
+    half = keep.shape[0] // 2
+
+    def kernel(keep, arrived, *refs):
+        loads, out = refs[:-1], refs[-1]
+        for ring in (0, 1):
+            rows = slice(ring * half, (ring + 1) * half)
+            out[rows] = summed((keep[rows], arrived[place, rows], *(load[half:] for load in loads[2 * ring:2 * ring + 2])))
+
+    return small(kernel, [keep, arrived, *rings], [], [keep.shape])[0]
 
 
 def scaled_values(product, upper, lower, scale):
@@ -330,7 +329,8 @@
 
 
 def finish_kernel(total, gain, weight, grad_weight_in, grad_gain_in, grad_weight, grad_gain):
-    summed = total[...].astype(F32).T
+    half = total.shape[1] // 2
+    summed = jnp.concatenate([total[:, :half].astype(F32).T, total[:, half:].astype(F32).T], axis=1)
     grad_weight[0] = grad_weight_in[0] + as_column(gain[...].astype(F32)) * summed
     grad_gain[...] = grad_gain_in[...] + as_row(jnp.sum(weight[0].astype(F32) * summed, axis=1, keepdims=True))
 
@@ -359,35 +359,44 @@
     early = [visits[0]] * len(SWAPS)
     sends_1, keeps_1 = gradient(table, held, cot_t, early, cot_t, 0, GROUPS[0], width)
     sends_2, keeps_2 = gradient(table, held, cot_t, visits, sends_1[-1], FIRST, GROUPS[1], width)
-    arrived = [swap_x(send) for send in (*sends_1, *sends_2)]
     keeps = [*keeps_1, *keeps_2]
-    places = [(i, j) for i, size in enumerate(GROUPS[0] + GROUPS[1]) for j in range(size)]
-    mine = {off: (keeps[i], arrived[places[i][0]]) for i, off in enumerate(OFFSETS)}
-    place = {off: places[i][1] for i, off in enumerate(OFFSETS)}
-
-    layer = pair(*layer, [arrived[0]])
-    up, down = begin(mine[4], (place[4],), [])
-    weights = {0: [layer]}
-    layer_up = layer_down = layer
-    for step in (1, 2, 3):
-        layer_up, layer_down = along_z(layer_up, 1), along_z(layer_down, -1)
+    mine = {}
+
+    def send_group(group, index, after):
+        first = sum((GROUPS[0] + GROUPS[1])[:index])
+        arrived = swap_x(tie([group], after)[0] if after else group)
+        for j in range(group.shape[0]):
+            mine[OFFSETS[first + j]] = (keeps[first + j], arrived, j)
+        return arrived
+
+    arrived = send_group(sends_1[0], 0, [])
+    send_group(sends_2[0], 1, [*layer, arrived])
+
+    weights = {0: [(layer[0], width), (layer[1], width)]}
+    loads = [begin(layer[ring], mine[4], ring, [keeps_2[-1]]) for ring in (0, 1)]
+    for step in (1, 2, 3, 4):
         off = 4 - step
-        up, down = along_z(up, 1), along_z(down, -1)
-        ready = [mine[0][1]] if step == 3 else []
-        up, down = carry((*mine[off], up), (*mine[-off], down), (place[off], place[-off]), ready)
-        if step < 3:
-            layer_up, layer_down = tie([layer_up, layer_down], [up, down])
-        else:
-            far_up, far_down = split(layer_up, layer_down, [up, down])
-        weights[-step], weights[step] = [layer_up], [layer_down]
-    weights[4] = [along_z(far_up, 1), along_z(far_down, -1)]
+        last = []
+        weights[step], weights[-step] = [], []
+        for ring in (0, 1):
+            up, down = along_z(loads[ring][0], 1), along_z(loads[ring][1], -1)
+            if step < 4:
+                weights[-step].append((up, width))
+                weights[step].append((down, width))
+                loads[ring] = advance(up, down, mine[off], mine[-off], ring, width, step, last)
+                last = [loads[ring][0]]
+                begun = last if ring == 0 else begun
+            else:
+                weights[step] += [(up, width // 2), (down, width // 2)]
+                loads[ring] = [up, down]
+        if step < 4:
+            send_group(sends_2[step], step + 1, begun)
+    total = along_blk(end([*loads[0], *loads[1]], mine[0]), -1, 0)
 
     near = {off: weights[off] for off in (0, -1, 1, -2, 2)}
     far = {off: weights[off] for off in (-3, 3, 4)}
-    products = project(table, held, visits, near, None, [up], width)
+    products = project(table, held, visits, near, None, [], width)
     product, *products = project(table, held, visits, far, products, [], width)
-    up, down = along_z(up, 1), along_z(down, -1)
-    total = along_blk(end((*mine[0], up, down), place[0], []), -1, 0)
     values = scaled_values(product, *(swap_core(p) for p in products), scale)
 
     return values, *finish(total, gain, value_weight, grad_weight_in, grad_gain_in)

time: 128 us -> 111 us (0.87)
  the two profiles are of different devices: /device:TPU:83 before, /device:TPU:4 now
where the time goes in v7:
time: 111 us; the launch traced here: 109 us
  starting transfers between devices  44.2 us (40%)
  waiting for transfers between devices  41.5 us (37%)
  Pallas kernels  19.8 us (18%)
  local copies, waits for them, and re-layouts  2.78 us (3%)
    ppermute x27, starting transfers between devices, move(): return lax.ppermute(value, ('x', 'z', 'core'), pairs)  36.4 us
    ppermute x27, waiting for transfers between devices, move(): return lax.ppermute(value, ('x', 'z', 'core'), pairs)  35.3 us
    ppermute x3, starting transfers between devices, along_blk(): return lax.ppermute(value, ('blk', 'x', 'z', 'core'), pairs)  7.79 us
    ppermute x3, waiting for transfers between devices, along_blk(): return lax.ppermute(value, ('blk', 'x', 'z', 'core'), pairs)  6.29 us
    pallas_call x2, Pallas kernels, project(): pl.pallas_call(functools.partial(project_kernel, tuple(weights), rows, bo...  5.79 us
    pallas_call x2, Pallas kernels, gradient(): pl.pallas_call(functools.partial(gradient_kernel, base, groups, width), i...  5.74 us
    pallas_call x1, Pallas kernels, prepare(): pl.pallas_call(functools.partial(prepare_kernel, width, steps), in_specs=...  5.12 us
    unnamed x14, local copies, waits for them, and re-layouts  2.68 us
  transfers between devices with their start and end apart: 30, of which 16 were waited for; matrix products, arithmetic and copies ran while one was open for 0% of the time, Pallas kernels for 12%

profile of v7, /device:TPU:4, one launch (start us, length us, event | category | flops | bytes accessed | tf_op | source)
XLA Modules:
  0.0 109.3 jit_solution(6965619753320999265)
XLA Ops:
  0.7 0.9 copy-done
  1.7 0.7 copy-done.4
  2.6 1.0 copy-done.2
  3.6 5.1 %shard_map.86 = (bf16[512,8192]{1,0:T(8,128)(2,1)S(1)}, f32[512,1]{1,0:T(8,128)S(1)}, bf16[512,512]{1,0:T(8,128)(2,1)S(1)}, bf16[512,1536]{1,0:T(8,128)(2,1)S(1)...) custom-call(s32[16]{0:T(128)S(1)} %stack.67.table, ...), custom_call_target="tpu_custom_call" | custom-call | bytes 16777216 | tf_op jit(solution)/shard_map/pallas_call | solution.py:122
  8.9 0.5 collective-permute-start.1
  9.5 0.4 collective-permute-start.3
  9.9 0.5 collective-permute-start.7
  10.4 1.9 %collective-permute-done.refs_0_.refs_1_.refs_2_.refs_3_ = bf16[512,1536]{1,0:T(8,128)(2,1)S(1)} collective-permute-done((bf16[512,1536]{1,0:T(8,128)(2,1)S(1)}, bf16[512,1536]{1,0:T(8,128)(2,1)S(1)}, u32[]{:S(2)}, u32[]{:S(2)}) %collective-permute-start) | collective-permute-done | bytes 1572896 | tf_op jit(solution)/shard_map/ppermute | solution.py:34
  12.3 1.2 %collective-permute-start.4 = (bf16[256,512]{1,0:T(8,128)(2,1)S(1)}, bf16[256,512]{1,0:T(8,128)(2,1)S(1)}, u32[]{:S(2)}, u32[]{:S(2)}) collective-permute-start(bf16[256,512]{1,0:T(8,128)(2,1)S(1)} %shard_map.85.after), channel_id=1, source_target_pairs={{0,32},{1,33},{2,34},{3,35},{4,36},{5,37},{6,38},{7,39},{8,40},{9,... | collective-permute-start | bytes 786440 | tf_op jit(solution)/shard_map/ppermute | solution.py:58
  13.5 1.2 %shard_map.87 = (bf16[1,256,512]{2,1,0:T(8,128)(2,1)S(1)}, bf16[256,512]{1,0:T(8,128)(2,1)S(1)}) custom-call(s32[16]{0:T(128)S(1)} %stack.67.table, bf16[512,8192]{1,0:T(8,128)(2,1)S(1)} %get-tuple-element.46.hidden, bf16[512,512]{1,0:T(8,128)(2,1)S(1)} %get-tuple-element.51.cot_t.refs_4_, ...), custom_call_target="tpu_custom_call" | custom-call | bytes 512 | tf_op jit(solution)/shard_map/pallas_call | solution.py:164
  14.7 1.3 %collective-permute-start.5 = (bf16[1,256,512]{2,1,0:T(8,128)(2,1)S(1)}, bf16[1,256,512]{2,1,0:T(8,128)(2,1)S(1)}, u32[]{:S(2)}, u32[]{:S(2)}) collective-permute-start(bf16[1,256,512]{2,1,0:T(8,128)(2,1)S(1)} %get-tuple-element.53.refs_4_), channel_id=1, source_target_pairs={{0,16},{1,17},{2,18},{3,19},{4,20},{5,21},{6,22},{7,23},{8,24},{9,... | collective-permute-start | bytes 786440 | tf_op jit(solution)/shard_map/ppermute | solution.py:34
  16.0 0.8 collective-permute-done.3.refs_3_
  16.8 4.5 %shard_map.88 = (bf16[2,256,512]{2,1,0:T(8,128)(2,1)S(1)}, bf16[2,256,512]{2,1,0:T(8,128)(2,1)S(1)}, bf16[2,256,512]{2,1,0:T(8,128)(2,1)S(1)}, bf16[1,256,512]{2...) custom-call(s32[16]{0:T(128)S(1)} %stack.67.table, ...), custom_call_target="tpu_custom_call" | custom-call | bytes 512 | tf_op jit(solution)/shard_map/pallas_call | solution.py:164
  21.3 2.2 %collective-permute-done.7.refs_2_.refs_0_.refs_5_ = bf16[256,512]{1,0:T(8,128)(2,1)S(1)} collective-permute-done((bf16[256,512]{1,0:T(8,128)(2,1)S(1)}, bf16[256,512]{1,0:T(8,128)(2,1)S(1)}, u32[]{:S(2)}, u32[]{:S(2)}) %collective-permute-start.7) | collective-permute-done | bytes 262176 | tf_op jit(solution)/shard_map/ppermute | solution.py:58
  23.5 3.2 %collective-permute-done.4.refs_0_.refs_1_.refs_4_ = bf16[256,512]{1,0:T(8,128)(2,1)S(1)} collective-permute-done((bf16[256,512]{1,0:T(8,128)(2,1)S(1)}, bf16[256,512]{1,0:T(8,128)(2,1)S(1)}, u32[]{:S(2)}, u32[]{:S(2)}) %collective-permute-start.4) | collective-permute-done | bytes 262176 | tf_op jit(solution)/shard_map/ppermute | solution.py:58
  26.7 3.4 %collective-permute-start.8 = (bf16[2,256,512]{2,1,0:T(8,128)(2,1)S(1)}, bf16[2,256,512]{2,1,0:T(8,128)(2,1)S(1)}, u32[]{:S(2)}, u32[]{:S(2)}) collective-permute-start(bf16[2,256,512]{2,1,0:T(8,128)(2,1)S(1)} %shard_map.90), channel_id=1, source_target_pairs={{0,16},{1,17},{2,18},{3,19},{4,20},{5,21},{6,22},{7,23},{8,24},{9,... | collective-permute-start | bytes 1572872 | tf_op jit(solution)/shard_map/ppermute | solution.py:34
  30.2 0.8 collective-permute-start.6
  31.0 4.2 %collective-permute-start.9 = (bf16[320,512]{1,0:T(8,128)(2,1)S(1)}, bf16[320,512]{1,0:T(8,128)(2,1)S(1)}, u32[]{:S(2)}, u32[]{:S(2)}) collective-permute-start(bf16[320,512]{1,0:T(8,128)(2,1)S(1)} %get-tuple-element.58), channel_id=1, source_target_pairs={{0,14},{1,15},{2,0},{3,1},{4,2},{5,3},{6,4},{7,5},{8,6},{9,7},{10,... | collective-permute-start | bytes 983048 | tf_op jit(solution)/shard_map/ppermute | solution.py:34
  35.4 3.2 %collective-permute-start.15 = (bf16[320,512]{1,0:T(8,128)(2,1)S(1)}, bf16[320,512]{1,0:T(8,128)(2,1)S(1)}, u32[]{:S(2)}, u32[]{:S(2)}) collective-permute-start(bf16[320,512]{1,0:T(8,128)(2,1)S(1)} %get-tuple-element.67), channel_id=1, source_target_pairs={{0,14},{1,15},{2,0},{3,1},{4,2},{5,3},{6,4},{7,5},{8,6},{9,7},{10,... | collective-permute-start | bytes 983048 | tf_op jit(solution)/shard_map/ppermute | solution.py:34
  38.6 5.0 %collective-permute-done.6.refs_0_.refs_6_ = bf16[320,512]{1,0:T(8,128)(2,1)S(1)} collective-permute-done((bf16[320,512]{1,0:T(8,128)(2,1)S(1)}, bf16[320,512]{1,0:T(8,128)(2,1)S(1)}, u32[]{:S(2)}, u32[]{:S(2)}) %collective-permute-start.6) | collective-permute-done | bytes 327712 | tf_op jit(solution)/shard_map/ppermute | solution.py:34
  43.7 1.3 %collective-permute-start.11 = (bf16[2,256,512]{2,1,0:T(8,128)(2,1)S(1)}, bf16[2,256,512]{2,1,0:T(8,128)(2,1)S(1)}, u32[]{:S(2)}, u32[]{:S(2)}) collective-permute-start(bf16[2,256,512]{2,1,0:T(8,128)(2,1)S(1)} %shard_map.92), channel_id=1, source_target_pairs={{0,16},{1,17},{2,18},{3,19},{4,20},{5,21},{6,22},{7,23},{8,24},{9,... | collective-permute-start | bytes 1572872 | tf_op jit(solution)/shard_map/ppermute | solution.py:34
  45.1 4.6 %collective-permute-start.12 = (bf16[384,512]{1,0:T(8,128)(2,1)S(1)}, bf16[384,512]{1,0:T(8,128)(2,1)S(1)}, u32[]{:S(2)}, u32[]{:S(2)}) collective-permute-start(bf16[384,512]{1,0:T(8,128)(2,1)S(1)} %get-tuple-element.63), channel_id=1, source_target_pairs={{0,14},{1,15},{2,0},{3,1},{4,2},{5,3},{6,4},{7,5},{8,6},{9,7},{10,... | collective-permute-start | bytes 1179656 | tf_op jit(solution)/shard_map/ppermute | solution.py:34
  49.8 0.7 collective-permute-start.16
  50.5 2.7 %collective-permute-start.17 = (bf16[384,512]{1,0:T(8,128)(2,1)S(1)}, bf16[384,512]{1,0:T(8,128)(2,1)S(1)}, u32[]{:S(2)}, u32[]{:S(2)}) collective-permute-start(bf16[384,512]{1,0:T(8,128)(2,1)S(1)} %get-tuple-element.69), channel_id=1, source_target_pairs={{0,14},{1,15},{2,0},{3,1},{4,2},{5,3},{6,4},{7,5},{8,6},{9,7},{10,... | collective-permute-start | bytes 1179656 | tf_op jit(solution)/shard_map/ppermute | solution.py:34
  53.2 6.0 %collective-permute-done.12.refs_3_.refs_12_ = bf16[384,512]{1,0:T(8,128)(2,1)S(1)} collective-permute-done((bf16[384,512]{1,0:T(8,128)(2,1)S(1)}, bf16[384,512]{1,0:T(8,128)(2,1)S(1)}, u32[]{:S(2)}, u32[]{:S(2)}) %collective-permute-start.12) | collective-permute-done | bytes 393248 | tf_op jit(solution)/shard_map/ppermute | solution.py:34
  59.2 3.7 %collective-permute-done.10.refs_0_.refs_10_ = bf16[384,512]{1,0:T(8,128)(2,1)S(1)} collective-permute-done((bf16[384,512]{1,0:T(8,128)(2,1)S(1)}, bf16[384,512]{1,0:T(8,128)(2,1)S(1)}, u32[]{:S(2)}, u32[]{:S(2)}) %collective-permute-start.10) | collective-permute-done | bytes 393248 | tf_op jit(solution)/shard_map/ppermute | solution.py:34
  62.9 0.1 shard_map.93
  63.1 1.2 %collective-permute-start.21 = (bf16[2,256,512]{2,1,0:T(8,128)(2,1)S(1)}, bf16[2,256,512]{2,1,0:T(8,128)(2,1)S(1)}, u32[]{:S(2)}, u32[]{:S(2)}) collective-permute-start(bf16[2,256,512]{2,1,0:T(8,128)(2,1)S(1)} %shard_map.97), channel_id=1, source_target_pairs={{0,16},{1,17},{2,18},{3,19},{4,20},{5,21},{6,22},{7,23},{8,24},{9,... | collective-permute-start | bytes 1572872 | tf_op jit(solution)/shard_map/ppermute | solution.py:34
  64.3 2.0 %collective-permute-start.13 = (bf16[384,512]{1,0:T(8,128)(2,1)S(1)}, bf16[384,512]{1,0:T(8,128)(2,1)S(1)}, u32[]{:S(2)}, u32[]{:S(2)}) collective-permute-start(bf16[384,512]{1,0:T(8,128)(2,1)S(1)} %get-tuple-element.65.refs_6_.refs_1_), channel_id=1, source_target_pairs={{0,2},{1,3},{2,4},{3,5},{4,6},{5,7},{6,8},{7,9},{8,10},{9,11},{10,... | collective-permute-start | bytes 1179656 | tf_op jit(solution)/shard_map/ppermute | solution.py:34
  66.3 5.0 %collective-permute-done.16.refs_0_.refs_11_ = bf16[384,512]{1,0:T(8,128)(2,1)S(1)} collective-permute-done((bf16[384,512]{1,0:T(8,128)(2,1)S(1)}, bf16[384,512]{1,0:T(8,128)(2,1)S(1)}, u32[]{:S(2)}, u32[]{:S(2)}) %collective-permute-start.16) | collective-permute-done | bytes 393248 | tf_op jit(solution)/shard_map/ppermute | solution.py:34
  71.6 3.2 %collective-permute-start.20 = (bf16[384,512]{1,0:T(8,128)(2,1)S(1)}, bf16[384,512]{1,0:T(8,128)(2,1)S(1)}, u32[]{:S(2)}, u32[]{:S(2)}) collective-permute-start(bf16[384,512]{1,0:T(8,128)(2,1)S(1)} %get-tuple-element.72), channel_id=1, source_target_pairs={{0,14},{1,15},{2,0},{3,1},{4,2},{5,3},{6,4},{7,5},{8,6},{9,7},{10,... | collective-permute-start | bytes 1179656 | tf_op jit(solution)/shard_map/ppermute | solution.py:34
  74.8 1.4 %collective-permute-done.19.refs_3_.refs_6_ = bf16[384,512]{1,0:T(8,128)(2,1)S(1)} collective-permute-done((bf16[384,512]{1,0:T(8,128)(2,1)S(1)}, bf16[384,512]{1,0:T(8,128)(2,1)S(1)}, u32[]{:S(2)}, u32[]{:S(2)}) %collective-permute-start.19) | collective-permute-done | bytes 393248 | tf_op jit(solution)/shard_map/ppermute | solution.py:34
  76.2 3.5 %collective-permute-done.13.refs_0_.refs_4_ = bf16[384,512]{1,0:T(8,128)(2,1)S(1)} collective-permute-done((bf16[384,512]{1,0:T(8,128)(2,1)S(1)}, bf16[384,512]{1,0:T(8,128)(2,1)S(1)}, u32[]{:S(2)}, u32[]{:S(2)}) %collective-permute-start.13) | collective-permute-done | bytes 393248 | tf_op jit(solution)/shard_map/ppermute | solution.py:34
  79.9 0.5 collective-permute-start.28
  80.4 4.6 %collective-permute-done.18.refs_0_.refs_5_ = bf16[384,512]{1,0:T(8,128)(2,1)S(1)} collective-permute-done((bf16[384,512]{1,0:T(8,128)(2,1)S(1)}, bf16[384,512]{1,0:T(8,128)(2,1)S(1)}, u32[]{:S(2)}, u32[]{:S(2)}) %collective-permute-start.18) | collective-permute-done | bytes 393248 | tf_op jit(solution)/shard_map/ppermute | solution.py:34
  85.2 3.2 %collective-permute-start.25 = (bf16[256,512]{1,0:T(8,128)(2,1)S(1)}, bf16[256,512]{1,0:T(8,128)(2,1)S(1)}, u32[]{:S(2)}, u32[]{:S(2)}) collective-permute-start(bf16[256,512]{1,0:T(8,128)(2,1)S(1)} %get-tuple-element.79), channel_id=1, source_target_pairs={{0,14},{1,15},{2,0},{3,1},{4,2},{5,3},{6,4},{7,5},{8,6},{9,7},{10,... | collective-permute-start | bytes 786440 | tf_op jit(solution)/shard_map/ppermute | solution.py:34
  88.5 2.0 %collective-permute-start.22 = (bf16[256,512]{1,0:T(8,128)(2,1)S(1)}, bf16[256,512]{1,0:T(8,128)(2,1)S(1)}, u32[]{:S(2)}, u32[]{:S(2)}) collective-permute-start(bf16[256,512]{1,0:T(8,128)(2,1)S(1)} %get-tuple-element.76.refs_6_.refs_1_), channel_id=1, source_target_pairs={{0,2},{1,3},{2,4},{3,5},{4,6},{5,7},{6,8},{7,9},{8,10},{9,11},{10,... | collective-permute-start | bytes 786440 | tf_op jit(solution)/shard_map/ppermute | solution.py:34
  90.5 3.4 %shard_map.100 = (f32[512,512]{1,0:T(8,128)S(1)}, f32[512,512]{1,0:T(8,128)S(1)}) custom-call(s32[16]{0:T(128)S(1)} %stack.67.table, bf16[512,8192]{1,0:T(8,128)(2,1)S(1)} %get-tuple-element.46.hidden, bf16[512,1536]{1,0:T(8,128)(2,1)S(1)} %collective-permute-done.refs_0_.refs_1_.refs_2_.refs_3_, bf16[512,1024]{1,0:T(8,128)(2,1)S(1)} %collective-permute-done.1.refs_1_, ...), custom_call_target="tpu_custom_call" | custom-call | flops 2684354560 | tf_op jit(solution)/shard_map/pallas_call | solution.py:209
  93.9 0.4 collective-permute-done.24.refs_10_.refs_4_
  94.3 2.1 %collective-permute-done.23.refs_9_.refs_3_ = bf16[256,512]{1,0:T(8,128)(2,1)S(1)} collective-permute-done((bf16[256,512]{1,0:T(8,128)(2,1)S(1)}, bf16[256,512]{1,0:T(8,128)(2,1)S(1)}, u32[]{:S(2)}, u32[]{:S(2)}) %collective-permute-start.23) | collective-permute-done | bytes 262176 | tf_op jit(solution)/shard_map/ppermute | solution.py:34
  96.4 0.7 collective-permute-done.22.refs_8_.refs_2_
  97.1 0.1 shard_map.104
  97.3 6.1 %collective-permute-start.29 = (bf16[256,512]{1,0:T(8,128)(2,1)S(1)}, bf16[256,512]{1,0:T(8,128)(2,1)S(1)}, u32[]{:S(2)}, u32[]{:S(2)}) collective-permute-start(bf16[256,512]{1,0:T(8,128)(2,1)S(1)} %shard_map.104), channel_id=1, source_target_pairs={{0,224},{1,225},{2,226},{3,227},{4,228},{5,229},{6,230},{7,231},{8... | collective-permute-start | bytes 786440 | tf_op jit(solution)/shard_map/ppermute | solution.py:58
  103.3 2.4 %shard_map.101 = (f32[512,512]{1,0:T(8,128)S(1)}, bf16[256,512]{1,0:T(8,128)(2,1)S(1)}, bf16[256,512]{1,0:T(8,128)(2,1)S(1)}) custom-call(s32[16]{0:T(128)S(1)} %stack.67.table, bf16[512,8192]{1,0:T(8,128)(2,1)S(1)} %get-tuple-element.46.hidden, bf16[512,1536]{1,0:T(8,128)(2,1)S(1)} %collective-permute-done.refs_0_.refs_1_.refs_2_.refs_3_, ...), custom_call_target="tpu_custom_call" | custom-call | flops 1610612736 | tf_op jit(solution)/shard_map/pallas_call | solution.py:209
  105.8 0.5 collective-permute-start.27
  106.3 0.9 collective-permute-done.29.total
  107.2 1.1 shard_map.105
  108.3 1.0 shard_map.102
  (48 shorter events, 1.6 us)
Async XLA Ops:
  0.7 1.0 copy-start
  1.7 0.7 copy-start.4
  2.6 1.0 copy-start.2
  8.8 3.5 %collective-permute-start = (bf16[512,1536]{1,0:T(8,128)(2,1)S(1)}, bf16[512,1536]{1,0:T(8,128)(2,1)S(1)}, u32[]{:S(2)}, u32[]{:S(2)}) collective-permute-start(bf16[512,1536]{1,0:T(8,128)(2,1)S(1)} %get-tuple-element.47), channel_id=1, source_target_pairs={{0,1},{1,0},{2,3},{3,2},{4,5},{5,4},{6,7},{7,6},{8,9},{9,8},{10,11... | collective-permute-start | bytes 4718600 | tf_op jit(solution)/shard_map/ppermute | solution.py:34
  8.9 5.8 %collective-permute-start.1 = (bf16[512,1024]{1,0:T(8,128)(2,1)S(1)}, bf16[512,1024]{1,0:T(8,128)(2,1)S(1)}, u32[]{:S(2)}, u32[]{:S(2)}) collective-permute-start(bf16[512,1024]{1,0:T(8,128)(2,1)S(1)} %get-tuple-element.48), channel_id=1, source_target_pairs={{0,1},{1,0},{2,3},{3,2},{4,5},{5,4},{6,7},{7,6},{8,9},{9,8},{10,11... | collective-permute-start | bytes 3145736 | tf_op jit(solution)/shard_map/ppermute | solution.py:34
  9.4 6.6 %collective-permute-start.2 = (bf16[512,1024]{1,0:T(8,128)(2,1)S(1)}, bf16[512,1024]{1,0:T(8,128)(2,1)S(1)}, u32[]{:S(2)}, u32[]{:S(2)}) collective-permute-start(bf16[512,1024]{1,0:T(8,128)(2,1)S(1)} %get-tuple-element.49), channel_id=1, source_target_pairs={{0,1},{1,0},{2,3},{3,2},{4,5},{5,4},{6,7},{7,6},{8,9},{9,8},{10,11... | collective-permute-start | bytes 3145736 | tf_op jit(solution)/shard_map/ppermute | solution.py:34
  9.5 7.3 %collective-permute-start.3 = (bf16[512,1024]{1,0:T(8,128)(2,1)S(1)}, bf16[512,1024]{1,0:T(8,128)(2,1)S(1)}, u32[]{:S(2)}, u32[]{:S(2)}) collective-permute-start(bf16[512,1024]{1,0:T(8,128)(2,1)S(1)} %get-tuple-element.50), channel_id=1, source_target_pairs={{0,1},{1,0},{2,3},{3,2},{4,5},{5,4},{6,7},{7,6},{8,9},{9,8},{10,11... | collective-permute-start | bytes 3145736 | tf_op jit(solution)/shard_map/ppermute | solution.py:34
  9.9 13.6 %collective-permute-start.7 = (bf16[256,512]{1,0:T(8,128)(2,1)S(1)}, bf16[256,512]{1,0:T(8,128)(2,1)S(1)}, u32[]{:S(2)}, u32[]{:S(2)}) collective-permute-start(bf16[256,512]{1,0:T(8,128)(2,1)S(1)} %shard_map.85.after), channel_id=1, source_target_pairs={{0,48},{1,49},{2,50},{3,51},{4,52},{5,53},{6,54},{7,55},{8,56},{9,... | collective-permute-start | bytes 786440 | tf_op jit(solution)/shard_map/ppermute | solution.py:58
  12.3 14.4 %collective-permute-start.4 = (bf16[256,512]{1,0:T(8,128)(2,1)S(1)}, bf16[256,512]{1,0:T(8,128)(2,1)S(1)}, u32[]{:S(2)}, u32[]{:S(2)}) collective-permute-start(bf16[256,512]{1,0:T(8,128)(2,1)S(1)} %shard_map.85.after), channel_id=1, source_target_pairs={{0,32},{1,33},{2,34},{3,35},{4,36},{5,37},{6,38},{7,39},{8,40},{9,... | collective-permute-start | bytes 786440 | tf_op jit(solution)/shard_map/ppermute | solution.py:58
  14.7 12.0 %collective-permute-start.5 = (bf16[1,256,512]{2,1,0:T(8,128)(2,1)S(1)}, bf16[1,256,512]{2,1,0:T(8,128)(2,1)S(1)}, u32[]{:S(2)}, u32[]{:S(2)}) collective-permute-start(bf16[1,256,512]{2,1,0:T(8,128)(2,1)S(1)} %get-tuple-element.53.refs_4_), channel_id=1, source_target_pairs={{0,16},{1,17},{2,18},{3,19},{4,20},{5,21},{6,22},{7,23},{8,24},{9,... | collective-permute-start | bytes 786440 | tf_op jit(solution)/shard_map/ppermute | solution.py:34
  26.7 16.8 %collective-permute-start.8 = (bf16[2,256,512]{2,1,0:T(8,128)(2,1)S(1)}, bf16[2,256,512]{2,1,0:T(8,128)(2,1)S(1)}, u32[]{:S(2)}, u32[]{:S(2)}) collective-permute-start(bf16[2,256,512]{2,1,0:T(8,128)(2,1)S(1)} %shard_map.90), channel_id=1, source_target_pairs={{0,16},{1,17},{2,18},{3,19},{4,20},{5,21},{6,22},{7,23},{8,24},{9,... | collective-permute-start | bytes 1572872 | tf_op jit(solution)/shard_map/ppermute | solution.py:34
  30.2 13.4 %collective-permute-start.6 = (bf16[320,512]{1,0:T(8,128)(2,1)S(1)}, bf16[320,512]{1,0:T(8,128)(2,1)S(1)}, u32[]{:S(2)}, u32[]{:S(2)}) collective-permute-start(bf16[320,512]{1,0:T(8,128)(2,1)S(1)} %get-tuple-element.55), channel_id=1, source_target_pairs={{0,2},{1,3},{2,4},{3,5},{4,6},{5,7},{6,8},{7,9},{8,10},{9,11},{10,... | collective-permute-start | bytes 983048 | tf_op jit(solution)/shard_map/ppermute | solution.py:34
  31.0 12.6 %collective-permute-start.9 = (bf16[320,512]{1,0:T(8,128)(2,1)S(1)}, bf16[320,512]{1,0:T(8,128)(2,1)S(1)}, u32[]{:S(2)}, u32[]{:S(2)}) collective-permute-start(bf16[320,512]{1,0:T(8,128)(2,1)S(1)} %get-tuple-element.58), channel_id=1, source_target_pairs={{0,14},{1,15},{2,0},{3,1},{4,2},{5,3},{6,4},{7,5},{8,6},{9,7},{10,... | collective-permute-start | bytes 983048 | tf_op jit(solution)/shard_map/ppermute | solution.py:34
  35.3 14.4 %collective-permute-start.14 = (bf16[320,512]{1,0:T(8,128)(2,1)S(1)}, bf16[320,512]{1,0:T(8,128)(2,1)S(1)}, u32[]{:S(2)}, u32[]{:S(2)}) collective-permute-start(bf16[320,512]{1,0:T(8,128)(2,1)S(1)} %get-tuple-element.66), channel_id=1, source_target_pairs={{0,2},{1,3},{2,4},{3,5},{4,6},{5,7},{6,8},{7,9},{8,10},{9,11},{10,... | collective-permute-start | bytes 983048 | tf_op jit(solution)/shard_map/ppermute | solution.py:34
  35.4 14.3 %collective-permute-start.15 = (bf16[320,512]{1,0:T(8,128)(2,1)S(1)}, bf16[320,512]{1,0:T(8,128)(2,1)S(1)}, u32[]{:S(2)}, u32[]{:S(2)}) collective-permute-start(bf16[320,512]{1,0:T(8,128)(2,1)S(1)} %get-tuple-element.67), channel_id=1, source_target_pairs={{0,14},{1,15},{2,0},{3,1},{4,2},{5,3},{6,4},{7,5},{8,6},{9,7},{10,... | collective-permute-start | bytes 983048 | tf_op jit(solution)/shard_map/ppermute | solution.py:34
  43.7 19.2 %collective-permute-start.11 = (bf16[2,256,512]{2,1,0:T(8,128)(2,1)S(1)}, bf16[2,256,512]{2,1,0:T(8,128)(2,1)S(1)}, u32[]{:S(2)}, u32[]{:S(2)}) collective-permute-start(bf16[2,256,512]{2,1,0:T(8,128)(2,1)S(1)} %shard_map.92), channel_id=1, source_target_pairs={{0,16},{1,17},{2,18},{3,19},{4,20},{5,21},{6,22},{7,23},{8,24},{9,... | collective-permute-start | bytes 1572872 | tf_op jit(solution)/shard_map/ppermute | solution.py:34
  45.1 14.2 %collective-permute-start.12 = (bf16[384,512]{1,0:T(8,128)(2,1)S(1)}, bf16[384,512]{1,0:T(8,128)(2,1)S(1)}, u32[]{:S(2)}, u32[]{:S(2)}) collective-permute-start(bf16[384,512]{1,0:T(8,128)(2,1)S(1)} %get-tuple-element.63), channel_id=1, source_target_pairs={{0,14},{1,15},{2,0},{3,1},{4,2},{5,3},{6,4},{7,5},{8,6},{9,7},{10,... | collective-permute-start | bytes 1179656 | tf_op jit(solution)/shard_map/ppermute | solution.py:34
  49.7 13.3 %collective-permute-start.10 = (bf16[384,512]{1,0:T(8,128)(2,1)S(1)}, bf16[384,512]{1,0:T(8,128)(2,1)S(1)}, u32[]{:S(2)}, u32[]{:S(2)}) collective-permute-start(bf16[384,512]{1,0:T(8,128)(2,1)S(1)} %get-tuple-element.60.refs_1_.refs_6_), channel_id=1, source_target_pairs={{0,2},{1,3},{2,4},{3,5},{4,6},{5,7},{6,8},{7,9},{8,10},{9,11},{10,... | collective-permute-start | bytes 1179656 | tf_op jit(solution)/shard_map/ppermute | solution.py:34
  49.8 21.6 %collective-permute-start.16 = (bf16[384,512]{1,0:T(8,128)(2,1)S(1)}, bf16[384,512]{1,0:T(8,128)(2,1)S(1)}, u32[]{:S(2)}, u32[]{:S(2)}) collective-permute-start(bf16[384,512]{1,0:T(8,128)(2,1)S(1)} %get-tuple-element.68), channel_id=1, source_target_pairs={{0,2},{1,3},{2,4},{3,5},{4,6},{5,7},{6,8},{7,9},{8,10},{9,11},{10,... | collective-permute-start | bytes 1179656 | tf_op jit(solution)/shard_map/ppermute | solution.py:34
  50.5 20.9 %collective-permute-start.17 = (bf16[384,512]{1,0:T(8,128)(2,1)S(1)}, bf16[384,512]{1,0:T(8,128)(2,1)S(1)}, u32[]{:S(2)}, u32[]{:S(2)}) collective-permute-start(bf16[384,512]{1,0:T(8,128)(2,1)S(1)} %get-tuple-element.69), channel_id=1, source_target_pairs={{0,14},{1,15},{2,0},{3,1},{4,2},{5,3},{6,4},{7,5},{8,6},{9,7},{10,... | collective-permute-start | bytes 1179656 | tf_op jit(solution)/shard_map/ppermute | solution.py:34
  63.1 16.7 %collective-permute-start.21 = (bf16[2,256,512]{2,1,0:T(8,128)(2,1)S(1)}, bf16[2,256,512]{2,1,0:T(8,128)(2,1)S(1)}, u32[]{:S(2)}, u32[]{:S(2)}) collective-permute-start(bf16[2,256,512]{2,1,0:T(8,128)(2,1)S(1)} %shard_map.97), channel_id=1, source_target_pairs={{0,16},{1,17},{2,18},{3,19},{4,20},{5,21},{6,22},{7,23},{8,24},{9,... | collective-permute-start | bytes 1572872 | tf_op jit(solution)/shard_map/ppermute | solution.py:34
  64.3 11.9 %collective-permute-start.19 = (bf16[384,512]{1,0:T(8,128)(2,1)S(1)}, bf16[384,512]{1,0:T(8,128)(2,1)S(1)}, u32[]{:S(2)}, u32[]{:S(2)}) collective-permute-start(bf16[384,512]{1,0:T(8,128)(2,1)S(1)} %get-tuple-element.71), channel_id=1, source_target_pairs={{0,14},{1,15},{2,0},{3,1},{4,2},{5,3},{6,4},{7,5},{8,6},{9,7},{10,... | collective-permute-start | bytes 1179656 | tf_op jit(solution)/shard_map/ppermute | solution.py:34
  64.3 15.5 %collective-permute-start.13 = (bf16[384,512]{1,0:T(8,128)(2,1)S(1)}, bf16[384,512]{1,0:T(8,128)(2,1)S(1)}, u32[]{:S(2)}, u32[]{:S(2)}) collective-permute-start(bf16[384,512]{1,0:T(8,128)(2,1)S(1)} %get-tuple-element.65.refs_6_.refs_1_), channel_id=1, source_target_pairs={{0,2},{1,3},{2,4},{3,5},{4,6},{5,7},{6,8},{7,9},{8,10},{9,11},{10,... | collective-permute-start | bytes 1179656 | tf_op jit(solution)/shard_map/ppermute | solution.py:34
  71.5 13.5 %collective-permute-start.18 = (bf16[384,512]{1,0:T(8,128)(2,1)S(1)}, bf16[384,512]{1,0:T(8,128)(2,1)S(1)}, u32[]{:S(2)}, u32[]{:S(2)}) collective-permute-start(bf16[384,512]{1,0:T(8,128)(2,1)S(1)} %get-tuple-element.70), channel_id=1, source_target_pairs={{0,2},{1,3},{2,4},{3,5},{4,6},{5,7},{6,8},{7,9},{8,10},{9,11},{10,... | collective-permute-start | bytes 1179656 | tf_op jit(solution)/shard_map/ppermute | solution.py:34
  71.6 13.4 %collective-permute-start.20 = (bf16[384,512]{1,0:T(8,128)(2,1)S(1)}, bf16[384,512]{1,0:T(8,128)(2,1)S(1)}, u32[]{:S(2)}, u32[]{:S(2)}) collective-permute-start(bf16[384,512]{1,0:T(8,128)(2,1)S(1)} %get-tuple-element.72), channel_id=1, source_target_pairs={{0,14},{1,15},{2,0},{3,1},{4,2},{5,3},{6,4},{7,5},{8,6},{9,7},{10,... | collective-permute-start | bytes 1179656 | tf_op jit(solution)/shard_map/ppermute | solution.py:34
  79.9 14.0 %collective-permute-start.28 = (bf16[1,256,512]{2,1,0:T(8,128)(2,1)S(1)}, bf16[1,256,512]{2,1,0:T(8,128)(2,1)S(1)}, u32[]{:S(2)}, u32[]{:S(2)}) collective-permute-start(bf16[1,256,512]{2,1,0:T(8,128)(2,1)S(1)} %shard_map.103), channel_id=1, source_target_pairs={{0,16},{1,17},{2,18},{3,19},{4,20},{5,21},{6,22},{7,23},{8,24},{9,... | collective-permute-start | bytes 786440 | tf_op jit(solution)/shard_map/ppermute | solution.py:34
  85.1 9.2 %collective-permute-start.24 = (bf16[256,512]{1,0:T(8,128)(2,1)S(1)}, bf16[256,512]{1,0:T(8,128)(2,1)S(1)}, u32[]{:S(2)}, u32[]{:S(2)}) collective-permute-start(bf16[256,512]{1,0:T(8,128)(2,1)S(1)} %get-tuple-element.78), channel_id=1, source_target_pairs={{0,2},{1,3},{2,4},{3,5},{4,6},{5,7},{6,8},{7,9},{8,10},{9,11},{10,... | collective-permute-start | bytes 786440 | tf_op jit(solution)/shard_map/ppermute | solution.py:34
  85.2 9.1 %collective-permute-start.25 = (bf16[256,512]{1,0:T(8,128)(2,1)S(1)}, bf16[256,512]{1,0:T(8,128)(2,1)S(1)}, u32[]{:S(2)}, u32[]{:S(2)}) collective-permute-start(bf16[256,512]{1,0:T(8,128)(2,1)S(1)} %get-tuple-element.79), channel_id=1, source_target_pairs={{0,14},{1,15},{2,0},{3,1},{4,2},{5,3},{6,4},{7,5},{8,6},{9,7},{10,... | collective-permute-start | bytes 786440 | tf_op jit(solution)/shard_map/ppermute | solution.py:34
  88.4 8.0 %collective-permute-start.23 = (bf16[256,512]{1,0:T(8,128)(2,1)S(1)}, bf16[256,512]{1,0:T(8,128)(2,1)S(1)}, u32[]{:S(2)}, u32[]{:S(2)}) collective-permute-start(bf16[256,512]{1,0:T(8,128)(2,1)S(1)} %get-tuple-element.77), channel_id=1, source_target_pairs={{0,14},{1,15},{2,0},{3,1},{4,2},{5,3},{6,4},{7,5},{8,6},{9,7},{10,... | collective-permute-start | bytes 786440 | tf_op jit(solution)/shard_map/ppermute | solution.py:34
  88.5 8.7 %collective-permute-start.22 = (bf16[256,512]{1,0:T(8,128)(2,1)S(1)}, bf16[256,512]{1,0:T(8,128)(2,1)S(1)}, u32[]{:S(2)}, u32[]{:S(2)}) collective-permute-start(bf16[256,512]{1,0:T(8,128)(2,1)S(1)} %get-tuple-element.76.refs_6_.refs_1_), channel_id=1, source_target_pairs={{0,2},{1,3},{2,4},{3,5},{4,6},{5,7},{6,8},{7,9},{8,10},{9,11},{10,... | collective-permute-start | bytes 786440 | tf_op jit(solution)/shard_map/ppermute | solution.py:34
  97.3 9.9 %collective-permute-start.29 = (bf16[256,512]{1,0:T(8,128)(2,1)S(1)}, bf16[256,512]{1,0:T(8,128)(2,1)S(1)}, u32[]{:S(2)}, u32[]{:S(2)}) collective-permute-start(bf16[256,512]{1,0:T(8,128)(2,1)S(1)} %shard_map.104), channel_id=1, source_target_pairs={{0,224},{1,225},{2,226},{3,227},{4,228},{5,229},{6,230},{7,231},{8... | collective-permute-start | bytes 786440 | tf_op jit(solution)/shard_map/ppermute | solution.py:58
  103.3 3.9 %copy-start.1 = (bf16[1,256,512]{2,1,0:T(8,128)(2,1)S(1)}, bf16[1,256,512]{2,1,0:T(8,128)(2,1)}, u32[]{:S(2)}) copy-start(bf16[1,256,512]{2,1,0:T(8,128)(2,1)} %weight.3) | copy-start | bytes 786436
  103.3 3.9 %copy-start.3 = (f32[1,256,512]{2,1,0:T(8,128)S(1)}, f32[1,256,512]{2,1,0:T(8,128)}, u32[]{:S(2)}) copy-start(f32[1,256,512]{2,1,0:T(8,128)} %grad_weight_in.1) | copy-start | bytes 1572868
  103.3 3.9 %copy-start.5 = (bf16[1,256]{1,0:T(2,128)(2,1)S(1)}, bf16[1,256]{1,0:T(2,128)(2,1)}, u32[]{:S(2)}) copy-start(bf16[1,256]{1,0:T(2,128)(2,1)} %gain.3) | copy-start | bytes 1540
  103.3 3.9 %copy-start.6 = (f32[1,256]{1,0:T(1,128)S(1)}, f32[1,256]{1,0:T(1,128)}, u32[]{:S(2)}) copy-start(f32[1,256]{1,0:T(1,128)} %grad_gain_in.1) | copy-start | bytes 3076
  105.7 2.6 %collective-permute-start.26 = (bf16[256,512]{1,0:T(8,128)(2,1)S(1)}, bf16[256,512]{1,0:T(8,128)(2,1)S(1)}, u32[]{:S(2)}, u32[]{:S(2)}) collective-permute-start(bf16[256,512]{1,0:T(8,128)(2,1)S(1)} %get-tuple-element.83), channel_id=1, source_target_pairs={{0,1},{1,0},{2,3},{3,2},{4,5},{5,4},{6,7},{7,6},{8,9},{9,8},{10,11... | collective-permute-start | bytes 786440 | tf_op jit(solution)/shard_map/ppermute | solution.py:34
  105.8 2.5 %collective-permute-start.27 = (bf16[256,512]{1,0:T(8,128)(2,1)S(1)}, bf16[256,512]{1,0:T(8,128)(2,1)S(1)}, u32[]{:S(2)}, u32[]{:S(2)}) collective-permute-start(bf16[256,512]{1,0:T(8,128)(2,1)S(1)} %get-tuple-element.84), channel_id=1, source_target_pairs={{0,1},{1,0},{2,3},{3,2},{4,5},{5,4},{6,7},{7,6},{8,9},{9,8},{10,11... | collective-permute-start | bytes 786440 | tf_op jit(solution)/shard_map/ppermute | solution.py:34

commit v8 on v7

--- a/solution.py
+++ b/solution.py
@@ -13,7 +13,7 @@
 BF16 = jnp.bfloat16
 F32 = jnp.float32
 OFFSETS = (4, 3, -3, 2, -2, 1, -1, 0)
-GROUPS = ((1,), (2, 2, 2, 1))
+GROUPS = ((1,), (2, 2, 3))
 FIRST = sum(GROUPS[0])
 SWAPS = (2, 2, 2, 2)
 VMEM_LIMIT = 16 * 1024 * 1024
@@ -46,10 +46,10 @@
     return move(value, lambda x, z, c: (x, z, 1 - c))
 
 
-def along_blk(value, steps, flip_x):
+def along_blk(value, steps, flip_x, up=0):
     size = NX * NZ * NC
     pairs = [
-        (b * size + fsdp_index(x, z, c), ((b + steps) % NB) * size + fsdp_index(x ^ flip_x, z, c))
+        (b * size + fsdp_index(x, z, c), ((b + steps) % NB) * size + fsdp_index(x ^ flip_x, (z + up) % NZ, c))
         for b in range(NB)
         for x in range(NX)
         for z in range(NZ)
@@ -178,7 +178,7 @@
     outs = refs[-3:] if more else refs[-2:]
     start = refs[-5 - extra:-3 - extra] if more else None
     refs = iter(refs)
-    weights = [[next(refs)[:count] for count in group] for group in rows]
+    weights = [[next(refs)[first:first + count] for first, count in group] for group in rows]
     totals = [ref[...] for ref in start] if more else []
     for at in range(0, len(offsets), 2):
         chosen = [OFFSETS.index(off) for off in offsets[at:at + 2]]
@@ -198,10 +198,10 @@
 
 def project(table, hidden, visits, weights, start, after, width):
     tokens = hidden.shape[0]
-    arrays = [w for group in weights.values() for w, _ in group]
-    rows = [[count for _, count in group] for group in weights.values()]
+    arrays = [w for group in weights.values() for w, _, _ in group]
+    rows = [[part[1:] for part in group] for group in weights.values()]
     values = arrays[0].shape[-1]
-    size = values * sum(map(sum, rows))
+    size = values * sum(count for group in rows for _, count in group)
     more = [] if start is None else list(start)
     whole = jax.ShapeDtypeStruct((tokens, values), F32)
     half = jax.ShapeDtypeStruct((tokens // 2, values), BF16)
@@ -265,11 +265,10 @@
     values = up.shape[1]
     half = width // 2
     rows = slice(ring * half, (ring + 1) * half)
-    layer_rows = half if step == 3 else width
 
     def kernel(up, keep_up, arrived_up, down, keep_down, arrived_down, next_up, next_down):
-        next_up[:layer_rows] = up[:layer_rows]
-        next_down[:layer_rows] = down[width - layer_rows:width]
+        next_up[:width] = up[:width]
+        next_down[:width] = down[:width]
         mine_up = keep_up[rows].astype(F32) + arrived_up[above[2], rows].astype(F32)
         mine_down = keep_down[rows].astype(F32) + arrived_down[below[2], rows].astype(F32)
         came_up, came_down = up[width:].astype(F32), down[width:].astype(F32)
@@ -280,23 +279,35 @@
         else:
             mine_up += came_up
             mine_down += came_down
-        next_up[layer_rows:] = mine_up.astype(BF16)
-        next_down[layer_rows:] = mine_down.astype(BF16)
-
-    return small(kernel, [up, *above[:2], down, *below[:2]], after, [(layer_rows + half, values)] * 2)
-
-
-def end(rings, own):
+        next_up[width:] = mine_up.astype(BF16)
+        next_down[width:] = mine_down.astype(BF16)
+
+    return small(kernel, [up, *above[:2], down, *below[:2]], after, [(width + half, values)] * 2)
+
+
+def nearest(loads, above, below, width, after):
+    half = width // 2
+
+    def kernel(*refs):
+        for i, place in enumerate((above[2], below[2])):
+            keep, arrived = refs[4 + 2 * i:6 + 2 * i]
+            sums, layers = refs[8 + i], refs[10 + i]
+            for ring in (0, 1):
+                load = refs[2 * ring + i]
+                rows = slice(ring * half, (ring + 1) * half)
+                sums[rows] = summed((keep[rows], arrived[place, rows], load[width:]))
+                layers[rows] = load[i * half:(i + 1) * half]
+
+    return small(kernel, [*loads, *above[:2], *below[:2]], after, [above[0].shape] * 4)
+
+
+def own_part(own):
     keep, arrived, place = own
-    half = keep.shape[0] // 2
-
-    def kernel(keep, arrived, *refs):
-        loads, out = refs[:-1], refs[-1]
-        for ring in (0, 1):
-            rows = slice(ring * half, (ring + 1) * half)
-            out[rows] = summed((keep[rows], arrived[place, rows], *(load[half:] for load in loads[2 * ring:2 * ring + 2])))
-
-    return small(kernel, [keep, arrived, *rings], [], [keep.shape])[0]
+
+    def kernel(keep, arrived, out):
+        out[...] = summed((keep[...], arrived[place]))
+
+    return small(kernel, [keep, arrived], [], [keep.shape])[0]
 
 
 def scaled_values(product, upper, lower, scale):
@@ -328,19 +339,20 @@
     return pl.pallas_call(scale_kernel, out_shape=jax.ShapeDtypeStruct(weight.shape[1:], BF16), compiler_params=params())(gain, weight)
 
 
-def finish_kernel(total, gain, weight, grad_weight_in, grad_gain_in, grad_weight, grad_gain):
+def finish_kernel(own, up, down, gain, weight, grad_weight_in, grad_gain_in, grad_weight, grad_gain):
+    total = own[...].astype(F32) + up[...].astype(F32) + down[...].astype(F32)
     half = total.shape[1] // 2
-    summed = jnp.concatenate([total[:, :half].astype(F32).T, total[:, half:].astype(F32).T], axis=1)
-    grad_weight[0] = grad_weight_in[0] + as_column(gain[...].astype(F32)) * summed
-    grad_gain[...] = grad_gain_in[...] + as_row(jnp.sum(weight[0].astype(F32) * summed, axis=1, keepdims=True))
-
-
-def finish(total, gain, weight, grad_weight_in, grad_gain_in):
+    total = jnp.concatenate([total[:, :half].T, total[:, half:].T], axis=1)
+    grad_weight[0] = grad_weight_in[0] + as_column(gain[...].astype(F32)) * total
+    grad_gain[...] = grad_gain_in[...] + as_row(jnp.sum(weight[0].astype(F32) * total, axis=1, keepdims=True))
+
+
+def finish(totals, gain, weight, grad_weight_in, grad_gain_in):
     return pl.pallas_call(
         finish_kernel,
         out_shape=[jax.ShapeDtypeStruct(a.shape, F32) for a in (grad_weight_in, grad_gain_in)],
         compiler_params=params(),
-    )(total, gain, weight, grad_weight_in, grad_gain_in)
+    )(*totals, gain, weight, grad_weight_in, grad_gain_in)
 
 
 def per_device(hidden, gain, value_weight, cotangent, grad_weight_in, grad_gain_in):
@@ -372,34 +384,42 @@
     arrived = send_group(sends_1[0], 0, [])
     send_group(sends_2[0], 1, [*layer, arrived])
 
-    weights = {0: [(layer[0], width), (layer[1], width)]}
+    weights = {0: [(layer[0], 0, width), (layer[1], 0, width)]}
     loads = [begin(layer[ring], mine[4], ring, [keeps_2[-1]]) for ring in (0, 1)]
-    for step in (1, 2, 3, 4):
+    send_group(sends_2[1], 2, [loads[1][0]])
+    for step in (1, 2, 3):
         off = 4 - step
-        last = []
+        last = [loads[1][0]] if step == 1 else []
         weights[step], weights[-step] = [], []
         for ring in (0, 1):
             up, down = along_z(loads[ring][0], 1), along_z(loads[ring][1], -1)
-            if step < 4:
-                weights[-step].append((up, width))
-                weights[step].append((down, width))
+            if step == 3 and ring == 0:
+                near = {off: weights[off] for off in (0, -1, 1, -2, 2)}
+                products = project(table, held, visits, near, None, last, width)
+            if step == 3:
+                up, down = tie([up, down], [*last, products[0]] if ring else last)
+            weights[-step].append((up, 0, width))
+            weights[step].append((down, 0, width))
+            if step < 3:
                 loads[ring] = advance(up, down, mine[off], mine[-off], ring, width, step, last)
-                last = [loads[ring][0]]
-                begun = last if ring == 0 else begun
             else:
-                weights[step] += [(up, width // 2), (down, width // 2)]
                 loads[ring] = [up, down]
-        if step < 4:
-            send_group(sends_2[step], step + 1, begun)
-    total = along_blk(end([*loads[0], *loads[1]], mine[0]), -1, 0)
-
-    near = {off: weights[off] for off in (0, -1, 1, -2, 2)}
+            last = [loads[ring][0]]
+            if (step, ring) == (1, 0):
+                send_group(sends_2[2], 3, last)
+
+    own = along_blk(own_part(mine[0]), -1, 0)
+    sum_up, sum_down, layer_up, layer_down = nearest([*loads[0], *loads[1]], mine[1], mine[-1], width, [own])
+    totals = [own, along_blk(sum_up, -1, 0, 1), along_blk(sum_down, -1, 0, -1)]
+    up, down = along_z(layer_up, 1), along_z(layer_down, -1)
+    half = width // 2
+    weights[4] = [(far, ring * half, half) for ring in (0, 1) for far in (up, down)]
+
     far = {off: weights[off] for off in (-3, 3, 4)}
-    products = project(table, held, visits, near, None, [], width)
     product, *products = project(table, held, visits, far, products, [], width)
     values = scaled_values(product, *(swap_core(p) for p in products), scale)
 
-    return values, *finish(total, gain, value_weight, grad_weight_in, grad_gain_in)
+    return values, *finish(totals, gain, value_weight, grad_weight_in, grad_gain_in)
 
 
 def solution(mesh):

time: 111 us -> 107 us (0.964)
  waiting for transfers between devices: 41.5 us -> 29.7 us
  starting transfers between devices: 44.2 us -> 52.7 us
    ppermute x27 -> x24, waiting for transfers between devices: 35.3 us -> 19.7 us  [move(): return lax.ppermute(value, ('x', 'z', 'core'), pairs)]
    ppermute x3 -> x5, starting transfers between devices: 7.79 us -> 13.3 us  [along_blk(): return lax.ppermute(value, ('blk', 'x', 'z', 'core'), pairs)]
    ppermute x3 -> x5, waiting for transfers between devices: 6.29 us -> 9.99 us  [along_blk(): return lax.ppermute(value, ('blk', 'x', 'z', 'core'), pairs)]
    ppermute x27 -> x24, starting transfers between devices: 36.4 us -> 39.4 us  [move(): return lax.ppermute(value, ('x', 'z', 'core'), pairs)]
  transfers between devices with their start and end apart: 30 -> 29, of which waited for: 16 -> 14; matrix products, arithmetic and copies ran while one was open for 0% -> 0% of each run, Pallas kernels for 12% -> 13%
where the time goes in v8:
time: 107 us; the launch traced here: 106 us
  starting transfers between devices  52.7 us (49%)
  waiting for transfers between devices  29.7 us (28%)
  Pallas kernels  19.8 us (19%)
  local copies, waits for them, and re-layouts  2.78 us (3%)
    ppermute x24, starting transfers between devices, move(): return lax.ppermute(value, ('x', 'z', 'core'), pairs)  39.4 us
    ppermute x24, waiting for transfers between devices, move(): return lax.ppermute(value, ('x', 'z', 'core'), pairs)  19.7 us
    ppermute x5, starting transfers between devices, along_blk(): return lax.ppermute(value, ('blk', 'x', 'z', 'core'), pairs)  13.3 us
    ppermute x5, waiting for transfers between devices, along_blk(): return lax.ppermute(value, ('blk', 'x', 'z', 'core'), pairs)  9.99 us
    pallas_call x2, Pallas kernels, project(): pl.pallas_call(functools.partial(project_kernel, tuple(weights), rows, bo...  5.77 us
    pallas_call x2, Pallas kernels, gradient(): pl.pallas_call(functools.partial(gradient_kernel, base, groups, width), i...  5.74 us
    pallas_call x1, Pallas kernels, prepare(): pl.pallas_call(functools.partial(prepare_kernel, width, steps), in_specs=...  5.12 us
    unnamed x14, local copies, waits for them, and re-layouts  2.68 us
  transfers between devices with their start and end apart: 29, of which 14 were waited for; matrix products, arithmetic and copies ran while one was open for 0% of the time, Pallas kernels for 13%

profile of v8, /device:TPU:4, one launch (start us, length us, event | category | flops | bytes accessed | tf_op | source)
XLA Modules:
  0.0 105.9 jit_solution(10440473095568591751)
XLA Ops:
  0.7 0.9 copy-done
  1.7 0.7 copy-done.4
  2.6 1.0 copy-done.2
  3.6 5.1 %shard_map.86 = (bf16[512,8192]{1,0:T(8,128)(2,1)S(1)}, f32[512,1]{1,0:T(8,128)S(1)}, bf16[512,512]{1,0:T(8,128)(2,1)S(1)}, bf16[512,1536]{1,0:T(8,128)(2,1)S(1)...) custom-call(s32[16]{0:T(128)S(1)} %stack.67.table, ...), custom_call_target="tpu_custom_call" | custom-call | bytes 16777216 | tf_op jit(solution)/shard_map/pallas_call | solution.py:122
  8.9 0.5 collective-permute-start.1
  9.5 0.4 collective-permute-start.3
  9.9 0.5 collective-permute-start.7
  10.4 1.9 %collective-permute-done.refs_0_.refs_1_.refs_2_.refs_3_ = bf16[512,1536]{1,0:T(8,128)(2,1)S(1)} collective-permute-done((bf16[512,1536]{1,0:T(8,128)(2,1)S(1)}, bf16[512,1536]{1,0:T(8,128)(2,1)S(1)}, u32[]{:S(2)}, u32[]{:S(2)}) %collective-permute-start) | collective-permute-done | bytes 1572896 | tf_op jit(solution)/shard_map/ppermute | solution.py:34
  12.3 1.2 %collective-permute-start.4 = (bf16[256,512]{1,0:T(8,128)(2,1)S(1)}, bf16[256,512]{1,0:T(8,128)(2,1)S(1)}, u32[]{:S(2)}, u32[]{:S(2)}) collective-permute-start(bf16[256,512]{1,0:T(8,128)(2,1)S(1)} %shard_map.85.after), channel_id=1, source_target_pairs={{0,32},{1,33},{2,34},{3,35},{4,36},{5,37},{6,38},{7,39},{8,40},{9,... | collective-permute-start | bytes 786440 | tf_op jit(solution)/shard_map/ppermute | solution.py:58
  13.5 1.2 %shard_map.87 = (bf16[1,256,512]{2,1,0:T(8,128)(2,1)S(1)}, bf16[256,512]{1,0:T(8,128)(2,1)S(1)}) custom-call(s32[16]{0:T(128)S(1)} %stack.67.table, bf16[512,8192]{1,0:T(8,128)(2,1)S(1)} %get-tuple-element.49.hidden, bf16[512,512]{1,0:T(8,128)(2,1)S(1)} %get-tuple-element.54.cot_t.refs_4_, ...), custom_call_target="tpu_custom_call" | custom-call | bytes 512 | tf_op jit(solution)/shard_map/pallas_call | solution.py:164
  14.7 1.3 %collective-permute-start.5 = (bf16[1,256,512]{2,1,0:T(8,128)(2,1)S(1)}, bf16[1,256,512]{2,1,0:T(8,128)(2,1)S(1)}, u32[]{:S(2)}, u32[]{:S(2)}) collective-permute-start(bf16[1,256,512]{2,1,0:T(8,128)(2,1)S(1)} %get-tuple-element.56.refs_4_), channel_id=1, source_target_pairs={{0,16},{1,17},{2,18},{3,19},{4,20},{5,21},{6,22},{7,23},{8,24},{9,... | collective-permute-start | bytes 786440 | tf_op jit(solution)/shard_map/ppermute | solution.py:34
  16.0 0.8 collective-permute-done.3.refs_3_
  16.8 4.5 %shard_map.88 = (bf16[2,256,512]{2,1,0:T(8,128)(2,1)S(1)}, bf16[2,256,512]{2,1,0:T(8,128)(2,1)S(1)}, bf16[3,256,512]{2,1,0:T(8,128)(2,1)S(1)}, bf16[256,512]{1,0...) custom-call(s32[16]{0:T(128)S(1)} %stack.67.table, ...), custom_call_target="tpu_custom_call" | custom-call | bytes 512 | tf_op jit(solution)/shard_map/pallas_call | solution.py:164
  21.3 2.2 %collective-permute-done.7.refs_2_.refs_0_.refs_5_ = bf16[256,512]{1,0:T(8,128)(2,1)S(1)} collective-permute-done((bf16[256,512]{1,0:T(8,128)(2,1)S(1)}, bf16[256,512]{1,0:T(8,128)(2,1)S(1)}, u32[]{:S(2)}, u32[]{:S(2)}) %collective-permute-start.7) | collective-permute-done | bytes 262176 | tf_op jit(solution)/shard_map/ppermute | solution.py:58
  23.5 3.2 %collective-permute-done.4.refs_0_.refs_1_.refs_4_ = bf16[256,512]{1,0:T(8,128)(2,1)S(1)} collective-permute-done((bf16[256,512]{1,0:T(8,128)(2,1)S(1)}, bf16[256,512]{1,0:T(8,128)(2,1)S(1)}, u32[]{:S(2)}, u32[]{:S(2)}) %collective-permute-start.4) | collective-permute-done | bytes 262176 | tf_op jit(solution)/shard_map/ppermute | solution.py:58
  26.7 3.4 %collective-permute-start.8 = (bf16[2,256,512]{2,1,0:T(8,128)(2,1)S(1)}, bf16[2,256,512]{2,1,0:T(8,128)(2,1)S(1)}, u32[]{:S(2)}, u32[]{:S(2)}) collective-permute-start(bf16[2,256,512]{2,1,0:T(8,128)(2,1)S(1)} %shard_map.90), channel_id=1, source_target_pairs={{0,16},{1,17},{2,18},{3,19},{4,20},{5,21},{6,22},{7,23},{8,24},{9,... | collective-permute-start | bytes 1572872 | tf_op jit(solution)/shard_map/ppermute | solution.py:34
  30.2 0.8 collective-permute-start.6
  31.0 4.2 %collective-permute-start.9 = (bf16[320,512]{1,0:T(8,128)(2,1)S(1)}, bf16[320,512]{1,0:T(8,128)(2,1)S(1)}, u32[]{:S(2)}, u32[]{:S(2)}) collective-permute-start(bf16[320,512]{1,0:T(8,128)(2,1)S(1)} %get-tuple-element.61), channel_id=1, source_target_pairs={{0,14},{1,15},{2,0},{3,1},{4,2},{5,3},{6,4},{7,5},{8,6},{9,7},{10,... | collective-permute-start | bytes 983048 | tf_op jit(solution)/shard_map/ppermute | solution.py:34
  35.3 1.3 %collective-permute-start.11 = (bf16[2,256,512]{2,1,0:T(8,128)(2,1)S(1)}, bf16[2,256,512]{2,1,0:T(8,128)(2,1)S(1)}, u32[]{:S(2)}, u32[]{:S(2)}) collective-permute-start(bf16[2,256,512]{2,1,0:T(8,128)(2,1)S(1)} %shard_map.93), channel_id=1, source_target_pairs={{0,16},{1,17},{2,18},{3,19},{4,20},{5,21},{6,22},{7,23},{8,24},{9,... | collective-permute-start | bytes 1572872 | tf_op jit(solution)/shard_map/ppermute | solution.py:34
  36.6 1.8 %collective-permute-start.16 = (bf16[320,512]{1,0:T(8,128)(2,1)S(1)}, bf16[320,512]{1,0:T(8,128)(2,1)S(1)}, u32[]{:S(2)}, u32[]{:S(2)}) collective-permute-start(bf16[320,512]{1,0:T(8,128)(2,1)S(1)} %get-tuple-element.72), channel_id=1, source_target_pairs={{0,14},{1,15},{2,0},{3,1},{4,2},{5,3},{6,4},{7,5},{8,6},{9,7},{10,... | collective-permute-start | bytes 983048 | tf_op jit(solution)/shard_map/ppermute | solution.py:34
  38.4 3.5 %collective-permute-done.6.refs_0_.refs_6_ = bf16[320,512]{1,0:T(8,128)(2,1)S(1)} collective-permute-done((bf16[320,512]{1,0:T(8,128)(2,1)S(1)}, bf16[320,512]{1,0:T(8,128)(2,1)S(1)}, u32[]{:S(2)}, u32[]{:S(2)}) %collective-permute-start.6) | collective-permute-done | bytes 327712 | tf_op jit(solution)/shard_map/ppermute | solution.py:34
  41.9 1.5 %collective-permute-done.9.refs_3_.refs_8_ = bf16[320,512]{1,0:T(8,128)(2,1)S(1)} collective-permute-done((bf16[320,512]{1,0:T(8,128)(2,1)S(1)}, bf16[320,512]{1,0:T(8,128)(2,1)S(1)}, u32[]{:S(2)}, u32[]{:S(2)}) %collective-permute-start.9) | collective-permute-done | bytes 327712 | tf_op jit(solution)/shard_map/ppermute | solution.py:34
  43.5 3.2 %collective-permute-start.21 = (bf16[3,256,512]{2,1,0:T(8,128)(2,1)S(1)}, bf16[3,256,512]{2,1,0:T(8,128)(2,1)S(1)}, u32[]{:S(2)}, u32[]{:S(2)}) collective-permute-start(bf16[3,256,512]{2,1,0:T(8,128)(2,1)S(1)} %shard_map.100), channel_id=1, source_target_pairs={{0,16},{1,17},{2,18},{3,19},{4,20},{5,21},{6,22},{7,23},{8,24},{9,... | collective-permute-start | bytes 2359304 | tf_op jit(solution)/shard_map/ppermute | solution.py:34
  46.7 4.7 %collective-permute-start.12 = (bf16[384,512]{1,0:T(8,128)(2,1)S(1)}, bf16[384,512]{1,0:T(8,128)(2,1)S(1)}, u32[]{:S(2)}, u32[]{:S(2)}) collective-permute-start(bf16[384,512]{1,0:T(8,128)(2,1)S(1)} %get-tuple-element.67), channel_id=1, source_target_pairs={{0,14},{1,15},{2,0},{3,1},{4,2},{5,3},{6,4},{7,5},{8,6},{9,7},{10,... | collective-permute-start | bytes 1179656 | tf_op jit(solution)/shard_map/ppermute | solution.py:34
  51.5 2.3 %collective-permute-start.17 = (bf16[384,512]{1,0:T(8,128)(2,1)S(1)}, bf16[384,512]{1,0:T(8,128)(2,1)S(1)}, u32[]{:S(2)}, u32[]{:S(2)}) collective-permute-start(bf16[384,512]{1,0:T(8,128)(2,1)S(1)} %get-tuple-element.73), channel_id=1, source_target_pairs={{0,2},{1,3},{2,4},{3,5},{4,6},{5,7},{6,8},{7,9},{8,10},{9,11},{10,... | collective-permute-start | bytes 1179656 | tf_op jit(solution)/shard_map/ppermute | solution.py:34
  53.8 0.5 collective-permute-done.11.refs_2_.refs_5_
  54.3 5.8 %collective-permute-start.18 = (bf16[384,512]{1,0:T(8,128)(2,1)S(1)}, bf16[384,512]{1,0:T(8,128)(2,1)S(1)}, u32[]{:S(2)}, u32[]{:S(2)}) collective-permute-start(bf16[384,512]{1,0:T(8,128)(2,1)S(1)} %get-tuple-element.74), channel_id=1, source_target_pairs={{0,14},{1,15},{2,0},{3,1},{4,2},{5,3},{6,4},{7,5},{8,6},{9,7},{10,... | collective-permute-start | bytes 1179656 | tf_op jit(solution)/shard_map/ppermute | solution.py:34
  60.1 4.5 %collective-permute-done.10.refs_0_.refs_10_ = bf16[384,512]{1,0:T(8,128)(2,1)S(1)} collective-permute-done((bf16[384,512]{1,0:T(8,128)(2,1)S(1)}, bf16[384,512]{1,0:T(8,128)(2,1)S(1)}, u32[]{:S(2)}, u32[]{:S(2)}) %collective-permute-start.10) | collective-permute-done | bytes 393248 | tf_op jit(solution)/shard_map/ppermute | solution.py:34
  64.7 0.1 shard_map.94
  64.9 2.0 %collective-permute-start.13 = (bf16[384,512]{1,0:T(8,128)(2,1)S(1)}, bf16[384,512]{1,0:T(8,128)(2,1)S(1)}, u32[]{:S(2)}, u32[]{:S(2)}) collective-permute-start(bf16[384,512]{1,0:T(8,128)(2,1)S(1)} %get-tuple-element.69.refs_6_), channel_id=1, source_target_pairs={{0,2},{1,3},{2,4},{3,5},{4,6},{5,7},{6,8},{7,9},{8,10},{9,11},{10,... | collective-permute-start | bytes 1179656 | tf_op jit(solution)/shard_map/ppermute | solution.py:34
  66.9 6.2 %collective-permute-done.17.refs_0_.refs_11_ = bf16[384,512]{1,0:T(8,128)(2,1)S(1)} collective-permute-done((bf16[384,512]{1,0:T(8,128)(2,1)S(1)}, bf16[384,512]{1,0:T(8,128)(2,1)S(1)}, u32[]{:S(2)}, u32[]{:S(2)}) %collective-permute-start.17) | collective-permute-done | bytes 393248 | tf_op jit(solution)/shard_map/ppermute | solution.py:34
  73.1 0.1 shard_map.97
  73.3 3.2 %collective-permute-start.20 = (bf16[384,512]{1,0:T(8,128)(2,1)S(1)}, bf16[384,512]{1,0:T(8,128)(2,1)S(1)}, u32[]{:S(2)}, u32[]{:S(2)}) collective-permute-start(bf16[384,512]{1,0:T(8,128)(2,1)S(1)} %get-tuple-element.76), channel_id=1, source_target_pairs={{0,14},{1,15},{2,0},{3,1},{4,2},{5,3},{6,4},{7,5},{8,6},{9,7},{10,... | collective-permute-start | bytes 1179656 | tf_op jit(solution)/shard_map/ppermute | solution.py:34
  76.6 6.2 %collective-permute-start.22 = (bf16[256,512]{1,0:T(8,128)(2,1)S(1)}, bf16[256,512]{1,0:T(8,128)(2,1)S(1)}, u32[]{:S(2)}, u32[]{:S(2)}) collective-permute-start(bf16[256,512]{1,0:T(8,128)(2,1)S(1)} %shard_map.101), channel_id=1, source_target_pairs={{0,224},{1,225},{2,226},{3,227},{4,228},{5,229},{6,230},{7,231},{8... | collective-permute-start | bytes 786440 | tf_op jit(solution)/shard_map/ppermute | solution.py:58
  82.8 3.4 %shard_map.98 = (f32[512,512]{1,0:T(8,128)S(1)}, f32[512,512]{1,0:T(8,128)S(1)}) custom-call(s32[16]{0:T(128)S(1)} %stack.67.table, bf16[512,8192]{1,0:T(8,128)(2,1)S(1)} %get-tuple-element.49.hidden, bf16[512,1536]{1,0:T(8,128)(2,1)S(1)} %collective-permute-done.refs_0_.refs_1_.refs_2_.refs_3_, bf16[512,1024]{1,0:T(8,128)(2,1)S(1)} %collective-permute-done.1.refs_1_, ...), custom_call_target="tpu_custom_call" | custom-call | flops 2684354560 | tf_op jit(solution)/shard_map/pallas_call | solution.py:209
  86.2 0.4 collective-permute-done.22.refs_8_.own
  86.6 0.2 shard_map.102
  86.8 0.3 collective-permute-start.23
  87.1 3.2 %collective-permute-start.24 = (bf16[256,512]{1,0:T(8,128)(2,1)S(1)}, bf16[256,512]{1,0:T(8,128)(2,1)S(1)}, u32[]{:S(2)}, u32[]{:S(2)}) collective-permute-start(bf16[256,512]{1,0:T(8,128)(2,1)S(1)} %get-tuple-element.85), channel_id=1, source_target_pairs={{0,14},{1,15},{2,0},{3,1},{4,2},{5,3},{6,4},{7,5},{8,6},{9,7},{10,... | collective-permute-start | bytes 786440 | tf_op jit(solution)/shard_map/ppermute | solution.py:34
  90.4 3.3 %collective-permute-start.27 = (bf16[256,512]{1,0:T(8,128)(2,1)S(1)}, bf16[256,512]{1,0:T(8,128)(2,1)S(1)}, u32[]{:S(2)}, u32[]{:S(2)}) collective-permute-start(bf16[256,512]{1,0:T(8,128)(2,1)S(1)} %get-tuple-element.91), channel_id=1, source_target_pairs={{0,226},{1,227},{2,228},{3,229},{4,230},{5,231},{6,232},{7,233},{8... | collective-permute-start | bytes 786440 | tf_op jit(solution)/shard_map/ppermute | solution.py:58
  93.7 2.1 %collective-permute-start.28 = (bf16[256,512]{1,0:T(8,128)(2,1)S(1)}, bf16[256,512]{1,0:T(8,128)(2,1)S(1)}, u32[]{:S(2)}, u32[]{:S(2)}) collective-permute-start(bf16[256,512]{1,0:T(8,128)(2,1)S(1)} %get-tuple-element.92), channel_id=1, source_target_pairs={{0,238},{1,239},{2,224},{3,225},{4,226},{5,227},{6,228},{7,229},{8... | collective-permute-start | bytes 786440 | tf_op jit(solution)/shard_map/ppermute | solution.py:58
  95.7 0.8 collective-permute-done.23.refs_8_.refs_10_
  96.6 2.4 %shard_map.103 = (f32[512,512]{1,0:T(8,128)S(1)}, bf16[256,512]{1,0:T(8,128)(2,1)S(1)}, bf16[256,512]{1,0:T(8,128)(2,1)S(1)}) custom-call(s32[16]{0:T(128)S(1)} %stack.67.table, bf16[512,8192]{1,0:T(8,128)(2,1)S(1)} %get-tuple-element.49.hidden, bf16[512,1536]{1,0:T(8,128)(2,1)S(1)} %collective-permute-done.refs_0_.refs_1_.refs_2_.refs_3_, ...), custom_call_target="tpu_custom_call" | custom-call | flops 1610612736 | tf_op jit(solution)/shard_map/pallas_call | solution.py:209
  99.1 0.5 collective-permute-start.26
  99.6 3.6 %collective-permute-done.27.up = bf16[256,512]{1,0:T(8,128)(2,1)S(1)} collective-permute-done((bf16[256,512]{1,0:T(8,128)(2,1)S(1)}, bf16[256,512]{1,0:T(8,128)(2,1)S(1)}, u32[]{:S(2)}, u32[]{:S(2)}) %collective-permute-start.27) | collective-permute-done | bytes 262176 | tf_op jit(solution)/shard_map/ppermute | solution.py:58
  103.1 0.6 collective-permute-done.28.down
  103.8 1.2 %shard_map.105 = (f32[1,256,512]{2,1,0:T(8,128)}, f32[1,256]{1,0:T(1,128)}) custom-call(bf16[256,512]{1,0:T(8,128)(2,1)S(1)} %collective-permute-done.22.refs_8_.own, bf16[256,512]{1,0:T(8,128)(2,1)S(1)} %collective-permute-done.27.up, bf16[256,512]{1,0:T(8,128)(2,1)S(1)} %collective-permute-done.28.down, bf16[1,256]{1,0:T(2,128)(2,1)S(1)} %copy-done.5, ...), custom_call_target="tpu_custom_call" | custom-call | tf_op jit(solution)/shard_map/pallas_call | solution.py:351
  104.9 1.0 shard_map.104
  (46 shorter events, 1.3 us)
Async XLA Ops:
  0.7 1.0 copy-start
  1.7 0.7 copy-start.4
  2.6 1.0 copy-start.2
  8.8 3.5 %collective-permute-start = (bf16[512,1536]{1,0:T(8,128)(2,1)S(1)}, bf16[512,1536]{1,0:T(8,128)(2,1)S(1)}, u32[]{:S(2)}, u32[]{:S(2)}) collective-permute-start(bf16[512,1536]{1,0:T(8,128)(2,1)S(1)} %get-tuple-element.50), channel_id=1, source_target_pairs={{0,1},{1,0},{2,3},{3,2},{4,5},{5,4},{6,7},{7,6},{8,9},{9,8},{10,11... | collective-permute-start | bytes 4718600 | tf_op jit(solution)/shard_map/ppermute | solution.py:34
  8.9 5.8 %collective-permute-start.1 = (bf16[512,1024]{1,0:T(8,128)(2,1)S(1)}, bf16[512,1024]{1,0:T(8,128)(2,1)S(1)}, u32[]{:S(2)}, u32[]{:S(2)}) collective-permute-start(bf16[512,1024]{1,0:T(8,128)(2,1)S(1)} %get-tuple-element.51), channel_id=1, source_target_pairs={{0,1},{1,0},{2,3},{3,2},{4,5},{5,4},{6,7},{7,6},{8,9},{9,8},{10,11... | collective-permute-start | bytes 3145736 | tf_op jit(solution)/shard_map/ppermute | solution.py:34
  9.4 6.6 %collective-permute-start.2 = (bf16[512,1024]{1,0:T(8,128)(2,1)S(1)}, bf16[512,1024]{1,0:T(8,128)(2,1)S(1)}, u32[]{:S(2)}, u32[]{:S(2)}) collective-permute-start(bf16[512,1024]{1,0:T(8,128)(2,1)S(1)} %get-tuple-element.52), channel_id=1, source_target_pairs={{0,1},{1,0},{2,3},{3,2},{4,5},{5,4},{6,7},{7,6},{8,9},{9,8},{10,11... | collective-permute-start | bytes 3145736 | tf_op jit(solution)/shard_map/ppermute | solution.py:34
  9.5 7.3 %collective-permute-start.3 = (bf16[512,1024]{1,0:T(8,128)(2,1)S(1)}, bf16[512,1024]{1,0:T(8,128)(2,1)S(1)}, u32[]{:S(2)}, u32[]{:S(2)}) collective-permute-start(bf16[512,1024]{1,0:T(8,128)(2,1)S(1)} %get-tuple-element.53), channel_id=1, source_target_pairs={{0,1},{1,0},{2,3},{3,2},{4,5},{5,4},{6,7},{7,6},{8,9},{9,8},{10,11... | collective-permute-start | bytes 3145736 | tf_op jit(solution)/shard_map/ppermute | solution.py:34
  9.9 13.6 %collective-permute-start.7 = (bf16[256,512]{1,0:T(8,128)(2,1)S(1)}, bf16[256,512]{1,0:T(8,128)(2,1)S(1)}, u32[]{:S(2)}, u32[]{:S(2)}) collective-permute-start(bf16[256,512]{1,0:T(8,128)(2,1)S(1)} %shard_map.85.after), channel_id=1, source_target_pairs={{0,48},{1,49},{2,50},{3,51},{4,52},{5,53},{6,54},{7,55},{8,56},{9,... | collective-permute-start | bytes 786440 | tf_op jit(solution)/shard_map/ppermute | solution.py:58
  12.3 14.4 %collective-permute-start.4 = (bf16[256,512]{1,0:T(8,128)(2,1)S(1)}, bf16[256,512]{1,0:T(8,128)(2,1)S(1)}, u32[]{:S(2)}, u32[]{:S(2)}) collective-permute-start(bf16[256,512]{1,0:T(8,128)(2,1)S(1)} %shard_map.85.after), channel_id=1, source_target_pairs={{0,32},{1,33},{2,34},{3,35},{4,36},{5,37},{6,38},{7,39},{8,40},{9,... | collective-permute-start | bytes 786440 | tf_op jit(solution)/shard_map/ppermute | solution.py:58
  14.7 12.0 %collective-permute-start.5 = (bf16[1,256,512]{2,1,0:T(8,128)(2,1)S(1)}, bf16[1,256,512]{2,1,0:T(8,128)(2,1)S(1)}, u32[]{:S(2)}, u32[]{:S(2)}) collective-permute-start(bf16[1,256,512]{2,1,0:T(8,128)(2,1)S(1)} %get-tuple-element.56.refs_4_), channel_id=1, source_target_pairs={{0,16},{1,17},{2,18},{3,19},{4,20},{5,21},{6,22},{7,23},{8,24},{9,... | collective-permute-start | bytes 786440 | tf_op jit(solution)/shard_map/ppermute | solution.py:34
  26.7 16.6 %collective-permute-start.8 = (bf16[2,256,512]{2,1,0:T(8,128)(2,1)S(1)}, bf16[2,256,512]{2,1,0:T(8,128)(2,1)S(1)}, u32[]{:S(2)}, u32[]{:S(2)}) collective-permute-start(bf16[2,256,512]{2,1,0:T(8,128)(2,1)S(1)} %shard_map.90), channel_id=1, source_target_pairs={{0,16},{1,17},{2,18},{3,19},{4,20},{5,21},{6,22},{7,23},{8,24},{9,... | collective-permute-start | bytes 1572872 | tf_op jit(solution)/shard_map/ppermute | solution.py:34
  30.2 11.7 %collective-permute-start.6 = (bf16[320,512]{1,0:T(8,128)(2,1)S(1)}, bf16[320,512]{1,0:T(8,128)(2,1)S(1)}, u32[]{:S(2)}, u32[]{:S(2)}) collective-permute-start(bf16[320,512]{1,0:T(8,128)(2,1)S(1)} %get-tuple-element.58), channel_id=1, source_target_pairs={{0,2},{1,3},{2,4},{3,5},{4,6},{5,7},{6,8},{7,9},{8,10},{9,11},{10,... | collective-permute-start | bytes 983048 | tf_op jit(solution)/shard_map/ppermute | solution.py:34
  31.0 12.4 %collective-permute-start.9 = (bf16[320,512]{1,0:T(8,128)(2,1)S(1)}, bf16[320,512]{1,0:T(8,128)(2,1)S(1)}, u32[]{:S(2)}, u32[]{:S(2)}) collective-permute-start(bf16[320,512]{1,0:T(8,128)(2,1)S(1)} %get-tuple-element.61), channel_id=1, source_target_pairs={{0,14},{1,15},{2,0},{3,1},{4,2},{5,3},{6,4},{7,5},{8,6},{9,7},{10,... | collective-permute-start | bytes 983048 | tf_op jit(solution)/shard_map/ppermute | solution.py:34
  35.3 19.0 %collective-permute-start.11 = (bf16[2,256,512]{2,1,0:T(8,128)(2,1)S(1)}, bf16[2,256,512]{2,1,0:T(8,128)(2,1)S(1)}, u32[]{:S(2)}, u32[]{:S(2)}) collective-permute-start(bf16[2,256,512]{2,1,0:T(8,128)(2,1)S(1)} %shard_map.93), channel_id=1, source_target_pairs={{0,16},{1,17},{2,18},{3,19},{4,20},{5,21},{6,22},{7,23},{8,24},{9,... | collective-permute-start | bytes 1572872 | tf_op jit(solution)/shard_map/ppermute | solution.py:34
  36.6 14.8 %collective-permute-start.16 = (bf16[320,512]{1,0:T(8,128)(2,1)S(1)}, bf16[320,512]{1,0:T(8,128)(2,1)S(1)}, u32[]{:S(2)}, u32[]{:S(2)}) collective-permute-start(bf16[320,512]{1,0:T(8,128)(2,1)S(1)} %get-tuple-element.72), channel_id=1, source_target_pairs={{0,14},{1,15},{2,0},{3,1},{4,2},{5,3},{6,4},{7,5},{8,6},{9,7},{10,... | collective-permute-start | bytes 983048 | tf_op jit(solution)/shard_map/ppermute | solution.py:34
  41.8 9.5 %collective-permute-start.15 = (bf16[320,512]{1,0:T(8,128)(2,1)S(1)}, bf16[320,512]{1,0:T(8,128)(2,1)S(1)}, u32[]{:S(2)}, u32[]{:S(2)}) collective-permute-start(bf16[320,512]{1,0:T(8,128)(2,1)S(1)} %get-tuple-element.63.refs_6_.refs_1_), channel_id=1, source_target_pairs={{0,2},{1,3},{2,4},{3,5},{4,6},{5,7},{6,8},{7,9},{8,10},{9,11},{10,... | collective-permute-start | bytes 983048 | tf_op jit(solution)/shard_map/ppermute | solution.py:34
  43.5 33.0 %collective-permute-start.21 = (bf16[3,256,512]{2,1,0:T(8,128)(2,1)S(1)}, bf16[3,256,512]{2,1,0:T(8,128)(2,1)S(1)}, u32[]{:S(2)}, u32[]{:S(2)}) collective-permute-start(bf16[3,256,512]{2,1,0:T(8,128)(2,1)S(1)} %shard_map.100), channel_id=1, source_target_pairs={{0,16},{1,17},{2,18},{3,19},{4,20},{5,21},{6,22},{7,23},{8,24},{9,... | collective-permute-start | bytes 2359304 | tf_op jit(solution)/shard_map/ppermute | solution.py:34
  46.7 13.4 %collective-permute-start.12 = (bf16[384,512]{1,0:T(8,128)(2,1)S(1)}, bf16[384,512]{1,0:T(8,128)(2,1)S(1)}, u32[]{:S(2)}, u32[]{:S(2)}) collective-permute-start(bf16[384,512]{1,0:T(8,128)(2,1)S(1)} %get-tuple-element.67), channel_id=1, source_target_pairs={{0,14},{1,15},{2,0},{3,1},{4,2},{5,3},{6,4},{7,5},{8,6},{9,7},{10,... | collective-permute-start | bytes 1179656 | tf_op jit(solution)/shard_map/ppermute | solution.py:34
  51.4 13.3 %collective-permute-start.10 = (bf16[384,512]{1,0:T(8,128)(2,1)S(1)}, bf16[384,512]{1,0:T(8,128)(2,1)S(1)}, u32[]{:S(2)}, u32[]{:S(2)}) collective-permute-start(bf16[384,512]{1,0:T(8,128)(2,1)S(1)} %get-tuple-element.64.refs_6_.refs_1_), channel_id=1, source_target_pairs={{0,2},{1,3},{2,4},{3,5},{4,6},{5,7},{6,8},{7,9},{8,10},{9,11},{10,... | collective-permute-start | bytes 1179656 | tf_op jit(solution)/shard_map/ppermute | solution.py:34
  51.5 21.6 %collective-permute-start.17 = (bf16[384,512]{1,0:T(8,128)(2,1)S(1)}, bf16[384,512]{1,0:T(8,128)(2,1)S(1)}, u32[]{:S(2)}, u32[]{:S(2)}) collective-permute-start(bf16[384,512]{1,0:T(8,128)(2,1)S(1)} %get-tuple-element.73), channel_id=1, source_target_pairs={{0,2},{1,3},{2,4},{3,5},{4,6},{5,7},{6,8},{7,9},{8,10},{9,11},{10,... | collective-permute-start | bytes 1179656 | tf_op jit(solution)/shard_map/ppermute | solution.py:34
  54.3 18.8 %collective-permute-start.18 = (bf16[384,512]{1,0:T(8,128)(2,1)S(1)}, bf16[384,512]{1,0:T(8,128)(2,1)S(1)}, u32[]{:S(2)}, u32[]{:S(2)}) collective-permute-start(bf16[384,512]{1,0:T(8,128)(2,1)S(1)} %get-tuple-element.74), channel_id=1, source_target_pairs={{0,14},{1,15},{2,0},{3,1},{4,2},{5,3},{6,4},{7,5},{8,6},{9,7},{10,... | collective-permute-start | bytes 1179656 | tf_op jit(solution)/shard_map/ppermute | solution.py:34
  64.8 21.4 %collective-permute-start.14 = (bf16[384,512]{1,0:T(8,128)(2,1)S(1)}, bf16[384,512]{1,0:T(8,128)(2,1)S(1)}, u32[]{:S(2)}, u32[]{:S(2)}) collective-permute-start(bf16[384,512]{1,0:T(8,128)(2,1)S(1)} %get-tuple-element.70), channel_id=1, source_target_pairs={{0,14},{1,15},{2,0},{3,1},{4,2},{5,3},{6,4},{7,5},{8,6},{9,7},{10,... | collective-permute-start | bytes 1179656 | tf_op jit(solution)/shard_map/ppermute | solution.py:34
  64.9 21.3 %collective-permute-start.13 = (bf16[384,512]{1,0:T(8,128)(2,1)S(1)}, bf16[384,512]{1,0:T(8,128)(2,1)S(1)}, u32[]{:S(2)}, u32[]{:S(2)}) collective-permute-start(bf16[384,512]{1,0:T(8,128)(2,1)S(1)} %get-tuple-element.69.refs_6_), channel_id=1, source_target_pairs={{0,2},{1,3},{2,4},{3,5},{4,6},{5,7},{6,8},{7,9},{8,10},{9,11},{10,... | collective-permute-start | bytes 1179656 | tf_op jit(solution)/shard_map/ppermute | solution.py:34
  73.2 13.0 %collective-permute-start.19 = (bf16[384,512]{1,0:T(8,128)(2,1)S(1)}, bf16[384,512]{1,0:T(8,128)(2,1)S(1)}, u32[]{:S(2)}, u32[]{:S(2)}) collective-permute-start(bf16[384,512]{1,0:T(8,128)(2,1)S(1)} %get-tuple-element.75), channel_id=1, source_target_pairs={{0,2},{1,3},{2,4},{3,5},{4,6},{5,7},{6,8},{7,9},{8,10},{9,11},{10,... | collective-permute-start | bytes 1179656 | tf_op jit(solution)/shard_map/ppermute | solution.py:34
  73.3 12.9 %collective-permute-start.20 = (bf16[384,512]{1,0:T(8,128)(2,1)S(1)}, bf16[384,512]{1,0:T(8,128)(2,1)S(1)}, u32[]{:S(2)}, u32[]{:S(2)}) collective-permute-start(bf16[384,512]{1,0:T(8,128)(2,1)S(1)} %get-tuple-element.76), channel_id=1, source_target_pairs={{0,14},{1,15},{2,0},{3,1},{4,2},{5,3},{6,4},{7,5},{8,6},{9,7},{10,... | collective-permute-start | bytes 1179656 | tf_op jit(solution)/shard_map/ppermute | solution.py:34
  76.6 10.0 %collective-permute-start.22 = (bf16[256,512]{1,0:T(8,128)(2,1)S(1)}, bf16[256,512]{1,0:T(8,128)(2,1)S(1)}, u32[]{:S(2)}, u32[]{:S(2)}) collective-permute-start(bf16[256,512]{1,0:T(8,128)(2,1)S(1)} %shard_map.101), channel_id=1, source_target_pairs={{0,224},{1,225},{2,226},{3,227},{4,228},{5,229},{6,230},{7,231},{8... | collective-permute-start | bytes 786440 | tf_op jit(solution)/shard_map/ppermute | solution.py:58
  86.8 9.7 %collective-permute-start.23 = (bf16[256,512]{1,0:T(8,128)(2,1)S(1)}, bf16[256,512]{1,0:T(8,128)(2,1)S(1)}, u32[]{:S(2)}, u32[]{:S(2)}) collective-permute-start(bf16[256,512]{1,0:T(8,128)(2,1)S(1)} %get-tuple-element.84), channel_id=1, source_target_pairs={{0,2},{1,3},{2,4},{3,5},{4,6},{5,7},{6,8},{7,9},{8,10},{9,11},{10,... | collective-permute-start | bytes 786440 | tf_op jit(solution)/shard_map/ppermute | solution.py:34
  87.1 9.4 %collective-permute-start.24 = (bf16[256,512]{1,0:T(8,128)(2,1)S(1)}, bf16[256,512]{1,0:T(8,128)(2,1)S(1)}, u32[]{:S(2)}, u32[]{:S(2)}) collective-permute-start(bf16[256,512]{1,0:T(8,128)(2,1)S(1)} %get-tuple-element.85), channel_id=1, source_target_pairs={{0,14},{1,15},{2,0},{3,1},{4,2},{5,3},{6,4},{7,5},{8,6},{9,7},{10,... | collective-permute-start | bytes 786440 | tf_op jit(solution)/shard_map/ppermute | solution.py:34
  90.4 12.8 %collective-permute-start.27 = (bf16[256,512]{1,0:T(8,128)(2,1)S(1)}, bf16[256,512]{1,0:T(8,128)(2,1)S(1)}, u32[]{:S(2)}, u32[]{:S(2)}) collective-permute-start(bf16[256,512]{1,0:T(8,128)(2,1)S(1)} %get-tuple-element.91), channel_id=1, source_target_pairs={{0,226},{1,227},{2,228},{3,229},{4,230},{5,231},{6,232},{7,233},{8... | collective-permute-start | bytes 786440 | tf_op jit(solution)/shard_map/ppermute | solution.py:58
  93.7 10.1 %collective-permute-start.28 = (bf16[256,512]{1,0:T(8,128)(2,1)S(1)}, bf16[256,512]{1,0:T(8,128)(2,1)S(1)}, u32[]{:S(2)}, u32[]{:S(2)}) collective-permute-start(bf16[256,512]{1,0:T(8,128)(2,1)S(1)} %get-tuple-element.92), channel_id=1, source_target_pairs={{0,238},{1,239},{2,224},{3,225},{4,226},{5,227},{6,228},{7,229},{8... | collective-permute-start | bytes 786440 | tf_op jit(solution)/shard_map/ppermute | solution.py:58
  96.6 7.2 %copy-start.1 = (bf16[1,256,512]{2,1,0:T(8,128)(2,1)S(1)}, bf16[1,256,512]{2,1,0:T(8,128)(2,1)}, u32[]{:S(2)}) copy-start(bf16[1,256,512]{2,1,0:T(8,128)(2,1)} %weight.3) | copy-start | bytes 786436
  96.6 7.2 %copy-start.3 = (f32[1,256,512]{2,1,0:T(8,128)S(1)}, f32[1,256,512]{2,1,0:T(8,128)}, u32[]{:S(2)}) copy-start(f32[1,256,512]{2,1,0:T(8,128)} %grad_weight_in.1) | copy-start | bytes 1572868
  96.6 7.2 %copy-start.5 = (bf16[1,256]{1,0:T(2,128)(2,1)S(1)}, bf16[1,256]{1,0:T(2,128)(2,1)}, u32[]{:S(2)}) copy-start(bf16[1,256]{1,0:T(2,128)(2,1)} %gain.3) | copy-start | bytes 1540
  96.6 7.2 %copy-start.6 = (f32[1,256]{1,0:T(1,128)S(1)}, f32[1,256]{1,0:T(1,128)}, u32[]{:S(2)}) copy-start(f32[1,256]{1,0:T(1,128)} %grad_gain_in.1) | copy-start | bytes 3076
  99.0 6.0 %collective-permute-start.25 = (bf16[256,512]{1,0:T(8,128)(2,1)S(1)}, bf16[256,512]{1,0:T(8,128)(2,1)S(1)}, u32[]{:S(2)}, u32[]{:S(2)}) collective-permute-start(bf16[256,512]{1,0:T(8,128)(2,1)S(1)} %get-tuple-element.88), channel_id=1, source_target_pairs={{0,1},{1,0},{2,3},{3,2},{4,5},{5,4},{6,7},{7,6},{8,9},{9,8},{10,11... | collective-permute-start | bytes 786440 | tf_op jit(solution)/shard_map/ppermute | solution.py:34
  99.1 5.9 %collective-permute-start.26 = (bf16[256,512]{1,0:T(8,128)(2,1)S(1)}, bf16[256,512]{1,0:T(8,128)(2,1)S(1)}, u32[]{:S(2)}, u32[]{:S(2)}) collective-permute-start(bf16[256,512]{1,0:T(8,128)(2,1)S(1)} %get-tuple-element.89), channel_id=1, source_target_pairs={{0,1},{1,0},{2,3},{3,2},{4,5},{5,4},{6,7},{7,6},{8,9},{9,8},{10,11... | collective-permute-start | bytes 786440 | tf_op jit(solution)/shard_map/ppermute | solution.py:34

commit v9 on v8

--- a/solution.py
+++ b/solution.py
@@ -15,7 +15,9 @@
 OFFSETS = (4, 3, -3, 2, -2, 1, -1, 0)
 GROUPS = ((1,), (2, 2, 3))
 FIRST = sum(GROUPS[0])
+SENT_AFTER = ((1, 0), (1, 1), (2, 0))
 SWAPS = (2, 2, 2, 2)
+PIECES = 4
 VMEM_LIMIT = 16 * 1024 * 1024
 LOAD_LIMIT = 36 * 1024 * 1024
 
@@ -173,10 +175,11 @@
     return outs[:len(groups)], outs[len(groups):]
 
 
-def project_kernel(offsets, rows, more, extra, width, table, hidden, *refs):
+def project_kernel(offsets, rows, more, final, extra, width, table, hidden, *refs):
     visits, refs = refs[:len(SWAPS)], refs[len(SWAPS):]
-    outs = refs[-3:] if more else refs[-2:]
-    start = refs[-5 - extra:-3 - extra] if more else None
+    count = 1 + PIECES if final else 2
+    outs = refs[-count:]
+    start = refs[-count - extra - 2:-count - extra]
     refs = iter(refs)
     weights = [[next(refs)[first:first + count] for first, count in group] for group in rows]
     totals = [ref[...] for ref in start] if more else []
@@ -188,15 +191,15 @@
         products = [jnp.dot(rows, weight, preferred_element_type=F32) for rows in (own, visitors)]
         totals = [t + p for t, p in zip(totals, products)] if totals else products
     outs[0][...] = totals[0]
-    if more:
-        half = outs[1].shape[0]
-        outs[1][...] = totals[1][:half].astype(BF16)
-        outs[2][...] = totals[1][half:].astype(BF16)
+    if final:
+        part = outs[1].shape[0]
+        for i, out in enumerate(outs[1:]):
+            out[...] = totals[1][i * part:(i + 1) * part].astype(BF16)
     else:
         outs[1][...] = totals[1]
 
 
-def project(table, hidden, visits, weights, start, after, width):
+def project(table, hidden, visits, weights, start, after, width, final=False):
     tokens = hidden.shape[0]
     arrays = [w for group in weights.values() for w, _, _ in group]
     rows = [[part[1:] for part in group] for group in weights.values()]
@@ -204,10 +207,10 @@
     size = values * sum(count for group in rows for _, count in group)
     more = [] if start is None else list(start)
     whole = jax.ShapeDtypeStruct((tokens, values), F32)
-    half = jax.ShapeDtypeStruct((tokens // 2, values), BF16)
-    out_shape = [whole, half, half] if more else [whole, whole]
+    part = jax.ShapeDtypeStruct((tokens // PIECES, values), BF16)
+    out_shape = [whole, *[part] * PIECES] if final else [whole, whole]
     return pl.pallas_call(
-        functools.partial(project_kernel, tuple(weights), rows, bool(more), len(after), width),
+        functools.partial(project_kernel, tuple(weights), rows, bool(more), final, len(after), width),
         in_specs=[IN_SMEM] + [IN_VMEM] * (1 + len(SWAPS) + len(arrays) + len(more)) + [ANYWHERE] * len(after),
         out_specs=[IN_VMEM] * len(out_shape),
         out_shape=out_shape,
@@ -247,28 +250,29 @@
     return sum(t.astype(F32) for t in terms).astype(BF16)
 
 
-def begin(layer, far, ring, after):
+def begin(layers, far, ring, after):
     keep, arrived, place = far
-    width, values = layer.shape
+    width, values = layers[0].shape
     part = width // 4
 
-    def kernel(layer, keep, arrived, up, down):
-        for i, out in enumerate((up, down)):
+    def kernel(layer_up, layer_down, keep, arrived, up, down):
+        for i, (layer, out) in enumerate(((layer_up, up), (layer_down, down))):
             rows = slice((2 * ring + i) * part, (2 * ring + i + 1) * part)
             out[:width] = layer[...]
             out[width:] = summed((keep[rows], arrived[place, rows]))
 
-    return small(kernel, [layer, keep, arrived], after, [(width + part, values)] * 2)
+    return small(kernel, [*layers, keep, arrived], after, [(width + part, values)] * 2)
 
 
 def advance(up, down, above, below, ring, width, step, after):
     values = up.shape[1]
     half = width // 2
     rows = slice(ring * half, (ring + 1) * half)
+    layer_rows = width if step == 1 else half
 
     def kernel(up, keep_up, arrived_up, down, keep_down, arrived_down, next_up, next_down):
-        next_up[:width] = up[:width]
-        next_down[:width] = down[:width]
+        next_up[:layer_rows] = up[:layer_rows]
+        next_down[:layer_rows] = down[width - layer_rows:width]
         mine_up = keep_up[rows].astype(F32) + arrived_up[above[2], rows].astype(F32)
         mine_down = keep_down[rows].astype(F32) + arrived_down[below[2], rows].astype(F32)
         came_up, came_down = up[width:].astype(F32), down[width:].astype(F32)
@@ -279,26 +283,23 @@
         else:
             mine_up += came_up
             mine_down += came_down
-        next_up[width:] = mine_up.astype(BF16)
-        next_down[width:] = mine_down.astype(BF16)
-
-    return small(kernel, [up, *above[:2], down, *below[:2]], after, [(width + half, values)] * 2)
-
-
-def nearest(loads, above, below, width, after):
-    half = width // 2
+        next_up[layer_rows:] = mine_up.astype(BF16)
+        next_down[layer_rows:] = mine_down.astype(BF16)
+
+    return small(kernel, [up, *above[:2], down, *below[:2]], after, [(layer_rows + half, values)] * 2)
+
+
+def nearest(loads, above, below, after):
+    half = above[0].shape[0] // 2
 
     def kernel(*refs):
         for i, place in enumerate((above[2], below[2])):
             keep, arrived = refs[4 + 2 * i:6 + 2 * i]
-            sums, layers = refs[8 + i], refs[10 + i]
             for ring in (0, 1):
-                load = refs[2 * ring + i]
                 rows = slice(ring * half, (ring + 1) * half)
-                sums[rows] = summed((keep[rows], arrived[place, rows], load[width:]))
-                layers[rows] = load[i * half:(i + 1) * half]
-
-    return small(kernel, [*loads, *above[:2], *below[:2]], after, [above[0].shape] * 4)
+                refs[8 + i][rows] = summed((keep[rows], arrived[place, rows], refs[2 * ring + i][half:]))
+
+    return small(kernel, [*loads, *above[:2], *below[:2]], after, [above[0].shape] * 2)
 
 
 def own_part(own):
@@ -310,13 +311,15 @@
     return small(kernel, [keep, arrived], [], [keep.shape])[0]
 
 
-def scaled_values(product, upper, lower, scale):
-    def kernel(product, upper, lower, scale, out):
-        half = upper.shape[0]
-        for arrived, rows in ((upper, slice(0, half)), (lower, slice(half, 2 * half))):
-            out[rows, :] = ((product[rows, :] + arrived[...].astype(F32)) * scale[rows, :]).astype(BF16)
-
-    return small(kernel, [product, upper, lower, scale], [], [product.shape])[0]
+def scaled_values(product, pieces, scale):
+    def kernel(product, *refs):
+        arrived, scale, out = refs[:PIECES], refs[-2], refs[-1]
+        part = arrived[0].shape[0]
+        for i, piece in enumerate(arrived):
+            rows = slice(i * part, (i + 1) * part)
+            out[rows, :] = ((product[rows, :] + piece[...].astype(F32)) * scale[rows, :]).astype(BF16)
+
+    return small(kernel, [product, *pieces, scale], [], [product.shape])[0]
 
 
 def diagonal(width):
@@ -381,43 +384,46 @@
             mine[OFFSETS[first + j]] = (keeps[first + j], arrived, j)
         return arrived
 
-    arrived = send_group(sends_1[0], 0, [])
-    send_group(sends_2[0], 1, [*layer, arrived])
+    layer = tie(layer, [keeps_2[-1]])
+    send_group(sends_1[0], 0, layer)
 
     weights = {0: [(layer[0], 0, width), (layer[1], 0, width)]}
-    loads = [begin(layer[ring], mine[4], ring, [keeps_2[-1]]) for ring in (0, 1)]
-    send_group(sends_2[1], 2, [loads[1][0]])
-    for step in (1, 2, 3):
-        off = 4 - step
-        last = [loads[1][0]] if step == 1 else []
+    loads = [(layer[ring], layer[ring]) for ring in (0, 1)]
+    for step in (1, 2, 3, 4):
         weights[step], weights[-step] = [], []
+        moved = [(along_z(load[0], 1), along_z(load[1], -1)) for load in loads]
+        last = [*moved[1]] if step == 1 else []
         for ring in (0, 1):
-            up, down = along_z(loads[ring][0], 1), along_z(loads[ring][1], -1)
-            if step == 3 and ring == 0:
-                near = {off: weights[off] for off in (0, -1, 1, -2, 2)}
-                products = project(table, held, visits, near, None, last, width)
-            if step == 3:
-                up, down = tie([up, down], [*last, products[0]] if ring else last)
-            weights[-step].append((up, 0, width))
-            weights[step].append((down, 0, width))
-            if step < 3:
-                loads[ring] = advance(up, down, mine[off], mine[-off], ring, width, step, last)
+            up, down = moved[ring]
+            if step == 4:
+                if ring == 1:
+                    middle = {off: weights[off] for off in (-3, 3)}
+                    products = project(table, held, visits, middle, products, last, width)
+                    last = [*last, products[0]]
+                up, down = tie([up, down], last)
+                weights[step] += [(up, 0, width // 2), (down, 0, width // 2)]
+                loads[ring] = [up, down]
             else:
-                loads[ring] = [up, down]
+                weights[-step].append((up, 0, width))
+                weights[step].append((down, 0, width))
+                if (step, ring) == (3, 1):
+                    near = {off: weights[off] for off in (0, -1, 1, -2, 2)}
+                    products = project(table, held, visits, near, None, [], width)
+                    last = [*last, products[0]]
+                if step == 1:
+                    loads[ring] = begin((up, down), mine[4], ring, last)
+                else:
+                    loads[ring] = advance(up, down, mine[5 - step], mine[step - 5], ring, width, step - 1, last)
             last = [loads[ring][0]]
-            if (step, ring) == (1, 0):
-                send_group(sends_2[2], 3, last)
+            if (step, ring) in SENT_AFTER:
+                group = SENT_AFTER.index((step, ring))
+                send_group(sends_2[group], group + 1, last)
 
     own = along_blk(own_part(mine[0]), -1, 0)
-    sum_up, sum_down, layer_up, layer_down = nearest([*loads[0], *loads[1]], mine[1], mine[-1], width, [own])
+    sum_up, sum_down = nearest([*loads[0], *loads[1]], mine[1], mine[-1], [own])
     totals = [own, along_blk(sum_up, -1, 0, 1), along_blk(sum_down, -1, 0, -1)]
-    up, down = along_z(layer_up, 1), along_z(layer_down, -1)
-    half = width // 2
-    weights[4] = [(far, ring * half, half) for ring in (0, 1) for far in (up, down)]
-
-    far = {off: weights[off] for off in (-3, 3, 4)}
-    product, *products = project(table, held, visits, far, products, [], width)
-    values = scaled_values(product, *(swap_core(p) for p in products), scale)
+    product, *products = project(table, held, visits, {4: weights[4]}, products, [sum_up], width, final=True)
+    values = scaled_values(product, [swap_core(p) for p in products], scale)
 
     return values, *finish(totals, gain, value_weight, grad_weight_in, grad_gain_in)
 

time: 107 us -> 123 us (1.15); the launches traced: 106 us -> 121 us
  waiting for transfers between devices: 29.7 us -> 55 us
  starting transfers between devices: 52.7 us -> 41.3 us
    ppermute x24 -> x28, waiting for transfers between devices: 19.7 us -> 40.1 us  [move(): return lax.ppermute(value, ('x', 'z', 'core'), pairs)]
    ppermute x5, starting transfers between devices: 13.3 us -> 7.27 us  [along_blk(): return lax.ppermute(value, ('blk', 'x', 'z', 'core'), pairs)]
    ppermute x24 -> x28, starting transfers between devices: 39.4 us -> 34.1 us  [move(): return lax.ppermute(value, ('x', 'z', 'core'), pairs)]
    ppermute x5, waiting for transfers between devices: 9.99 us -> 15 us  [along_blk(): return lax.ppermute(value, ('blk', 'x', 'z', 'core'), pairs)]
    pallas_call x2 -> x3, Pallas kernels: 5.77 us -> 6.51 us  [project(): pl.pallas_call(functools.partial(project_kernel, tuple(weights), rows, bo...]
  transfers between devices with their start and end apart: 29 -> 33, of which waited for: 14 -> 20; matrix products, arithmetic and copies ran while one was open for 0% -> 0% of each run, Pallas kernels for 13% -> 10%
where the time goes in v9:
time: 123 us; the launch traced here: 121 us
  waiting for transfers between devices  55 us (45%)
  starting transfers between devices  41.3 us (34%)
  Pallas kernels  20.5 us (17%)
  local copies, waits for them, and re-layouts  2.79 us (2%)
    ppermute x28, waiting for transfers between devices, move(): return lax.ppermute(value, ('x', 'z', 'core'), pairs)  40.1 us
    ppermute x28, starting transfers between devices, move(): return lax.ppermute(value, ('x', 'z', 'core'), pairs)  34.1 us
    ppermute x5, waiting for transfers between devices, along_blk(): return lax.ppermute(value, ('blk', 'x', 'z', 'core'), pairs)  15 us
    ppermute x5, starting transfers between devices, along_blk(): return lax.ppermute(value, ('blk', 'x', 'z', 'core'), pairs)  7.27 us
    pallas_call x3, Pallas kernels, project(): pl.pallas_call(functools.partial(project_kernel, tuple(weights), rows, bo...  6.51 us
    pallas_call x2, Pallas kernels, gradient(): pl.pallas_call(functools.partial(gradient_kernel, base, groups, width), i...  5.74 us
    pallas_call x1, Pallas kernels, prepare(): pl.pallas_call(functools.partial(prepare_kernel, width, steps), in_specs=...  5.12 us
    unnamed x14, local copies, waits for them, and re-layouts  2.69 us
  transfers between devices with their start and end apart: 33, of which 20 were waited for; matrix products, arithmetic and copies ran while one was open for 0% of the time, Pallas kernels for 10%

profile of v9, /device:TPU:4, one launch (start us, length us, event | category | flops | bytes accessed | tf_op | source)
XLA Modules:
  0.0 120.6 jit_solution(17187363488291686391)
XLA Ops:
  0.7 0.9 copy-done
  1.7 0.7 copy-done.4
  2.6 1.0 copy-done.2
  3.6 5.1 %shard_map.86 = (bf16[512,8192]{1,0:T(8,128)(2,1)S(1)}, f32[512,1]{1,0:T(8,128)S(1)}, bf16[512,512]{1,0:T(8,128)(2,1)S(1)}, bf16[512,1536]{1,0:T(8,128)(2,1)S(1)...) custom-call(s32[16]{0:T(128)S(1)} %stack.67.table, ...), custom_call_target="tpu_custom_call" | custom-call | bytes 16777216 | tf_op jit(solution)/shard_map/pallas_call | solution.py:124
  8.9 0.5 collective-permute-start.1
  9.9 0.5 collective-permute-start.5
  10.4 1.9 %collective-permute-done.refs_0_.refs_1_.refs_2_.refs_3_ = bf16[512,1536]{1,0:T(8,128)(2,1)S(1)} collective-permute-done((bf16[512,1536]{1,0:T(8,128)(2,1)S(1)}, bf16[512,1536]{1,0:T(8,128)(2,1)S(1)}, u32[]{:S(2)}, u32[]{:S(2)}) %collective-permute-start) | collective-permute-done | bytes 1572896 | tf_op jit(solution)/shard_map/ppermute | solution.py:36
  12.3 1.2 collective-permute-start.4
  13.5 1.2 %shard_map.87 = (bf16[1,256,512]{2,1,0:T(8,128)(2,1)S(1)}, bf16[256,512]{1,0:T(8,128)(2,1)S(1)}) custom-call(s32[16]{0:T(128)S(1)} %stack.67.table, bf16[512,8192]{1,0:T(8,128)(2,1)S(1)} %get-tuple-element.53.hidden, bf16[512,512]{1,0:T(8,128)(2,1)S(1)} %get-tuple-element.58.cot_t.refs_4_, ...), custom_call_target="tpu_custom_call" | custom-call | bytes 512 | tf_op jit(solution)/shard_map/pallas_call | solution.py:166
  14.7 0.5 collective-permute-done.2.refs_2_
  15.3 1.5 %collective-permute-done.3.refs_3_ = bf16[512,1024]{1,0:T(8,128)(2,1)S(1)} collective-permute-done((bf16[512,1024]{1,0:T(8,128)(2,1)S(1)}, bf16[512,1024]{1,0:T(8,128)(2,1)S(1)}, u32[]{:S(2)}, u32[]{:S(2)}) %collective-permute-start.3) | collective-permute-done | bytes 1048608 | tf_op jit(solution)/shard_map/ppermute | solution.py:36
  16.8 4.5 %shard_map.88 = (bf16[2,256,512]{2,1,0:T(8,128)(2,1)S(1)}, bf16[2,256,512]{2,1,0:T(8,128)(2,1)S(1)}, bf16[3,256,512]{2,1,0:T(8,128)(2,1)S(1)}, bf16[256,512]{1,0...) custom-call(s32[16]{0:T(128)S(1)} %stack.67.table, ...), custom_call_target="tpu_custom_call" | custom-call | bytes 512 | tf_op jit(solution)/shard_map/pallas_call | solution.py:166
  21.3 2.2 %collective-permute-done.5.refs_1_ = bf16[256,512]{1,0:T(8,128)(2,1)S(1)} collective-permute-done((bf16[256,512]{1,0:T(8,128)(2,1)S(1)}, bf16[256,512]{1,0:T(8,128)(2,1)S(1)}, u32[]{:S(2)}, u32[]{:S(2)}) %collective-permute-start.5) | collective-permute-done | bytes 262176 | tf_op jit(solution)/shard_map/ppermute | solution.py:60
  23.5 2.4 %collective-permute-done.4.refs_0_ = bf16[256,512]{1,0:T(8,128)(2,1)S(1)} collective-permute-done((bf16[256,512]{1,0:T(8,128)(2,1)S(1)}, bf16[256,512]{1,0:T(8,128)(2,1)S(1)}, u32[]{:S(2)}, u32[]{:S(2)}) %collective-permute-start.4) | collective-permute-done | bytes 262176 | tf_op jit(solution)/shard_map/ppermute | solution.py:60
  25.9 3.6 %collective-permute-start.8 = (bf16[1,256,512]{2,1,0:T(8,128)(2,1)S(1)}, bf16[1,256,512]{2,1,0:T(8,128)(2,1)S(1)}, u32[]{:S(2)}, u32[]{:S(2)}) collective-permute-start(bf16[1,256,512]{2,1,0:T(8,128)(2,1)S(1)} %shard_map.90), channel_id=1, source_target_pairs={{0,16},{1,17},{2,18},{3,19},{4,20},{5,21},{6,22},{7,23},{8,24},{9,... | collective-permute-start | bytes 786440 | tf_op jit(solution)/shard_map/ppermute | solution.py:36
  29.5 4.1 %collective-permute-start.7 = (bf16[256,512]{1,0:T(8,128)(2,1)S(1)}, bf16[256,512]{1,0:T(8,128)(2,1)S(1)}, u32[]{:S(2)}, u32[]{:S(2)}) collective-permute-start(bf16[256,512]{1,0:T(8,128)(2,1)S(1)} %get-tuple-element.61.refs_1_.refs_4_), channel_id=1, source_target_pairs={{0,14},{1,15},{2,0},{3,1},{4,2},{5,3},{6,4},{7,5},{8,6},{9,7},{10,... | collective-permute-start | bytes 786440 | tf_op jit(solution)/shard_map/ppermute | solution.py:36
  33.6 3.2 %collective-permute-start.10 = (bf16[256,512]{1,0:T(8,128)(2,1)S(1)}, bf16[256,512]{1,0:T(8,128)(2,1)S(1)}, u32[]{:S(2)}, u32[]{:S(2)}) collective-permute-start(bf16[256,512]{1,0:T(8,128)(2,1)S(1)} %get-tuple-element.63.refs_2_.refs_5_), channel_id=1, source_target_pairs={{0,14},{1,15},{2,0},{3,1},{4,2},{5,3},{6,4},{7,5},{8,6},{9,7},{10,... | collective-permute-start | bytes 786440 | tf_op jit(solution)/shard_map/ppermute | solution.py:36
  36.9 3.5 %collective-permute-done.7.refs_1_.refs_8_ = bf16[256,512]{1,0:T(8,128)(2,1)S(1)} collective-permute-done((bf16[256,512]{1,0:T(8,128)(2,1)S(1)}, bf16[256,512]{1,0:T(8,128)(2,1)S(1)}, u32[]{:S(2)}, u32[]{:S(2)}) %collective-permute-start.7) | collective-permute-done | bytes 262176 | tf_op jit(solution)/shard_map/ppermute | solution.py:36
  40.4 3.7 %collective-permute-done.6.refs_0_.refs_6_ = bf16[256,512]{1,0:T(8,128)(2,1)S(1)} collective-permute-done((bf16[256,512]{1,0:T(8,128)(2,1)S(1)}, bf16[256,512]{1,0:T(8,128)(2,1)S(1)}, u32[]{:S(2)}, u32[]{:S(2)}) %collective-permute-start.6) | collective-permute-done | bytes 262176 | tf_op jit(solution)/shard_map/ppermute | solution.py:36
  44.1 3.0 %collective-permute-done.9.refs_4_.refs_0_.refs_7_ = bf16[256,512]{1,0:T(8,128)(2,1)S(1)} collective-permute-done((bf16[256,512]{1,0:T(8,128)(2,1)S(1)}, bf16[256,512]{1,0:T(8,128)(2,1)S(1)}, u32[]{:S(2)}, u32[]{:S(2)}) %collective-permute-start.9) | collective-permute-done | bytes 262176 | tf_op jit(solution)/shard_map/ppermute | solution.py:36
  47.2 2.0 %collective-permute-start.12 = (bf16[2,256,512]{2,1,0:T(8,128)(2,1)S(1)}, bf16[2,256,512]{2,1,0:T(8,128)(2,1)S(1)}, u32[]{:S(2)}, u32[]{:S(2)}) collective-permute-start(bf16[2,256,512]{2,1,0:T(8,128)(2,1)S(1)} %shard_map.92), channel_id=1, source_target_pairs={{0,16},{1,17},{2,18},{3,19},{4,20},{5,21},{6,22},{7,23},{8,24},{9,... | collective-permute-start | bytes 1572872 | tf_op jit(solution)/shard_map/ppermute | solution.py:36
  49.5 1.7 %collective-permute-start.11 = (bf16[320,512]{1,0:T(8,128)(2,1)S(1)}, bf16[320,512]{1,0:T(8,128)(2,1)S(1)}, u32[]{:S(2)}, u32[]{:S(2)}) collective-permute-start(bf16[320,512]{1,0:T(8,128)(2,1)S(1)} %get-tuple-element.64.refs_1_.refs_4_), channel_id=1, source_target_pairs={{0,2},{1,3},{2,4},{3,5},{4,6},{5,7},{6,8},{7,9},{8,10},{9,11},{10,... | collective-permute-start | bytes 983048 | tf_op jit(solution)/shard_map/ppermute | solution.py:36
  51.3 1.6 %collective-permute-start.20 = (bf16[320,512]{1,0:T(8,128)(2,1)S(1)}, bf16[320,512]{1,0:T(8,128)(2,1)S(1)}, u32[]{:S(2)}, u32[]{:S(2)}) collective-permute-start(bf16[320,512]{1,0:T(8,128)(2,1)S(1)} %get-tuple-element.79), channel_id=1, source_target_pairs={{0,14},{1,15},{2,0},{3,1},{4,2},{5,3},{6,4},{7,5},{8,6},{9,7},{10,... | collective-permute-start | bytes 983048 | tf_op jit(solution)/shard_map/ppermute | solution.py:36
  52.9 1.6 %collective-permute-start.15 = (bf16[2,256,512]{2,1,0:T(8,128)(2,1)S(1)}, bf16[2,256,512]{2,1,0:T(8,128)(2,1)S(1)}, u32[]{:S(2)}, u32[]{:S(2)}) collective-permute-start(bf16[2,256,512]{2,1,0:T(8,128)(2,1)S(1)} %shard_map.95), channel_id=1, source_target_pairs={{0,16},{1,17},{2,18},{3,19},{4,20},{5,21},{6,22},{7,23},{8,24},{9,... | collective-permute-start | bytes 1572872 | tf_op jit(solution)/shard_map/ppermute | solution.py:36
  54.5 5.4 %collective-permute-done.13.refs_3_.refs_12_ = bf16[320,512]{1,0:T(8,128)(2,1)S(1)} collective-permute-done((bf16[320,512]{1,0:T(8,128)(2,1)S(1)}, bf16[320,512]{1,0:T(8,128)(2,1)S(1)}, u32[]{:S(2)}, u32[]{:S(2)}) %collective-permute-start.13) | collective-permute-done | bytes 327712 | tf_op jit(solution)/shard_map/ppermute | solution.py:36
  59.8 3.8 %collective-permute-done.12.refs_2_.refs_5_ = bf16[2,256,512]{2,1,0:T(8,128)(2,1)S(1)} collective-permute-done((bf16[2,256,512]{2,1,0:T(8,128)(2,1)S(1)}, bf16[2,256,512]{2,1,0:T(8,128)(2,1)S(1)}, u32[]{:S(2)}, u32[]{:S(2)}) %collective-permute-start.12) | collective-permute-done | bytes 524320 | tf_op jit(solution)/shard_map/ppermute | solution.py:36
  63.8 2.0 %collective-permute-start.25 = (bf16[3,256,512]{2,1,0:T(8,128)(2,1)S(1)}, bf16[3,256,512]{2,1,0:T(8,128)(2,1)S(1)}, u32[]{:S(2)}, u32[]{:S(2)}) collective-permute-start(bf16[3,256,512]{2,1,0:T(8,128)(2,1)S(1)} %shard_map.103), channel_id=1, source_target_pairs={{0,16},{1,17},{2,18},{3,19},{4,20},{5,21},{6,22},{7,23},{8,24},{9,... | collective-permute-start | bytes 2359304 | tf_op jit(solution)/shard_map/ppermute | solution.py:36
  65.8 3.2 %collective-permute-start.16 = (bf16[384,512]{1,0:T(8,128)(2,1)S(1)}, bf16[384,512]{1,0:T(8,128)(2,1)S(1)}, u32[]{:S(2)}, u32[]{:S(2)}) collective-permute-start(bf16[384,512]{1,0:T(8,128)(2,1)S(1)} %get-tuple-element.73), channel_id=1, source_target_pairs={{0,14},{1,15},{2,0},{3,1},{4,2},{5,3},{6,4},{7,5},{8,6},{9,7},{10,... | collective-permute-start | bytes 1179656 | tf_op jit(solution)/shard_map/ppermute | solution.py:36
  69.0 8.6 %collective-permute-done.19.refs_0_.refs_11_ = bf16[320,512]{1,0:T(8,128)(2,1)S(1)} collective-permute-done((bf16[320,512]{1,0:T(8,128)(2,1)S(1)}, bf16[320,512]{1,0:T(8,128)(2,1)S(1)}, u32[]{:S(2)}, u32[]{:S(2)}) %collective-permute-start.19) | collective-permute-done | bytes 327712 | tf_op jit(solution)/shard_map/ppermute | solution.py:36
  77.9 3.2 %collective-permute-start.22 = (bf16[384,512]{1,0:T(8,128)(2,1)S(1)}, bf16[384,512]{1,0:T(8,128)(2,1)S(1)}, u32[]{:S(2)}, u32[]{:S(2)}) collective-permute-start(bf16[384,512]{1,0:T(8,128)(2,1)S(1)} %get-tuple-element.81), channel_id=1, source_target_pairs={{0,14},{1,15},{2,0},{3,1},{4,2},{5,3},{6,4},{7,5},{8,6},{9,7},{10,... | collective-permute-start | bytes 1179656 | tf_op jit(solution)/shard_map/ppermute | solution.py:36
  81.1 5.0 %collective-permute-done.14.refs_0_.refs_4_ = bf16[384,512]{1,0:T(8,128)(2,1)S(1)} collective-permute-done((bf16[384,512]{1,0:T(8,128)(2,1)S(1)}, bf16[384,512]{1,0:T(8,128)(2,1)S(1)}, u32[]{:S(2)}, u32[]{:S(2)}) %collective-permute-start.14) | collective-permute-done | bytes 393248 | tf_op jit(solution)/shard_map/ppermute | solution.py:36
  86.3 2.0 %collective-permute-start.17 = (bf16[256,512]{1,0:T(8,128)(2,1)S(1)}, bf16[256,512]{1,0:T(8,128)(2,1)S(1)}, u32[]{:S(2)}, u32[]{:S(2)}) collective-permute-start(bf16[256,512]{1,0:T(8,128)(2,1)S(1)} %get-tuple-element.75.refs_6_), channel_id=1, source_target_pairs={{0,2},{1,3},{2,4},{3,5},{4,6},{5,7},{6,8},{7,9},{8,10},{9,11},{10,... | collective-permute-start | bytes 786440 | tf_op jit(solution)/shard_map/ppermute | solution.py:36
  88.3 3.4 %shard_map.99 = (f32[512,512]{1,0:T(8,128)S(1)}, f32[512,512]{1,0:T(8,128)S(1)}) custom-call(s32[16]{0:T(128)S(1)} %stack.67.table, bf16[512,8192]{1,0:T(8,128)(2,1)S(1)} %get-tuple-element.53.hidden, bf16[512,1536]{1,0:T(8,128)(2,1)S(1)} %collective-permute-done.refs_0_.refs_1_.refs_2_.refs_3_, bf16[512,1024]{1,0:T(8,128)(2,1)S(1)} %collective-permute-done.1.refs_1_, ...), custom_call_target="tpu_custom_call" | custom-call | flops 2684354560 | tf_op jit(solution)/shard_map/pallas_call | solution.py:212
  91.7 0.7 collective-permute-done.21.refs_0_.refs_5_
  92.8 3.2 %collective-permute-start.24 = (bf16[256,512]{1,0:T(8,128)(2,1)S(1)}, bf16[256,512]{1,0:T(8,128)(2,1)S(1)}, u32[]{:S(2)}, u32[]{:S(2)}) collective-permute-start(bf16[256,512]{1,0:T(8,128)(2,1)S(1)} %get-tuple-element.84), channel_id=1, source_target_pairs={{0,14},{1,15},{2,0},{3,1},{4,2},{5,3},{6,4},{7,5},{8,6},{9,7},{10,... | collective-permute-start | bytes 786440 | tf_op jit(solution)/shard_map/ppermute | solution.py:36
  96.1 1.3 %collective-permute-start.26 = (bf16[256,512]{1,0:T(8,128)(2,1)S(1)}, bf16[256,512]{1,0:T(8,128)(2,1)S(1)}, u32[]{:S(2)}, u32[]{:S(2)}) collective-permute-start(bf16[256,512]{1,0:T(8,128)(2,1)S(1)} %shard_map.104), channel_id=1, source_target_pairs={{0,224},{1,225},{2,226},{3,227},{4,228},{5,229},{6,230},{7,231},{8... | collective-permute-start | bytes 786440 | tf_op jit(solution)/shard_map/ppermute | solution.py:60
  97.4 1.8 %shard_map.101 = (f32[512,512]{1,0:T(8,128)S(1)}, f32[512,512]{1,0:T(8,128)S(1)}) custom-call(s32[16]{0:T(128)S(1)} %stack.67.table, bf16[512,8192]{1,0:T(8,128)(2,1)S(1)} %get-tuple-element.53.hidden, bf16[512,1536]{1,0:T(8,128)(2,1)S(1)} %collective-permute-done.refs_0_.refs_1_.refs_2_.refs_3_, bf16[512,1024]{1,0:T(8,128)(2,1)S(1)} %collective-permute-done.1.refs_1_, ...), custom_call_target="tpu_custom_call" | custom-call | flops 1073741824 | tf_op jit(solution)/shard_map/pallas_call | solution.py:212
  99.3 1.2 collective-permute-done.23.refs_0_
  100.4 2.2 %collective-permute-done.26.refs_8_.own = bf16[256,512]{1,0:T(8,128)(2,1)S(1)} collective-permute-done((bf16[256,512]{1,0:T(8,128)(2,1)S(1)}, bf16[256,512]{1,0:T(8,128)(2,1)S(1)}, u32[]{:S(2)}, u32[]{:S(2)}) %collective-permute-start.26) | collective-permute-done | bytes 262176 | tf_op jit(solution)/shard_map/ppermute | solution.py:60
  102.8 1.3 %shard_map.106 = (f32[512,512]{1,0:T(8,128)S(1)}, bf16[128,512]{1,0:T(8,128)(2,1)S(1)}, bf16[128,512]{1,0:T(8,128)(2,1)S(1)}, bf16[128,512]{1,0:T(8,128)(2,1)S(1)}, bf16[128,512]{1,0:T(8,128)(2,1)S(1)}) custom-call(s32[16]{0:T(128)S(1)} %stack.67.table, bf16[512,8192]{1,0:T(8,128)(2,1)S(1)} %get-tuple-element.53.hidden, ...), custom_call_target="tpu_custom_call" | custom-call | flops 536870912 | tf_op jit(solution)/shard_map/pallas_call | solution.py:212
  104.2 2.8 %collective-permute-start.32 = (bf16[256,512]{1,0:T(8,128)(2,1)S(1)}, bf16[256,512]{1,0:T(8,128)(2,1)S(1)}, u32[]{:S(2)}, u32[]{:S(2)}) collective-permute-start(bf16[256,512]{1,0:T(8,128)(2,1)S(1)} %get-tuple-element.100), channel_id=1, source_target_pairs={{0,238},{1,239},{2,224},{3,225},{4,226},{5,227},{6,228},{7,229},{8... | collective-permute-start | bytes 786440 | tf_op jit(solution)/shard_map/ppermute | solution.py:60
  107.0 1.4 %collective-permute-start.31 = (bf16[256,512]{1,0:T(8,128)(2,1)S(1)}, bf16[256,512]{1,0:T(8,128)(2,1)S(1)}, u32[]{:S(2)}, u32[]{:S(2)}) collective-permute-start(bf16[256,512]{1,0:T(8,128)(2,1)S(1)} %get-tuple-element.93.refs_10_), channel_id=1, source_target_pairs={{0,226},{1,227},{2,228},{3,229},{4,230},{5,231},{6,232},{7,233},{8... | collective-permute-start | bytes 786440 | tf_op jit(solution)/shard_map/ppermute | solution.py:60
  108.4 0.5 collective-permute-start.29
  109.0 0.8 collective-permute-done.28.refs_2_
  110.3 1.0 shard_map.107
  111.3 5.1 %collective-permute-done.32.down = bf16[256,512]{1,0:T(8,128)(2,1)S(1)} collective-permute-done((bf16[256,512]{1,0:T(8,128)(2,1)S(1)}, bf16[256,512]{1,0:T(8,128)(2,1)S(1)}, u32[]{:S(2)}, u32[]{:S(2)}) %collective-permute-start.32) | collective-permute-done | bytes 262176 | tf_op jit(solution)/shard_map/ppermute | solution.py:60
  116.3 3.1 %collective-permute-done.31.up = bf16[256,512]{1,0:T(8,128)(2,1)S(1)} collective-permute-done((bf16[256,512]{1,0:T(8,128)(2,1)S(1)}, bf16[256,512]{1,0:T(8,128)(2,1)S(1)}, u32[]{:S(2)}, u32[]{:S(2)}) %collective-permute-start.31) | collective-permute-done | bytes 262176 | tf_op jit(solution)/shard_map/ppermute | solution.py:60
  119.5 1.2 shard_map.108
  (57 shorter events, 3.1 us)
Async XLA Ops:
  0.7 1.0 copy-start
  1.7 0.7 copy-start.4
  2.6 1.0 copy-start.2
  8.8 3.5 %collective-permute-start = (bf16[512,1536]{1,0:T(8,128)(2,1)S(1)}, bf16[512,1536]{1,0:T(8,128)(2,1)S(1)}, u32[]{:S(2)}, u32[]{:S(2)}) collective-permute-start(bf16[512,1536]{1,0:T(8,128)(2,1)S(1)} %get-tuple-element.54), channel_id=1, source_target_pairs={{0,1},{1,0},{2,3},{3,2},{4,5},{5,4},{6,7},{7,6},{8,9},{9,8},{10,11... | collective-permute-start | bytes 4718600 | tf_op jit(solution)/shard_map/ppermute | solution.py:36
  8.9 5.8 %collective-permute-start.1 = (bf16[512,1024]{1,0:T(8,128)(2,1)S(1)}, bf16[512,1024]{1,0:T(8,128)(2,1)S(1)}, u32[]{:S(2)}, u32[]{:S(2)}) collective-permute-start(bf16[512,1024]{1,0:T(8,128)(2,1)S(1)} %get-tuple-element.55), channel_id=1, source_target_pairs={{0,1},{1,0},{2,3},{3,2},{4,5},{5,4},{6,7},{7,6},{8,9},{9,8},{10,11... | collective-permute-start | bytes 3145736 | tf_op jit(solution)/shard_map/ppermute | solution.py:36
  9.4 5.9 %collective-permute-start.2 = (bf16[512,1024]{1,0:T(8,128)(2,1)S(1)}, bf16[512,1024]{1,0:T(8,128)(2,1)S(1)}, u32[]{:S(2)}, u32[]{:S(2)}) collective-permute-start(bf16[512,1024]{1,0:T(8,128)(2,1)S(1)} %get-tuple-element.56), channel_id=1, source_target_pairs={{0,1},{1,0},{2,3},{3,2},{4,5},{5,4},{6,7},{7,6},{8,9},{9,8},{10,11... | collective-permute-start | bytes 3145736 | tf_op jit(solution)/shard_map/ppermute | solution.py:36
  9.5 7.3 %collective-permute-start.3 = (bf16[512,1024]{1,0:T(8,128)(2,1)S(1)}, bf16[512,1024]{1,0:T(8,128)(2,1)S(1)}, u32[]{:S(2)}, u32[]{:S(2)}) collective-permute-start(bf16[512,1024]{1,0:T(8,128)(2,1)S(1)} %get-tuple-element.57), channel_id=1, source_target_pairs={{0,1},{1,0},{2,3},{3,2},{4,5},{5,4},{6,7},{7,6},{8,9},{9,8},{10,11... | collective-permute-start | bytes 3145736 | tf_op jit(solution)/shard_map/ppermute | solution.py:36
  9.9 13.6 %collective-permute-start.5 = (bf16[256,512]{1,0:T(8,128)(2,1)S(1)}, bf16[256,512]{1,0:T(8,128)(2,1)S(1)}, u32[]{:S(2)}, u32[]{:S(2)}) collective-permute-start(bf16[256,512]{1,0:T(8,128)(2,1)S(1)} %shard_map.85.after), channel_id=1, source_target_pairs={{0,48},{1,49},{2,50},{3,51},{4,52},{5,53},{6,54},{7,55},{8,56},{9,... | collective-permute-start | bytes 786440 | tf_op jit(solution)/shard_map/ppermute | solution.py:60
  12.3 13.6 %collective-permute-start.4 = (bf16[256,512]{1,0:T(8,128)(2,1)S(1)}, bf16[256,512]{1,0:T(8,128)(2,1)S(1)}, u32[]{:S(2)}, u32[]{:S(2)}) collective-permute-start(bf16[256,512]{1,0:T(8,128)(2,1)S(1)} %shard_map.85.after), channel_id=1, source_target_pairs={{0,32},{1,33},{2,34},{3,35},{4,36},{5,37},{6,38},{7,39},{8,40},{9,... | collective-permute-start | bytes 786440 | tf_op jit(solution)/shard_map/ppermute | solution.py:60
  25.9 11.0 %collective-permute-start.8 = (bf16[1,256,512]{2,1,0:T(8,128)(2,1)S(1)}, bf16[1,256,512]{2,1,0:T(8,128)(2,1)S(1)}, u32[]{:S(2)}, u32[]{:S(2)}) collective-permute-start(bf16[1,256,512]{2,1,0:T(8,128)(2,1)S(1)} %shard_map.90), channel_id=1, source_target_pairs={{0,16},{1,17},{2,18},{3,19},{4,20},{5,21},{6,22},{7,23},{8,24},{9,... | collective-permute-start | bytes 786440 | tf_op jit(solution)/shard_map/ppermute | solution.py:36
  29.5 10.9 %collective-permute-start.7 = (bf16[256,512]{1,0:T(8,128)(2,1)S(1)}, bf16[256,512]{1,0:T(8,128)(2,1)S(1)}, u32[]{:S(2)}, u32[]{:S(2)}) collective-permute-start(bf16[256,512]{1,0:T(8,128)(2,1)S(1)} %get-tuple-element.61.refs_1_.refs_4_), channel_id=1, source_target_pairs={{0,14},{1,15},{2,0},{3,1},{4,2},{5,3},{6,4},{7,5},{8,6},{9,7},{10,... | collective-permute-start | bytes 786440 | tf_op jit(solution)/shard_map/ppermute | solution.py:36
  33.6 10.5 %collective-permute-start.6 = (bf16[256,512]{1,0:T(8,128)(2,1)S(1)}, bf16[256,512]{1,0:T(8,128)(2,1)S(1)}, u32[]{:S(2)}, u32[]{:S(2)}) collective-permute-start(bf16[256,512]{1,0:T(8,128)(2,1)S(1)} %get-tuple-element.61.refs_1_.refs_4_), channel_id=1, source_target_pairs={{0,2},{1,3},{2,4},{3,5},{4,6},{5,7},{6,8},{7,9},{8,10},{9,11},{10,... | collective-permute-start | bytes 786440 | tf_op jit(solution)/shard_map/ppermute | solution.py:36
  33.6 10.5 %collective-permute-start.10 = (bf16[256,512]{1,0:T(8,128)(2,1)S(1)}, bf16[256,512]{1,0:T(8,128)(2,1)S(1)}, u32[]{:S(2)}, u32[]{:S(2)}) collective-permute-start(bf16[256,512]{1,0:T(8,128)(2,1)S(1)} %get-tuple-element.63.refs_2_.refs_5_), channel_id=1, source_target_pairs={{0,14},{1,15},{2,0},{3,1},{4,2},{5,3},{6,4},{7,5},{8,6},{9,7},{10,... | collective-permute-start | bytes 786440 | tf_op jit(solution)/shard_map/ppermute | solution.py:36
  36.9 10.2 %collective-permute-start.9 = (bf16[256,512]{1,0:T(8,128)(2,1)S(1)}, bf16[256,512]{1,0:T(8,128)(2,1)S(1)}, u32[]{:S(2)}, u32[]{:S(2)}) collective-permute-start(bf16[256,512]{1,0:T(8,128)(2,1)S(1)} %get-tuple-element.63.refs_2_.refs_5_), channel_id=1, source_target_pairs={{0,2},{1,3},{2,4},{3,5},{4,6},{5,7},{6,8},{7,9},{8,10},{9,11},{10,... | collective-permute-start | bytes 786440 | tf_op jit(solution)/shard_map/ppermute | solution.py:36
  47.2 16.5 %collective-permute-start.12 = (bf16[2,256,512]{2,1,0:T(8,128)(2,1)S(1)}, bf16[2,256,512]{2,1,0:T(8,128)(2,1)S(1)}, u32[]{:S(2)}, u32[]{:S(2)}) collective-permute-start(bf16[2,256,512]{2,1,0:T(8,128)(2,1)S(1)} %shard_map.92), channel_id=1, source_target_pairs={{0,16},{1,17},{2,18},{3,19},{4,20},{5,21},{6,22},{7,23},{8,24},{9,... | collective-permute-start | bytes 1572872 | tf_op jit(solution)/shard_map/ppermute | solution.py:36
  49.2 10.6 %collective-permute-start.13 = (bf16[320,512]{1,0:T(8,128)(2,1)S(1)}, bf16[320,512]{1,0:T(8,128)(2,1)S(1)}, u32[]{:S(2)}, u32[]{:S(2)}) collective-permute-start(bf16[320,512]{1,0:T(8,128)(2,1)S(1)} %get-tuple-element.67), channel_id=1, source_target_pairs={{0,14},{1,15},{2,0},{3,1},{4,2},{5,3},{6,4},{7,5},{8,6},{9,7},{10,... | collective-permute-start | bytes 983048 | tf_op jit(solution)/shard_map/ppermute | solution.py:36
  49.5 10.3 %collective-permute-start.11 = (bf16[320,512]{1,0:T(8,128)(2,1)S(1)}, bf16[320,512]{1,0:T(8,128)(2,1)S(1)}, u32[]{:S(2)}, u32[]{:S(2)}) collective-permute-start(bf16[320,512]{1,0:T(8,128)(2,1)S(1)} %get-tuple-element.64.refs_1_.refs_4_), channel_id=1, source_target_pairs={{0,2},{1,3},{2,4},{3,5},{4,6},{5,7},{6,8},{7,9},{8,10},{9,11},{10,... | collective-permute-start | bytes 983048 | tf_op jit(solution)/shard_map/ppermute | solution.py:36
  51.3 17.7 %collective-permute-start.20 = (bf16[320,512]{1,0:T(8,128)(2,1)S(1)}, bf16[320,512]{1,0:T(8,128)(2,1)S(1)}, u32[]{:S(2)}, u32[]{:S(2)}) collective-permute-start(bf16[320,512]{1,0:T(8,128)(2,1)S(1)} %get-tuple-element.79), channel_id=1, source_target_pairs={{0,14},{1,15},{2,0},{3,1},{4,2},{5,3},{6,4},{7,5},{8,6},{9,7},{10,... | collective-permute-start | bytes 983048 | tf_op jit(solution)/shard_map/ppermute | solution.py:36
  52.9 25.0 %collective-permute-start.15 = (bf16[2,256,512]{2,1,0:T(8,128)(2,1)S(1)}, bf16[2,256,512]{2,1,0:T(8,128)(2,1)S(1)}, u32[]{:S(2)}, u32[]{:S(2)}) collective-permute-start(bf16[2,256,512]{2,1,0:T(8,128)(2,1)S(1)} %shard_map.95), channel_id=1, source_target_pairs={{0,16},{1,17},{2,18},{3,19},{4,20},{5,21},{6,22},{7,23},{8,24},{9,... | collective-permute-start | bytes 1572872 | tf_op jit(solution)/shard_map/ppermute | solution.py:36
  63.8 32.3 %collective-permute-start.25 = (bf16[3,256,512]{2,1,0:T(8,128)(2,1)S(1)}, bf16[3,256,512]{2,1,0:T(8,128)(2,1)S(1)}, u32[]{:S(2)}, u32[]{:S(2)}) collective-permute-start(bf16[3,256,512]{2,1,0:T(8,128)(2,1)S(1)} %shard_map.103), channel_id=1, source_target_pairs={{0,16},{1,17},{2,18},{3,19},{4,20},{5,21},{6,22},{7,23},{8,24},{9,... | collective-permute-start | bytes 2359304 | tf_op jit(solution)/shard_map/ppermute | solution.py:36
  65.8 11.9 %collective-permute-start.19 = (bf16[320,512]{1,0:T(8,128)(2,1)S(1)}, bf16[320,512]{1,0:T(8,128)(2,1)S(1)}, u32[]{:S(2)}, u32[]{:S(2)}) collective-permute-start(bf16[320,512]{1,0:T(8,128)(2,1)S(1)} %get-tuple-element.72.refs_1_), channel_id=1, source_target_pairs={{0,2},{1,3},{2,4},{3,5},{4,6},{5,7},{6,8},{7,9},{8,10},{9,11},{10,... | collective-permute-start | bytes 983048 | tf_op jit(solution)/shard_map/ppermute | solution.py:36
  65.8 15.3 %collective-permute-start.16 = (bf16[384,512]{1,0:T(8,128)(2,1)S(1)}, bf16[384,512]{1,0:T(8,128)(2,1)S(1)}, u32[]{:S(2)}, u32[]{:S(2)}) collective-permute-start(bf16[384,512]{1,0:T(8,128)(2,1)S(1)} %get-tuple-element.73), channel_id=1, source_target_pairs={{0,14},{1,15},{2,0},{3,1},{4,2},{5,3},{6,4},{7,5},{8,6},{9,7},{10,... | collective-permute-start | bytes 1179656 | tf_op jit(solution)/shard_map/ppermute | solution.py:36
  69.0 17.0 %collective-permute-start.14 = (bf16[384,512]{1,0:T(8,128)(2,1)S(1)}, bf16[384,512]{1,0:T(8,128)(2,1)S(1)}, u32[]{:S(2)}, u32[]{:S(2)}) collective-permute-start(bf16[384,512]{1,0:T(8,128)(2,1)S(1)} %get-tuple-element.69.refs_6_.refs_1_), channel_id=1, source_target_pairs={{0,2},{1,3},{2,4},{3,5},{4,6},{5,7},{6,8},{7,9},{8,10},{9,11},{10,... | collective-permute-start | bytes 1179656 | tf_op jit(solution)/shard_map/ppermute | solution.py:36
  77.8 14.6 %collective-permute-start.21 = (bf16[384,512]{1,0:T(8,128)(2,1)S(1)}, bf16[384,512]{1,0:T(8,128)(2,1)S(1)}, u32[]{:S(2)}, u32[]{:S(2)}) collective-permute-start(bf16[384,512]{1,0:T(8,128)(2,1)S(1)} %get-tuple-element.80), channel_id=1, source_target_pairs={{0,2},{1,3},{2,4},{3,5},{4,6},{5,7},{6,8},{7,9},{8,10},{9,11},{10,... | collective-permute-start | bytes 1179656 | tf_op jit(solution)/shard_map/ppermute | solution.py:36
  77.9 14.5 %collective-permute-start.22 = (bf16[384,512]{1,0:T(8,128)(2,1)S(1)}, bf16[384,512]{1,0:T(8,128)(2,1)S(1)}, u32[]{:S(2)}, u32[]{:S(2)}) collective-permute-start(bf16[384,512]{1,0:T(8,128)(2,1)S(1)} %get-tuple-element.81), channel_id=1, source_target_pairs={{0,14},{1,15},{2,0},{3,1},{4,2},{5,3},{6,4},{7,5},{8,6},{9,7},{10,... | collective-permute-start | bytes 1179656 | tf_op jit(solution)/shard_map/ppermute | solution.py:36
  86.2 11.2 %collective-permute-start.18 = (bf16[256,512]{1,0:T(8,128)(2,1)S(1)}, bf16[256,512]{1,0:T(8,128)(2,1)S(1)}, u32[]{:S(2)}, u32[]{:S(2)}) collective-permute-start(bf16[256,512]{1,0:T(8,128)(2,1)S(1)} %get-tuple-element.76), channel_id=1, source_target_pairs={{0,14},{1,15},{2,0},{3,1},{4,2},{5,3},{6,4},{7,5},{8,6},{9,7},{10,... | collective-permute-start | bytes 786440 | tf_op jit(solution)/shard_map/ppermute | solution.py:36
  86.3 11.1 %collective-permute-start.17 = (bf16[256,512]{1,0:T(8,128)(2,1)S(1)}, bf16[256,512]{1,0:T(8,128)(2,1)S(1)}, u32[]{:S(2)}, u32[]{:S(2)}) collective-permute-start(bf16[256,512]{1,0:T(8,128)(2,1)S(1)} %get-tuple-element.75.refs_6_), channel_id=1, source_target_pairs={{0,2},{1,3},{2,4},{3,5},{4,6},{5,7},{6,8},{7,9},{8,10},{9,11},{10,... | collective-permute-start | bytes 786440 | tf_op jit(solution)/shard_map/ppermute | solution.py:36
  92.5 7.9 %collective-permute-start.23 = (bf16[256,512]{1,0:T(8,128)(2,1)S(1)}, bf16[256,512]{1,0:T(8,128)(2,1)S(1)}, u32[]{:S(2)}, u32[]{:S(2)}) collective-permute-start(bf16[256,512]{1,0:T(8,128)(2,1)S(1)} %get-tuple-element.83), channel_id=1, source_target_pairs={{0,2},{1,3},{2,4},{3,5},{4,6},{5,7},{6,8},{7,9},{8,10},{9,11},{10,... | collective-permute-start | bytes 786440 | tf_op jit(solution)/shard_map/ppermute | solution.py:36
  92.8 7.6 %collective-permute-start.24 = (bf16[256,512]{1,0:T(8,128)(2,1)S(1)}, bf16[256,512]{1,0:T(8,128)(2,1)S(1)}, u32[]{:S(2)}, u32[]{:S(2)}) collective-permute-start(bf16[256,512]{1,0:T(8,128)(2,1)S(1)} %get-tuple-element.84), channel_id=1, source_target_pairs={{0,14},{1,15},{2,0},{3,1},{4,2},{5,3},{6,4},{7,5},{8,6},{9,7},{10,... | collective-permute-start | bytes 786440 | tf_op jit(solution)/shard_map/ppermute | solution.py:36
  96.1 6.4 %collective-permute-start.26 = (bf16[256,512]{1,0:T(8,128)(2,1)S(1)}, bf16[256,512]{1,0:T(8,128)(2,1)S(1)}, u32[]{:S(2)}, u32[]{:S(2)}) collective-permute-start(bf16[256,512]{1,0:T(8,128)(2,1)S(1)} %shard_map.104), channel_id=1, source_target_pairs={{0,224},{1,225},{2,226},{3,227},{4,228},{5,229},{6,230},{7,231},{8... | collective-permute-start | bytes 786440 | tf_op jit(solution)/shard_map/ppermute | solution.py:60
  102.8 16.7 %copy-start.1 = (bf16[1,256,512]{2,1,0:T(8,128)(2,1)S(1)}, bf16[1,256,512]{2,1,0:T(8,128)(2,1)}, u32[]{:S(2)}) copy-start(bf16[1,256,512]{2,1,0:T(8,128)(2,1)} %weight.3) | copy-start | bytes 786436
  102.8 16.7 %copy-start.3 = (f32[1,256,512]{2,1,0:T(8,128)S(1)}, f32[1,256,512]{2,1,0:T(8,128)}, u32[]{:S(2)}) copy-start(f32[1,256,512]{2,1,0:T(8,128)} %grad_weight_in.1) | copy-start | bytes 1572868
  102.8 16.6 %copy-start.5 = (bf16[1,256]{1,0:T(2,128)(2,1)S(1)}, bf16[1,256]{1,0:T(2,128)(2,1)}, u32[]{:S(2)}) copy-start(bf16[1,256]{1,0:T(2,128)(2,1)} %gain.3) | copy-start | bytes 1540
  102.8 16.6 %copy-start.6 = (f32[1,256]{1,0:T(1,128)S(1)}, f32[1,256]{1,0:T(1,128)}, u32[]{:S(2)}) copy-start(f32[1,256]{1,0:T(1,128)} %grad_gain_in.1) | copy-start | bytes 3076
  104.1 4.9 %collective-permute-start.27 = (bf16[128,512]{1,0:T(8,128)(2,1)S(1)}, bf16[128,512]{1,0:T(8,128)(2,1)S(1)}, u32[]{:S(2)}, u32[]{:S(2)}) collective-permute-start(bf16[128,512]{1,0:T(8,128)(2,1)S(1)} %get-tuple-element.95), channel_id=1, source_target_pairs={{0,1},{1,0},{2,3},{3,2},{4,5},{5,4},{6,7},{7,6},{8,9},{9,8},{10,11... | collective-permute-start | bytes 393224 | tf_op jit(solution)/shard_map/ppermute | solution.py:36
  104.2 12.2 %collective-permute-start.32 = (bf16[256,512]{1,0:T(8,128)(2,1)S(1)}, bf16[256,512]{1,0:T(8,128)(2,1)S(1)}, u32[]{:S(2)}, u32[]{:S(2)}) collective-permute-start(bf16[256,512]{1,0:T(8,128)(2,1)S(1)} %get-tuple-element.100), channel_id=1, source_target_pairs={{0,238},{1,239},{2,224},{3,225},{4,226},{5,227},{6,228},{7,229},{8... | collective-permute-start | bytes 786440 | tf_op jit(solution)/shard_map/ppermute | solution.py:60
  107.0 12.4 %collective-permute-start.31 = (bf16[256,512]{1,0:T(8,128)(2,1)S(1)}, bf16[256,512]{1,0:T(8,128)(2,1)S(1)}, u32[]{:S(2)}, u32[]{:S(2)}) collective-permute-start(bf16[256,512]{1,0:T(8,128)(2,1)S(1)} %get-tuple-element.93.refs_10_), channel_id=1, source_target_pairs={{0,226},{1,227},{2,228},{3,229},{4,230},{5,231},{6,232},{7,233},{8... | collective-permute-start | bytes 786440 | tf_op jit(solution)/shard_map/ppermute | solution.py:60
  108.4 1.3 %collective-permute-start.28 = (bf16[128,512]{1,0:T(8,128)(2,1)S(1)}, bf16[128,512]{1,0:T(8,128)(2,1)S(1)}, u32[]{:S(2)}, u32[]{:S(2)}) collective-permute-start(bf16[128,512]{1,0:T(8,128)(2,1)S(1)} %get-tuple-element.96), channel_id=1, source_target_pairs={{0,1},{1,0},{2,3},{3,2},{4,5},{5,4},{6,7},{7,6},{8,9},{9,8},{10,11... | collective-permute-start | bytes 393224 | tf_op jit(solution)/shard_map/ppermute | solution.py:36
  108.4 1.5 %collective-permute-start.29 = (bf16[128,512]{1,0:T(8,128)(2,1)S(1)}, bf16[128,512]{1,0:T(8,128)(2,1)S(1)}, u32[]{:S(2)}, u32[]{:S(2)}) collective-permute-start(bf16[128,512]{1,0:T(8,128)(2,1)S(1)} %get-tuple-element.97), channel_id=1, source_target_pairs={{0,1},{1,0},{2,3},{3,2},{4,5},{5,4},{6,7},{7,6},{8,9},{9,8},{10,11... | collective-permute-start | bytes 393224 | tf_op jit(solution)/shard_map/ppermute | solution.py:36
  108.9 1.3 %collective-permute-start.30 = (bf16[128,512]{1,0:T(8,128)(2,1)S(1)}, bf16[128,512]{1,0:T(8,128)(2,1)S(1)}, u32[]{:S(2)}, u32[]{:S(2)}) collective-permute-start(bf16[128,512]{1,0:T(8,128)(2,1)S(1)} %get-tuple-element.98), channel_id=1, source_target_pairs={{0,1},{1,0},{2,3},{3,2},{4,5},{5,4},{6,7},{7,6},{8,9},{9,8},{10,11... | collective-permute-start | bytes 393224 | tf_op jit(solution)/shard_map/ppermute | solution.py:36

commit v10 on v8

--- a/solution.py
+++ b/solution.py
@@ -83,7 +83,7 @@
         index -= size
 
 
-def prepare_kernel(width, steps, table, hidden, cot, after, held, scale, cot_t, *rest):
+def prepare_kernel(width, steps, table, hidden, cot, held, scale, cot_t, *rest):
     sends, arrivals = rest[:-1], rest[-1]
     step = hidden.shape[0] // steps
     lanes = 128
@@ -113,7 +113,7 @@
                 i += 1
 
 
-def prepare(table, hidden, cot, after, width):
+def prepare(table, hidden, cot, width):
     tokens, features = hidden.shape
     values = cot.shape[1]
     steps = 4
@@ -121,7 +121,7 @@
     columns[0] += tokens
     return pl.pallas_call(
         functools.partial(prepare_kernel, width, steps),
-        in_specs=[IN_SMEM, IN_HBM, IN_VMEM, ANYWHERE],
+        in_specs=[IN_SMEM, IN_HBM, IN_VMEM],
         out_specs=[IN_VMEM] * (3 + len(columns)),
         out_shape=[
             jax.ShapeDtypeStruct((tokens, features), BF16),
@@ -131,7 +131,7 @@
         scratch_shapes=[pltpu.SemaphoreType.DMA((steps,))],
         compiler_params=params(LOAD_LIMIT),
         cost_estimate=cost(0, 4 * tokens * features),
-    )(table, hidden, cot, after)
+    )(table, hidden, cot)
 
 
 def gradient_kernel(base, groups, width, table, hidden, cot_t, *refs):
@@ -173,10 +173,11 @@
     return outs[:len(groups)], outs[len(groups):]
 
 
-def project_kernel(offsets, rows, more, extra, width, table, hidden, *refs):
+def project_kernel(offsets, rows, more, final, extra, width, table, hidden, *refs):
     visits, refs = refs[:len(SWAPS)], refs[len(SWAPS):]
-    outs = refs[-3:] if more else refs[-2:]
-    start = refs[-5 - extra:-3 - extra] if more else None
+    count = 3 if final else 2
+    outs = refs[-count:]
+    start = refs[-count - extra - 2:-count - extra]
     refs = iter(refs)
     weights = [[next(refs)[first:first + count] for first, count in group] for group in rows]
     totals = [ref[...] for ref in start] if more else []
@@ -188,7 +189,7 @@
         products = [jnp.dot(rows, weight, preferred_element_type=F32) for rows in (own, visitors)]
         totals = [t + p for t, p in zip(totals, products)] if totals else products
     outs[0][...] = totals[0]
-    if more:
+    if final:
         half = outs[1].shape[0]
         outs[1][...] = totals[1][:half].astype(BF16)
         outs[2][...] = totals[1][half:].astype(BF16)
@@ -196,7 +197,7 @@
         outs[1][...] = totals[1]
 
 
-def project(table, hidden, visits, weights, start, after, width):
+def project(table, hidden, visits, weights, start, after, width, final=False):
     tokens = hidden.shape[0]
     arrays = [w for group in weights.values() for w, _, _ in group]
     rows = [[part[1:] for part in group] for group in weights.values()]
@@ -205,9 +206,9 @@
     more = [] if start is None else list(start)
     whole = jax.ShapeDtypeStruct((tokens, values), F32)
     half = jax.ShapeDtypeStruct((tokens // 2, values), BF16)
-    out_shape = [whole, half, half] if more else [whole, whole]
+    out_shape = [whole, half, half] if final else [whole, whole]
     return pl.pallas_call(
-        functools.partial(project_kernel, tuple(weights), rows, bool(more), len(after), width),
+        functools.partial(project_kernel, tuple(weights), rows, bool(more), final, len(after), width),
         in_specs=[IN_SMEM] + [IN_VMEM] * (1 + len(SWAPS) + len(arrays) + len(more)) + [ANYWHERE] * len(after),
         out_specs=[IN_VMEM] * len(out_shape),
         out_shape=out_shape,
@@ -365,7 +366,7 @@
     scaled_weight = scale_weight(gain, value_weight)
     layer = [along_blk(scaled_weight, 1, flip) for flip in (0, 1)]
 
-    held, scale, cot_t, *sends = prepare(table, hidden, cotangent, scaled_weight, width)
+    held, scale, cot_t, *sends = prepare(table, hidden, cotangent, width)
     visits = [swap_core(send) for send in sends]
 
     early = [visits[0]] * len(SWAPS)
@@ -415,8 +416,9 @@
     half = width // 2
     weights[4] = [(far, ring * half, half) for ring in (0, 1) for far in (up, down)]
 
-    far = {off: weights[off] for off in (-3, 3, 4)}
-    product, *products = project(table, held, visits, far, products, [], width)
+    middle = {off: weights[off] for off in (-3, 3)}
+    products = project(table, held, visits, middle, products, [sum_up], width)
+    product, *products = project(table, held, visits, {4: weights[4]}, products, [], width, final=True)
     values = scaled_values(product, *(swap_core(p) for p in products), scale)
 
     return values, *finish(totals, gain, value_weight, grad_weight_in, grad_gain_in)

time: 107 us -> 105 us (0.981); the launches traced: 106 us -> 105 us
  local copies, waits for them, and re-layouts: 2.78 us -> 1.15 us
    ppermute x5, waiting for transfers between devices: 9.99 us -> 12 us  [along_blk(): return lax.ppermute(value, ('blk', 'x', 'z', 'core'), pairs)]
    unnamed x14 -> x10, local copies, waits for them, and re-layouts: 2.68 us -> 1.06 us
    ppermute x24, waiting for transfers between devices: 19.7 us -> 18.6 us  [move(): return lax.ppermute(value, ('x', 'z', 'core'), pairs)]
    pallas_call x2 -> x3, Pallas kernels: 5.77 us -> 6.47 us  [project(): pl.pallas_call(functools.partial(project_kernel, tuple(weights), rows, bo...]
  transfers between devices with their start and end apart: 29 -> 29, of which waited for: 14 -> 13; matrix products, arithmetic and copies ran while one was open for 0% -> 0% of each run, Pallas kernels for 13% -> 13%
where the time goes in v10:
time: 105 us
  starting transfers between devices  51.8 us (49%)
  waiting for transfers between devices  30.6 us (29%)
  Pallas kernels  20.5 us (20%)
  local copies, waits for them, and re-layouts  1.15 us (1%)
    ppermute x24, starting transfers between devices, move(): return lax.ppermute(value, ('x', 'z', 'core'), pairs)  39.5 us
    ppermute x24, waiting for transfers between devices, move(): return lax.ppermute(value, ('x', 'z', 'core'), pairs)  18.6 us
    ppermute x5, starting transfers between devices, along_blk(): return lax.ppermute(value, ('blk', 'x', 'z', 'core'), pairs)  12.3 us
    ppermute x5, waiting for transfers between devices, along_blk(): return lax.ppermute(value, ('blk', 'x', 'z', 'core'), pairs)  12 us
    pallas_call x3, Pallas kernels, project(): pl.pallas_call(functools.partial(project_kernel, tuple(weights), rows, bo...  6.47 us
    pallas_call x2, Pallas kernels, gradient(): pl.pallas_call(functools.partial(gradient_kernel, base, groups, width), i...  5.74 us
    pallas_call x1, Pallas kernels, prepare(): pl.pallas_call(functools.partial(prepare_kernel, width, steps), in_specs=...  5.12 us
  transfers between devices with their start and end apart: 29, of which 13 were waited for; matrix products, arithmetic and copies ran while one was open for 0% of the time, Pallas kernels for 13%

profile of v10, /device:TPU:4, one launch (start us, length us, event | category | flops | bytes accessed | tf_op | source)
XLA Modules:
  0.0 105.1 jit_solution(4729603661437238979)
XLA Ops:
  0.9 1.0 copy-done.1
  1.9 5.1 %shard_map.85 = (bf16[512,8192]{1,0:T(8,128)(2,1)S(1)}, f32[512,1]{1,0:T(8,128)S(1)}, bf16[512,512]{1,0:T(8,128)(2,1)S(1)}, bf16[512,1536]{1,0:T(8,128)(2,1)S(1)...) custom-call(s32[16]{0:T(128)S(1)} %stack.67.table, ...), custom_call_target="tpu_custom_call" | custom-call | bytes 16777216 | tf_op jit(solution)/shard_map/pallas_call | solution.py:122
  7.1 0.5 collective-permute-start.1
  7.7 0.4 collective-permute-start.3
  8.1 0.1 shard_map.86
  8.3 0.6 collective-permute-start.7
  8.9 1.6 %collective-permute-done.refs_0_.refs_1_.refs_2_.refs_3_ = bf16[512,1536]{1,0:T(8,128)(2,1)S(1)} collective-permute-done((bf16[512,1536]{1,0:T(8,128)(2,1)S(1)}, bf16[512,1536]{1,0:T(8,128)(2,1)S(1)}, u32[]{:S(2)}, u32[]{:S(2)}) %collective-permute-start) | collective-permute-done | bytes 1572896 | tf_op jit(solution)/shard_map/ppermute | solution.py:34
  10.5 1.2 %collective-permute-start.4 = (bf16[256,512]{1,0:T(8,128)(2,1)S(1)}, bf16[256,512]{1,0:T(8,128)(2,1)S(1)}, u32[]{:S(2)}, u32[]{:S(2)}) collective-permute-start(bf16[256,512]{1,0:T(8,128)(2,1)S(1)} %shard_map.86), channel_id=1, source_target_pairs={{0,32},{1,33},{2,34},{3,35},{4,36},{5,37},{6,38},{7,39},{8,40},{9,... | collective-permute-start | bytes 786440 | tf_op jit(solution)/shard_map/ppermute | solution.py:58
  11.7 1.2 %shard_map.87 = (bf16[1,256,512]{2,1,0:T(8,128)(2,1)S(1)}, bf16[256,512]{1,0:T(8,128)(2,1)S(1)}) custom-call(s32[16]{0:T(128)S(1)} %stack.67.table, bf16[512,8192]{1,0:T(8,128)(2,1)S(1)} %get-tuple-element.51.hidden, bf16[512,512]{1,0:T(8,128)(2,1)S(1)} %get-tuple-element.56.cot_t.refs_4_, ...), custom_call_target="tpu_custom_call" | custom-call | bytes 512 | tf_op jit(solution)/shard_map/pallas_call | solution.py:164
  13.0 1.3 %collective-permute-start.5 = (bf16[1,256,512]{2,1,0:T(8,128)(2,1)S(1)}, bf16[1,256,512]{2,1,0:T(8,128)(2,1)S(1)}, u32[]{:S(2)}, u32[]{:S(2)}) collective-permute-start(bf16[1,256,512]{2,1,0:T(8,128)(2,1)S(1)} %get-tuple-element.58.refs_4_), channel_id=1, source_target_pairs={{0,16},{1,17},{2,18},{3,19},{4,20},{5,21},{6,22},{7,23},{8,24},{9,... | collective-permute-start | bytes 786440 | tf_op jit(solution)/shard_map/ppermute | solution.py:34
  14.3 0.8 collective-permute-done.3.refs_3_
  15.0 4.5 %shard_map.88 = (bf16[2,256,512]{2,1,0:T(8,128)(2,1)S(1)}, bf16[2,256,512]{2,1,0:T(8,128)(2,1)S(1)}, bf16[3,256,512]{2,1,0:T(8,128)(2,1)S(1)}, bf16[256,512]{1,0...) custom-call(s32[16]{0:T(128)S(1)} %stack.67.table, ...), custom_call_target="tpu_custom_call" | custom-call | bytes 512 | tf_op jit(solution)/shard_map/pallas_call | solution.py:164
  19.5 2.6 %collective-permute-done.7.refs_2_.refs_0_.refs_5_ = bf16[256,512]{1,0:T(8,128)(2,1)S(1)} collective-permute-done((bf16[256,512]{1,0:T(8,128)(2,1)S(1)}, bf16[256,512]{1,0:T(8,128)(2,1)S(1)}, u32[]{:S(2)}, u32[]{:S(2)}) %collective-permute-start.7) | collective-permute-done | bytes 262176 | tf_op jit(solution)/shard_map/ppermute | solution.py:58
  22.2 3.0 %collective-permute-done.4.refs_0_.refs_1_.refs_4_ = bf16[256,512]{1,0:T(8,128)(2,1)S(1)} collective-permute-done((bf16[256,512]{1,0:T(8,128)(2,1)S(1)}, bf16[256,512]{1,0:T(8,128)(2,1)S(1)}, u32[]{:S(2)}, u32[]{:S(2)}) %collective-permute-start.4) | collective-permute-done | bytes 262176 | tf_op jit(solution)/shard_map/ppermute | solution.py:58
  25.1 3.5 %collective-permute-start.8 = (bf16[2,256,512]{2,1,0:T(8,128)(2,1)S(1)}, bf16[2,256,512]{2,1,0:T(8,128)(2,1)S(1)}, u32[]{:S(2)}, u32[]{:S(2)}) collective-permute-start(bf16[2,256,512]{2,1,0:T(8,128)(2,1)S(1)} %shard_map.90), channel_id=1, source_target_pairs={{0,16},{1,17},{2,18},{3,19},{4,20},{5,21},{6,22},{7,23},{8,24},{9,... | collective-permute-start | bytes 1572872 | tf_op jit(solution)/shard_map/ppermute | solution.py:34
  28.7 0.7 collective-permute-start.6
  29.4 4.2 %collective-permute-start.9 = (bf16[320,512]{1,0:T(8,128)(2,1)S(1)}, bf16[320,512]{1,0:T(8,128)(2,1)S(1)}, u32[]{:S(2)}, u32[]{:S(2)}) collective-permute-start(bf16[320,512]{1,0:T(8,128)(2,1)S(1)} %get-tuple-element.63), channel_id=1, source_target_pairs={{0,14},{1,15},{2,0},{3,1},{4,2},{5,3},{6,4},{7,5},{8,6},{9,7},{10,... | collective-permute-start | bytes 983048 | tf_op jit(solution)/shard_map/ppermute | solution.py:34
  33.6 1.5 %collective-permute-start.11 = (bf16[2,256,512]{2,1,0:T(8,128)(2,1)S(1)}, bf16[2,256,512]{2,1,0:T(8,128)(2,1)S(1)}, u32[]{:S(2)}, u32[]{:S(2)}) collective-permute-start(bf16[2,256,512]{2,1,0:T(8,128)(2,1)S(1)} %shard_map.93), channel_id=1, source_target_pairs={{0,16},{1,17},{2,18},{3,19},{4,20},{5,21},{6,22},{7,23},{8,24},{9,... | collective-permute-start | bytes 1572872 | tf_op jit(solution)/shard_map/ppermute | solution.py:34
  35.1 1.8 %collective-permute-start.16 = (bf16[320,512]{1,0:T(8,128)(2,1)S(1)}, bf16[320,512]{1,0:T(8,128)(2,1)S(1)}, u32[]{:S(2)}, u32[]{:S(2)}) collective-permute-start(bf16[320,512]{1,0:T(8,128)(2,1)S(1)} %get-tuple-element.75), channel_id=1, source_target_pairs={{0,14},{1,15},{2,0},{3,1},{4,2},{5,3},{6,4},{7,5},{8,6},{9,7},{10,... | collective-permute-start | bytes 983048 | tf_op jit(solution)/shard_map/ppermute | solution.py:34
  36.9 3.2 %collective-permute-done.6.refs_0_.refs_6_ = bf16[320,512]{1,0:T(8,128)(2,1)S(1)} collective-permute-done((bf16[320,512]{1,0:T(8,128)(2,1)S(1)}, bf16[320,512]{1,0:T(8,128)(2,1)S(1)}, u32[]{:S(2)}, u32[]{:S(2)}) %collective-permute-start.6) | collective-permute-done | bytes 327712 | tf_op jit(solution)/shard_map/ppermute | solution.py:34
  40.1 1.6 %collective-permute-done.9.refs_3_.refs_8_ = bf16[320,512]{1,0:T(8,128)(2,1)S(1)} collective-permute-done((bf16[320,512]{1,0:T(8,128)(2,1)S(1)}, bf16[320,512]{1,0:T(8,128)(2,1)S(1)}, u32[]{:S(2)}, u32[]{:S(2)}) %collective-permute-start.9) | collective-permute-done | bytes 327712 | tf_op jit(solution)/shard_map/ppermute | solution.py:34
  41.7 0.1 shard_map.92
  41.9 3.3 %collective-permute-start.21 = (bf16[3,256,512]{2,1,0:T(8,128)(2,1)S(1)}, bf16[3,256,512]{2,1,0:T(8,128)(2,1)S(1)}, u32[]{:S(2)}, u32[]{:S(2)}) collective-permute-start(bf16[3,256,512]{2,1,0:T(8,128)(2,1)S(1)} %shard_map.100), channel_id=1, source_target_pairs={{0,16},{1,17},{2,18},{3,19},{4,20},{5,21},{6,22},{7,23},{8,24},{9,... | collective-permute-start | bytes 2359304 | tf_op jit(solution)/shard_map/ppermute | solution.py:34
  45.2 4.6 %collective-permute-start.12 = (bf16[384,512]{1,0:T(8,128)(2,1)S(1)}, bf16[384,512]{1,0:T(8,128)(2,1)S(1)}, u32[]{:S(2)}, u32[]{:S(2)}) collective-permute-start(bf16[384,512]{1,0:T(8,128)(2,1)S(1)} %get-tuple-element.69), channel_id=1, source_target_pairs={{0,14},{1,15},{2,0},{3,1},{4,2},{5,3},{6,4},{7,5},{8,6},{9,7},{10,... | collective-permute-start | bytes 1179656 | tf_op jit(solution)/shard_map/ppermute | solution.py:34
  49.8 0.1 shard_map.96
  49.9 2.3 %collective-permute-start.17 = (bf16[384,512]{1,0:T(8,128)(2,1)S(1)}, bf16[384,512]{1,0:T(8,128)(2,1)S(1)}, u32[]{:S(2)}, u32[]{:S(2)}) collective-permute-start(bf16[384,512]{1,0:T(8,128)(2,1)S(1)} %get-tuple-element.76), channel_id=1, source_target_pairs={{0,2},{1,3},{2,4},{3,5},{4,6},{5,7},{6,8},{7,9},{8,10},{9,11},{10,... | collective-permute-start | bytes 1179656 | tf_op jit(solution)/shard_map/ppermute | solution.py:34
  52.2 0.6 collective-permute-done.11.refs_2_.refs_5_
  52.7 5.9 %collective-permute-start.18 = (bf16[384,512]{1,0:T(8,128)(2,1)S(1)}, bf16[384,512]{1,0:T(8,128)(2,1)S(1)}, u32[]{:S(2)}, u32[]{:S(2)}) collective-permute-start(bf16[384,512]{1,0:T(8,128)(2,1)S(1)} %get-tuple-element.77), channel_id=1, source_target_pairs={{0,14},{1,15},{2,0},{3,1},{4,2},{5,3},{6,4},{7,5},{8,6},{9,7},{10,... | collective-permute-start | bytes 1179656 | tf_op jit(solution)/shard_map/ppermute | solution.py:34
  58.6 4.4 %collective-permute-done.10.refs_0_.refs_10_ = bf16[384,512]{1,0:T(8,128)(2,1)S(1)} collective-permute-done((bf16[384,512]{1,0:T(8,128)(2,1)S(1)}, bf16[384,512]{1,0:T(8,128)(2,1)S(1)}, u32[]{:S(2)}, u32[]{:S(2)}) %collective-permute-start.10) | collective-permute-done | bytes 393248 | tf_op jit(solution)/shard_map/ppermute | solution.py:34
  63.0 0.1 shard_map.94
  63.2 2.0 %collective-permute-start.13 = (bf16[384,512]{1,0:T(8,128)(2,1)S(1)}, bf16[384,512]{1,0:T(8,128)(2,1)S(1)}, u32[]{:S(2)}, u32[]{:S(2)}) collective-permute-start(bf16[384,512]{1,0:T(8,128)(2,1)S(1)} %get-tuple-element.71.refs_6_), channel_id=1, source_target_pairs={{0,2},{1,3},{2,4},{3,5},{4,6},{5,7},{6,8},{7,9},{8,10},{9,11},{10,... | collective-permute-start | bytes 1179656 | tf_op jit(solution)/shard_map/ppermute | solution.py:34
  65.2 6.2 %collective-permute-done.17.refs_0_.refs_11_ = bf16[384,512]{1,0:T(8,128)(2,1)S(1)} collective-permute-done((bf16[384,512]{1,0:T(8,128)(2,1)S(1)}, bf16[384,512]{1,0:T(8,128)(2,1)S(1)}, u32[]{:S(2)}, u32[]{:S(2)}) %collective-permute-start.17) | collective-permute-done | bytes 393248 | tf_op jit(solution)/shard_map/ppermute | solution.py:34
  71.4 0.1 shard_map.97
  71.7 3.2 %collective-permute-start.20 = (bf16[384,512]{1,0:T(8,128)(2,1)S(1)}, bf16[384,512]{1,0:T(8,128)(2,1)S(1)}, u32[]{:S(2)}, u32[]{:S(2)}) collective-permute-start(bf16[384,512]{1,0:T(8,128)(2,1)S(1)} %get-tuple-element.79), channel_id=1, source_target_pairs={{0,14},{1,15},{2,0},{3,1},{4,2},{5,3},{6,4},{7,5},{8,6},{9,7},{10,... | collective-permute-start | bytes 1179656 | tf_op jit(solution)/shard_map/ppermute | solution.py:34
  75.0 6.3 %collective-permute-start.22 = (bf16[256,512]{1,0:T(8,128)(2,1)S(1)}, bf16[256,512]{1,0:T(8,128)(2,1)S(1)}, u32[]{:S(2)}, u32[]{:S(2)}) collective-permute-start(bf16[256,512]{1,0:T(8,128)(2,1)S(1)} %shard_map.101), channel_id=1, source_target_pairs={{0,224},{1,225},{2,226},{3,227},{4,228},{5,229},{6,230},{7,231},{8... | collective-permute-start | bytes 786440 | tf_op jit(solution)/shard_map/ppermute | solution.py:58
  81.2 3.4 %shard_map.98 = (f32[512,512]{1,0:T(8,128)S(1)}, f32[512,512]{1,0:T(8,128)S(1)}) custom-call(s32[16]{0:T(128)S(1)} %stack.67.table, bf16[512,8192]{1,0:T(8,128)(2,1)S(1)} %get-tuple-element.51.hidden, bf16[512,1536]{1,0:T(8,128)(2,1)S(1)} %collective-permute-done.refs_0_.refs_1_.refs_2_.refs_3_, bf16[512,1024]{1,0:T(8,128)(2,1)S(1)} %collective-permute-done.1.refs_1_, ...), custom_call_target="tpu_custom_call" | custom-call | flops 2684354560 | tf_op jit(solution)/shard_map/pallas_call | solution.py:210
  84.7 0.4 collective-permute-done.22.refs_8_.own
  85.1 0.2 shard_map.102
  85.3 0.3 collective-permute-start.23
  85.6 3.2 %collective-permute-start.24 = (bf16[256,512]{1,0:T(8,128)(2,1)S(1)}, bf16[256,512]{1,0:T(8,128)(2,1)S(1)}, u32[]{:S(2)}, u32[]{:S(2)}) collective-permute-start(bf16[256,512]{1,0:T(8,128)(2,1)S(1)} %get-tuple-element.87), channel_id=1, source_target_pairs={{0,14},{1,15},{2,0},{3,1},{4,2},{5,3},{6,4},{7,5},{8,6},{9,7},{10,... | collective-permute-start | bytes 786440 | tf_op jit(solution)/shard_map/ppermute | solution.py:34
  88.8 4.3 %collective-permute-start.28 = (bf16[256,512]{1,0:T(8,128)(2,1)S(1)}, bf16[256,512]{1,0:T(8,128)(2,1)S(1)}, u32[]{:S(2)}, u32[]{:S(2)}) collective-permute-start(bf16[256,512]{1,0:T(8,128)(2,1)S(1)} %get-tuple-element.96), channel_id=1, source_target_pairs={{0,238},{1,239},{2,224},{3,225},{4,226},{5,227},{6,228},{7,229},{8... | collective-permute-start | bytes 786440 | tf_op jit(solution)/shard_map/ppermute | solution.py:58
  93.1 1.8 %shard_map.103 = (f32[512,512]{1,0:T(8,128)S(1)}, f32[512,512]{1,0:T(8,128)S(1)}) custom-call(s32[16]{0:T(128)S(1)} %stack.67.table, bf16[512,8192]{1,0:T(8,128)(2,1)S(1)} %get-tuple-element.51.hidden, bf16[512,1536]{1,0:T(8,128)(2,1)S(1)} %collective-permute-done.refs_0_.refs_1_.refs_2_.refs_3_, bf16[512,1024]{1,0:T(8,128)(2,1)S(1)} %collective-permute-done.1.refs_1_, ...), custom_call_target="tpu_custom_call" | custom-call | flops 1073741824 | tf_op jit(solution)/shard_map/pallas_call | solution.py:210
  95.0 1.3 %shard_map.104 = (f32[512,512]{1,0:T(8,128)S(1)}, bf16[256,512]{1,0:T(8,128)(2,1)S(1)}, bf16[256,512]{1,0:T(8,128)(2,1)S(1)}) custom-call(s32[16]{0:T(128)S(1)} %stack.67.table, bf16[512,8192]{1,0:T(8,128)(2,1)S(1)} %get-tuple-element.51.hidden, bf16[512,1536]{1,0:T(8,128)(2,1)S(1)} %collective-permute-done.refs_0_.refs_1_.refs_2_.refs_3_, ...), custom_call_target="tpu_custom_call" | custom-call | flops 536870912 | tf_op jit(solution)/shard_map/pallas_call | solution.py:210
  96.4 0.5 collective-permute-start.26
  96.9 3.4 %collective-permute-done.28.down = bf16[256,512]{1,0:T(8,128)(2,1)S(1)} collective-permute-done((bf16[256,512]{1,0:T(8,128)(2,1)S(1)}, bf16[256,512]{1,0:T(8,128)(2,1)S(1)}, u32[]{:S(2)}, u32[]{:S(2)}) %collective-permute-start.28) | collective-permute-done | bytes 262176 | tf_op jit(solution)/shard_map/ppermute | solution.py:58
  100.3 2.7 %collective-permute-done.27.up = bf16[256,512]{1,0:T(8,128)(2,1)S(1)} collective-permute-done((bf16[256,512]{1,0:T(8,128)(2,1)S(1)}, bf16[256,512]{1,0:T(8,128)(2,1)S(1)}, u32[]{:S(2)}, u32[]{:S(2)}) %collective-permute-start.27) | collective-permute-done | bytes 262176 | tf_op jit(solution)/shard_map/ppermute | solution.py:58
  102.9 1.2 %shard_map.106 = (f32[1,256,512]{2,1,0:T(8,128)}, f32[1,256]{1,0:T(1,128)}) custom-call(bf16[256,512]{1,0:T(8,128)(2,1)S(1)} %collective-permute-done.22.refs_8_.own, bf16[256,512]{1,0:T(8,128)(2,1)S(1)} %collective-permute-done.27.up, bf16[256,512]{1,0:T(8,128)(2,1)S(1)} %collective-permute-done.28.down, bf16[1,256]{1,0:T(2,128)(2,1)S(1)} %copy-done.3, ...), custom_call_target="tpu_custom_call" | custom-call | tf_op jit(solution)/shard_map/pallas_call | solution.py:352
  104.1 1.0 shard_map.105
  (43 shorter events, 0.9 us)
Async XLA Ops:
  0.6 7.5 %copy-start = (bf16[1,256,512]{2,1,0:T(8,128)(2,1)S(1)}, bf16[1,256,512]{2,1,0:T(8,128)(2,1)}, u32[]{:S(2)}) copy-start(bf16[1,256,512]{2,1,0:T(8,128)(2,1)} %weight.3) | copy-start | bytes 786436
  0.6 7.5 %copy-start.3 = (bf16[1,256]{1,0:T(2,128)(2,1)S(1)}, bf16[1,256]{1,0:T(2,128)(2,1)}, u32[]{:S(2)}) copy-start(bf16[1,256]{1,0:T(2,128)(2,1)} %gain.3) | copy-start | bytes 1540
  0.9 1.0 copy-start.1
  7.0 3.5 %collective-permute-start = (bf16[512,1536]{1,0:T(8,128)(2,1)S(1)}, bf16[512,1536]{1,0:T(8,128)(2,1)S(1)}, u32[]{:S(2)}, u32[]{:S(2)}) collective-permute-start(bf16[512,1536]{1,0:T(8,128)(2,1)S(1)} %get-tuple-element.52), channel_id=1, source_target_pairs={{0,1},{1,0},{2,3},{3,2},{4,5},{5,4},{6,7},{7,6},{8,9},{9,8},{10,11... | collective-permute-start | bytes 4718600 | tf_op jit(solution)/shard_map/ppermute | solution.py:34
  7.1 5.8 %collective-permute-start.1 = (bf16[512,1024]{1,0:T(8,128)(2,1)S(1)}, bf16[512,1024]{1,0:T(8,128)(2,1)S(1)}, u32[]{:S(2)}, u32[]{:S(2)}) collective-permute-start(bf16[512,1024]{1,0:T(8,128)(2,1)S(1)} %get-tuple-element.53), channel_id=1, source_target_pairs={{0,1},{1,0},{2,3},{3,2},{4,5},{5,4},{6,7},{7,6},{8,9},{9,8},{10,11... | collective-permute-start | bytes 3145736 | tf_op jit(solution)/shard_map/ppermute | solution.py:34
  7.6 6.6 %collective-permute-start.2 = (bf16[512,1024]{1,0:T(8,128)(2,1)S(1)}, bf16[512,1024]{1,0:T(8,128)(2,1)S(1)}, u32[]{:S(2)}, u32[]{:S(2)}) collective-permute-start(bf16[512,1024]{1,0:T(8,128)(2,1)S(1)} %get-tuple-element.54), channel_id=1, source_target_pairs={{0,1},{1,0},{2,3},{3,2},{4,5},{5,4},{6,7},{7,6},{8,9},{9,8},{10,11... | collective-permute-start | bytes 3145736 | tf_op jit(solution)/shard_map/ppermute | solution.py:34
  7.7 7.3 %collective-permute-start.3 = (bf16[512,1024]{1,0:T(8,128)(2,1)S(1)}, bf16[512,1024]{1,0:T(8,128)(2,1)S(1)}, u32[]{:S(2)}, u32[]{:S(2)}) collective-permute-start(bf16[512,1024]{1,0:T(8,128)(2,1)S(1)} %get-tuple-element.55), channel_id=1, source_target_pairs={{0,1},{1,0},{2,3},{3,2},{4,5},{5,4},{6,7},{7,6},{8,9},{9,8},{10,11... | collective-permute-start | bytes 3145736 | tf_op jit(solution)/shard_map/ppermute | solution.py:34
  8.3 13.9 %collective-permute-start.7 = (bf16[256,512]{1,0:T(8,128)(2,1)S(1)}, bf16[256,512]{1,0:T(8,128)(2,1)S(1)}, u32[]{:S(2)}, u32[]{:S(2)}) collective-permute-start(bf16[256,512]{1,0:T(8,128)(2,1)S(1)} %shard_map.86), channel_id=1, source_target_pairs={{0,48},{1,49},{2,50},{3,51},{4,52},{5,53},{6,54},{7,55},{8,56},{9,... | collective-permute-start | bytes 786440 | tf_op jit(solution)/shard_map/ppermute | solution.py:58
  10.5 14.6 %collective-permute-start.4 = (bf16[256,512]{1,0:T(8,128)(2,1)S(1)}, bf16[256,512]{1,0:T(8,128)(2,1)S(1)}, u32[]{:S(2)}, u32[]{:S(2)}) collective-permute-start(bf16[256,512]{1,0:T(8,128)(2,1)S(1)} %shard_map.86), channel_id=1, source_target_pairs={{0,32},{1,33},{2,34},{3,35},{4,36},{5,37},{6,38},{7,39},{8,40},{9,... | collective-permute-start | bytes 786440 | tf_op jit(solution)/shard_map/ppermute | solution.py:58
  13.0 12.2 %collective-permute-start.5 = (bf16[1,256,512]{2,1,0:T(8,128)(2,1)S(1)}, bf16[1,256,512]{2,1,0:T(8,128)(2,1)S(1)}, u32[]{:S(2)}, u32[]{:S(2)}) collective-permute-start(bf16[1,256,512]{2,1,0:T(8,128)(2,1)S(1)} %get-tuple-element.58.refs_4_), channel_id=1, source_target_pairs={{0,16},{1,17},{2,18},{3,19},{4,20},{5,21},{6,22},{7,23},{8,24},{9,... | collective-permute-start | bytes 786440 | tf_op jit(solution)/shard_map/ppermute | solution.py:34
  25.1 16.6 %collective-permute-start.8 = (bf16[2,256,512]{2,1,0:T(8,128)(2,1)S(1)}, bf16[2,256,512]{2,1,0:T(8,128)(2,1)S(1)}, u32[]{:S(2)}, u32[]{:S(2)}) collective-permute-start(bf16[2,256,512]{2,1,0:T(8,128)(2,1)S(1)} %shard_map.90), channel_id=1, source_target_pairs={{0,16},{1,17},{2,18},{3,19},{4,20},{5,21},{6,22},{7,23},{8,24},{9,... | collective-permute-start | bytes 1572872 | tf_op jit(solution)/shard_map/ppermute | solution.py:34
  28.7 11.4 %collective-permute-start.6 = (bf16[320,512]{1,0:T(8,128)(2,1)S(1)}, bf16[320,512]{1,0:T(8,128)(2,1)S(1)}, u32[]{:S(2)}, u32[]{:S(2)}) collective-permute-start(bf16[320,512]{1,0:T(8,128)(2,1)S(1)} %get-tuple-element.60), channel_id=1, source_target_pairs={{0,2},{1,3},{2,4},{3,5},{4,6},{5,7},{6,8},{7,9},{8,10},{9,11},{10,... | collective-permute-start | bytes 983048 | tf_op jit(solution)/shard_map/ppermute | solution.py:34
  29.4 12.4 %collective-permute-start.9 = (bf16[320,512]{1,0:T(8,128)(2,1)S(1)}, bf16[320,512]{1,0:T(8,128)(2,1)S(1)}, u32[]{:S(2)}, u32[]{:S(2)}) collective-permute-start(bf16[320,512]{1,0:T(8,128)(2,1)S(1)} %get-tuple-element.63), channel_id=1, source_target_pairs={{0,14},{1,15},{2,0},{3,1},{4,2},{5,3},{6,4},{7,5},{8,6},{9,7},{10,... | collective-permute-start | bytes 983048 | tf_op jit(solution)/shard_map/ppermute | solution.py:34
  33.6 19.1 %collective-permute-start.11 = (bf16[2,256,512]{2,1,0:T(8,128)(2,1)S(1)}, bf16[2,256,512]{2,1,0:T(8,128)(2,1)S(1)}, u32[]{:S(2)}, u32[]{:S(2)}) collective-permute-start(bf16[2,256,512]{2,1,0:T(8,128)(2,1)S(1)} %shard_map.93), channel_id=1, source_target_pairs={{0,16},{1,17},{2,18},{3,19},{4,20},{5,21},{6,22},{7,23},{8,24},{9,... | collective-permute-start | bytes 1572872 | tf_op jit(solution)/shard_map/ppermute | solution.py:34
  35.1 14.6 %collective-permute-start.16 = (bf16[320,512]{1,0:T(8,128)(2,1)S(1)}, bf16[320,512]{1,0:T(8,128)(2,1)S(1)}, u32[]{:S(2)}, u32[]{:S(2)}) collective-permute-start(bf16[320,512]{1,0:T(8,128)(2,1)S(1)} %get-tuple-element.75), channel_id=1, source_target_pairs={{0,14},{1,15},{2,0},{3,1},{4,2},{5,3},{6,4},{7,5},{8,6},{9,7},{10,... | collective-permute-start | bytes 983048 | tf_op jit(solution)/shard_map/ppermute | solution.py:34
  40.1 9.6 %collective-permute-start.15 = (bf16[320,512]{1,0:T(8,128)(2,1)S(1)}, bf16[320,512]{1,0:T(8,128)(2,1)S(1)}, u32[]{:S(2)}, u32[]{:S(2)}) collective-permute-start(bf16[320,512]{1,0:T(8,128)(2,1)S(1)} %get-tuple-element.65.refs_6_.refs_1_), channel_id=1, source_target_pairs={{0,2},{1,3},{2,4},{3,5},{4,6},{5,7},{6,8},{7,9},{8,10},{9,11},{10,... | collective-permute-start | bytes 983048 | tf_op jit(solution)/shard_map/ppermute | solution.py:34
  41.9 33.0 %collective-permute-start.21 = (bf16[3,256,512]{2,1,0:T(8,128)(2,1)S(1)}, bf16[3,256,512]{2,1,0:T(8,128)(2,1)S(1)}, u32[]{:S(2)}, u32[]{:S(2)}) collective-permute-start(bf16[3,256,512]{2,1,0:T(8,128)(2,1)S(1)} %shard_map.100), channel_id=1, source_target_pairs={{0,16},{1,17},{2,18},{3,19},{4,20},{5,21},{6,22},{7,23},{8,24},{9,... | collective-permute-start | bytes 2359304 | tf_op jit(solution)/shard_map/ppermute | solution.py:34
  45.2 13.4 %collective-permute-start.12 = (bf16[384,512]{1,0:T(8,128)(2,1)S(1)}, bf16[384,512]{1,0:T(8,128)(2,1)S(1)}, u32[]{:S(2)}, u32[]{:S(2)}) collective-permute-start(bf16[384,512]{1,0:T(8,128)(2,1)S(1)} %get-tuple-element.69), channel_id=1, source_target_pairs={{0,14},{1,15},{2,0},{3,1},{4,2},{5,3},{6,4},{7,5},{8,6},{9,7},{10,... | collective-permute-start | bytes 1179656 | tf_op jit(solution)/shard_map/ppermute | solution.py:34
  49.7 13.3 %collective-permute-start.10 = (bf16[384,512]{1,0:T(8,128)(2,1)S(1)}, bf16[384,512]{1,0:T(8,128)(2,1)S(1)}, u32[]{:S(2)}, u32[]{:S(2)}) collective-permute-start(bf16[384,512]{1,0:T(8,128)(2,1)S(1)} %get-tuple-element.66.refs_6_.refs_1_), channel_id=1, source_target_pairs={{0,2},{1,3},{2,4},{3,5},{4,6},{5,7},{6,8},{7,9},{8,10},{9,11},{10,... | collective-permute-start | bytes 1179656 | tf_op jit(solution)/shard_map/ppermute | solution.py:34
  49.9 21.6 %collective-permute-start.17 = (bf16[384,512]{1,0:T(8,128)(2,1)S(1)}, bf16[384,512]{1,0:T(8,128)(2,1)S(1)}, u32[]{:S(2)}, u32[]{:S(2)}) collective-permute-start(bf16[384,512]{1,0:T(8,128)(2,1)S(1)} %get-tuple-element.76), channel_id=1, source_target_pairs={{0,2},{1,3},{2,4},{3,5},{4,6},{5,7},{6,8},{7,9},{8,10},{9,11},{10,... | collective-permute-start | bytes 1179656 | tf_op jit(solution)/shard_map/ppermute | solution.py:34
  52.7 18.7 %collective-permute-start.18 = (bf16[384,512]{1,0:T(8,128)(2,1)S(1)}, bf16[384,512]{1,0:T(8,128)(2,1)S(1)}, u32[]{:S(2)}, u32[]{:S(2)}) collective-permute-start(bf16[384,512]{1,0:T(8,128)(2,1)S(1)} %get-tuple-element.77), channel_id=1, source_target_pairs={{0,14},{1,15},{2,0},{3,1},{4,2},{5,3},{6,4},{7,5},{8,6},{9,7},{10,... | collective-permute-start | bytes 1179656 | tf_op jit(solution)/shard_map/ppermute | solution.py:34
  63.1 21.5 %collective-permute-start.14 = (bf16[384,512]{1,0:T(8,128)(2,1)S(1)}, bf16[384,512]{1,0:T(8,128)(2,1)S(1)}, u32[]{:S(2)}, u32[]{:S(2)}) collective-permute-start(bf16[384,512]{1,0:T(8,128)(2,1)S(1)} %get-tuple-element.72), channel_id=1, source_target_pairs={{0,14},{1,15},{2,0},{3,1},{4,2},{5,3},{6,4},{7,5},{8,6},{9,7},{10,... | collective-permute-start | bytes 1179656 | tf_op jit(solution)/shard_map/ppermute | solution.py:34
  63.2 21.4 %collective-permute-start.13 = (bf16[384,512]{1,0:T(8,128)(2,1)S(1)}, bf16[384,512]{1,0:T(8,128)(2,1)S(1)}, u32[]{:S(2)}, u32[]{:S(2)}) collective-permute-start(bf16[384,512]{1,0:T(8,128)(2,1)S(1)} %get-tuple-element.71.refs_6_), channel_id=1, source_target_pairs={{0,2},{1,3},{2,4},{3,5},{4,6},{5,7},{6,8},{7,9},{8,10},{9,11},{10,... | collective-permute-start | bytes 1179656 | tf_op jit(solution)/shard_map/ppermute | solution.py:34
  71.6 13.1 %collective-permute-start.19 = (bf16[384,512]{1,0:T(8,128)(2,1)S(1)}, bf16[384,512]{1,0:T(8,128)(2,1)S(1)}, u32[]{:S(2)}, u32[]{:S(2)}) collective-permute-start(bf16[384,512]{1,0:T(8,128)(2,1)S(1)} %get-tuple-element.78), channel_id=1, source_target_pairs={{0,2},{1,3},{2,4},{3,5},{4,6},{5,7},{6,8},{7,9},{8,10},{9,11},{10,... | collective-permute-start | bytes 1179656 | tf_op jit(solution)/shard_map/ppermute | solution.py:34
  71.7 13.0 %collective-permute-start.20 = (bf16[384,512]{1,0:T(8,128)(2,1)S(1)}, bf16[384,512]{1,0:T(8,128)(2,1)S(1)}, u32[]{:S(2)}, u32[]{:S(2)}) collective-permute-start(bf16[384,512]{1,0:T(8,128)(2,1)S(1)} %get-tuple-element.79), channel_id=1, source_target_pairs={{0,14},{1,15},{2,0},{3,1},{4,2},{5,3},{6,4},{7,5},{8,6},{9,7},{10,... | collective-permute-start | bytes 1179656 | tf_op jit(solution)/shard_map/ppermute | solution.py:34
  75.0 10.2 %collective-permute-start.22 = (bf16[256,512]{1,0:T(8,128)(2,1)S(1)}, bf16[256,512]{1,0:T(8,128)(2,1)S(1)}, u32[]{:S(2)}, u32[]{:S(2)}) collective-permute-start(bf16[256,512]{1,0:T(8,128)(2,1)S(1)} %shard_map.101), channel_id=1, source_target_pairs={{0,224},{1,225},{2,226},{3,227},{4,228},{5,229},{6,230},{7,231},{8... | collective-permute-start | bytes 786440 | tf_op jit(solution)/shard_map/ppermute | solution.py:58
  85.3 9.7 %collective-permute-start.23 = (bf16[256,512]{1,0:T(8,128)(2,1)S(1)}, bf16[256,512]{1,0:T(8,128)(2,1)S(1)}, u32[]{:S(2)}, u32[]{:S(2)}) collective-permute-start(bf16[256,512]{1,0:T(8,128)(2,1)S(1)} %get-tuple-element.86), channel_id=1, source_target_pairs={{0,2},{1,3},{2,4},{3,5},{4,6},{5,7},{6,8},{7,9},{8,10},{9,11},{10,... | collective-permute-start | bytes 786440 | tf_op jit(solution)/shard_map/ppermute | solution.py:34
  85.6 9.4 %collective-permute-start.24 = (bf16[256,512]{1,0:T(8,128)(2,1)S(1)}, bf16[256,512]{1,0:T(8,128)(2,1)S(1)}, u32[]{:S(2)}, u32[]{:S(2)}) collective-permute-start(bf16[256,512]{1,0:T(8,128)(2,1)S(1)} %get-tuple-element.87), channel_id=1, source_target_pairs={{0,14},{1,15},{2,0},{3,1},{4,2},{5,3},{6,4},{7,5},{8,6},{9,7},{10,... | collective-permute-start | bytes 786440 | tf_op jit(solution)/shard_map/ppermute | solution.py:34
  88.8 11.4 %collective-permute-start.28 = (bf16[256,512]{1,0:T(8,128)(2,1)S(1)}, bf16[256,512]{1,0:T(8,128)(2,1)S(1)}, u32[]{:S(2)}, u32[]{:S(2)}) collective-permute-start(bf16[256,512]{1,0:T(8,128)(2,1)S(1)} %get-tuple-element.96), channel_id=1, source_target_pairs={{0,238},{1,239},{2,224},{3,225},{4,226},{5,227},{6,228},{7,229},{8... | collective-permute-start | bytes 786440 | tf_op jit(solution)/shard_map/ppermute | solution.py:58
  93.1 9.8 %collective-permute-start.27 = (bf16[256,512]{1,0:T(8,128)(2,1)S(1)}, bf16[256,512]{1,0:T(8,128)(2,1)S(1)}, u32[]{:S(2)}, u32[]{:S(2)}) collective-permute-start(bf16[256,512]{1,0:T(8,128)(2,1)S(1)} %get-tuple-element.89.refs_10_), channel_id=1, source_target_pairs={{0,226},{1,227},{2,228},{3,229},{4,230},{5,231},{6,232},{7,233},{8... | collective-permute-start | bytes 786440 | tf_op jit(solution)/shard_map/ppermute | solution.py:58
  94.9 8.0 %copy-start.2 = (f32[1,256,512]{2,1,0:T(8,128)S(1)}, f32[1,256,512]{2,1,0:T(8,128)}, u32[]{:S(2)}) copy-start(f32[1,256,512]{2,1,0:T(8,128)} %grad_weight_in.1) | copy-start | bytes 1572868
  94.9 8.0 %copy-start.4 = (f32[1,256]{1,0:T(1,128)S(1)}, f32[1,256]{1,0:T(1,128)}, u32[]{:S(2)}) copy-start(f32[1,256]{1,0:T(1,128)} %grad_gain_in.1) | copy-start | bytes 3076
  96.3 7.8 %collective-permute-start.25 = (bf16[256,512]{1,0:T(8,128)(2,1)S(1)}, bf16[256,512]{1,0:T(8,128)(2,1)S(1)}, u32[]{:S(2)}, u32[]{:S(2)}) collective-permute-start(bf16[256,512]{1,0:T(8,128)(2,1)S(1)} %get-tuple-element.93), channel_id=1, source_target_pairs={{0,1},{1,0},{2,3},{3,2},{4,5},{5,4},{6,7},{7,6},{8,9},{9,8},{10,11... | collective-permute-start | bytes 786440 | tf_op jit(solution)/shard_map/ppermute | solution.py:34
  96.4 7.7 %collective-permute-start.26 = (bf16[256,512]{1,0:T(8,128)(2,1)S(1)}, bf16[256,512]{1,0:T(8,128)(2,1)S(1)}, u32[]{:S(2)}, u32[]{:S(2)}) collective-permute-start(bf16[256,512]{1,0:T(8,128)(2,1)S(1)} %get-tuple-element.94), channel_id=1, source_target_pairs={{0,1},{1,0},{2,3},{3,2},{4,5},{5,4},{6,7},{7,6},{8,9},{9,8},{10,11... | collective-permute-start | bytes 786440 | tf_op jit(solution)/shard_map/ppermute | solution.py:34

commit v11 on v10

--- a/solution.py
+++ b/solution.py
@@ -12,8 +12,8 @@
 EPS = 1e-05
 BF16 = jnp.bfloat16
 F32 = jnp.float32
-OFFSETS = (4, 3, -3, 2, -2, 1, -1, 0)
-GROUPS = ((1,), (2, 2, 3))
+OFFSETS = (4, 3, -3, 2, -2, 0, 1, -1)
+GROUPS = ((1,), (2, 2, 1, 2))
 FIRST = sum(GROUPS[0])
 SWAPS = (2, 2, 2, 2)
 VMEM_LIMIT = 16 * 1024 * 1024
@@ -406,8 +406,8 @@
             else:
                 loads[ring] = [up, down]
             last = [loads[ring][0]]
-            if (step, ring) == (1, 0):
-                send_group(sends_2[2], 3, last)
+            if step == 1:
+                send_group(sends_2[2 + ring], 3 + ring, last)
 
     own = along_blk(own_part(mine[0]), -1, 0)
     sum_up, sum_down, layer_up, layer_down = nearest([*loads[0], *loads[1]], mine[1], mine[-1], width, [own])

time: 105 us -> 106 us (level)
  waiting for transfers between devices: 30.6 us -> 36.1 us
  starting transfers between devices: 51.8 us -> 47.1 us
    ppermute x24 -> x25, starting transfers between devices: 39.5 us -> 32 us  [move(): return lax.ppermute(value, ('x', 'z', 'core'), pairs)]
    ppermute x24 -> x25, waiting for transfers between devices: 18.6 us -> 25.4 us  [move(): return lax.ppermute(value, ('x', 'z', 'core'), pairs)]
    ppermute x5, starting transfers between devices: 12.3 us -> 15 us  [along_blk(): return lax.ppermute(value, ('blk', 'x', 'z', 'core'), pairs)]
    ppermute x5, waiting for transfers between devices: 12 us -> 10.8 us  [along_blk(): return lax.ppermute(value, ('blk', 'x', 'z', 'core'), pairs)]
  transfers between devices with their start and end apart: 29 -> 30, of which waited for: 13 -> 16; matrix products, arithmetic and copies ran while one was open for 0% -> 0% of each run, Pallas kernels for 13% -> 13%
where the time goes in v11:
time: 106 us
  starting transfers between devices  47.1 us (44%)
  waiting for transfers between devices  36.1 us (34%)
  Pallas kernels  20.5 us (19%)
  local copies, waits for them, and re-layouts  1.15 us (1%)
    ppermute x25, starting transfers between devices, move(): return lax.ppermute(value, ('x', 'z', 'core'), pairs)  32 us
    ppermute x25, waiting for transfers between devices, move(): return lax.ppermute(value, ('x', 'z', 'core'), pairs)  25.4 us
    ppermute x5, starting transfers between devices, along_blk(): return lax.ppermute(value, ('blk', 'x', 'z', 'core'), pairs)  15 us
    ppermute x5, waiting for transfers between devices, along_blk(): return lax.ppermute(value, ('blk', 'x', 'z', 'core'), pairs)  10.8 us
    pallas_call x3, Pallas kernels, project(): pl.pallas_call(functools.partial(project_kernel, tuple(weights), rows, bo...  6.49 us
    pallas_call x2, Pallas kernels, gradient(): pl.pallas_call(functools.partial(gradient_kernel, base, groups, width), i...  5.74 us
    pallas_call x1, Pallas kernels, prepare(): pl.pallas_call(functools.partial(prepare_kernel, width, steps), in_specs=...  5.12 us
  transfers between devices with their start and end apart: 30, of which 16 were waited for; matrix products, arithmetic and copies ran while one was open for 0% of the time, Pallas kernels for 13%

profile of v11, /device:TPU:4, one launch (start us, length us, event | category | flops | bytes accessed | tf_op | source)
XLA Modules:
  0.0 105.8 jit_solution(856398663242877154)
XLA Ops:
  0.9 1.0 copy-done.1
  1.9 5.1 %shard_map.85 = (bf16[512,8192]{1,0:T(8,128)(2,1)S(1)}, f32[512,1]{1,0:T(8,128)S(1)}, bf16[512,512]{1,0:T(8,128)(2,1)S(1)}, bf16[512,1536]{1,0:T(8,128)(2,1)S(1)...) custom-call(s32[16]{0:T(128)S(1)} %stack.67.table, ...), custom_call_target="tpu_custom_call" | custom-call | bytes 16777216 | tf_op jit(solution)/shard_map/pallas_call | solution.py:122
  7.1 0.5 collective-permute-start.1
  7.7 0.4 collective-permute-start.3
  8.3 0.6 collective-permute-start.7
  8.9 1.6 %collective-permute-done.refs_0_.refs_1_.refs_2_.refs_3_ = bf16[512,1536]{1,0:T(8,128)(2,1)S(1)} collective-permute-done((bf16[512,1536]{1,0:T(8,128)(2,1)S(1)}, bf16[512,1536]{1,0:T(8,128)(2,1)S(1)}, u32[]{:S(2)}, u32[]{:S(2)}) %collective-permute-start) | collective-permute-done | bytes 1572896 | tf_op jit(solution)/shard_map/ppermute | solution.py:34
  10.5 1.2 %collective-permute-start.4 = (bf16[256,512]{1,0:T(8,128)(2,1)S(1)}, bf16[256,512]{1,0:T(8,128)(2,1)S(1)}, u32[]{:S(2)}, u32[]{:S(2)}) collective-permute-start(bf16[256,512]{1,0:T(8,128)(2,1)S(1)} %shard_map.86), channel_id=1, source_target_pairs={{0,32},{1,33},{2,34},{3,35},{4,36},{5,37},{6,38},{7,39},{8,40},{9,... | collective-permute-start | bytes 786440 | tf_op jit(solution)/shard_map/ppermute | solution.py:58
  11.7 1.2 %shard_map.87 = (bf16[1,256,512]{2,1,0:T(8,128)(2,1)S(1)}, bf16[256,512]{1,0:T(8,128)(2,1)S(1)}) custom-call(s32[16]{0:T(128)S(1)} %stack.67.table, bf16[512,8192]{1,0:T(8,128)(2,1)S(1)} %get-tuple-element.52.hidden, bf16[512,512]{1,0:T(8,128)(2,1)S(1)} %get-tuple-element.57.cot_t.refs_4_, ...), custom_call_target="tpu_custom_call" | custom-call | bytes 512 | tf_op jit(solution)/shard_map/pallas_call | solution.py:164
  13.0 1.3 %collective-permute-start.5 = (bf16[1,256,512]{2,1,0:T(8,128)(2,1)S(1)}, bf16[1,256,512]{2,1,0:T(8,128)(2,1)S(1)}, u32[]{:S(2)}, u32[]{:S(2)}) collective-permute-start(bf16[1,256,512]{2,1,0:T(8,128)(2,1)S(1)} %get-tuple-element.59.refs_4_), channel_id=1, source_target_pairs={{0,16},{1,17},{2,18},{3,19},{4,20},{5,21},{6,22},{7,23},{8,24},{9,... | collective-permute-start | bytes 786440 | tf_op jit(solution)/shard_map/ppermute | solution.py:34
  14.3 0.8 collective-permute-done.3.refs_3_
  15.0 4.5 %shard_map.88 = (bf16[2,256,512]{2,1,0:T(8,128)(2,1)S(1)}, bf16[2,256,512]{2,1,0:T(8,128)(2,1)S(1)}, bf16[1,256,512]{2,1,0:T(8,128)(2,1)S(1)}, bf16[2,256,512]{2...) custom-call(s32[16]{0:T(128)S(1)} %stack.67.table, ...), custom_call_target="tpu_custom_call" | custom-call | bytes 512 | tf_op jit(solution)/shard_map/pallas_call | solution.py:164
  19.5 2.6 %collective-permute-done.7.refs_2_.refs_0_.refs_5_ = bf16[256,512]{1,0:T(8,128)(2,1)S(1)} collective-permute-done((bf16[256,512]{1,0:T(8,128)(2,1)S(1)}, bf16[256,512]{1,0:T(8,128)(2,1)S(1)}, u32[]{:S(2)}, u32[]{:S(2)}) %collective-permute-start.7) | collective-permute-done | bytes 262176 | tf_op jit(solution)/shard_map/ppermute | solution.py:58
  22.2 3.0 %collective-permute-done.4.refs_0_.refs_1_.refs_4_ = bf16[256,512]{1,0:T(8,128)(2,1)S(1)} collective-permute-done((bf16[256,512]{1,0:T(8,128)(2,1)S(1)}, bf16[256,512]{1,0:T(8,128)(2,1)S(1)}, u32[]{:S(2)}, u32[]{:S(2)}) %collective-permute-start.4) | collective-permute-done | bytes 262176 | tf_op jit(solution)/shard_map/ppermute | solution.py:58
  25.1 3.5 %collective-permute-start.8 = (bf16[2,256,512]{2,1,0:T(8,128)(2,1)S(1)}, bf16[2,256,512]{2,1,0:T(8,128)(2,1)S(1)}, u32[]{:S(2)}, u32[]{:S(2)}) collective-permute-start(bf16[2,256,512]{2,1,0:T(8,128)(2,1)S(1)} %shard_map.90), channel_id=1, source_target_pairs={{0,16},{1,17},{2,18},{3,19},{4,20},{5,21},{6,22},{7,23},{8,24},{9,... | collective-permute-start | bytes 1572872 | tf_op jit(solution)/shard_map/ppermute | solution.py:34
  28.7 0.7 collective-permute-start.6
  29.4 4.2 %collective-permute-start.9 = (bf16[320,512]{1,0:T(8,128)(2,1)S(1)}, bf16[320,512]{1,0:T(8,128)(2,1)S(1)}, u32[]{:S(2)}, u32[]{:S(2)}) collective-permute-start(bf16[320,512]{1,0:T(8,128)(2,1)S(1)} %get-tuple-element.64), channel_id=1, source_target_pairs={{0,14},{1,15},{2,0},{3,1},{4,2},{5,3},{6,4},{7,5},{8,6},{9,7},{10,... | collective-permute-start | bytes 983048 | tf_op jit(solution)/shard_map/ppermute | solution.py:34
  33.6 1.5 %collective-permute-start.11 = (bf16[2,256,512]{2,1,0:T(8,128)(2,1)S(1)}, bf16[2,256,512]{2,1,0:T(8,128)(2,1)S(1)}, u32[]{:S(2)}, u32[]{:S(2)}) collective-permute-start(bf16[2,256,512]{2,1,0:T(8,128)(2,1)S(1)} %shard_map.93), channel_id=1, source_target_pairs={{0,16},{1,17},{2,18},{3,19},{4,20},{5,21},{6,22},{7,23},{8,24},{9,... | collective-permute-start | bytes 1572872 | tf_op jit(solution)/shard_map/ppermute | solution.py:34
  35.1 1.8 %collective-permute-start.16 = (bf16[320,512]{1,0:T(8,128)(2,1)S(1)}, bf16[320,512]{1,0:T(8,128)(2,1)S(1)}, u32[]{:S(2)}, u32[]{:S(2)}) collective-permute-start(bf16[320,512]{1,0:T(8,128)(2,1)S(1)} %get-tuple-element.76), channel_id=1, source_target_pairs={{0,14},{1,15},{2,0},{3,1},{4,2},{5,3},{6,4},{7,5},{8,6},{9,7},{10,... | collective-permute-start | bytes 983048 | tf_op jit(solution)/shard_map/ppermute | solution.py:34
  36.9 3.2 %collective-permute-done.6.refs_0_.refs_6_ = bf16[320,512]{1,0:T(8,128)(2,1)S(1)} collective-permute-done((bf16[320,512]{1,0:T(8,128)(2,1)S(1)}, bf16[320,512]{1,0:T(8,128)(2,1)S(1)}, u32[]{:S(2)}, u32[]{:S(2)}) %collective-permute-start.6) | collective-permute-done | bytes 327712 | tf_op jit(solution)/shard_map/ppermute | solution.py:34
  40.1 1.6 %collective-permute-done.9.refs_3_.refs_8_ = bf16[320,512]{1,0:T(8,128)(2,1)S(1)} collective-permute-done((bf16[320,512]{1,0:T(8,128)(2,1)S(1)}, bf16[320,512]{1,0:T(8,128)(2,1)S(1)}, u32[]{:S(2)}, u32[]{:S(2)}) %collective-permute-start.9) | collective-permute-done | bytes 327712 | tf_op jit(solution)/shard_map/ppermute | solution.py:34
  41.9 5.7 %collective-permute-start.12 = (bf16[384,512]{1,0:T(8,128)(2,1)S(1)}, bf16[384,512]{1,0:T(8,128)(2,1)S(1)}, u32[]{:S(2)}, u32[]{:S(2)}) collective-permute-start(bf16[384,512]{1,0:T(8,128)(2,1)S(1)} %get-tuple-element.70), channel_id=1, source_target_pairs={{0,14},{1,15},{2,0},{3,1},{4,2},{5,3},{6,4},{7,5},{8,6},{9,7},{10,... | collective-permute-start | bytes 1179656 | tf_op jit(solution)/shard_map/ppermute | solution.py:34
  47.6 1.2 %collective-permute-done.16.refs_3_.refs_9_ = bf16[320,512]{1,0:T(8,128)(2,1)S(1)} collective-permute-done((bf16[320,512]{1,0:T(8,128)(2,1)S(1)}, bf16[320,512]{1,0:T(8,128)(2,1)S(1)}, u32[]{:S(2)}, u32[]{:S(2)}) %collective-permute-start.16) | collective-permute-done | bytes 327712 | tf_op jit(solution)/shard_map/ppermute | solution.py:34
  48.8 3.2 %collective-permute-done.15.refs_0_.refs_7_ = bf16[320,512]{1,0:T(8,128)(2,1)S(1)} collective-permute-done((bf16[320,512]{1,0:T(8,128)(2,1)S(1)}, bf16[320,512]{1,0:T(8,128)(2,1)S(1)}, u32[]{:S(2)}, u32[]{:S(2)}) %collective-permute-start.15) | collective-permute-done | bytes 327712 | tf_op jit(solution)/shard_map/ppermute | solution.py:34
  52.1 0.6 collective-permute-start.18
  52.7 1.5 %collective-permute-start.17 = (bf16[384,512]{1,0:T(8,128)(2,1)S(1)}, bf16[384,512]{1,0:T(8,128)(2,1)S(1)}, u32[]{:S(2)}, u32[]{:S(2)}) collective-permute-start(bf16[384,512]{1,0:T(8,128)(2,1)S(1)} %get-tuple-element.77.refs_1_), channel_id=1, source_target_pairs={{0,2},{1,3},{2,4},{3,5},{4,6},{5,7},{6,8},{7,9},{8,10},{9,11},{10,... | collective-permute-start | bytes 1179656 | tf_op jit(solution)/shard_map/ppermute | solution.py:34
  54.2 3.0 %collective-permute-done.12.refs_3_.refs_12_ = bf16[384,512]{1,0:T(8,128)(2,1)S(1)} collective-permute-done((bf16[384,512]{1,0:T(8,128)(2,1)S(1)}, bf16[384,512]{1,0:T(8,128)(2,1)S(1)}, u32[]{:S(2)}, u32[]{:S(2)}) %collective-permute-start.12) | collective-permute-done | bytes 393248 | tf_op jit(solution)/shard_map/ppermute | solution.py:34
  57.2 3.6 %collective-permute-done.10.refs_0_.refs_10_ = bf16[384,512]{1,0:T(8,128)(2,1)S(1)} collective-permute-done((bf16[384,512]{1,0:T(8,128)(2,1)S(1)}, bf16[384,512]{1,0:T(8,128)(2,1)S(1)}, u32[]{:S(2)}, u32[]{:S(2)}) %collective-permute-start.10) | collective-permute-done | bytes 393248 | tf_op jit(solution)/shard_map/ppermute | solution.py:34
  61.0 0.2 collective-permute-start.14
  61.1 2.1 %collective-permute-start.21 = (bf16[2,256,512]{2,1,0:T(8,128)(2,1)S(1)}, bf16[2,256,512]{2,1,0:T(8,128)(2,1)S(1)}, u32[]{:S(2)}, u32[]{:S(2)}) collective-permute-start(bf16[2,256,512]{2,1,0:T(8,128)(2,1)S(1)} %shard_map.100), channel_id=1, source_target_pairs={{0,16},{1,17},{2,18},{3,19},{4,20},{5,21},{6,22},{7,23},{8,24},{9,... | collective-permute-start | bytes 1572872 | tf_op jit(solution)/shard_map/ppermute | solution.py:34
  63.2 2.4 %collective-permute-done.18.refs_3_.refs_13_ = bf16[384,512]{1,0:T(8,128)(2,1)S(1)} collective-permute-done((bf16[384,512]{1,0:T(8,128)(2,1)S(1)}, bf16[384,512]{1,0:T(8,128)(2,1)S(1)}, u32[]{:S(2)}, u32[]{:S(2)}) %collective-permute-start.18) | collective-permute-done | bytes 393248 | tf_op jit(solution)/shard_map/ppermute | solution.py:34
  65.6 0.2 collective-permute-start.13
  65.8 0.3 collective-permute-done.17.refs_0_.refs_11_
  66.2 2.8 %collective-permute-start.19 = (bf16[384,512]{1,0:T(8,128)(2,1)S(1)}, bf16[384,512]{1,0:T(8,128)(2,1)S(1)}, u32[]{:S(2)}, u32[]{:S(2)}) collective-permute-start(bf16[384,512]{1,0:T(8,128)(2,1)S(1)} %get-tuple-element.79), channel_id=1, source_target_pairs={{0,2},{1,3},{2,4},{3,5},{4,6},{5,7},{6,8},{7,9},{8,10},{9,11},{10,... | collective-permute-start | bytes 1179656 | tf_op jit(solution)/shard_map/ppermute | solution.py:34
  69.0 0.6 collective-permute-start.20
  69.7 4.3 %collective-permute-done.14.refs_1_ = bf16[384,512]{1,0:T(8,128)(2,1)S(1)} collective-permute-done((bf16[384,512]{1,0:T(8,128)(2,1)S(1)}, bf16[384,512]{1,0:T(8,128)(2,1)S(1)}, u32[]{:S(2)}, u32[]{:S(2)}) %collective-permute-start.14) | collective-permute-done | bytes 393248 | tf_op jit(solution)/shard_map/ppermute | solution.py:34
  74.0 7.2 %collective-permute-start.23 = (bf16[256,512]{1,0:T(8,128)(2,1)S(1)}, bf16[256,512]{1,0:T(8,128)(2,1)S(1)}, u32[]{:S(2)}, u32[]{:S(2)}) collective-permute-start(bf16[256,512]{1,0:T(8,128)(2,1)S(1)} %shard_map.102), channel_id=1, source_target_pairs={{0,224},{1,225},{2,226},{3,227},{4,228},{5,229},{6,230},{7,231},{8... | collective-permute-start | bytes 786440 | tf_op jit(solution)/shard_map/ppermute | solution.py:58
  81.3 3.4 %shard_map.98 = (f32[512,512]{1,0:T(8,128)S(1)}, f32[512,512]{1,0:T(8,128)S(1)}) custom-call(s32[16]{0:T(128)S(1)} %stack.67.table, bf16[512,8192]{1,0:T(8,128)(2,1)S(1)} %get-tuple-element.52.hidden, bf16[512,1536]{1,0:T(8,128)(2,1)S(1)} %collective-permute-done.refs_0_.refs_1_.refs_2_.refs_3_, bf16[512,1024]{1,0:T(8,128)(2,1)S(1)} %collective-permute-done.1.refs_1_, ...), custom_call_target="tpu_custom_call" | custom-call | flops 2684354560 | tf_op jit(solution)/shard_map/pallas_call | solution.py:210
  84.7 0.4 collective-permute-done.23.refs_8_.own
  85.2 0.2 shard_map.103
  85.5 3.8 %collective-permute-start.25 = (bf16[256,512]{1,0:T(8,128)(2,1)S(1)}, bf16[256,512]{1,0:T(8,128)(2,1)S(1)}, u32[]{:S(2)}, u32[]{:S(2)}) collective-permute-start(bf16[256,512]{1,0:T(8,128)(2,1)S(1)} %get-tuple-element.89), channel_id=1, source_target_pairs={{0,14},{1,15},{2,0},{3,1},{4,2},{5,3},{6,4},{7,5},{8,6},{9,7},{10,... | collective-permute-start | bytes 786440 | tf_op jit(solution)/shard_map/ppermute | solution.py:34
  89.2 6.0 %collective-permute-start.29 = (bf16[256,512]{1,0:T(8,128)(2,1)S(1)}, bf16[256,512]{1,0:T(8,128)(2,1)S(1)}, u32[]{:S(2)}, u32[]{:S(2)}) collective-permute-start(bf16[256,512]{1,0:T(8,128)(2,1)S(1)} %get-tuple-element.98), channel_id=1, source_target_pairs={{0,238},{1,239},{2,224},{3,225},{4,226},{5,227},{6,228},{7,229},{8... | collective-permute-start | bytes 786440 | tf_op jit(solution)/shard_map/ppermute | solution.py:58
  95.2 1.8 %shard_map.104 = (f32[512,512]{1,0:T(8,128)S(1)}, f32[512,512]{1,0:T(8,128)S(1)}) custom-call(s32[16]{0:T(128)S(1)} %stack.67.table, bf16[512,8192]{1,0:T(8,128)(2,1)S(1)} %get-tuple-element.52.hidden, bf16[512,1536]{1,0:T(8,128)(2,1)S(1)} %collective-permute-done.refs_0_.refs_1_.refs_2_.refs_3_, bf16[512,1024]{1,0:T(8,128)(2,1)S(1)} %collective-permute-done.1.refs_1_, ...), custom_call_target="tpu_custom_call" | custom-call | flops 1073741824 | tf_op jit(solution)/shard_map/pallas_call | solution.py:210
  97.0 1.3 %shard_map.105 = (f32[512,512]{1,0:T(8,128)S(1)}, bf16[256,512]{1,0:T(8,128)(2,1)S(1)}, bf16[256,512]{1,0:T(8,128)(2,1)S(1)}) custom-call(s32[16]{0:T(128)S(1)} %stack.67.table, bf16[512,8192]{1,0:T(8,128)(2,1)S(1)} %get-tuple-element.52.hidden, bf16[512,1536]{1,0:T(8,128)(2,1)S(1)} %collective-permute-done.refs_0_.refs_1_.refs_2_.refs_3_, ...), custom_call_target="tpu_custom_call" | custom-call | flops 536870912 | tf_op jit(solution)/shard_map/pallas_call | solution.py:210
  98.4 0.5 collective-permute-start.27
  98.9 0.9 collective-permute-done.29.down
  99.8 3.9 %collective-permute-done.28.up = bf16[256,512]{1,0:T(8,128)(2,1)S(1)} collective-permute-done((bf16[256,512]{1,0:T(8,128)(2,1)S(1)}, bf16[256,512]{1,0:T(8,128)(2,1)S(1)}, u32[]{:S(2)}, u32[]{:S(2)}) %collective-permute-start.28) | collective-permute-done | bytes 262176 | tf_op jit(solution)/shard_map/ppermute | solution.py:58
  103.7 1.2 %shard_map.107 = (f32[1,256,512]{2,1,0:T(8,128)}, f32[1,256]{1,0:T(1,128)}) custom-call(bf16[256,512]{1,0:T(8,128)(2,1)S(1)} %collective-permute-done.23.refs_8_.own, bf16[256,512]{1,0:T(8,128)(2,1)S(1)} %collective-permute-done.28.up, bf16[256,512]{1,0:T(8,128)(2,1)S(1)} %collective-permute-done.29.down, bf16[1,256]{1,0:T(2,128)(2,1)S(1)} %copy-done.3, ...), custom_call_target="tpu_custom_call" | custom-call | tf_op jit(solution)/shard_map/pallas_call | solution.py:352
  104.8 1.0 shard_map.106
  (46 shorter events, 1.4 us)
Async XLA Ops:
  0.6 7.5 %copy-start = (bf16[1,256,512]{2,1,0:T(8,128)(2,1)S(1)}, bf16[1,256,512]{2,1,0:T(8,128)(2,1)}, u32[]{:S(2)}) copy-start(bf16[1,256,512]{2,1,0:T(8,128)(2,1)} %weight.3) | copy-start | bytes 786436
  0.6 7.5 %copy-start.3 = (bf16[1,256]{1,0:T(2,128)(2,1)S(1)}, bf16[1,256]{1,0:T(2,128)(2,1)}, u32[]{:S(2)}) copy-start(bf16[1,256]{1,0:T(2,128)(2,1)} %gain.3) | copy-start | bytes 1540
  0.9 1.0 copy-start.1
  7.0 3.5 %collective-permute-start = (bf16[512,1536]{1,0:T(8,128)(2,1)S(1)}, bf16[512,1536]{1,0:T(8,128)(2,1)S(1)}, u32[]{:S(2)}, u32[]{:S(2)}) collective-permute-start(bf16[512,1536]{1,0:T(8,128)(2,1)S(1)} %get-tuple-element.53), channel_id=1, source_target_pairs={{0,1},{1,0},{2,3},{3,2},{4,5},{5,4},{6,7},{7,6},{8,9},{9,8},{10,11... | collective-permute-start | bytes 4718600 | tf_op jit(solution)/shard_map/ppermute | solution.py:34
  7.1 5.8 %collective-permute-start.1 = (bf16[512,1024]{1,0:T(8,128)(2,1)S(1)}, bf16[512,1024]{1,0:T(8,128)(2,1)S(1)}, u32[]{:S(2)}, u32[]{:S(2)}) collective-permute-start(bf16[512,1024]{1,0:T(8,128)(2,1)S(1)} %get-tuple-element.54), channel_id=1, source_target_pairs={{0,1},{1,0},{2,3},{3,2},{4,5},{5,4},{6,7},{7,6},{8,9},{9,8},{10,11... | collective-permute-start | bytes 3145736 | tf_op jit(solution)/shard_map/ppermute | solution.py:34
  7.6 6.6 %collective-permute-start.2 = (bf16[512,1024]{1,0:T(8,128)(2,1)S(1)}, bf16[512,1024]{1,0:T(8,128)(2,1)S(1)}, u32[]{:S(2)}, u32[]{:S(2)}) collective-permute-start(bf16[512,1024]{1,0:T(8,128)(2,1)S(1)} %get-tuple-element.55), channel_id=1, source_target_pairs={{0,1},{1,0},{2,3},{3,2},{4,5},{5,4},{6,7},{7,6},{8,9},{9,8},{10,11... | collective-permute-start | bytes 3145736 | tf_op jit(solution)/shard_map/ppermute | solution.py:34
  7.7 7.3 %collective-permute-start.3 = (bf16[512,1024]{1,0:T(8,128)(2,1)S(1)}, bf16[512,1024]{1,0:T(8,128)(2,1)S(1)}, u32[]{:S(2)}, u32[]{:S(2)}) collective-permute-start(bf16[512,1024]{1,0:T(8,128)(2,1)S(1)} %get-tuple-element.56), channel_id=1, source_target_pairs={{0,1},{1,0},{2,3},{3,2},{4,5},{5,4},{6,7},{7,6},{8,9},{9,8},{10,11... | collective-permute-start | bytes 3145736 | tf_op jit(solution)/shard_map/ppermute | solution.py:34
  8.3 13.9 %collective-permute-start.7 = (bf16[256,512]{1,0:T(8,128)(2,1)S(1)}, bf16[256,512]{1,0:T(8,128)(2,1)S(1)}, u32[]{:S(2)}, u32[]{:S(2)}) collective-permute-start(bf16[256,512]{1,0:T(8,128)(2,1)S(1)} %shard_map.86), channel_id=1, source_target_pairs={{0,48},{1,49},{2,50},{3,51},{4,52},{5,53},{6,54},{7,55},{8,56},{9,... | collective-permute-start | bytes 786440 | tf_op jit(solution)/shard_map/ppermute | solution.py:58
  10.5 14.6 %collective-permute-start.4 = (bf16[256,512]{1,0:T(8,128)(2,1)S(1)}, bf16[256,512]{1,0:T(8,128)(2,1)S(1)}, u32[]{:S(2)}, u32[]{:S(2)}) collective-permute-start(bf16[256,512]{1,0:T(8,128)(2,1)S(1)} %shard_map.86), channel_id=1, source_target_pairs={{0,32},{1,33},{2,34},{3,35},{4,36},{5,37},{6,38},{7,39},{8,40},{9,... | collective-permute-start | bytes 786440 | tf_op jit(solution)/shard_map/ppermute | solution.py:58
  13.0 12.2 %collective-permute-start.5 = (bf16[1,256,512]{2,1,0:T(8,128)(2,1)S(1)}, bf16[1,256,512]{2,1,0:T(8,128)(2,1)S(1)}, u32[]{:S(2)}, u32[]{:S(2)}) collective-permute-start(bf16[1,256,512]{2,1,0:T(8,128)(2,1)S(1)} %get-tuple-element.59.refs_4_), channel_id=1, source_target_pairs={{0,16},{1,17},{2,18},{3,19},{4,20},{5,21},{6,22},{7,23},{8,24},{9,... | collective-permute-start | bytes 786440 | tf_op jit(solution)/shard_map/ppermute | solution.py:34
  25.1 16.6 %collective-permute-start.8 = (bf16[2,256,512]{2,1,0:T(8,128)(2,1)S(1)}, bf16[2,256,512]{2,1,0:T(8,128)(2,1)S(1)}, u32[]{:S(2)}, u32[]{:S(2)}) collective-permute-start(bf16[2,256,512]{2,1,0:T(8,128)(2,1)S(1)} %shard_map.90), channel_id=1, source_target_pairs={{0,16},{1,17},{2,18},{3,19},{4,20},{5,21},{6,22},{7,23},{8,24},{9,... | collective-permute-start | bytes 1572872 | tf_op jit(solution)/shard_map/ppermute | solution.py:34
  28.7 11.4 %collective-permute-start.6 = (bf16[320,512]{1,0:T(8,128)(2,1)S(1)}, bf16[320,512]{1,0:T(8,128)(2,1)S(1)}, u32[]{:S(2)}, u32[]{:S(2)}) collective-permute-start(bf16[320,512]{1,0:T(8,128)(2,1)S(1)} %get-tuple-element.61), channel_id=1, source_target_pairs={{0,2},{1,3},{2,4},{3,5},{4,6},{5,7},{6,8},{7,9},{8,10},{9,11},{10,... | collective-permute-start | bytes 983048 | tf_op jit(solution)/shard_map/ppermute | solution.py:34
  29.4 12.4 %collective-permute-start.9 = (bf16[320,512]{1,0:T(8,128)(2,1)S(1)}, bf16[320,512]{1,0:T(8,128)(2,1)S(1)}, u32[]{:S(2)}, u32[]{:S(2)}) collective-permute-start(bf16[320,512]{1,0:T(8,128)(2,1)S(1)} %get-tuple-element.64), channel_id=1, source_target_pairs={{0,14},{1,15},{2,0},{3,1},{4,2},{5,3},{6,4},{7,5},{8,6},{9,7},{10,... | collective-permute-start | bytes 983048 | tf_op jit(solution)/shard_map/ppermute | solution.py:34
  33.6 20.6 %collective-permute-start.11 = (bf16[2,256,512]{2,1,0:T(8,128)(2,1)S(1)}, bf16[2,256,512]{2,1,0:T(8,128)(2,1)S(1)}, u32[]{:S(2)}, u32[]{:S(2)}) collective-permute-start(bf16[2,256,512]{2,1,0:T(8,128)(2,1)S(1)} %shard_map.93), channel_id=1, source_target_pairs={{0,16},{1,17},{2,18},{3,19},{4,20},{5,21},{6,22},{7,23},{8,24},{9,... | collective-permute-start | bytes 1572872 | tf_op jit(solution)/shard_map/ppermute | solution.py:34
  35.1 13.7 %collective-permute-start.16 = (bf16[320,512]{1,0:T(8,128)(2,1)S(1)}, bf16[320,512]{1,0:T(8,128)(2,1)S(1)}, u32[]{:S(2)}, u32[]{:S(2)}) collective-permute-start(bf16[320,512]{1,0:T(8,128)(2,1)S(1)} %get-tuple-element.76), channel_id=1, source_target_pairs={{0,14},{1,15},{2,0},{3,1},{4,2},{5,3},{6,4},{7,5},{8,6},{9,7},{10,... | collective-permute-start | bytes 983048 | tf_op jit(solution)/shard_map/ppermute | solution.py:34
  40.1 11.9 %collective-permute-start.15 = (bf16[320,512]{1,0:T(8,128)(2,1)S(1)}, bf16[320,512]{1,0:T(8,128)(2,1)S(1)}, u32[]{:S(2)}, u32[]{:S(2)}) collective-permute-start(bf16[320,512]{1,0:T(8,128)(2,1)S(1)} %get-tuple-element.66.refs_6_.refs_1_), channel_id=1, source_target_pairs={{0,2},{1,3},{2,4},{3,5},{4,6},{5,7},{6,8},{7,9},{8,10},{9,11},{10,... | collective-permute-start | bytes 983048 | tf_op jit(solution)/shard_map/ppermute | solution.py:34
  41.9 15.3 %collective-permute-start.12 = (bf16[384,512]{1,0:T(8,128)(2,1)S(1)}, bf16[384,512]{1,0:T(8,128)(2,1)S(1)}, u32[]{:S(2)}, u32[]{:S(2)}) collective-permute-start(bf16[384,512]{1,0:T(8,128)(2,1)S(1)} %get-tuple-element.70), channel_id=1, source_target_pairs={{0,14},{1,15},{2,0},{3,1},{4,2},{5,3},{6,4},{7,5},{8,6},{9,7},{10,... | collective-permute-start | bytes 1179656 | tf_op jit(solution)/shard_map/ppermute | solution.py:34
  47.6 13.3 %collective-permute-start.10 = (bf16[384,512]{1,0:T(8,128)(2,1)S(1)}, bf16[384,512]{1,0:T(8,128)(2,1)S(1)}, u32[]{:S(2)}, u32[]{:S(2)}) collective-permute-start(bf16[384,512]{1,0:T(8,128)(2,1)S(1)} %get-tuple-element.67.refs_6_.refs_1_), channel_id=1, source_target_pairs={{0,2},{1,3},{2,4},{3,5},{4,6},{5,7},{6,8},{7,9},{8,10},{9,11},{10,... | collective-permute-start | bytes 1179656 | tf_op jit(solution)/shard_map/ppermute | solution.py:34
  52.1 13.5 %collective-permute-start.18 = (bf16[384,512]{1,0:T(8,128)(2,1)S(1)}, bf16[384,512]{1,0:T(8,128)(2,1)S(1)}, u32[]{:S(2)}, u32[]{:S(2)}) collective-permute-start(bf16[384,512]{1,0:T(8,128)(2,1)S(1)} %get-tuple-element.78), channel_id=1, source_target_pairs={{0,14},{1,15},{2,0},{3,1},{4,2},{5,3},{6,4},{7,5},{8,6},{9,7},{10,... | collective-permute-start | bytes 1179656 | tf_op jit(solution)/shard_map/ppermute | solution.py:34
  52.7 13.4 %collective-permute-start.17 = (bf16[384,512]{1,0:T(8,128)(2,1)S(1)}, bf16[384,512]{1,0:T(8,128)(2,1)S(1)}, u32[]{:S(2)}, u32[]{:S(2)}) collective-permute-start(bf16[384,512]{1,0:T(8,128)(2,1)S(1)} %get-tuple-element.77.refs_1_), channel_id=1, source_target_pairs={{0,2},{1,3},{2,4},{3,5},{4,6},{5,7},{6,8},{7,9},{8,10},{9,11},{10,... | collective-permute-start | bytes 1179656 | tf_op jit(solution)/shard_map/ppermute | solution.py:34
  54.2 14.8 %collective-permute-start.22 = (bf16[1,256,512]{2,1,0:T(8,128)(2,1)S(1)}, bf16[1,256,512]{2,1,0:T(8,128)(2,1)S(1)}, u32[]{:S(2)}, u32[]{:S(2)}) collective-permute-start(bf16[1,256,512]{2,1,0:T(8,128)(2,1)S(1)} %shard_map.101), channel_id=1, source_target_pairs={{0,16},{1,17},{2,18},{3,19},{4,20},{5,21},{6,22},{7,23},{8,24},{9,... | collective-permute-start | bytes 786440 | tf_op jit(solution)/shard_map/ppermute | solution.py:34
  61.0 13.1 %collective-permute-start.14 = (bf16[384,512]{1,0:T(8,128)(2,1)S(1)}, bf16[384,512]{1,0:T(8,128)(2,1)S(1)}, u32[]{:S(2)}, u32[]{:S(2)}) collective-permute-start(bf16[384,512]{1,0:T(8,128)(2,1)S(1)} %get-tuple-element.73), channel_id=1, source_target_pairs={{0,14},{1,15},{2,0},{3,1},{4,2},{5,3},{6,4},{7,5},{8,6},{9,7},{10,... | collective-permute-start | bytes 1179656 | tf_op jit(solution)/shard_map/ppermute | solution.py:34
  61.1 24.0 %collective-permute-start.21 = (bf16[2,256,512]{2,1,0:T(8,128)(2,1)S(1)}, bf16[2,256,512]{2,1,0:T(8,128)(2,1)S(1)}, u32[]{:S(2)}, u32[]{:S(2)}) collective-permute-start(bf16[2,256,512]{2,1,0:T(8,128)(2,1)S(1)} %shard_map.100), channel_id=1, source_target_pairs={{0,16},{1,17},{2,18},{3,19},{4,20},{5,21},{6,22},{7,23},{8,24},{9,... | collective-permute-start | bytes 1572872 | tf_op jit(solution)/shard_map/ppermute | solution.py:34
  65.6 19.1 %collective-permute-start.13 = (bf16[384,512]{1,0:T(8,128)(2,1)S(1)}, bf16[384,512]{1,0:T(8,128)(2,1)S(1)}, u32[]{:S(2)}, u32[]{:S(2)}) collective-permute-start(bf16[384,512]{1,0:T(8,128)(2,1)S(1)} %get-tuple-element.72.refs_6_), channel_id=1, source_target_pairs={{0,2},{1,3},{2,4},{3,5},{4,6},{5,7},{6,8},{7,9},{8,10},{9,11},{10,... | collective-permute-start | bytes 1179656 | tf_op jit(solution)/shard_map/ppermute | solution.py:34
  66.2 18.5 %collective-permute-start.19 = (bf16[384,512]{1,0:T(8,128)(2,1)S(1)}, bf16[384,512]{1,0:T(8,128)(2,1)S(1)}, u32[]{:S(2)}, u32[]{:S(2)}) collective-permute-start(bf16[384,512]{1,0:T(8,128)(2,1)S(1)} %get-tuple-element.79), channel_id=1, source_target_pairs={{0,2},{1,3},{2,4},{3,5},{4,6},{5,7},{6,8},{7,9},{8,10},{9,11},{10,... | collective-permute-start | bytes 1179656 | tf_op jit(solution)/shard_map/ppermute | solution.py:34
  69.0 15.7 %collective-permute-start.20 = (bf16[384,512]{1,0:T(8,128)(2,1)S(1)}, bf16[384,512]{1,0:T(8,128)(2,1)S(1)}, u32[]{:S(2)}, u32[]{:S(2)}) collective-permute-start(bf16[384,512]{1,0:T(8,128)(2,1)S(1)} %get-tuple-element.80), channel_id=1, source_target_pairs={{0,14},{1,15},{2,0},{3,1},{4,2},{5,3},{6,4},{7,5},{8,6},{9,7},{10,... | collective-permute-start | bytes 1179656 | tf_op jit(solution)/shard_map/ppermute | solution.py:34
  74.0 11.1 %collective-permute-start.23 = (bf16[256,512]{1,0:T(8,128)(2,1)S(1)}, bf16[256,512]{1,0:T(8,128)(2,1)S(1)}, u32[]{:S(2)}, u32[]{:S(2)}) collective-permute-start(bf16[256,512]{1,0:T(8,128)(2,1)S(1)} %shard_map.102), channel_id=1, source_target_pairs={{0,224},{1,225},{2,226},{3,227},{4,228},{5,229},{6,230},{7,231},{8... | collective-permute-start | bytes 786440 | tf_op jit(solution)/shard_map/ppermute | solution.py:58
  85.4 11.7 %collective-permute-start.24 = (bf16[256,512]{1,0:T(8,128)(2,1)S(1)}, bf16[256,512]{1,0:T(8,128)(2,1)S(1)}, u32[]{:S(2)}, u32[]{:S(2)}) collective-permute-start(bf16[256,512]{1,0:T(8,128)(2,1)S(1)} %get-tuple-element.88), channel_id=1, source_target_pairs={{0,2},{1,3},{2,4},{3,5},{4,6},{5,7},{6,8},{7,9},{8,10},{9,11},{10,... | collective-permute-start | bytes 786440 | tf_op jit(solution)/shard_map/ppermute | solution.py:34
  85.5 11.6 %collective-permute-start.25 = (bf16[256,512]{1,0:T(8,128)(2,1)S(1)}, bf16[256,512]{1,0:T(8,128)(2,1)S(1)}, u32[]{:S(2)}, u32[]{:S(2)}) collective-permute-start(bf16[256,512]{1,0:T(8,128)(2,1)S(1)} %get-tuple-element.89), channel_id=1, source_target_pairs={{0,14},{1,15},{2,0},{3,1},{4,2},{5,3},{6,4},{7,5},{8,6},{9,7},{10,... | collective-permute-start | bytes 786440 | tf_op jit(solution)/shard_map/ppermute | solution.py:34
  89.2 10.6 %collective-permute-start.29 = (bf16[256,512]{1,0:T(8,128)(2,1)S(1)}, bf16[256,512]{1,0:T(8,128)(2,1)S(1)}, u32[]{:S(2)}, u32[]{:S(2)}) collective-permute-start(bf16[256,512]{1,0:T(8,128)(2,1)S(1)} %get-tuple-element.98), channel_id=1, source_target_pairs={{0,238},{1,239},{2,224},{3,225},{4,226},{5,227},{6,228},{7,229},{8... | collective-permute-start | bytes 786440 | tf_op jit(solution)/shard_map/ppermute | solution.py:58
  95.2 8.5 %collective-permute-start.28 = (bf16[256,512]{1,0:T(8,128)(2,1)S(1)}, bf16[256,512]{1,0:T(8,128)(2,1)S(1)}, u32[]{:S(2)}, u32[]{:S(2)}) collective-permute-start(bf16[256,512]{1,0:T(8,128)(2,1)S(1)} %get-tuple-element.91.refs_10_), channel_id=1, source_target_pairs={{0,226},{1,227},{2,228},{3,229},{4,230},{5,231},{6,232},{7,233},{8... | collective-permute-start | bytes 786440 | tf_op jit(solution)/shard_map/ppermute | solution.py:58
  97.0 6.7 %copy-start.2 = (f32[1,256,512]{2,1,0:T(8,128)S(1)}, f32[1,256,512]{2,1,0:T(8,128)}, u32[]{:S(2)}) copy-start(f32[1,256,512]{2,1,0:T(8,128)} %grad_weight_in.1) | copy-start | bytes 1572868
  97.0 6.7 %copy-start.4 = (f32[1,256]{1,0:T(1,128)S(1)}, f32[1,256]{1,0:T(1,128)}, u32[]{:S(2)}) copy-start(f32[1,256]{1,0:T(1,128)} %grad_gain_in.1) | copy-start | bytes 3076
  98.3 6.5 %collective-permute-start.26 = (bf16[256,512]{1,0:T(8,128)(2,1)S(1)}, bf16[256,512]{1,0:T(8,128)(2,1)S(1)}, u32[]{:S(2)}, u32[]{:S(2)}) collective-permute-start(bf16[256,512]{1,0:T(8,128)(2,1)S(1)} %get-tuple-element.95), channel_id=1, source_target_pairs={{0,1},{1,0},{2,3},{3,2},{4,5},{5,4},{6,7},{7,6},{8,9},{9,8},{10,11... | collective-permute-start | bytes 786440 | tf_op jit(solution)/shard_map/ppermute | solution.py:34
  98.4 6.4 %collective-permute-start.27 = (bf16[256,512]{1,0:T(8,128)(2,1)S(1)}, bf16[256,512]{1,0:T(8,128)(2,1)S(1)}, u32[]{:S(2)}, u32[]{:S(2)}) collective-permute-start(bf16[256,512]{1,0:T(8,128)(2,1)S(1)} %get-tuple-element.96), channel_id=1, source_target_pairs={{0,1},{1,0},{2,3},{3,2},{4,5},{5,4},{6,7},{7,6},{8,9},{9,8},{10,11... | collective-permute-start | bytes 786440 | tf_op jit(solution)/shard_map/ppermute | solution.py:34
